TPU v7x, 32 devices: a whole 2x2x4 slice. The times are simulated.
32 devices in a mesh: row: 4 (over z), col: 8 (over y, x, core).
Axes of the slice: x: 2, y: 2, z: 4, core: 2. Of those that a mesh axis runs over, the one named last changes fastest.
Arguments:
- initial_voltage: float32 [4, 16, 128, 128], P('row', 'col'), may hold values from -6 to 6
- inject: float32 [4, 16, 128, 128], P('row', 'col'), may hold values from -6 to 6
- conduct: float32 [4, 16, 128, 128], P('row', 'col'), as said below
- capacitance: float32 [4, 16, 128], P('row', 'col'), may hold values from 1 to 4
- track_gain: float32 [4, 16, 2, 32], P('row', 'col'), may hold values from 0.3 to 3
- driver_tile: int32 [4, 8, 64], P('row', 'col'), may hold values from 0 to 1
- sink_net: int32 [4, 8, 8, 8], P('row', 'col'), may hold values from 0 to 63
- sink_count: int32 [4, 8, 8], P('row', 'col'), may hold values from 0 to 8, as said below
- sink_tile: int32 [4, 8, 8, 8], P('row', 'col'), may hold values from 0 to 1
- sink_node: int32 [4, 8, 8, 8], P('row', 'col'), may hold values from 0 to 127
- sink_gain: float32 [4, 8, 8, 8], P('row', 'col'), may hold values from 0.5 to 2
Outputs:
- voltage: float32 [4, 16, 128, 128], P('row', 'col')
Inputs may be any that keep to these rules, and one draw needn't show every extreme that they name: Slots k >= sink_count[d, s] are ignored; some receiving device takes all 8 slots from some source device in every draw. `conduct`: each tile's block is symmetric with non-positive entries off the diagonal and rows summing to zero.
All inputs are finite; a program needn't handle non-finite values.
Results may differ from a plain program's by a relative error of at most 0.0001.
Values sent between devices are 32-bit elements; how exact they have to be, the bound alone decides.
No kernel may reach another device: no remote copies, remote signals or barrier semaphores. Data moves between devices by JAX's collectives and lax.ppermute only.
A program may use at most 64 MiB of HBM per device.

v0:
```python
import jax
import jax.numpy as jnp
from jax import lax
from jax.sharding import PartitionSpec as P

ITERS = 3


PRECISE = lax.Precision.HIGHEST


def padded_2(block, sides, width):
    for axis, dim in sides:
        count = lax.axis_size(axis)
        forward = [(i, i + 1) for i in range(count - 1)]
        backward = [(target, source) for source, target in forward]
        low = lax.ppermute(
            lax.slice_in_dim(block, block.shape[dim] - width, None, axis=dim), axis, forward
        )
        high = lax.ppermute(lax.slice_in_dim(block, 0, width, axis=dim), axis, backward)
        block = jnp.concatenate([low, block, high], axis=dim)
    return block


def shifted(block, axis, distance):
    devices = range(lax.axis_size(axis))
    route = [(i - distance, i) for i in devices if i - distance in devices]
    return lax.ppermute(block, axis, route)


def tile_inverse(conduct, capacitance):
    node_count = conduct.shape[-1]
    identity = jnp.eye(node_count, dtype=jnp.float32)
    whole_block = conduct + capacitance[..., None] * identity
    flat_blocks = whole_block.reshape((-1, node_count, node_count))
    factors = jnp.linalg.cholesky(flat_blocks)
    inverse = jax.vmap(lambda factor: jax.scipy.linalg.cho_solve((factor, True), identity))(factors)
    return inverse.reshape(whole_block.shape)


def apply_grid(voltage, conduct, capacitance, track_pad):
    edge_count = track_pad.shape[-1]
    inner_part = (
        jnp.einsum("rcij,rcjp->rcip", conduct, voltage, precision=PRECISE)
        + capacitance[..., None] * voltage
    )
    rim_cells = voltage[:, :, :edge_count, :]
    padded = padded_2(rim_cells, (("row", 0), ("col", 1)), 1)
    east_gain = track_pad[1:-1, 1:-1, 0][..., None]
    west_gain = track_pad[1:-1, :-2, 0][..., None]
    south_gain = track_pad[1:-1, 1:-1, 1][..., None]
    north_gain = track_pad[:-2, 1:-1, 1][..., None]
    track_flow = east_gain * (rim_cells - padded[1:-1, 2:]) + west_gain * (
        rim_cells - padded[1:-1, :-2]
    )
    track_flow = (
        track_flow
        + south_gain * (rim_cells - padded[2:, 1:-1])
        + north_gain * (rim_cells - padded[:-2, 1:-1])
    )
    return jnp.concatenate(
        [inner_part[:, :, :edge_count] + track_flow, inner_part[:, :, edge_count:]], axis=2
    )


def precondition(inverse, residual):
    return jnp.einsum("rcij,rcjp->rcip", inverse, residual, precision=PRECISE)


def inner_sum(left_vec, right_vec):
    return jnp.sum(left_vec * right_vec, axis=(0, 1, 2))


def residual_product(residual, precond):
    return lax.psum(inner_sum(residual, precond), ("row", "col"))


def solve_separate(right_side, initial, conduct, capacitance, track_pad, inverse):
    solution = initial
    residual = right_side - apply_grid(initial, conduct, capacitance, track_pad)
    precond = precondition(inverse, residual)
    direction = precond
    rz_now = residual_product(residual, precond)
    for sweep_idx in range(ITERS):
        applied = apply_grid(direction, conduct, capacitance, track_pad)
        curvature = lax.psum(inner_sum(direction, applied), ("row", "col"))
        step_size = rz_now / curvature
        solution = solution + step_size * direction
        residual = residual - step_size * applied
        precond = precondition(inverse, residual)
        rz_fresh = residual_product(residual, precond)
        direction = precond + rz_fresh / rz_now * direction
        rz_now = rz_fresh
    return solution


def driver_voltage(voltage, driver_tile):
    node_count = voltage.shape[2]
    flat_field = voltage.reshape((-1, voltage.shape[3]))
    net_count = driver_tile.shape[-1]
    row_index = (
        driver_tile.reshape(-1) * node_count + jnp.arange(net_count, dtype=jnp.int32) % node_count
    )
    return jnp.take(flat_field, row_index, axis=0)


def sink_current(values, sink_tile, sink_node, sink_gain, sink_count, node_count, tile_count):
    source_count, slot_count, pattern_count = values.shape
    live_slot = jnp.arange(slot_count, dtype=jnp.int32)[None, :] < sink_count.reshape(
        (source_count, 1)
    )
    weight = jnp.where(live_slot, sink_gain.reshape((source_count, slot_count)), jnp.float32(0.0))
    row_index = (sink_tile * node_count + sink_node).reshape(-1)
    scaled = (values * weight[..., None]).reshape((-1, pattern_count))
    injected = jnp.zeros((tile_count * node_count, pattern_count), jnp.float32)
    return injected.at[row_index].add(scaled)


def lower_rims(track_gain):
    west_piece = shifted(track_gain[:, -1:, 0, :], "col", 1)
    north_piece = shifted(track_gain[-1:, :, 1, :], "row", 1)
    track_pad = jnp.pad(track_gain, ((1, 1), (1, 1), (0, 0), (0, 0)))
    track_pad = track_pad.at[1:-1, 0, 0].set(west_piece[:, 0])
    return track_pad.at[0, 1:-1, 1].set(north_piece[0])


def local(
    initial_voltage,
    inject,
    conduct,
    capacitance,
    track_gain,
    driver_tile,
    sink_net,
    sink_count,
    sink_tile,
    sink_node,
    sink_gain,
):
    inverse = tile_inverse(conduct, capacitance)
    track_pad = lower_rims(track_gain)
    col_count = lax.axis_size("col")
    net_count = driver_tile.shape[-1]
    pattern_count = initial_voltage.shape[3]
    node_count = initial_voltage.shape[2]
    tile_count = initial_voltage.shape[0] * initial_voltage.shape[1]
    wanted = sink_net.reshape((sink_net.shape[2], sink_net.shape[3]))
    voltage = initial_voltage
    drivers = driver_voltage(voltage, driver_tile)
    gathered = lax.all_gather(drivers, "col", axis=0, tiled=True)
    offsets = jnp.arange(col_count, dtype=jnp.int32)[:, None] * net_count
    values = jnp.take(gathered, (wanted + offsets).reshape(-1), axis=0).reshape(
        wanted.shape + (pattern_count,)
    )
    injected = sink_current(
        values, sink_tile, sink_node, sink_gain, sink_count, node_count, tile_count
    )
    right_side = capacitance[..., None] * voltage + inject + injected.reshape(voltage.shape)
    voltage = solve_separate(right_side, voltage, conduct, capacitance, track_pad, inverse)
    return voltage


def solution(mesh):
    placed = (
        P("row", "col", None, None),
        P("row", "col", None, None),
        P("row", "col", None, None),
        P("row", "col", None),
        P("row", "col", None, None),
        P("row", "col", None),
        P("row", "col", None, None),
        P("row", "col", None),
        P("row", "col", None, None),
        P("row", "col", None, None),
        P("row", "col", None, None),
    )
    return jax.shard_map(
        local, mesh=mesh, in_specs=placed, out_specs=P("row", "col", None, None), check_vma=False
    )
```

profile of v0, /device:TPU:0, one launch (start us, length us, event | category | flops | bytes accessed | tf_op | source)
XLA Modules:
  0.0 342.8 jit_solution(16583133549726038812)
XLA Ops:
  0.0 1.0 copy.138
  1.0 4.9 %collective-permute-start.1 = (f32[1,2,32,128]{2,3,1,0:T(8,128)S(1)}, f32[1,2,32,128]{2,3,1,0:T(8,128)S(1)}, u32[]{:S(2)}, u32[]{:S(2)}) collective-permute-start(f32[1,2,32,128]{2,3,1,0:T(8,128)S(1)} %bitcast.152), channel_id=1, source_target_pairs={{0,8},{8,16},{16,24},{1,9},{9,17},{17,25},{2,10},{10,18},{18,26},{... | collective-permute-start | bytes 98312 | tf_op jit(solution)/shard_map/ppermute | solution.py:17
  6.0 1.3 collective-permute-start.2
  7.3 1.5 collective-permute-start
  8.8 4.5 %collective-permute-start.5 = (f32[1,2,32]{2,1,0:T(2,128)S(1)}, f32[1,2,32]{2,1,0:T(2,128)S(1)}, u32[]{:S(2)}, u32[]{:S(2)}) collective-permute-start(f32[1,2,32]{2,1,0:T(2,128)S(1)} %bitcast.185), channel_id=1, source_target_pairs={{0,8},{8,16},{16,24},{1,9},{9,17},{17,25},{2,10},{10,18},{18,26},{... | collective-permute-start | bytes 776 | tf_op jit(solution)/shard_map/ppermute | solution.py:28
  13.6 0.5 copy-done.4
  14.3 0.6 copy-done.9
  15.1 0.8 copy-done.1
  16.4 0.6 copy-done.6
  17.2 0.6 copy-done.10
  18.0 0.6 gather_fusion
  18.7 10.0 %all_gather.3 = f32[512,128]{1,0:T(8,128)S(1)} all-gather(f32[64,128]{1,0:T(8,128)S(1)} %broadcast_select_fusion), channel_id=1, replica_groups=mesh['row'=4,'col'=8] {'col'}, dimensions={0}, use_global_device_ids=true | all-gather | bytes 294912 | tf_op jit(solution)/shard_map/all_gather | solution.py:150
  28.6 1.1 scatter_custom_fusion
  29.9 0.8 copy-done.2
  31.1 1.3 collective-permute-start.3
  32.4 3.0 collective-permute-start.4
  35.4 0.8 collective-permute-done.4
  36.8 23.5 %custom-call.11 = f32[2,128,128]{2,1,0:T(8,128)S(1)} custom-call(f32[2,128,128]{2,1,0:T(8,128)S(1)} %fusion.13), custom_call_target="Cholesky" | custom-call | tf_op jit(solution)/shard_map/jit(cholesky)/cholesky | solution.py:36
  60.5 19.7 %custom-call.12 = f32[2,1,128,128]{2,3,1,0:T(8,128)S(1)} custom-call(f32[2,1,128,128]{3,2,1,0:T(8,128)S(1)} %select_bitcast_fusion), custom_call_target="InvertDiagBlocksLowerTriangular" | custom-call | tf_op jit(solution)/shard_map/vmap(jit(_cho_solve))/triangular_solve | solution.py:37
  81.4 3.5 %collective-permute-start.6 = (f32[1,2,32,128]{2,3,1,0:T(8,128)S(1)}, f32[1,2,32,128]{2,3,1,0:T(8,128)S(1)}, u32[]{:S(2)}, u32[]{:S(2)}) collective-permute-start(f32[1,2,32,128]{2,3,1,0:T(8,128)S(1)} %bitcast.144), channel_id=1, source_target_pairs={{0,8},{8,16},{16,24},{1,9},{9,17},{17,25},{2,10},{10,18},{18,26},{... | collective-permute-start | bytes 98312 | tf_op jit(solution)/shard_map/ppermute | solution.py:17
  84.9 1.3 collective-permute-start.7
  86.7 1.1 collective-permute-done.6
  87.9 4.7 %collective-permute-done.7 = f32[1,2,32,128]{2,3,1,0:T(8,128)S(1)} collective-permute-done((f32[1,2,32,128]{2,3,1,0:T(8,128)S(1)}, f32[1,2,32,128]{2,3,1,0:T(8,128)S(1)}, u32[]{:S(2)}, u32[]{:S(2)}) %collective-permute-start.7) | collective-permute-done | bytes 32800 | tf_op jit(solution)/shard_map/ppermute | solution.py:20
  92.7 1.3 collective-permute-start.8
  94.0 3.0 collective-permute-start.9
  97.1 0.7 collective-permute-done.9
  98.3 45.7 %all-reduce.1 = (f32[128]{0:T(128)S(1)}, f32[128]{0:T(128)S(1)}) all-reduce(f32[128]{0:T(128)S(1)} %multiply_reduce_fusion, f32[128]{0:T(128)S(1)} %fusion.8), channel_id=1, replica_groups=mesh['row'=4,'col'=8] {'row','col'}, use_global_device_ids=true, to_apply=%region_4.5 | all-reduce | flops 256 | bytes 2048 | tf_op jit(solution)/shard_map/psum | solution.py:75
  144.1 0.5 fusion.17
  144.6 40.4 %psum.44 = f32[128]{0:T(128)S(1)} all-reduce(f32[128]{0:T(128)S(1)} %get-tuple-element.56), channel_id=1, replica_groups=mesh['row'=4,'col'=8] {'row','col'}, use_global_device_ids=true, to_apply=%region_8.9 | all-reduce | flops 128 | bytes 1024 | tf_op jit(solution)/shard_map/psum | solution.py:75
  185.1 3.5 %collective-permute-start.10 = (f32[1,2,32,128]{2,3,1,0:T(8,128)S(1)}, f32[1,2,32,128]{2,3,1,0:T(8,128)S(1)}, u32[]{:S(2)}, u32[]{:S(2)}) collective-permute-start(f32[1,2,32,128]{2,3,1,0:T(8,128)S(1)} %bitcast.148), channel_id=1, source_target_pairs={{0,8},{8,16},{16,24},{1,9},{9,17},{17,25},{2,10},{10,18},{18,26},{... | collective-permute-start | bytes 98312 | tf_op jit(solution)/shard_map/ppermute | solution.py:17
  188.7 1.3 collective-permute-start.11
  190.4 0.7 collective-permute-done.10
  191.2 4.3 %collective-permute-done.11 = f32[1,2,32,128]{2,3,1,0:T(8,128)S(1)} collective-permute-done((f32[1,2,32,128]{2,3,1,0:T(8,128)S(1)}, f32[1,2,32,128]{2,3,1,0:T(8,128)S(1)}, u32[]{:S(2)}, u32[]{:S(2)}) %collective-permute-start.11) | collective-permute-done | bytes 32800 | tf_op jit(solution)/shard_map/ppermute | solution.py:20
  195.6 1.3 collective-permute-start.12
  196.9 3.0 collective-permute-start.13
  200.1 0.7 collective-permute-done.13
  201.3 41.7 %psum.45 = f32[128]{0:T(128)S(1)} all-reduce(f32[128]{0:T(128)S(1)} %fusion.10), channel_id=1, replica_groups=mesh['row'=4,'col'=8] {'row','col'}, use_global_device_ids=true, to_apply=%region_10.11 | all-reduce | flops 128 | bytes 1024 | tf_op jit(solution)/shard_map/psum | solution.py:86
  243.0 0.5 fusion.14
  243.5 41.4 %psum.46 = f32[128]{0:T(128)S(1)} all-reduce(f32[128]{0:T(128)S(1)} %get-tuple-element.58), channel_id=1, replica_groups=mesh['row'=4,'col'=8] {'row','col'}, use_global_device_ids=true, to_apply=%region_12.13 | all-reduce | flops 128 | bytes 1024 | tf_op jit(solution)/shard_map/psum | solution.py:75
  285.0 2.5 collective-permute-start.14
  287.5 1.3 collective-permute-start.15
  289.3 0.7 collective-permute-done.14
  290.1 4.3 %collective-permute-done.15 = f32[1,2,32,128]{2,3,1,0:T(8,128)S(1)} collective-permute-done((f32[1,2,32,128]{2,3,1,0:T(8,128)S(1)}, f32[1,2,32,128]{2,3,1,0:T(8,128)S(1)}, u32[]{:S(2)}, u32[]{:S(2)}) %collective-permute-start.15) | collective-permute-done | bytes 32800 | tf_op jit(solution)/shard_map/ppermute | solution.py:20
  294.5 1.3 collective-permute-start.16
  295.8 3.0 collective-permute-start.17
  299.0 0.8 collective-permute-done.17
  300.2 41.8 %psum.47 = f32[128]{0:T(128)S(1)} all-reduce(f32[128]{0:T(128)S(1)} %fusion.12), channel_id=1, replica_groups=mesh['row'=4,'col'=8] {'row','col'}, use_global_device_ids=true, to_apply=%region_14.15 | all-reduce | flops 128 | bytes 1024 | tf_op jit(solution)/shard_map/psum | solution.py:86
  342.1 0.8 copy.160
  (123 shorter events, 8.0 us)
Async XLA Ops:
  0.0 7.3 %copy-start.5 = (f32[1,2,2,32]{3,2,1,0:T(2,128)S(1)}, f32[1,2,2,32]{3,2,1,0:T(2,128)}, u32[]{:S(2)}) copy-start(f32[1,2,2,32]{3,2,1,0:T(2,128)} %param.19) | copy-start | bytes 1540
  1.0 29.9 %collective-permute-start.1 = (f32[1,2,32,128]{2,3,1,0:T(8,128)S(1)}, f32[1,2,32,128]{2,3,1,0:T(8,128)S(1)}, u32[]{:S(2)}, u32[]{:S(2)}) collective-permute-start(f32[1,2,32,128]{2,3,1,0:T(8,128)S(1)} %bitcast.152), channel_id=1, source_target_pairs={{0,8},{8,16},{16,24},{1,9},{9,17},{17,25},{2,10},{10,18},{18,26},{... | collective-permute-start | bytes 98312 | tf_op jit(solution)/shard_map/ppermute | solution.py:17
  6.0 25.0 %collective-permute-start.2 = (f32[1,2,32,128]{2,3,1,0:T(8,128)S(1)}, f32[1,2,32,128]{2,3,1,0:T(8,128)S(1)}, u32[]{:S(2)}, u32[]{:S(2)}) collective-permute-start(f32[1,2,32,128]{2,3,1,0:T(8,128)S(1)} %bitcast.153), channel_id=1, source_target_pairs={{8,0},{16,8},{24,16},{9,1},{17,9},{25,17},{10,2},{18,10},{26,18},{... | collective-permute-start | bytes 98312 | tf_op jit(solution)/shard_map/ppermute | solution.py:20
  7.3 23.5 %collective-permute-start = (f32[1,1,32]{2,1,0:T(1,128)S(1)}, f32[1,1,32]{2,1,0:T(1,128)S(1)}, u32[]{:S(2)}, u32[]{:S(2)}) collective-permute-start(f32[1,1,32]{2,1,0:T(1,128)S(1)} %slice_bitcast_fusion.1), channel_id=1, source_target_pairs={{0,1},{1,2},{2,3},{3,4},{4,5},{5,6},{6,7},{8,9},{9,10},{10,11},{11... | collective-permute-start | bytes 392 | tf_op jit(solution)/shard_map/ppermute | solution.py:28
  8.8 6.2 %copy-start = (f32[1,2,128,128]{3,2,1,0:T(8,128)S(1)}, f32[1,2,128,128]{3,2,1,0:T(8,128)}, u32[]{:S(2)}) copy-start(f32[1,2,128,128]{3,2,1,0:T(8,128)} %param.17) | copy-start | bytes 393220
  8.8 27.7 %collective-permute-start.5 = (f32[1,2,32]{2,1,0:T(2,128)S(1)}, f32[1,2,32]{2,1,0:T(2,128)S(1)}, u32[]{:S(2)}, u32[]{:S(2)}) collective-permute-start(f32[1,2,32]{2,1,0:T(2,128)S(1)} %bitcast.185), channel_id=1, source_target_pairs={{0,8},{8,16},{16,24},{1,9},{9,17},{17,25},{2,10},{10,18},{18,26},{... | collective-permute-start | bytes 776 | tf_op jit(solution)/shard_map/ppermute | solution.py:28
  13.4 0.7 copy-start.4
  14.2 0.7 copy-start.9
  15.0 0.9 copy-start.1
  15.1 0.8 copy-start.3
  16.4 0.7 copy-start.6
  16.4 0.7 copy-start.7
  17.1 0.7 copy-start.10
  17.2 0.7 copy-start.8
  29.8 0.9 copy-start.2
  31.1 4.4 %collective-permute-start.3 = (f32[3,1,32,128]{3,2,1,0:T(8,128)S(1)}, f32[3,1,32,128]{3,2,1,0:T(8,128)S(1)}, u32[]{:S(2)}, u32[]{:S(2)}) collective-permute-start(f32[3,1,32,128]{3,2,1,0:T(8,128)S(1)} %get-tuple-element.49), channel_id=1, source_target_pairs={{1,0},{2,1},{3,2},{4,3},{5,4},{6,5},{7,6},{9,8},{10,9},{11,10},{12... | collective-permute-start | bytes 147464 | tf_op jit(solution)/shard_map/ppermute | solution.py:20
  32.4 3.9 %collective-permute-start.4 = (f32[3,1,32,128]{3,2,1,0:T(8,128)S(1)}, f32[3,1,32,128]{3,2,1,0:T(8,128)S(1)}, u32[]{:S(2)}, u32[]{:S(2)}) collective-permute-start(f32[3,1,32,128]{3,2,1,0:T(8,128)S(1)} %get-tuple-element.50), channel_id=1, source_target_pairs={{0,1},{1,2},{2,3},{3,4},{4,5},{5,6},{6,7},{8,9},{9,10},{10,11},{11... | collective-permute-start | bytes 147464 | tf_op jit(solution)/shard_map/ppermute | solution.py:17
  81.4 6.5 %collective-permute-start.6 = (f32[1,2,32,128]{2,3,1,0:T(8,128)S(1)}, f32[1,2,32,128]{2,3,1,0:T(8,128)S(1)}, u32[]{:S(2)}, u32[]{:S(2)}) collective-permute-start(f32[1,2,32,128]{2,3,1,0:T(8,128)S(1)} %bitcast.144), channel_id=1, source_target_pairs={{0,8},{8,16},{16,24},{1,9},{9,17},{17,25},{2,10},{10,18},{18,26},{... | collective-permute-start | bytes 98312 | tf_op jit(solution)/shard_map/ppermute | solution.py:17
  84.9 7.7 %collective-permute-start.7 = (f32[1,2,32,128]{2,3,1,0:T(8,128)S(1)}, f32[1,2,32,128]{2,3,1,0:T(8,128)S(1)}, u32[]{:S(2)}, u32[]{:S(2)}) collective-permute-start(f32[1,2,32,128]{2,3,1,0:T(8,128)S(1)} %bitcast.145), channel_id=1, source_target_pairs={{8,0},{16,8},{24,16},{9,1},{17,9},{25,17},{10,2},{18,10},{26,18},{... | collective-permute-start | bytes 98312 | tf_op jit(solution)/shard_map/ppermute | solution.py:20
  92.7 4.5 %collective-permute-start.8 = (f32[3,1,32,128]{3,2,1,0:T(8,128)S(1)}, f32[3,1,32,128]{3,2,1,0:T(8,128)S(1)}, u32[]{:S(2)}, u32[]{:S(2)}) collective-permute-start(f32[3,1,32,128]{3,2,1,0:T(8,128)S(1)} %get-tuple-element.45), channel_id=1, source_target_pairs={{1,0},{2,1},{3,2},{4,3},{5,4},{6,5},{7,6},{9,8},{10,9},{11,10},{12... | collective-permute-start | bytes 147464 | tf_op jit(solution)/shard_map/ppermute | solution.py:20
  94.0 3.9 %collective-permute-start.9 = (f32[3,1,32,128]{3,2,1,0:T(8,128)S(1)}, f32[3,1,32,128]{3,2,1,0:T(8,128)S(1)}, u32[]{:S(2)}, u32[]{:S(2)}) collective-permute-start(f32[3,1,32,128]{3,2,1,0:T(8,128)S(1)} %get-tuple-element.46), channel_id=1, source_target_pairs={{0,1},{1,2},{2,3},{3,4},{4,5},{5,6},{6,7},{8,9},{9,10},{10,11},{11... | collective-permute-start | bytes 147464 | tf_op jit(solution)/shard_map/ppermute | solution.py:17
  185.1 6.1 %collective-permute-start.10 = (f32[1,2,32,128]{2,3,1,0:T(8,128)S(1)}, f32[1,2,32,128]{2,3,1,0:T(8,128)S(1)}, u32[]{:S(2)}, u32[]{:S(2)}) collective-permute-start(f32[1,2,32,128]{2,3,1,0:T(8,128)S(1)} %bitcast.148), channel_id=1, source_target_pairs={{0,8},{8,16},{16,24},{1,9},{9,17},{17,25},{2,10},{10,18},{18,26},{... | collective-permute-start | bytes 98312 | tf_op jit(solution)/shard_map/ppermute | solution.py:17
  188.7 6.9 %collective-permute-start.11 = (f32[1,2,32,128]{2,3,1,0:T(8,128)S(1)}, f32[1,2,32,128]{2,3,1,0:T(8,128)S(1)}, u32[]{:S(2)}, u32[]{:S(2)}) collective-permute-start(f32[1,2,32,128]{2,3,1,0:T(8,128)S(1)} %bitcast.149), channel_id=1, source_target_pairs={{8,0},{16,8},{24,16},{9,1},{17,9},{25,17},{10,2},{18,10},{26,18},{... | collective-permute-start | bytes 98312 | tf_op jit(solution)/shard_map/ppermute | solution.py:20
  195.6 4.4 %collective-permute-start.12 = (f32[3,1,32,128]{3,2,1,0:T(8,128)S(1)}, f32[3,1,32,128]{3,2,1,0:T(8,128)S(1)}, u32[]{:S(2)}, u32[]{:S(2)}) collective-permute-start(f32[3,1,32,128]{3,2,1,0:T(8,128)S(1)} %get-tuple-element.41), channel_id=1, source_target_pairs={{1,0},{2,1},{3,2},{4,3},{5,4},{6,5},{7,6},{9,8},{10,9},{11,10},{12... | collective-permute-start | bytes 147464 | tf_op jit(solution)/shard_map/ppermute | solution.py:20
  196.9 3.9 %collective-permute-start.13 = (f32[3,1,32,128]{3,2,1,0:T(8,128)S(1)}, f32[3,1,32,128]{3,2,1,0:T(8,128)S(1)}, u32[]{:S(2)}, u32[]{:S(2)}) collective-permute-start(f32[3,1,32,128]{3,2,1,0:T(8,128)S(1)} %get-tuple-element.42), channel_id=1, source_target_pairs={{0,1},{1,2},{2,3},{3,4},{4,5},{5,6},{6,7},{8,9},{9,10},{10,11},{11... | collective-permute-start | bytes 147464 | tf_op jit(solution)/shard_map/ppermute | solution.py:17
  285.0 5.0 %collective-permute-start.14 = (f32[1,2,32,128]{2,3,1,0:T(8,128)S(1)}, f32[1,2,32,128]{2,3,1,0:T(8,128)S(1)}, u32[]{:S(2)}, u32[]{:S(2)}) collective-permute-start(f32[1,2,32,128]{2,3,1,0:T(8,128)S(1)} %bitcast.155), channel_id=1, source_target_pairs={{0,8},{8,16},{16,24},{1,9},{9,17},{17,25},{2,10},{10,18},{18,26},{... | collective-permute-start | bytes 98312 | tf_op jit(solution)/shard_map/ppermute | solution.py:17
  287.5 6.9 %collective-permute-start.15 = (f32[1,2,32,128]{2,3,1,0:T(8,128)S(1)}, f32[1,2,32,128]{2,3,1,0:T(8,128)S(1)}, u32[]{:S(2)}, u32[]{:S(2)}) collective-permute-start(f32[1,2,32,128]{2,3,1,0:T(8,128)S(1)} %bitcast.156), channel_id=1, source_target_pairs={{8,0},{16,8},{24,16},{9,1},{17,9},{25,17},{10,2},{18,10},{26,18},{... | collective-permute-start | bytes 98312 | tf_op jit(solution)/shard_map/ppermute | solution.py:20
  294.5 4.4 %collective-permute-start.16 = (f32[3,1,32,128]{3,2,1,0:T(8,128)S(1)}, f32[3,1,32,128]{3,2,1,0:T(8,128)S(1)}, u32[]{:S(2)}, u32[]{:S(2)}) collective-permute-start(f32[3,1,32,128]{3,2,1,0:T(8,128)S(1)} %get-tuple-element.37), channel_id=1, source_target_pairs={{1,0},{2,1},{3,2},{4,3},{5,4},{6,5},{7,6},{9,8},{10,9},{11,10},{12... | collective-permute-start | bytes 147464 | tf_op jit(solution)/shard_map/ppermute | solution.py:20
  295.8 3.9 %collective-permute-start.17 = (f32[3,1,32,128]{3,2,1,0:T(8,128)S(1)}, f32[3,1,32,128]{3,2,1,0:T(8,128)S(1)}, u32[]{:S(2)}, u32[]{:S(2)}) collective-permute-start(f32[3,1,32,128]{3,2,1,0:T(8,128)S(1)} %get-tuple-element.38), channel_id=1, source_target_pairs={{0,1},{1,2},{2,3},{3,4},{4,5},{5,6},{6,7},{8,9},{9,10},{10,11},{11... | collective-permute-start | bytes 147464 | tf_op jit(solution)/shard_map/ppermute | solution.py:17
where the time goes:
time: 344 us; the launch traced here: 343 us
  blocking collectives  221 us (64%)
  other arithmetic  46.3 us (13%)
  starting transfers between devices  42.9 us (12%)
  waiting for transfers between devices  18.9 us (5%)
  local copies, waits for them, and re-layouts  9.55 us (3%)
  matrix products  3.62 us (1%)
    psum x3, blocking collectives, residual_product(): return lax.psum(inner_sum(residual, precond), ('row', 'col'))  127 us
    psum x2, blocking collectives, solve_separate(): curvature = lax.psum(inner_sum(direction, applied), ('row', 'col'))  83.5 us
    ppermute x8, starting transfers between devices, padded_2(): lax.ppermute(lax.slice_in_dim(block, block.shape[dim] - width, None, axis...  26.6 us
    another operation x4, other arithmetic, tile_inverse(): factors = jnp.linalg.cholesky(flat_blocks)  23.6 us
    another operation x3, other arithmetic, tile_inverse(): jax.scipy.linalg.cho_solve((factor, True), identity)  19.8 us
    ppermute x8, waiting for transfers between devices, padded_2(): lax.ppermute(lax.slice_in_dim(block, 0, width, axis=dim), axis, backward)  13.3 us
    ppermute x8, starting transfers between devices, padded_2(): lax.ppermute(lax.slice_in_dim(block, 0, width, axis=dim), axis, backward)  10.3 us
    all_gather x1, blocking collectives, local(): gathered = lax.all_gather(drivers, 'col', axis=0, tiled=True)  9.95 us
  transfers between devices with their start and end apart: 18, of which 10 were waited for; matrix products, arithmetic and copies ran while one was open for 2% of the time, Pallas kernels for 0%

commit v1 on v0

v1 whole, which is shorter than its diff:
```python
import functools

import jax
import jax.numpy as jnp
from jax import lax
from jax.experimental import pallas as pl
from jax.experimental.pallas import tpu as pltpu
from jax.sharding import PartitionSpec as P

PRECISE = lax.Precision.HIGHEST
DOUBLINGS = 5
SMALL = 2.0**-13


def tile_kernel(conduct_ref, cap_ref, volt_ref, inject_ref, inverse_ref, rest_ref, sum_ref, power_ref):
    tiles, nodes = conduct_ref.shape[0], conduct_ref.shape[1]
    dot = functools.partial(
        jnp.dot, precision=PRECISE, preferred_element_type=jnp.float32
    )
    row = lax.broadcasted_iota(jnp.int32, (nodes, nodes), 0)
    col = lax.broadcasted_iota(jnp.int32, (nodes, nodes), 1)
    eye = jnp.where(row == col, 1.0, 0.0).astype(jnp.float32)
    sums, powers, scales = [], [], []
    for t in range(tiles):
        conduct = conduct_ref[t]
        diagonal = (conduct + cap_ref[t : t + 1, :]) * eye
        down = jnp.sum(diagonal, axis=1, keepdims=True)
        across = jnp.sum(diagonal, axis=0, keepdims=True)
        power = (conduct * eye - conduct) / down
        sums.append(eye + power)
        powers.append(dot(power, power))
        scales.append(1.0 / across)
        rest_ref[t] = inject_ref[t] - dot(conduct, volt_ref[t])

    def step(sums, powers):
        out_sums, out_powers, largest = [], [], jnp.float32(0.0)
        for total, power in zip(sums, powers):
            both = dot(jnp.concatenate([total, power], axis=0), power)
            out_sums.append(total + both[:nodes])
            out_powers.append(both[nodes:])
            largest = jnp.maximum(largest, jnp.max(jnp.sum(power, axis=1)))
        return out_sums, out_powers, largest

    for _ in range(DOUBLINGS):
        sums, powers, largest = step(sums, powers)
    for t in range(tiles):
        sum_ref[t], power_ref[t] = sums[t], powers[t]

    def again(carry):
        sums, powers, largest = step(
            [sum_ref[t] for t in range(tiles)], [power_ref[t] for t in range(tiles)]
        )
        for t in range(tiles):
            sum_ref[t], power_ref[t] = sums[t], powers[t]
        return largest, carry[1] + 1

    lax.while_loop(
        lambda carry: (carry[0] > SMALL) & (carry[1] < 40), again, (largest, jnp.int32(0))
    )
    for t in range(tiles):
        inverse_ref[t] = sum_ref[t] * scales[t]


def tile_inverse(conduct, capacitance, voltage, inject):
    block = jax.ShapeDtypeStruct(conduct.shape, jnp.float32)
    vmem = pl.BlockSpec(memory_space=pltpu.VMEM)
    return pl.pallas_call(
        tile_kernel,
        out_shape=(block, block),
        in_specs=[vmem] * 4,
        out_specs=(vmem, vmem),
        scratch_shapes=[pltpu.VMEM(conduct.shape, jnp.float32)] * 2,
    )(conduct, capacitance, voltage, inject)


def other(block, axis, count, distance):
    return lax.ppermute(block, axis, [(i, i ^ distance) for i in range(count)])


def xor_gather(block, axis, count):
    blocks, held = [block], 1
    while held < count:
        whole = jnp.concatenate(blocks, axis=0)
        reach = 2 if (count // held).bit_length() % 2 == 0 else 4
        blocks = [whole] + [other(whole, axis, count, held * k) for k in range(1, reach)]
        held *= reach
    return jnp.concatenate(blocks, axis=0)


def xor_sum(block, axis, count):
    held = 1
    while held < count:
        reach = 2 if (count // held).bit_length() % 2 == 0 else 4
        block = sum([other(block, axis, count, held * k) for k in range(1, reach)], block)
        held *= reach
    return block


def outer(block, axis, count):
    pairs = [(i, (i + 1) % count if i % 2 else (i - 1) % count) for i in range(count)]
    return lax.ppermute(block, axis, pairs)


def south_flow(rim, gain, not_last):
    below = jnp.roll(rim, -1, axis=0) * not_last
    return gain * (rim - below), rim - below


def net_flow(east, south, not_first):
    return east[:, 1:] - east[:, :-1] + south - jnp.roll(south, 1, axis=0) * not_first


def local(
    initial_voltage,
    inject,
    conduct,
    capacitance,
    track_gain,
    driver_tile,
    sink_net,
    sink_count,
    sink_tile,
    sink_node,
    sink_gain,
):
    rows, cols = lax.axis_size("row"), lax.axis_size("col")
    my_row, my_col = lax.axis_index("row"), lax.axis_index("col")
    odd = my_col % 2 == 1
    has_west = (my_col > 0).astype(jnp.float32)
    has_east = (my_col < cols - 1).astype(jnp.float32)
    has_far = (my_col < cols - 2).astype(jnp.float32)
    tiles, nodes, patterns = initial_voltage.shape[1:]
    edge = track_gain.shape[-1]
    nets = driver_tile.shape[-1]
    voltage = initial_voltage[0]
    rims = voltage[:, :edge]
    east_gain, south_gain = track_gain[0, :, 0, :, None], track_gain[0, :, 1, :, None]

    picked = driver_tile.reshape((nets, 1))
    node_of = voltage[:, :nets] if nets <= nodes else jnp.tile(voltage, (1, -(-nets // nodes), 1))[:, :nets]
    drivers = sum(jnp.where(picked == t, node_of[t], 0.0) for t in range(tiles))
    gathered = xor_gather(drivers, "col", cols)

    wide = jnp.broadcast_to(east_gain[-1], (edge, patterns))
    inner0 = other(jnp.concatenate([jnp.where(odd, rims[0], rims[1]), wide]), "col", cols, 1)
    outer0 = outer(jnp.concatenate([jnp.where(odd, rims[1], rims[0]), wide]), "col", cols)
    west0 = jnp.where(odd, inner0, outer0) * has_west
    east0 = jnp.where(odd, outer0, inner0) * has_east

    inverse, rest = tile_inverse(conduct[0], capacitance[0], voltage, inject[0])

    source = jnp.arange(cols, dtype=jnp.int32)[:, None] ^ my_col
    slots = sink_net.shape[-1]
    place = (source * nets + sink_net[0, 0]).reshape(-1)
    live = jnp.arange(slots, dtype=jnp.int32)[None] < sink_count[0, 0][:, None]
    weight = jnp.where(live, sink_gain[0, 0], 0.0).reshape((-1, 1))
    target = (sink_tile * nodes + sink_node).reshape(-1)
    take = (place[:, None] == jnp.arange(cols * nets, dtype=jnp.int32)).astype(jnp.float32)
    put = (target[:, None] == jnp.arange(tiles * nodes, dtype=jnp.int32)).astype(jnp.float32)
    take, put = lax.optimization_barrier((take, put * weight))
    spread_drivers = lax.dot_general(put, take, (((0,), (0,)), ((), ())), precision=PRECISE)
    injected = jnp.dot(spread_drivers, gathered, precision=PRECISE).reshape(voltage.shape)

    flow0 = jnp.stack(
        [
            west0[edge:] * (west0[:edge] - rims[0]),
            east_gain[0] * (rims[0] - rims[1]),
            east_gain[1] * (rims[1] - east0[:edge]),
        ]
    )
    residual = rest + injected
    residual = jnp.concatenate(
        [residual[:, :edge] - (flow0[1:] - flow0[:-1]), residual[:, edge:]], axis=1
    )
    precond = jnp.einsum("cij,cjp->cip", inverse, residual, precision=PRECISE)
    first = jnp.sum(precond * residual, axis=(0, 1))

    core = inverse[:, :edge, :edge]
    extras = jnp.concatenate(
        [core[0], core[1], east_gain[0], east_gain[1], south_gain[0], south_gain[1]], axis=1
    )
    extras = jnp.pad(extras, ((0, 0), (0, patterns - extras.shape[1])))
    message = jnp.concatenate(
        [
            precond[:, :edge].reshape((-1, patterns)),
            rims.reshape((-1, patterns)),
            extras,
            jnp.pad(first[None], ((0, 7), (0, 0))),
        ]
    )
    column = jnp.stack(
        [message]
        + [
            lax.ppermute(message, "row", [((i + k) % rows, i) for i in range(rows)])
            for k in range(1, rows)
        ]
    )
    true_row = (my_row + jnp.arange(rows, dtype=jnp.int32)) % rows
    not_first = (true_row > 0).astype(jnp.float32)[:, None, None, None]
    not_last = (true_row < rows - 1).astype(jnp.float32)[:, None, None, None]
    span = tiles * edge
    raw = column[:, :span].reshape((rows, tiles, edge, patterns))
    start = column[:, span : 2 * span].reshape((rows, tiles, edge, patterns))
    table = column[:, 2 * span : 2 * span + edge]
    first = jnp.sum(column[:, 2 * span + edge], axis=0)

    def unpack(table):
        cores = jnp.stack([table[:, :, :edge], table[:, :, edge : 2 * edge]], axis=1)
        gains = [table[:, :, 2 * edge + k : 2 * edge + k + 1] for k in range(4)]
        return cores, jnp.stack(gains[:2], axis=1), jnp.stack(gains[2:], axis=1)

    def spread(cores, flow):
        return jnp.einsum("rcij,rcjp->rcip", cores, flow, precision=PRECISE)

    cores, easts, souths = unpack(table)
    south0, _ = south_flow(start, souths, not_last)
    vertical = south0 - jnp.roll(south0, 1, axis=0) * not_first
    u0 = raw - spread(cores, vertical)
    first = first - jnp.sum(vertical * (raw + u0), axis=(0, 1, 2))
    precond = precond - jnp.einsum(
        "cij,cjp->cip", inverse[:, :, :edge], vertical[0], precision=PRECISE
    )

    message = jnp.concatenate([u0.reshape((rows, span, patterns)), table], axis=1)
    inner = other(message, "col", cols, 1)
    beyond = outer(message, "col", cols)
    far = lax.ppermute(u0[:, :1], "col", [((i + 2) % cols, i) for i in range(cols)]) * has_far
    west = jnp.where(odd, inner, beyond) * has_west
    east = jnp.where(odd, beyond, inner) * has_east

    def parts(block):
        return (block[:, :span].reshape((rows, tiles, edge, patterns)),) + unpack(block[:, span:])

    west_u, west_cores, west_easts, west_souths = parts(west)
    east_u, east_cores, east_easts, east_souths = parts(east)
    u0 = jnp.concatenate([west_u, u0, east_u, far], axis=1)
    cores = jnp.concatenate([west_cores[:, 1:], cores, east_cores], axis=1)
    easts = jnp.concatenate([west_easts, easts, east_easts], axis=1)
    souths = jnp.concatenate([west_souths[:, 1:], souths, east_souths], axis=1)

    south, _ = south_flow(u0[:, 1:-1], souths, not_last)
    t0 = net_flow(easts * (u0[:, :-1] - u0[:, 1:]), south, not_first)
    u1 = spread(cores, t0)
    south, _ = south_flow(u1[:, 1:-1], souths[:, 1:-1], not_last)
    t1 = net_flow(easts[:, 1:-1] * (u1[:, :-1] - u1[:, 1:]), south, not_first)
    u2 = spread(cores[:, 1:-1], t1)
    south, drop = south_flow(u2[:, :-1], souths[:, 1:3], not_last)
    ahead = u2[:, :-1] - u2[:, 1:]

    def total(left, right):
        return jnp.sum(left * right, axis=(0, 1, 2))

    own_t0, own_u1, own_t1 = t0[:, 1:3], u1[:, 1:3], t1[:, :2]
    moments = jnp.stack(
        [
            first,
            total(u0[:, 2:4], own_t0),
            total(own_u1, own_t0),
            total(own_u1, own_t1),
            total(u2[:, :2], own_t1),
            total(south, drop) + total(easts[:, 2:4] * ahead, ahead),
            jnp.zeros_like(first),
            jnp.zeros_like(first),
        ]
    )
    m = xor_sum(moments, "col", cols)

    a00, a01, a02 = m[0] + m[1], m[1] + m[2], m[2] + m[3]
    a12, a22 = m[3] + m[4], m[4] + m[5]
    l1, l2 = a01 / a00, a02 / a00
    d1 = a02 - l1 * a01
    e12 = a12 - l2 * a01
    l12 = e12 / d1
    d2 = a22 - l2 * a02 - l12 * e12
    y1 = m[1] - l1 * m[0]
    y2 = m[2] - l2 * m[0] - l12 * y1
    c2 = y2 / d2
    c1 = y1 / d1 - l12 * c2
    c0 = m[0] / a00 - l1 * c1 - l2 * c2
    mixed = c1 * t0[0, 1:3] + c2 * t1[0, :2]
    update = jnp.einsum("cij,cjp->cip", inverse[:, :, :edge], mixed, precision=PRECISE)
    return (voltage + c0 * precond + update)[None]


def solution(mesh):
    whole = P("row", "col", None, None)
    third = P("row", "col", None)
    placed = (whole, whole, whole, third, whole, third, whole, third, whole, whole, whole)
    return jax.shard_map(local, mesh=mesh, in_specs=placed, out_specs=whole, check_vma=False)
```

time: 344 us -> 59.8 us (0.17)
  blocking collectives: 221 us -> 0 us
  other arithmetic: 46.3 us -> 3.66 us
  starting transfers between devices: 42.9 us -> 18.6 us
  Pallas kernels: 0 us -> 3.79 us
    psum x5 -> x0, blocking collectives: 211 us -> none  [the longest x3 127 us: residual_product(): return lax.psum(inner_sum(residual, precond), ('row', 'col'))]
    another operation x7 -> x4, other arithmetic: 43.4 us -> 0.12 us  [the longest x1 0.08 us: local(): jnp.stack([west0[edge:] * (west0[:edge] - rims[0]), east_gain[0] * (rims[...]
    ppermute x18 -> x16, starting transfers between devices: 42.9 us -> 18.6 us  [the longest x10 8.81 us: other(): return lax.ppermute(block, axis, [(i, i ^ distance) for i in range(count)])]
    all_gather x1 -> x0, blocking collectives: 9.95 us -> none  [local(): gathered = lax.all_gather(drivers, 'col', axis=0, tiled=True)]
    pallas_call x0 -> x1, Pallas kernels: none -> 3.79 us  [tile_inverse(): pl.pallas_call(tile_kernel, out_shape=(block, block), in_specs=[vmem] * 4...]
    ppermute x18 -> x16, waiting for transfers between devices: 18.9 us -> 17.6 us  [the longest x10 7.15 us: other(): return lax.ppermute(block, axis, [(i, i ^ distance) for i in range(count)])]
  transfers between devices with their start and end apart: 18 -> 16, of which waited for: 10 -> 10; matrix products, arithmetic and copies ran while one was open for 2% -> 5% of each run, Pallas kernels for 0% -> 6%
where the time goes in v1:
time: 59.8 us; the launch traced here: 59.1 us
  starting transfers between devices  18.6 us (31%)
  waiting for transfers between devices  17.6 us (29%)
  local copies, waits for them, and re-layouts  11.1 us (19%)
  Pallas kernels  3.79 us (6%)
  matrix products  3.7 us (6%)
  other arithmetic  3.66 us (6%)
  between operations  0.63 us (1%)
    ppermute x10, starting transfers between devices, other(): return lax.ppermute(block, axis, [(i, i ^ distance) for i in range(count)])  8.81 us
    ppermute x10, waiting for transfers between devices, other(): return lax.ppermute(block, axis, [(i, i ^ distance) for i in range(count)])  7.15 us
    unnamed x46, local copies, waits for them, and re-layouts  5.8 us
    ppermute x3, waiting for transfers between devices, local(): lax.ppermute(message, 'row', [((i + k) % rows, i) for i in range(rows)])  5.61 us
    ppermute x1, waiting for transfers between devices, local(): lax.ppermute(u0[:, :1], 'col', [((i + 2) % cols, i) for i in range(cols)])  4.44 us
    ppermute x3, starting transfers between devices, local(): lax.ppermute(message, 'row', [((i + k) % rows, i) for i in range(rows)])  4.32 us
    pallas_call x1, Pallas kernels, tile_inverse(): pl.pallas_call(tile_kernel, out_shape=(block, block), in_specs=[vmem] * 4...  3.79 us
    ppermute x2, starting transfers between devices, outer(): return lax.ppermute(block, axis, pairs)  3.47 us
  transfers between devices with their start and end apart: 16, of which 10 were waited for; matrix products, arithmetic and copies ran while one was open for 5% of the time, Pallas kernels for 6%

profile of v1, /device:TPU:0, one launch (start us, length us, event | category | flops | bytes accessed | tf_op | source)
XLA Modules:
  0.0 59.1 jit_solution(3105797579457790875)
XLA Ops:
  0.0 0.8 %slice_bitcast_fusion.13 = (f32[32,1]{0,1:T(1,128)S(1)}, f32[32,1]{0,1:T(1,128)S(1)}, f32[32,1]{0,1:T(1,128)S(1)}, f32[32]{0:T(128)S(1)}, f32[32]{0:T(128)S(1)}, /*index=5*/f32[32,1]{0,1:T(1,128)S(1)}) fusion(f32[1,2,2,32]{3,2,1,0:T(2,128)} %param.15), kind=kLoop, calls=%fused_computation.182 | loop fusion | bytes 1280 | tf_op jit(solution)/shard_map/squeeze | solution.py:180
  0.8 0.7 %bitcast_select_fusion.1 = (f32[32,128]{1,0:T(8,128)S(1)}, f32[32,128]{1,0:T(8,128)S(1)}) fusion(f32[2,128,128]{2,1,0:T(8,128)} %bitcast.258, pred[]{:T(512)S(6)} %eq.76), kind=kLoop, calls=%fused_computation.139 | loop fusion | flops 8192 | bytes 65537 | tf_op jit(solution)/shard_map/jit(_where)/select_n | solution.py:146
  1.6 3.4 %collective-permute-start.4 = (f32[64,128]{1,0:T(8,128)S(1)}, f32[64,128]{1,0:T(8,128)S(1)}, u32[]{:S(2)}, u32[]{:S(2)}) collective-permute-start(f32[64,128]{1,0:T(8,128)S(1)} %get-tuple-element.59), channel_id=1, source_target_pairs={{0,7},{1,2},{2,1},{3,4},{4,3},{5,6},{6,5},{7,0},{8,15},{9,10},{10,... | collective-permute-start | bytes 98312 | tf_op jit(solution)/shard_map/ppermute | solution.py:101
  5.1 0.6 collective-permute-start
  5.9 0.7 %copy-done.14 = s32[1,1,8]{2,1,0:T(1,128)S(1)} copy-done((s32[1,1,8]{2,1,0:T(1,128)S(1)}, s32[1,1,8]{2,1,0:T(1,128)}, u32[]{:S(2)}) %copy-start.14) | copy-done | bytes 56
  6.9 0.5 copy-done.9
  7.7 3.8 %shard_map.109 = (f32[2,128,128]{2,1,0:T(8,128)}, f32[2,128,128]{2,1,0:T(8,128)}) custom-call(f32[2,128,128]{2,1,0:T(8,128)} %bitcast.280, f32[2,128]{1,0:T(2,128)} %bitcast.303, f32[2,128,128]{2,1,0:T(8,128)} %bitcast.259, f32[2,128,128]{2,1,0:T(8,128)} %bitcast.281), custom_call_target="tpu_custom_call" | custom-call | tf_op jit(solution)/shard_map/pallas_call | solution.py:67
  11.5 0.7 %slice_bitcast_fusion.11 = (f32[32,32]{1,0:T(8,128)S(1)}, f32[32,32]{1,0:T(8,128)S(1)}) fusion(f32[2,128,128]{2,1,0:T(8,128)} %get-tuple-element.9), kind=kLoop, calls=%fused_computation.142 | loop fusion | bytes 16384 | tf_op jit(solution)/shard_map/squeeze | solution.py:180
  12.2 0.6 %fusion.69 = f32[256,512]{1,0:T(8,128)S(1)} fusion(f32[64,256]{1,0:T(8,128)S(1)} %fusion.34, f32[64,512]{1,0:T(8,128)S(1)} %fusion.27), kind=kOutput, calls=%fused_computation.198 | convolution fusion | flops 100663296 | bytes 720896 | tf_op jit(solution)/shard_map/dot_general | solution.py:161
  12.9 0.3 copy-done.6
  13.7 1.2 %collective-permute-start.3 = (f32[128,128]{1,0:T(8,128)S(1)}, f32[128,128]{1,0:T(8,128)S(1)}, u32[]{:S(2)}, u32[]{:S(2)}) collective-permute-start(f32[128,128]{1,0:T(8,128)S(1)} %pad_maximum_fusion.10), channel_id=1, source_target_pairs={{0,6},{1,7},{2,4},{3,5},{4,2},{5,3},{6,0},{7,1},{8,14},{9,15},{10,... | collective-permute-start | bytes 196616 | tf_op jit(solution)/shard_map/ppermute | solution.py:77
  14.9 1.9 %collective-permute-start.2 = (f32[128,128]{1,0:T(8,128)S(1)}, f32[128,128]{1,0:T(8,128)S(1)}, u32[]{:S(2)}, u32[]{:S(2)}) collective-permute-start(f32[128,128]{1,0:T(8,128)S(1)} %pad_maximum_fusion.10), channel_id=1, source_target_pairs={{0,4},{1,5},{2,6},{3,7},{4,0},{5,1},{6,2},{7,3},{8,12},{9,13},{10,... | collective-permute-start | bytes 196616 | tf_op jit(solution)/shard_map/ppermute | solution.py:77
  16.8 0.5 collective-permute-start.1
  17.3 3.7 %collective-permute-done.1 = f32[128,128]{1,0:T(8,128)S(1)} collective-permute-done((f32[128,128]{1,0:T(8,128)S(1)}, f32[128,128]{1,0:T(8,128)S(1)}, u32[]{:S(2)}, u32[]{:S(2)}) %collective-permute-start.1) | collective-permute-done | bytes 65568 | tf_op jit(solution)/shard_map/ppermute | solution.py:77
  21.1 0.6 fusion.70
  21.7 0.3 copy-done.8
  22.1 0.9 %copy-done.7 = f32[2,128,128]{2,1,0:T(8,128)S(1)} copy-done((f32[2,128,128]{2,1,0:T(8,128)S(1)}, f32[2,128,128]{2,1,0:T(8,128)}, u32[]{:S(2)}) %copy-start.7) | copy-done | bytes 131096
  22.9 0.3 multiply_reduce_fusion.5
  23.2 2.3 %collective-permute-start.7 = (f32[168,128]{1,0:T(8,128)S(1)}, f32[168,128]{1,0:T(8,128)S(1)}, u32[]{:S(2)}, u32[]{:S(2)}) collective-permute-start(f32[168,128]{1,0:T(8,128)S(1)} %get-tuple-element.58), channel_id=1, source_target_pairs={{16,0},{24,8},{0,16},{8,24},{17,1},{25,9},{1,17},{9,25},{18,2},{26... | collective-permute-start | bytes 258056 | tf_op jit(solution)/shard_map/ppermute | solution.py:194
  25.5 1.3 %collective-permute-start.6 = (f32[168,128]{1,0:T(8,128)S(1)}, f32[168,128]{1,0:T(8,128)S(1)}, u32[]{:S(2)}, u32[]{:S(2)}) collective-permute-start(f32[168,128]{1,0:T(8,128)S(1)} %get-tuple-element.58), channel_id=1, source_target_pairs={{8,0},{16,8},{24,16},{0,24},{9,1},{17,9},{25,17},{1,25},{10,2},{18... | collective-permute-start | bytes 258056 | tf_op jit(solution)/shard_map/ppermute | solution.py:194
  26.9 0.7 %collective-permute-start.8 = (f32[168,128]{1,0:T(8,128)S(1)}, f32[168,128]{1,0:T(8,128)S(1)}, u32[]{:S(2)}, u32[]{:S(2)}) collective-permute-start(f32[168,128]{1,0:T(8,128)S(1)} %get-tuple-element.58), channel_id=1, source_target_pairs={{24,0},{0,8},{8,16},{16,24},{25,1},{1,9},{9,17},{17,25},{26,2},{2,... | collective-permute-start | bytes 258056 | tf_op jit(solution)/shard_map/ppermute | solution.py:194
  27.6 3.8 %collective-permute-done.7 = f32[168,128]{1,0:T(8,128)S(1)} collective-permute-done((f32[168,128]{1,0:T(8,128)S(1)}, f32[168,128]{1,0:T(8,128)S(1)}, u32[]{:S(2)}, u32[]{:S(2)}) %collective-permute-start.7) | collective-permute-done | bytes 86048 | tf_op jit(solution)/shard_map/ppermute | solution.py:194
  31.5 1.7 %collective-permute-done.8 = f32[168,128]{1,0:T(8,128)S(1)} collective-permute-done((f32[168,128]{1,0:T(8,128)S(1)}, f32[168,128]{1,0:T(8,128)S(1)}, u32[]{:S(2)}, u32[]{:S(2)}) %collective-permute-start.8) | collective-permute-done | bytes 86048 | tf_op jit(solution)/shard_map/ppermute | solution.py:194
  33.3 0.3 slice_reduce_fusion.5
  33.6 0.4 copy-done
  34.5 0.8 %slice-done = f32[4,32,128]{2,1,0:T(8,128)S(1)} async-done(((f32[4,168,128]{2,1,0:T(8,128)}), f32[4,32,128]{2,1,0:T(8,128)S(1)}, s32[]{:S(2)}) %slice-start) | async-done | bytes 65560 | tf_op jit(solution)/shard_map/slice | solution.py:204
  35.4 1.0 %collective-permute-start.9 = (f32[4,96,128]{2,1,0:T(8,128)S(1)}, f32[4,96,128]{2,1,0:T(8,128)S(1)}, u32[]{:S(2)}, u32[]{:S(2)}) collective-permute-start(f32[4,96,128]{2,1,0:T(8,128)S(1)} %pad_maximum_fusion.5), channel_id=1, source_target_pairs={{0,1},{1,0},{2,3},{3,2},{4,5},{5,4},{6,7},{7,6},{8,9},{9,8},{10,11... | collective-permute-start | bytes 589832 | tf_op jit(solution)/shard_map/ppermute | solution.py:77
  36.4 2.0 %collective-permute-start.11 = (f32[4,1,32,128]{3,2,1,0:T(8,128)S(1)}, f32[4,1,32,128]{3,2,1,0:T(8,128)S(1)}, u32[]{:S(2)}, u32[]{:S(2)}) collective-permute-start(f32[4,1,32,128]{3,2,1,0:T(8,128)S(1)} %slice.442), channel_id=1, source_target_pairs={{2,0},{3,1},{4,2},{5,3},{6,4},{7,5},{0,6},{1,7},{10,8},{11,9},{12,... | collective-permute-start | bytes 196616 | tf_op jit(solution)/shard_map/ppermute | solution.py:227
  38.5 4.4 %collective-permute-done.11 = f32[4,1,32,128]{3,2,1,0:T(8,128)S(1)} collective-permute-done((f32[4,1,32,128]{3,2,1,0:T(8,128)S(1)}, f32[4,1,32,128]{3,2,1,0:T(8,128)S(1)}, u32[]{:S(2)}, u32[]{:S(2)}) %collective-permute-start.11) | collective-permute-done | bytes 65568 | tf_op jit(solution)/shard_map/ppermute | solution.py:227
  42.9 0.4 collective-permute-done.10
  43.4 0.3 slice_reduce_fusion.3
  44.6 0.7 %copy-done.2 = f32[4,5,32,128]{3,2,1,0:T(8,128)} copy-done((f32[4,5,32,128]{3,2,1,0:T(8,128)}, f32[4,5,32,128]{3,2,1,0:T(8,128)S(1)}, u32[]{:S(2)}) %copy-start.2) | copy-done | bytes 327704
  45.3 0.4 copy-done.1
  45.9 0.8 %slice-done.1 = f32[3,5,32,128]{3,2,1,0:T(8,128)S(1)} async-done(((f32[4,5,32,128]{3,2,1,0:T(8,128)}), f32[3,5,32,128]{3,2,1,0:T(8,128)S(1)}, s32[]{:S(2)}) %slice-start.1) | async-done | bytes 245784 | tf_op jit(solution)/shard_map/jit(_roll_static)/slice | solution.py:110
  46.6 1.1 %fusion.7 = f32[4,5,32,128]{3,2,1,0:T(8,128)S(1)} fusion(f32[4,5,32,128]{3,2,1,0:T(8,128)} %copy-done.2, f32[4,6,32,128]{3,2,1,0:T(8,128)S(1)} %get-tuple-element.43, f32[3,5,32,128]{3,2,1,0:T(8,128)S(1)} %slice-done.1, f32[1,5,32,128]{3,2,1,0:T(8,128)S(1)} %slice.451, f32[4]{0:T(128)S(1)} %get-tuple-element.71), kind=kLoop, calls=%fused_computation.17 | loop fusion | flops 409600 | bytes 1638416 | tf_op jit(solution)/shard_map/sub | solution.py:110
  47.7 0.4 fusion.71
  48.4 0.6 %copy-done.3 = f32[4,3,32,128]{3,2,1,0:T(8,128)} copy-done((f32[4,3,32,128]{3,2,1,0:T(8,128)}, f32[4,3,32,128]{3,2,1,0:T(8,128)S(1)}, u32[]{:S(2)}) %copy-start.3) | copy-done | bytes 196632
  49.2 0.8 %copy-done.4 = f32[4,3,32,128]{3,2,1,0:T(8,128)S(1)} copy-done((f32[4,3,32,128]{3,2,1,0:T(8,128)S(1)}, f32[4,3,32,128]{3,2,1,0:T(8,128)}, u32[]{:S(2)}) %copy-start.4) | copy-done | bytes 196632
  50.1 0.3 fusion.12
  51.0 1.0 %collective-permute-done.12 = f32[8,128]{1,0:T(8,128)S(1)} collective-permute-done((f32[8,128]{1,0:T(8,128)S(1)}, f32[8,128]{1,0:T(8,128)S(1)}, u32[]{:S(2)}, u32[]{:S(2)}) %collective-permute-start.12) | collective-permute-done | bytes 4128 | tf_op jit(solution)/shard_map/ppermute | solution.py:77
  52.0 1.9 %collective-permute-start.15 = (f32[8,128]{1,0:T(8,128)S(1)}, f32[8,128]{1,0:T(8,128)S(1)}, u32[]{:S(2)}, u32[]{:S(2)}) collective-permute-start(f32[8,128]{1,0:T(8,128)S(1)} %add.180), channel_id=1, source_target_pairs={{0,6},{1,7},{2,4},{3,5},{4,2},{5,3},{6,0},{7,1},{8,14},{9,15},{10,... | collective-permute-start | bytes 12296 | tf_op jit(solution)/shard_map/ppermute | solution.py:77
  53.9 0.4 collective-permute-start.14
  54.3 1.2 %collective-permute-start.13 = (f32[8,128]{1,0:T(8,128)S(1)}, f32[8,128]{1,0:T(8,128)S(1)}, u32[]{:S(2)}, u32[]{:S(2)}) collective-permute-start(f32[8,128]{1,0:T(8,128)S(1)} %add.180), channel_id=1, source_target_pairs={{0,2},{1,3},{2,0},{3,1},{4,6},{5,7},{6,4},{7,5},{8,10},{9,11},{10,... | collective-permute-start | bytes 12296 | tf_op jit(solution)/shard_map/ppermute | solution.py:77
  55.5 1.0 %collective-permute-done.15 = f32[8,128]{1,0:T(8,128)S(1)} collective-permute-done((f32[8,128]{1,0:T(8,128)S(1)}, f32[8,128]{1,0:T(8,128)S(1)}, u32[]{:S(2)}, u32[]{:S(2)}) %collective-permute-start.15) | collective-permute-done | bytes 4128 | tf_op jit(solution)/shard_map/ppermute | solution.py:77
  56.5 1.0 %collective-permute-done.14 = f32[8,128]{1,0:T(8,128)S(1)} collective-permute-done((f32[8,128]{1,0:T(8,128)S(1)}, f32[8,128]{1,0:T(8,128)S(1)}, u32[]{:S(2)}, u32[]{:S(2)}) %collective-permute-start.14) | collective-permute-done | bytes 4128 | tf_op jit(solution)/shard_map/ppermute | solution.py:77
  57.5 0.4 collective-permute-done.13
  57.9 0.3 fusion.2
  58.2 0.9 %fusion = f32[1,2,128,128]{3,2,1,0:T(8,128)} fusion(f32[2,128,128]{2,1,0:T(8,128)S(1)} %fusion.2, f32[2,128,128]{2,1,0:T(8,128)S(1)} %copy-done.7, f32[4,3,32,128]{3,2,1,0:T(8,128)S(1)} %fusion.11, f32[4,5,32,128]{3,2,1,0:T(8,128)S(1)} %fusion.7, f32[128]{0:T(128)S(1)} %get-tuple-element.36, f32[128]{0:T(128)S(1)} %get-tuple-element.35), kind=kOutput, calls=%fused_computation.1 | convolution fusion | flops 12640256 | bytes 459776 | tf_op jit(solution)/shard_map/cij,cjp->cip/dot_general | solution.py:281
  (139 shorter events, 4.6 us)
Async XLA Ops:
  0.0 5.0 %copy-start.5 = (f32[1,2,128,128]{3,2,1,0:T(8,128)S(1)}, f32[1,2,128,128]{3,2,1,0:T(8,128)}, u32[]{:S(2)}) copy-start(f32[1,2,128,128]{3,2,1,0:T(8,128)} %param.11) | copy-start | bytes 393220
  1.6 3.4 %copy-start.13 = (s32[1,1,64]{2,1,0:T(1,128)S(1)}, s32[1,1,64]{2,1,0:T(1,128)}, u32[]{:S(2)}) copy-start(s32[1,1,64]{2,1,0:T(1,128)} %param.16) | copy-start | bytes 772
  1.6 15.6 %collective-permute-start.4 = (f32[64,128]{1,0:T(8,128)S(1)}, f32[64,128]{1,0:T(8,128)S(1)}, u32[]{:S(2)}, u32[]{:S(2)}) collective-permute-start(f32[64,128]{1,0:T(8,128)S(1)} %get-tuple-element.59), channel_id=1, source_target_pairs={{0,7},{1,2},{2,1},{3,4},{4,3},{5,6},{6,5},{7,0},{8,15},{9,10},{10,... | collective-permute-start | bytes 98312 | tf_op jit(solution)/shard_map/ppermute | solution.py:101
  5.0 12.2 %collective-permute-start.5 = (f32[64,128]{1,0:T(8,128)S(1)}, f32[64,128]{1,0:T(8,128)S(1)}, u32[]{:S(2)}, u32[]{:S(2)}) collective-permute-start(f32[64,128]{1,0:T(8,128)S(1)} %get-tuple-element.60), channel_id=1, source_target_pairs={{0,1},{1,0},{2,3},{3,2},{4,5},{5,4},{6,7},{7,6},{8,9},{9,8},{10,11... | collective-permute-start | bytes 98312 | tf_op jit(solution)/shard_map/ppermute | solution.py:77
  5.0 0.7 %copy-start.11 = (s32[1,1,8,8]{3,2,1,0:T(8,128)S(1)}, s32[1,1,8,8]{3,2,1,0:T(8,128)}, u32[]{:S(2)}) copy-start(s32[1,1,8,8]{3,2,1,0:T(8,128)} %param.17) | copy-start | bytes 772
  5.1 0.7 %copy-start.12 = (f32[1,1,8,8]{3,2,1,0:T(8,128)S(1)}, f32[1,1,8,8]{3,2,1,0:T(8,128)}, u32[]{:S(2)}) copy-start(f32[1,1,8,8]{3,2,1,0:T(8,128)} %param.21) | copy-start | bytes 772
  5.1 8.5 %collective-permute-start = (f32[64,128]{1,0:T(8,128)S(1)}, f32[64,128]{1,0:T(8,128)S(1)}, u32[]{:S(2)}, u32[]{:S(2)}) collective-permute-start(f32[64,128]{1,0:T(8,128)S(1)} %get-tuple-element.42), channel_id=1, source_target_pairs={{0,1},{1,0},{2,3},{3,2},{4,5},{5,4},{6,7},{7,6},{8,9},{9,8},{10,11... | collective-permute-start | bytes 98312 | tf_op jit(solution)/shard_map/ppermute | solution.py:77
  5.9 0.7 %copy-start.14 = (s32[1,1,8]{2,1,0:T(1,128)S(1)}, s32[1,1,8]{2,1,0:T(1,128)}, u32[]{:S(2)}) copy-start(s32[1,1,8]{2,1,0:T(1,128)} %param.18) | copy-start | bytes 100
  6.7 0.7 %copy-start.9 = (s32[1,1,8,8]{3,2,1,0:T(8,128)S(1)}, s32[1,1,8,8]{3,2,1,0:T(8,128)}, u32[]{:S(2)}) copy-start(s32[1,1,8,8]{3,2,1,0:T(8,128)} %param.20) | copy-start | bytes 772
  6.7 0.7 %copy-start.10 = (s32[1,1,8,8]{3,2,1,0:T(8,128)S(1)}, s32[1,1,8,8]{3,2,1,0:T(8,128)}, u32[]{:S(2)}) copy-start(s32[1,1,8,8]{3,2,1,0:T(8,128)} %param.19) | copy-start | bytes 772
  12.2 0.9 %copy-start.6 = (f32[1,2,128,128]{3,2,1,0:T(8,128)S(1)}, f32[1,2,128,128]{3,2,1,0:T(8,128)}, u32[]{:S(2)}) copy-start(f32[1,2,128,128]{3,2,1,0:T(8,128)} %param.11) | copy-start | bytes 393220
  13.7 7.4 %collective-permute-start.3 = (f32[128,128]{1,0:T(8,128)S(1)}, f32[128,128]{1,0:T(8,128)S(1)}, u32[]{:S(2)}, u32[]{:S(2)}) collective-permute-start(f32[128,128]{1,0:T(8,128)S(1)} %pad_maximum_fusion.10), channel_id=1, source_target_pairs={{0,6},{1,7},{2,4},{3,5},{4,2},{5,3},{6,0},{7,1},{8,14},{9,15},{10,... | collective-permute-start | bytes 196616 | tf_op jit(solution)/shard_map/ppermute | solution.py:77
  14.9 6.2 %collective-permute-start.2 = (f32[128,128]{1,0:T(8,128)S(1)}, f32[128,128]{1,0:T(8,128)S(1)}, u32[]{:S(2)}, u32[]{:S(2)}) collective-permute-start(f32[128,128]{1,0:T(8,128)S(1)} %pad_maximum_fusion.10), channel_id=1, source_target_pairs={{0,4},{1,5},{2,6},{3,7},{4,0},{5,1},{6,2},{7,3},{8,12},{9,13},{10,... | collective-permute-start | bytes 196616 | tf_op jit(solution)/shard_map/ppermute | solution.py:77
  16.8 4.3 %collective-permute-start.1 = (f32[128,128]{1,0:T(8,128)S(1)}, f32[128,128]{1,0:T(8,128)S(1)}, u32[]{:S(2)}, u32[]{:S(2)}) collective-permute-start(f32[128,128]{1,0:T(8,128)S(1)} %pad_maximum_fusion.10), channel_id=1, source_target_pairs={{0,2},{1,3},{2,0},{3,1},{4,6},{5,7},{6,4},{7,5},{8,10},{9,11},{10,... | collective-permute-start | bytes 196616 | tf_op jit(solution)/shard_map/ppermute | solution.py:77
  21.1 0.9 %copy-start.8 = (f32[2,128,128]{2,1,0:T(8,128)S(1)}, f32[2,128,128]{2,1,0:T(8,128)}, u32[]{:S(2)}) copy-start(f32[2,128,128]{2,1,0:T(8,128)} %get-tuple-element.10) | copy-start | bytes 393220
  22.0 0.9 %copy-start.7 = (f32[2,128,128]{2,1,0:T(8,128)S(1)}, f32[2,128,128]{2,1,0:T(8,128)}, u32[]{:S(2)}) copy-start(f32[2,128,128]{2,1,0:T(8,128)} %get-tuple-element.9) | copy-start | bytes 393220
  23.2 8.1 %collective-permute-start.7 = (f32[168,128]{1,0:T(8,128)S(1)}, f32[168,128]{1,0:T(8,128)S(1)}, u32[]{:S(2)}, u32[]{:S(2)}) collective-permute-start(f32[168,128]{1,0:T(8,128)S(1)} %get-tuple-element.58), channel_id=1, source_target_pairs={{16,0},{24,8},{0,16},{8,24},{17,1},{25,9},{1,17},{9,25},{18,2},{26... | collective-permute-start | bytes 258056 | tf_op jit(solution)/shard_map/ppermute | solution.py:194
  25.5 6.0 %collective-permute-start.6 = (f32[168,128]{1,0:T(8,128)S(1)}, f32[168,128]{1,0:T(8,128)S(1)}, u32[]{:S(2)}, u32[]{:S(2)}) collective-permute-start(f32[168,128]{1,0:T(8,128)S(1)} %get-tuple-element.58), channel_id=1, source_target_pairs={{8,0},{16,8},{24,16},{0,24},{9,1},{17,9},{25,17},{1,25},{10,2},{18... | collective-permute-start | bytes 258056 | tf_op jit(solution)/shard_map/ppermute | solution.py:194
  26.9 6.3 %collective-permute-start.8 = (f32[168,128]{1,0:T(8,128)S(1)}, f32[168,128]{1,0:T(8,128)S(1)}, u32[]{:S(2)}, u32[]{:S(2)}) collective-permute-start(f32[168,128]{1,0:T(8,128)S(1)} %get-tuple-element.58), channel_id=1, source_target_pairs={{24,0},{0,8},{8,16},{16,24},{25,1},{1,9},{9,17},{17,25},{26,2},{2,... | collective-permute-start | bytes 258056 | tf_op jit(solution)/shard_map/ppermute | solution.py:194
  33.2 0.7 %copy-start = (f32[4,168,128]{2,1,0:T(8,128)}, f32[4,168,128]{2,1,0:T(8,128)S(1)}, u32[]{:S(2)}) copy-start(f32[4,168,128]{2,1,0:T(8,128)S(1)} %pad_maximum_fusion.4) | copy-start | bytes 1032196
  34.5 0.8 %slice-start = ((f32[4,168,128]{2,1,0:T(8,128)}), f32[4,32,128]{2,1,0:T(8,128)S(1)}, s32[]{:S(2)}) async-start(f32[4,168,128]{2,1,0:T(8,128)} %copy-done), calls=%async_computation | async-start | bytes 131072 | tf_op jit(solution)/shard_map/slice | solution.py:204
  35.4 8.0 %collective-permute-start.10 = (f32[4,96,128]{2,1,0:T(8,128)S(1)}, f32[4,96,128]{2,1,0:T(8,128)S(1)}, u32[]{:S(2)}, u32[]{:S(2)}) collective-permute-start(f32[4,96,128]{2,1,0:T(8,128)S(1)} %pad_maximum_fusion.5), channel_id=1, source_target_pairs={{0,7},{1,2},{2,1},{3,4},{4,3},{5,6},{6,5},{7,0},{8,15},{9,10},{10,... | collective-permute-start | bytes 589832 | tf_op jit(solution)/shard_map/ppermute | solution.py:101
  35.4 7.9 %collective-permute-start.9 = (f32[4,96,128]{2,1,0:T(8,128)S(1)}, f32[4,96,128]{2,1,0:T(8,128)S(1)}, u32[]{:S(2)}, u32[]{:S(2)}) collective-permute-start(f32[4,96,128]{2,1,0:T(8,128)S(1)} %pad_maximum_fusion.5), channel_id=1, source_target_pairs={{0,1},{1,0},{2,3},{3,2},{4,5},{5,4},{6,7},{7,6},{8,9},{9,8},{10,11... | collective-permute-start | bytes 589832 | tf_op jit(solution)/shard_map/ppermute | solution.py:77
  36.4 6.5 %collective-permute-start.11 = (f32[4,1,32,128]{3,2,1,0:T(8,128)S(1)}, f32[4,1,32,128]{3,2,1,0:T(8,128)S(1)}, u32[]{:S(2)}, u32[]{:S(2)}) collective-permute-start(f32[4,1,32,128]{3,2,1,0:T(8,128)S(1)} %slice.442), channel_id=1, source_target_pairs={{2,0},{3,1},{4,2},{5,3},{6,4},{7,5},{0,6},{1,7},{10,8},{11,9},{12,... | collective-permute-start | bytes 196616 | tf_op jit(solution)/shard_map/ppermute | solution.py:227
  44.6 0.7 %copy-start.2 = (f32[4,5,32,128]{3,2,1,0:T(8,128)}, f32[4,5,32,128]{3,2,1,0:T(8,128)S(1)}, u32[]{:S(2)}) copy-start(f32[4,5,32,128]{3,2,1,0:T(8,128)S(1)} %fusion.5) | copy-start | bytes 983044
  44.6 1.1 %copy-start.1 = (f32[4,168,128]{2,1,0:T(8,128)S(1)}, f32[4,168,128]{2,1,0:T(8,128)}, u32[]{:S(2)}) copy-start(f32[4,168,128]{2,1,0:T(8,128)} %copy-done) | copy-start | bytes 1032196
  45.7 0.9 %slice-start.1 = ((f32[4,5,32,128]{3,2,1,0:T(8,128)}), f32[3,5,32,128]{3,2,1,0:T(8,128)S(1)}, s32[]{:S(2)}) async-start(f32[4,5,32,128]{3,2,1,0:T(8,128)} %copy-done.2), calls=%async_computation.1 | async-start | bytes 491520 | tf_op jit(solution)/shard_map/jit(_roll_static)/slice | solution.py:110
  48.4 0.7 %copy-start.3 = (f32[4,3,32,128]{3,2,1,0:T(8,128)}, f32[4,3,32,128]{3,2,1,0:T(8,128)S(1)}, u32[]{:S(2)}) copy-start(f32[4,3,32,128]{3,2,1,0:T(8,128)S(1)} %fusion.9) | copy-start | bytes 589828
  49.1 0.9 %copy-start.4 = (f32[4,3,32,128]{3,2,1,0:T(8,128)S(1)}, f32[4,3,32,128]{3,2,1,0:T(8,128)}, u32[]{:S(2)}) copy-start(f32[4,3,32,128]{3,2,1,0:T(8,128)} %copy-done.3) | copy-start | bytes 589828
  49.1 1.0 %slice-start.2 = ((f32[4,3,32,128]{3,2,1,0:T(8,128)}), f32[3,3,32,128]{3,2,1,0:T(8,128)S(1)}, s32[]{:S(2)}) async-start(f32[4,3,32,128]{3,2,1,0:T(8,128)} %copy-done.3), calls=%async_computation.2 | async-start | bytes 294912 | tf_op jit(solution)/shard_map/jit(_roll_static)/slice | solution.py:110
  50.8 1.2 %collective-permute-start.12 = (f32[8,128]{1,0:T(8,128)S(1)}, f32[8,128]{1,0:T(8,128)S(1)}, u32[]{:S(2)}, u32[]{:S(2)}) collective-permute-start(f32[8,128]{1,0:T(8,128)S(1)} %stack.140), channel_id=1, source_target_pairs={{0,1},{1,0},{2,3},{3,2},{4,5},{5,4},{6,7},{7,6},{8,9},{9,8},{10,11... | collective-permute-start | bytes 12296 | tf_op jit(solution)/shard_map/ppermute | solution.py:77
  52.0 4.5 %collective-permute-start.15 = (f32[8,128]{1,0:T(8,128)S(1)}, f32[8,128]{1,0:T(8,128)S(1)}, u32[]{:S(2)}, u32[]{:S(2)}) collective-permute-start(f32[8,128]{1,0:T(8,128)S(1)} %add.180), channel_id=1, source_target_pairs={{0,6},{1,7},{2,4},{3,5},{4,2},{5,3},{6,0},{7,1},{8,14},{9,15},{10,... | collective-permute-start | bytes 12296 | tf_op jit(solution)/shard_map/ppermute | solution.py:77
  53.9 3.6 %collective-permute-start.14 = (f32[8,128]{1,0:T(8,128)S(1)}, f32[8,128]{1,0:T(8,128)S(1)}, u32[]{:S(2)}, u32[]{:S(2)}) collective-permute-start(f32[8,128]{1,0:T(8,128)S(1)} %add.180), channel_id=1, source_target_pairs={{0,4},{1,5},{2,6},{3,7},{4,0},{5,1},{6,2},{7,3},{8,12},{9,13},{10,... | collective-permute-start | bytes 12296 | tf_op jit(solution)/shard_map/ppermute | solution.py:77
  54.3 3.6 %collective-permute-start.13 = (f32[8,128]{1,0:T(8,128)S(1)}, f32[8,128]{1,0:T(8,128)S(1)}, u32[]{:S(2)}, u32[]{:S(2)}) collective-permute-start(f32[8,128]{1,0:T(8,128)S(1)} %add.180), channel_id=1, source_target_pairs={{0,2},{1,3},{2,0},{3,1},{4,6},{5,7},{6,4},{7,5},{8,10},{9,11},{10,... | collective-permute-start | bytes 12296 | tf_op jit(solution)/shard_map/ppermute | solution.py:77

commit v2 on v1

--- a/solution.py
+++ b/solution.py
@@ -77,8 +77,8 @@
     return lax.ppermute(block, axis, [(i, i ^ distance) for i in range(count)])
 
 
-def xor_gather(block, axis, count):
-    blocks, held = [block], 1
+def xor_gather(block, axis, count, held):
+    blocks = [block]
     while held < count:
         whole = jnp.concatenate(blocks, axis=0)
         reach = 2 if (count // held).bit_length() % 2 == 0 else 4
@@ -99,15 +99,6 @@
 def outer(block, axis, count):
     pairs = [(i, (i + 1) % count if i % 2 else (i - 1) % count) for i in range(count)]
     return lax.ppermute(block, axis, pairs)
-
-
-def south_flow(rim, gain, not_last):
-    below = jnp.roll(rim, -1, axis=0) * not_last
-    return gain * (rim - below), rim - below
-
-
-def net_flow(east, south, not_first):
-    return east[:, 1:] - east[:, :-1] + south - jnp.roll(south, 1, axis=0) * not_first
 
 
 def local(
@@ -133,13 +124,41 @@
     edge = track_gain.shape[-1]
     nets = driver_tile.shape[-1]
     voltage = initial_voltage[0]
-    rims = voltage[:, :edge]
-    east_gain, south_gain = track_gain[0, :, 0, :, None], track_gain[0, :, 1, :, None]
 
     picked = driver_tile.reshape((nets, 1))
     node_of = voltage[:, :nets] if nets <= nodes else jnp.tile(voltage, (1, -(-nets // nodes), 1))[:, :nets]
     drivers = sum(jnp.where(picked == t, node_of[t], 0.0) for t in range(tiles))
-    gathered = xor_gather(drivers, "col", cols)
+    paired = jnp.concatenate([drivers, other(drivers, "col", cols, 1)], axis=0)
+    (
+        paired,
+        voltage,
+        inject,
+        conduct,
+        capacitance,
+        track_gain,
+        sink_net,
+        sink_count,
+        sink_tile,
+        sink_node,
+        sink_gain,
+    ) = lax.optimization_barrier(
+        (
+            paired,
+            voltage,
+            inject,
+            conduct,
+            capacitance,
+            track_gain,
+            sink_net,
+            sink_count,
+            sink_tile,
+            sink_node,
+            sink_gain,
+        )
+    )
+    rims = voltage[:, :edge]
+    east_gain, south_gain = track_gain[0, :, 0, :, None], track_gain[0, :, 1, :, None]
+    gathered = xor_gather(paired, "col", cols, 2)
 
     wide = jnp.broadcast_to(east_gain[-1], (edge, patterns))
     inner0 = other(jnp.concatenate([jnp.where(odd, rims[0], rims[1]), wide]), "col", cols, 1)
@@ -188,77 +207,93 @@
             jnp.pad(first[None], ((0, 7), (0, 0))),
         ]
     )
-    column = jnp.stack(
-        [message]
-        + [
-            lax.ppermute(message, "row", [((i + k) % rows, i) for i in range(rows)])
-            for k in range(1, rows)
-        ]
-    )
-    true_row = (my_row + jnp.arange(rows, dtype=jnp.int32)) % rows
-    not_first = (true_row > 0).astype(jnp.float32)[:, None, None, None]
-    not_last = (true_row < rows - 1).astype(jnp.float32)[:, None, None, None]
+    column = [message] + [
+        lax.ppermute(message, "row", [((i + k) % rows, i) for i in range(rows)])
+        for k in range(1, rows)
+    ]
+    true_row = [(my_row + k) % rows for k in range(rows)]
+    not_first = [(r > 0).astype(jnp.float32) for r in true_row]
+    not_last = [(r < rows - 1).astype(jnp.float32) for r in true_row]
     span = tiles * edge
-    raw = column[:, :span].reshape((rows, tiles, edge, patterns))
-    start = column[:, span : 2 * span].reshape((rows, tiles, edge, patterns))
-    table = column[:, 2 * span : 2 * span + edge]
-    first = jnp.sum(column[:, 2 * span + edge], axis=0)
 
     def unpack(table):
-        cores = jnp.stack([table[:, :, :edge], table[:, :, edge : 2 * edge]], axis=1)
-        gains = [table[:, :, 2 * edge + k : 2 * edge + k + 1] for k in range(4)]
-        return cores, jnp.stack(gains[:2], axis=1), jnp.stack(gains[2:], axis=1)
+        cores = jnp.stack([table[:, :edge], table[:, edge : 2 * edge]])
+        gains = [table[:, 2 * edge + k : 2 * edge + k + 1] for k in range(4)]
+        return cores, jnp.stack(gains[:2]), jnp.stack(gains[2:])
 
     def spread(cores, flow):
-        return jnp.einsum("rcij,rcjp->rcip", cores, flow, precision=PRECISE)
-
-    cores, easts, souths = unpack(table)
-    south0, _ = south_flow(start, souths, not_last)
-    vertical = south0 - jnp.roll(south0, 1, axis=0) * not_first
-    u0 = raw - spread(cores, vertical)
-    first = first - jnp.sum(vertical * (raw + u0), axis=(0, 1, 2))
-    precond = precond - jnp.einsum(
-        "cij,cjp->cip", inverse[:, :, :edge], vertical[0], precision=PRECISE
-    )
-
-    message = jnp.concatenate([u0.reshape((rows, span, patterns)), table], axis=1)
+        return jnp.einsum("cij,cjp->cip", cores, flow, precision=PRECISE)
+
+    def south_drops(rims):
+        return [rims[k] - rims[(k + 1) % rows] * not_last[k] for k in range(rows)]
+
+    def vertical(flows):
+        return [flows[k] - flows[k - 1] * not_first[k] for k in range(rows)]
+
+    raw = [block[:span].reshape((tiles, edge, patterns)) for block in column]
+    start = [block[span : 2 * span].reshape((tiles, edge, patterns)) for block in column]
+    table = [block[2 * span : 2 * span + edge] for block in column]
+    first = sum(block[2 * span + edge] for block in column)
+    cores, easts, souths = zip(*[unpack(t) for t in table])
+    flow = vertical([g * d for g, d in zip(souths, south_drops(start))])
+    u0 = [raw[k] - spread(cores[k], flow[k]) for k in range(rows)]
+    first = first - sum(jnp.sum(flow[k] * (raw[k] + u0[k]), axis=(0, 1)) for k in range(rows))
+    precond = precond - spread(inverse[:, :, :edge], flow[0])
+
+    message = jnp.concatenate(
+        [piece for k in range(rows) for piece in (u0[k].reshape((span, patterns)), table[k])]
+    )
     inner = other(message, "col", cols, 1)
     beyond = outer(message, "col", cols)
-    far = lax.ppermute(u0[:, :1], "col", [((i + 2) % cols, i) for i in range(cols)]) * has_far
+    far = lax.ppermute(
+        jnp.concatenate([u[0] for u in u0]), "col", [((i + 2) % cols, i) for i in range(cols)]
+    )
+    far = far * has_far
     west = jnp.where(odd, inner, beyond) * has_west
     east = jnp.where(odd, beyond, inner) * has_east
-
-    def parts(block):
-        return (block[:, :span].reshape((rows, tiles, edge, patterns)),) + unpack(block[:, span:])
-
-    west_u, west_cores, west_easts, west_souths = parts(west)
-    east_u, east_cores, east_easts, east_souths = parts(east)
-    u0 = jnp.concatenate([west_u, u0, east_u, far], axis=1)
-    cores = jnp.concatenate([west_cores[:, 1:], cores, east_cores], axis=1)
-    easts = jnp.concatenate([west_easts, easts, east_easts], axis=1)
-    souths = jnp.concatenate([west_souths[:, 1:], souths, east_souths], axis=1)
-
-    south, _ = south_flow(u0[:, 1:-1], souths, not_last)
-    t0 = net_flow(easts * (u0[:, :-1] - u0[:, 1:]), south, not_first)
-    u1 = spread(cores, t0)
-    south, _ = south_flow(u1[:, 1:-1], souths[:, 1:-1], not_last)
-    t1 = net_flow(easts[:, 1:-1] * (u1[:, :-1] - u1[:, 1:]), south, not_first)
-    u2 = spread(cores[:, 1:-1], t1)
-    south, drop = south_flow(u2[:, :-1], souths[:, 1:3], not_last)
-    ahead = u2[:, :-1] - u2[:, 1:]
+    stride = span + edge
+
+    def parts(block, k):
+        block = block[k * stride : (k + 1) * stride]
+        return (block[:span].reshape((tiles, edge, patterns)),) + unpack(block[span:])
+
+    wide_u0, wide_cores, wide_easts, wide_souths, mid_cores = [], [], [], [], []
+    for k in range(rows):
+        west_u, west_cores, west_easts, west_souths = parts(west, k)
+        east_u, east_cores, east_easts, east_souths = parts(east, k)
+        wide_u0.append(
+            jnp.concatenate([west_u, u0[k], east_u, far[None, k * edge : (k + 1) * edge]])
+        )
+        wide_cores.append(jnp.concatenate([west_cores[1:], cores[k], east_cores]))
+        mid_cores.append(jnp.concatenate([cores[k], east_cores[:1]]))
+        wide_easts.append(jnp.concatenate([west_easts, easts[k], east_easts]))
+        wide_souths.append(jnp.concatenate([west_souths[1:], souths[k], east_souths]))
+
+    def net_flow(rims, easts, souths):
+        across = [g * (u[:-1] - u[1:]) for g, u in zip(easts, rims)]
+        down = vertical([g * d for g, d in zip(souths, south_drops([u[1:-1] for u in rims]))])
+        return [a[1:] - a[:-1] + d for a, d in zip(across, down)]
+
+    t0 = net_flow(wide_u0, wide_easts, wide_souths)
+    u1 = [spread(c, t) for c, t in zip(wide_cores, t0)]
+    t1 = net_flow(u1, [g[1:-1] for g in wide_easts], [g[1:-1] for g in wide_souths])
+    u2 = [spread(c, t) for c, t in zip(mid_cores, t1)]
+    drops = south_drops([u[:2] for u in u2])
 
     def total(left, right):
-        return jnp.sum(left * right, axis=(0, 1, 2))
-
-    own_t0, own_u1, own_t1 = t0[:, 1:3], u1[:, 1:3], t1[:, :2]
+        return sum(jnp.sum(a * b, axis=(0, 1)) for a, b in zip(left, right))
+
+    own_t0, own_u1, own_t1 = [t[1:3] for t in t0], [u[1:3] for u in u1], [t[:2] for t in t1]
+    ahead = [u[:2] - u[1:] for u in u2]
     moments = jnp.stack(
         [
             first,
-            total(u0[:, 2:4], own_t0),
+            total([u[2:4] for u in wide_u0], own_t0),
             total(own_u1, own_t0),
             total(own_u1, own_t1),
-            total(u2[:, :2], own_t1),
-            total(south, drop) + total(easts[:, 2:4] * ahead, ahead),
+            total([u[:2] for u in u2], own_t1),
+            total([g[1:3] * d for g, d in zip(wide_souths, drops)], drops)
+            + total([g[2:4] * d for g, d in zip(wide_easts, ahead)], ahead),
             jnp.zeros_like(first),
             jnp.zeros_like(first),
         ]
@@ -277,7 +312,7 @@
     c2 = y2 / d2
     c1 = y1 / d1 - l12 * c2
     c0 = m[0] / a00 - l1 * c1 - l2 * c2
-    mixed = c1 * t0[0, 1:3] + c2 * t1[0, :2]
+    mixed = c1 * own_t0[0] + c2 * own_t1[0]
     update = jnp.einsum("cij,cjp->cip", inverse[:, :, :edge], mixed, precision=PRECISE)
     return (voltage + c0 * precond + update)[None]
 

time: 59.8 us -> 54.2 us (0.906)
  local copies, waits for them, and re-layouts: 11.1 us -> 6.13 us
  waiting for transfers between devices: 17.6 us -> 14 us
  matrix products: 3.7 us -> 4.9 us
  starting transfers between devices: 18.6 us -> 19.7 us
    unnamed x46 -> x74, local copies, waits for them, and re-layouts: 5.8 us -> 2.26 us
    ppermute x10, waiting for transfers between devices: 7.15 us -> 4.74 us  [other(): return lax.ppermute(block, axis, [(i, i ^ distance) for i in range(count)])]
    ppermute x3, waiting for transfers between devices: 5.61 us -> 4.22 us  [local(): lax.ppermute(message, 'row', [((i + k) % rows, i) for i in range(rows)])]
    add x1 -> x10, other arithmetic: 0.01 us -> 1.39 us  [the longest x1 0.86 us: local(): sum((jnp.where(picked == t, node_of[t], 0.0) for t in range(tiles)))]
    ppermute x10, starting transfers between devices: 8.81 us -> 10.2 us  [other(): return lax.ppermute(block, axis, [(i, i ^ distance) for i in range(count)])]
    ppermute x3, starting transfers between devices: 4.32 us -> 5.56 us  [local(): lax.ppermute(message, 'row', [((i + k) % rows, i) for i in range(rows)])]
    dot_general x4 -> x13, matrix products: 1.28 us -> 2.48 us  [spread(): return jnp.einsum('cij,cjp->cip', cores, flow, precision=PRECISE)]
    sub x4 -> x2, other arithmetic: 1.25 us -> 0.12 us  [the longest x1 0.1 us: vertical(): return [flows[k] - flows[k - 1] * not_first[k] for k in range(rows)]]
  transfers between devices with their start and end apart: 16 -> 16, of which waited for: 10 -> 8; matrix products, arithmetic and copies ran while one was open for 5% -> 6% of each run, Pallas kernels for 6% -> 8%
where the time goes in v2:
time: 54.2 us; the launch traced here: 53.7 us
  starting transfers between devices  19.7 us (36%)
  waiting for transfers between devices  14 us (26%)
  local copies, waits for them, and re-layouts  6.13 us (11%)
  matrix products  4.9 us (9%)
  Pallas kernels  4.16 us (8%)
  other arithmetic  3.92 us (7%)
  between operations  0.94 us (2%)
    ppermute x10, starting transfers between devices, other(): return lax.ppermute(block, axis, [(i, i ^ distance) for i in range(count)])  10.2 us
    ppermute x3, starting transfers between devices, local(): lax.ppermute(message, 'row', [((i + k) % rows, i) for i in range(rows)])  5.56 us
    ppermute x1, waiting for transfers between devices, local(): lax.ppermute(jnp.concatenate([u[0] for u in u0]), 'col', [((i + 2) % cols...  5.05 us
    ppermute x10, waiting for transfers between devices, other(): return lax.ppermute(block, axis, [(i, i ^ distance) for i in range(count)])  4.74 us
    ppermute x3, waiting for transfers between devices, local(): lax.ppermute(message, 'row', [((i + k) % rows, i) for i in range(rows)])  4.22 us
    pallas_call x1, Pallas kernels, tile_inverse(): pl.pallas_call(tile_kernel, out_shape=(block, block), in_specs=[vmem] * 4...  4.16 us
    ppermute x2, starting transfers between devices, outer(): return lax.ppermute(block, axis, pairs)  2.52 us
    dot_general x13, matrix products, spread(): return jnp.einsum('cij,cjp->cip', cores, flow, precision=PRECISE)  2.48 us
  transfers between devices with their start and end apart: 16, of which 8 were waited for; matrix products, arithmetic and copies ran while one was open for 6% of the time, Pallas kernels for 8%

profile of v2, /device:TPU:0, one launch (start us, length us, event | category | flops | bytes accessed | tf_op | source)
XLA Modules:
  0.0 53.7 jit_solution(1035623498978126317)
XLA Ops:
  0.0 0.7 %compare_bitcast_fusion.1 = (pred[64]{0:T(512)(128)(4,1)S(1)}, pred[64]{0:T(512)(128)(4,1)S(1)}) fusion(s32[1,1,64]{2,1,0:T(1,128)} %param.16), kind=kLoop, calls=%fused_computation.359 | loop fusion | flops 128 | bytes 384 | tf_op jit(solution)/shard_map/eq | solution.py:130
  0.7 0.9 %fusion.75 = f32[64,128]{1,0:T(8,128)S(1)} fusion(f32[2,128,128]{2,1,0:T(8,128)} %bitcast.423, pred[64]{0:T(512)(128)(4,1)S(1)} %get-tuple-element.208, pred[64]{0:T(512)(128)(4,1)S(1)} %get-tuple-element.207), kind=kLoop, calls=%fused_computation.210 | loop fusion | flops 24576 | bytes 98432 | tf_op jit(solution)/shard_map/add | solution.py:130
  1.5 0.5 collective-permute-start
  2.2 0.7 %collective-permute-done = f32[64,128]{1,0:T(8,128)S(1)} collective-permute-done((f32[64,128]{1,0:T(8,128)S(1)}, f32[64,128]{1,0:T(8,128)S(1)}, u32[]{:S(2)}, u32[]{:S(2)}) %collective-permute-start) | collective-permute-done | bytes 32800 | tf_op jit(solution)/shard_map/ppermute | solution.py:77
  2.9 3.9 %collective-permute-start.3 = (f32[128,128]{1,0:T(8,128)S(1)}, f32[128,128]{1,0:T(8,128)S(1)}, u32[]{:S(2)}, u32[]{:S(2)}) collective-permute-start(f32[128,128]{1,0:T(8,128)S(1)} %pad_maximum_fusion.18), channel_id=1, source_target_pairs={{0,6},{1,7},{2,4},{3,5},{4,2},{5,3},{6,0},{7,1},{8,14},{9,15},{10,... | collective-permute-start | bytes 196616 | tf_op jit(solution)/shard_map/ppermute | solution.py:77
  6.8 0.5 collective-permute-start.2
  7.6 0.5 copy-done.9
  8.3 0.6 %copy-done.4 = f32[1,2,2,32]{3,2,1,0:T(2,128)S(1)} copy-done((f32[1,2,2,32]{3,2,1,0:T(2,128)S(1)}, f32[1,2,2,32]{3,2,1,0:T(2,128)}, u32[]{:S(2)}) %copy-start.4) | copy-done | bytes 536
  9.1 1.8 %collective-permute-start.4 = (f32[64,128]{1,0:T(8,128)S(1)}, f32[64,128]{1,0:T(8,128)S(1)}, u32[]{:S(2)}, u32[]{:S(2)}) collective-permute-start(f32[64,128]{1,0:T(8,128)S(1)} %get-tuple-element.191), channel_id=1, source_target_pairs={{0,7},{1,2},{2,1},{3,4},{4,3},{5,6},{6,5},{7,0},{8,15},{9,10},{10,... | collective-permute-start | bytes 98312 | tf_op jit(solution)/shard_map/ppermute | solution.py:101
  10.8 0.3 collective-permute-start.5
  11.3 4.2 %shard_map.109 = (f32[2,128,128]{2,1,0:T(8,128)}, f32[2,128,128]{2,1,0:T(8,128)}) custom-call(f32[2,128,128]{2,1,0:T(8,128)} %bitcast.436, f32[2,128]{1,0:T(2,128)} %bitcast.517, f32[2,128,128]{2,1,0:T(8,128)} %bitcast.424, f32[2,128,128]{2,1,0:T(8,128)} %bitcast.437), custom_call_target="tpu_custom_call" | custom-call | tf_op jit(solution)/shard_map/pallas_call | solution.py:67
  15.4 0.7 %slice_bitcast_fusion.28 = (f32[32,32]{1,0:T(8,128)S(1)}, f32[32,32]{1,0:T(8,128)S(1)}) fusion(f32[2,128,128]{2,1,0:T(8,128)} %get-tuple-element.24), kind=kLoop, calls=%fused_computation.336 | loop fusion | bytes 16384 | tf_op jit(solution)/shard_map/squeeze | solution.py:199
  16.2 0.6 %fusion.127 = f32[256,512]{1,0:T(8,128)S(1)} fusion(f32[64,256]{1,0:T(8,128)S(1)} %fusion.39, f32[64,512]{1,0:T(8,128)S(1)} %fusion.11), kind=kOutput, calls=%fused_computation.431 | convolution fusion | flops 100663296 | bytes 720896 | tf_op jit(solution)/shard_map/dot_general | solution.py:180
  16.8 0.3 copy-done.1
  17.7 0.6 %fusion.3 = f32[256,128]{1,0:T(8,128)S(1)} fusion(f32[256,512]{1,0:T(8,128)S(1)} %fusion.127, f32[128,128]{1,0:T(8,128)S(1)} %collective-permute-done.3, f32[128,128]{1,0:T(8,128)S(1)} %collective-permute-done.2, f32[128,128]{1,0:T(8,128)S(1)} %collective-permute-done.1, f32[128,128]{1,0:T(8,128)S(1)} %pad_maximum_fusion.18), kind=kOutput, calls=%fused_computation.9 | convolution fusion | flops 201523200 | bytes 917504 | tf_op jit(solution)/shard_map/dot_general | solution.py:181
  18.3 0.3 copy-done.3
  18.7 0.3 multiply_reduce_fusion
  19.0 1.3 %collective-permute-start.8 = (f32[168,128]{1,0:T(8,128)S(1)}, f32[168,128]{1,0:T(8,128)S(1)}, u32[]{:S(2)}, u32[]{:S(2)}) collective-permute-start(f32[168,128]{1,0:T(8,128)S(1)} %select_maximum_fusion), channel_id=1, source_target_pairs={{24,0},{0,8},{8,16},{16,24},{25,1},{1,9},{9,17},{17,25},{26,2},{2,... | collective-permute-start | bytes 258056 | tf_op jit(solution)/shard_map/ppermute | solution.py:211
  20.3 2.6 %collective-permute-start.7 = (f32[168,128]{1,0:T(8,128)S(1)}, f32[168,128]{1,0:T(8,128)S(1)}, u32[]{:S(2)}, u32[]{:S(2)}) collective-permute-start(f32[168,128]{1,0:T(8,128)S(1)} %select_maximum_fusion), channel_id=1, source_target_pairs={{16,0},{24,8},{0,16},{8,24},{17,1},{25,9},{1,17},{9,25},{18,2},{26... | collective-permute-start | bytes 258056 | tf_op jit(solution)/shard_map/ppermute | solution.py:211
  22.9 1.7 %collective-permute-start.6 = (f32[168,128]{1,0:T(8,128)S(1)}, f32[168,128]{1,0:T(8,128)S(1)}, u32[]{:S(2)}, u32[]{:S(2)}) collective-permute-start(f32[168,128]{1,0:T(8,128)S(1)} %select_maximum_fusion), channel_id=1, source_target_pairs={{8,0},{16,8},{24,16},{0,24},{9,1},{17,9},{25,17},{1,25},{10,2},{18... | collective-permute-start | bytes 258056 | tf_op jit(solution)/shard_map/ppermute | solution.py:211
  24.6 1.4 %collective-permute-done.8 = f32[168,128]{1,0:T(8,128)S(1)} collective-permute-done((f32[168,128]{1,0:T(8,128)S(1)}, f32[168,128]{1,0:T(8,128)S(1)}, u32[]{:S(2)}, u32[]{:S(2)}) %collective-permute-start.8) | collective-permute-done | bytes 86048 | tf_op jit(solution)/shard_map/ppermute | solution.py:211
  25.9 0.2 slice_reduce_fusion.2
  26.2 2.8 %collective-permute-done.7 = f32[168,128]{1,0:T(8,128)S(1)} collective-permute-done((f32[168,128]{1,0:T(8,128)S(1)}, f32[168,128]{1,0:T(8,128)S(1)}, u32[]{:S(2)}, u32[]{:S(2)}) %collective-permute-start.7) | collective-permute-done | bytes 86048 | tf_op jit(solution)/shard_map/ppermute | solution.py:211
  29.0 0.2 slice_reduce_fusion.11
  29.3 0.2 slice_reduce_fusion.20
  30.7 0.8 %collective-permute-start.10 = (f32[384,128]{1,0:T(8,128)S(1)}, f32[384,128]{1,0:T(8,128)S(1)}, u32[]{:S(2)}, u32[]{:S(2)}) collective-permute-start(f32[384,128]{1,0:T(8,128)S(1)} %constant_dynamic-update-slice_fusion), channel_id=1, source_target_pairs={{0,7},{1,2},{2,1},{3,4},{4,3},{5,6},{6,5},{7,0},{8,15},{9,10},{10,... | collective-permute-start | bytes 589832 | tf_op jit(solution)/shard_map/ppermute | solution.py:101
  31.4 0.9 %collective-permute-start.9 = (f32[384,128]{1,0:T(8,128)S(1)}, f32[384,128]{1,0:T(8,128)S(1)}, u32[]{:S(2)}, u32[]{:S(2)}) collective-permute-start(f32[384,128]{1,0:T(8,128)S(1)} %constant_dynamic-update-slice_fusion), channel_id=1, source_target_pairs={{0,1},{1,0},{2,3},{3,2},{4,5},{5,4},{6,7},{7,6},{8,9},{9,8},{10,11... | collective-permute-start | bytes 589832 | tf_op jit(solution)/shard_map/ppermute | solution.py:77
  32.4 1.4 %collective-permute-start.11 = (f32[128,128]{1,0:T(8,128)S(1)}, f32[128,128]{1,0:T(8,128)S(1)}, u32[]{:S(2)}, u32[]{:S(2)}) collective-permute-start(f32[128,128]{1,0:T(8,128)S(1)} %pad_maximum_fusion.19), channel_id=1, source_target_pairs={{2,0},{3,1},{4,2},{5,3},{6,4},{7,5},{0,6},{1,7},{10,8},{11,9},{12,... | collective-permute-start | bytes 196616 | tf_op jit(solution)/shard_map/ppermute | solution.py:248
  33.8 5.0 %collective-permute-done.11 = f32[128,128]{1,0:T(8,128)S(1)} collective-permute-done((f32[128,128]{1,0:T(8,128)S(1)}, f32[128,128]{1,0:T(8,128)S(1)}, u32[]{:S(2)}, u32[]{:S(2)}) %collective-permute-start.11) | collective-permute-done | bytes 65568 | tf_op jit(solution)/shard_map/ppermute | solution.py:248
  38.9 0.4 slice_reduce_fusion.22
  39.3 0.5 slice_reduce_fusion.18
  41.6 0.2 fusion.130
  42.0 0.2 fusion.128
  42.2 0.2 fusion.129
  42.4 0.2 fusion.27
  43.3 0.2 fusion.48
  43.7 0.2 fusion.54
  43.9 0.2 fusion.60
  44.5 0.4 collective-permute-start.12
  45.0 0.8 %collective-permute-done.12 = f32[8,128]{1,0:T(8,128)S(1)} collective-permute-done((f32[8,128]{1,0:T(8,128)S(1)}, f32[8,128]{1,0:T(8,128)S(1)}, u32[]{:S(2)}, u32[]{:S(2)}) %collective-permute-start.12) | collective-permute-done | bytes 4128 | tf_op jit(solution)/shard_map/ppermute | solution.py:77
  45.8 2.4 %collective-permute-start.15 = (f32[8,128]{1,0:T(8,128)S(1)}, f32[8,128]{1,0:T(8,128)S(1)}, u32[]{:S(2)}, u32[]{:S(2)}) collective-permute-start(f32[8,128]{1,0:T(8,128)S(1)} %add.497), channel_id=1, source_target_pairs={{0,6},{1,7},{2,4},{3,5},{4,2},{5,3},{6,0},{7,1},{8,14},{9,15},{10,... | collective-permute-start | bytes 12296 | tf_op jit(solution)/shard_map/ppermute | solution.py:77
  48.2 0.7 %collective-permute-start.14 = (f32[8,128]{1,0:T(8,128)S(1)}, f32[8,128]{1,0:T(8,128)S(1)}, u32[]{:S(2)}, u32[]{:S(2)}) collective-permute-start(f32[8,128]{1,0:T(8,128)S(1)} %add.497), channel_id=1, source_target_pairs={{0,4},{1,5},{2,6},{3,7},{4,0},{5,1},{6,2},{7,3},{8,12},{9,13},{10,... | collective-permute-start | bytes 12296 | tf_op jit(solution)/shard_map/ppermute | solution.py:77
  48.9 0.4 collective-permute-start.13
  49.3 1.0 %collective-permute-done.15 = f32[8,128]{1,0:T(8,128)S(1)} collective-permute-done((f32[8,128]{1,0:T(8,128)S(1)}, f32[8,128]{1,0:T(8,128)S(1)}, u32[]{:S(2)}, u32[]{:S(2)}) %collective-permute-start.15) | collective-permute-done | bytes 4128 | tf_op jit(solution)/shard_map/ppermute | solution.py:77
  50.3 1.5 %collective-permute-done.14 = f32[8,128]{1,0:T(8,128)S(1)} collective-permute-done((f32[8,128]{1,0:T(8,128)S(1)}, f32[8,128]{1,0:T(8,128)S(1)}, u32[]{:S(2)}, u32[]{:S(2)}) %collective-permute-start.14) | collective-permute-done | bytes 4128 | tf_op jit(solution)/shard_map/ppermute | solution.py:77
  51.8 0.7 %collective-permute-done.13 = f32[8,128]{1,0:T(8,128)S(1)} collective-permute-done((f32[8,128]{1,0:T(8,128)S(1)}, f32[8,128]{1,0:T(8,128)S(1)}, u32[]{:S(2)}, u32[]{:S(2)}) %collective-permute-start.13) | collective-permute-done | bytes 4128 | tf_op jit(solution)/shard_map/ppermute | solution.py:77
  52.5 0.3 fusion.2
  52.8 0.9 %fusion = f32[1,2,128,128]{3,2,1,0:T(8,128)} fusion(f32[2,128,128]{2,1,0:T(8,128)S(1)} %fusion.2, f32[2,128,128]{2,1,0:T(8,128)S(1)} %copy-done.2, f32[3,32,128]{2,1,0:T(8,128)S(1)} %get-tuple-element.152, f32[5,32,128]{2,1,0:T(8,128)S(1)} %get-tuple-element.126, f32[128]{0:T(128)S(1)} %get-tuple-element.114, f32[128]{0:T(128)S(1)} %get-tuple-element.113), kind=kOutput, calls=%fused_computation.1 | convolution fusion | flops 12640256 | bytes 459776 | tf_op jit(solution)/shard_map/cij,cjp->cip/dot_general | solution.py:316
  (189 shorter events, 5.7 us)
Async XLA Ops:
  1.5 1.4 %collective-permute-start = (f32[64,128]{1,0:T(8,128)S(1)}, f32[64,128]{1,0:T(8,128)S(1)}, u32[]{:S(2)}, u32[]{:S(2)}) collective-permute-start(f32[64,128]{1,0:T(8,128)S(1)} %fusion.75), channel_id=1, source_target_pairs={{0,1},{1,0},{2,3},{3,2},{4,5},{5,4},{6,7},{7,6},{8,9},{9,8},{10,11... | collective-permute-start | bytes 98312 | tf_op jit(solution)/shard_map/ppermute | solution.py:77
  2.0 6.9 %copy-start = (f32[1,2,128,128]{3,2,1,0:T(8,128)S(1)}, f32[1,2,128,128]{3,2,1,0:T(8,128)}, u32[]{:S(2)}) copy-start(f32[1,2,128,128]{3,2,1,0:T(8,128)} %param.11) | copy-start | bytes 393220
  2.2 5.2 %copy-start.7 = (s32[1,1,8,8]{3,2,1,0:T(8,128)S(1)}, s32[1,1,8,8]{3,2,1,0:T(8,128)}, u32[]{:S(2)}) copy-start(s32[1,1,8,8]{3,2,1,0:T(8,128)} %param.17) | copy-start | bytes 772
  2.9 4.6 %copy-start.8 = (f32[1,1,8,8]{3,2,1,0:T(8,128)S(1)}, f32[1,1,8,8]{3,2,1,0:T(8,128)}, u32[]{:S(2)}) copy-start(f32[1,1,8,8]{3,2,1,0:T(8,128)} %param.21) | copy-start | bytes 772
  2.9 14.8 %collective-permute-start.3 = (f32[128,128]{1,0:T(8,128)S(1)}, f32[128,128]{1,0:T(8,128)S(1)}, u32[]{:S(2)}, u32[]{:S(2)}) collective-permute-start(f32[128,128]{1,0:T(8,128)S(1)} %pad_maximum_fusion.18), channel_id=1, source_target_pairs={{0,6},{1,7},{2,4},{3,5},{4,2},{5,3},{6,0},{7,1},{8,14},{9,15},{10,... | collective-permute-start | bytes 196616 | tf_op jit(solution)/shard_map/ppermute | solution.py:77
  6.8 11.0 %collective-permute-start.2 = (f32[128,128]{1,0:T(8,128)S(1)}, f32[128,128]{1,0:T(8,128)S(1)}, u32[]{:S(2)}, u32[]{:S(2)}) collective-permute-start(f32[128,128]{1,0:T(8,128)S(1)} %pad_maximum_fusion.18), channel_id=1, source_target_pairs={{0,4},{1,5},{2,6},{3,7},{4,0},{5,1},{6,2},{7,3},{8,12},{9,13},{10,... | collective-permute-start | bytes 196616 | tf_op jit(solution)/shard_map/ppermute | solution.py:77
  7.3 10.5 %collective-permute-start.1 = (f32[128,128]{1,0:T(8,128)S(1)}, f32[128,128]{1,0:T(8,128)S(1)}, u32[]{:S(2)}, u32[]{:S(2)}) collective-permute-start(f32[128,128]{1,0:T(8,128)S(1)} %pad_maximum_fusion.18), channel_id=1, source_target_pairs={{0,2},{1,3},{2,0},{3,1},{4,6},{5,7},{6,4},{7,5},{8,10},{9,11},{10,... | collective-permute-start | bytes 196616 | tf_op jit(solution)/shard_map/ppermute | solution.py:77
  7.4 0.7 %copy-start.9 = (s32[1,1,8]{2,1,0:T(1,128)S(1)}, s32[1,1,8]{2,1,0:T(1,128)}, u32[]{:S(2)}) copy-start(s32[1,1,8]{2,1,0:T(1,128)} %param.18) | copy-start | bytes 100
  7.5 0.7 %copy-start.5 = (s32[1,1,8,8]{3,2,1,0:T(8,128)S(1)}, s32[1,1,8,8]{3,2,1,0:T(8,128)}, u32[]{:S(2)}) copy-start(s32[1,1,8,8]{3,2,1,0:T(8,128)} %param.20) | copy-start | bytes 772
  7.5 0.7 %copy-start.6 = (s32[1,1,8,8]{3,2,1,0:T(8,128)S(1)}, s32[1,1,8,8]{3,2,1,0:T(8,128)}, u32[]{:S(2)}) copy-start(s32[1,1,8,8]{3,2,1,0:T(8,128)} %param.19) | copy-start | bytes 772
  8.3 0.7 %copy-start.4 = (f32[1,2,2,32]{3,2,1,0:T(2,128)S(1)}, f32[1,2,2,32]{3,2,1,0:T(2,128)}, u32[]{:S(2)}) copy-start(f32[1,2,2,32]{3,2,1,0:T(2,128)} %param.15) | copy-start | bytes 1540
  9.1 8.6 %collective-permute-start.4 = (f32[64,128]{1,0:T(8,128)S(1)}, f32[64,128]{1,0:T(8,128)S(1)}, u32[]{:S(2)}, u32[]{:S(2)}) collective-permute-start(f32[64,128]{1,0:T(8,128)S(1)} %get-tuple-element.191), channel_id=1, source_target_pairs={{0,7},{1,2},{2,1},{3,4},{4,3},{5,6},{6,5},{7,0},{8,15},{9,10},{10,... | collective-permute-start | bytes 98312 | tf_op jit(solution)/shard_map/ppermute | solution.py:101
  10.8 6.8 %collective-permute-start.5 = (f32[64,128]{1,0:T(8,128)S(1)}, f32[64,128]{1,0:T(8,128)S(1)}, u32[]{:S(2)}, u32[]{:S(2)}) collective-permute-start(f32[64,128]{1,0:T(8,128)S(1)} %get-tuple-element.192), channel_id=1, source_target_pairs={{0,1},{1,0},{2,3},{3,2},{4,5},{5,4},{6,7},{7,6},{8,9},{9,8},{10,11... | collective-permute-start | bytes 98312 | tf_op jit(solution)/shard_map/ppermute | solution.py:77
  16.2 0.9 %copy-start.1 = (f32[1,2,128,128]{3,2,1,0:T(8,128)S(1)}, f32[1,2,128,128]{3,2,1,0:T(8,128)}, u32[]{:S(2)}) copy-start(f32[1,2,128,128]{3,2,1,0:T(8,128)} %param.11) | copy-start | bytes 393220
  16.2 1.0 %copy-start.2 = (f32[2,128,128]{2,1,0:T(8,128)S(1)}, f32[2,128,128]{2,1,0:T(8,128)}, u32[]{:S(2)}) copy-start(f32[2,128,128]{2,1,0:T(8,128)} %get-tuple-element.24) | copy-start | bytes 393220
  17.7 0.9 %copy-start.3 = (f32[2,128,128]{2,1,0:T(8,128)S(1)}, f32[2,128,128]{2,1,0:T(8,128)}, u32[]{:S(2)}) copy-start(f32[2,128,128]{2,1,0:T(8,128)} %get-tuple-element.25) | copy-start | bytes 393220
  19.0 7.0 %collective-permute-start.8 = (f32[168,128]{1,0:T(8,128)S(1)}, f32[168,128]{1,0:T(8,128)S(1)}, u32[]{:S(2)}, u32[]{:S(2)}) collective-permute-start(f32[168,128]{1,0:T(8,128)S(1)} %select_maximum_fusion), channel_id=1, source_target_pairs={{24,0},{0,8},{8,16},{16,24},{25,1},{1,9},{9,17},{17,25},{26,2},{2,... | collective-permute-start | bytes 258056 | tf_op jit(solution)/shard_map/ppermute | solution.py:211
  20.3 8.8 %collective-permute-start.7 = (f32[168,128]{1,0:T(8,128)S(1)}, f32[168,128]{1,0:T(8,128)S(1)}, u32[]{:S(2)}, u32[]{:S(2)}) collective-permute-start(f32[168,128]{1,0:T(8,128)S(1)} %select_maximum_fusion), channel_id=1, source_target_pairs={{16,0},{24,8},{0,16},{8,24},{17,1},{25,9},{1,17},{9,25},{18,2},{26... | collective-permute-start | bytes 258056 | tf_op jit(solution)/shard_map/ppermute | solution.py:211
  22.9 6.4 %collective-permute-start.6 = (f32[168,128]{1,0:T(8,128)S(1)}, f32[168,128]{1,0:T(8,128)S(1)}, u32[]{:S(2)}, u32[]{:S(2)}) collective-permute-start(f32[168,128]{1,0:T(8,128)S(1)} %select_maximum_fusion), channel_id=1, source_target_pairs={{8,0},{16,8},{24,16},{0,24},{9,1},{17,9},{25,17},{1,25},{10,2},{18... | collective-permute-start | bytes 258056 | tf_op jit(solution)/shard_map/ppermute | solution.py:211
  30.7 8.2 %collective-permute-start.10 = (f32[384,128]{1,0:T(8,128)S(1)}, f32[384,128]{1,0:T(8,128)S(1)}, u32[]{:S(2)}, u32[]{:S(2)}) collective-permute-start(f32[384,128]{1,0:T(8,128)S(1)} %constant_dynamic-update-slice_fusion), channel_id=1, source_target_pairs={{0,7},{1,2},{2,1},{3,4},{4,3},{5,6},{6,5},{7,0},{8,15},{9,10},{10,... | collective-permute-start | bytes 589832 | tf_op jit(solution)/shard_map/ppermute | solution.py:101
  31.4 7.4 %collective-permute-start.9 = (f32[384,128]{1,0:T(8,128)S(1)}, f32[384,128]{1,0:T(8,128)S(1)}, u32[]{:S(2)}, u32[]{:S(2)}) collective-permute-start(f32[384,128]{1,0:T(8,128)S(1)} %constant_dynamic-update-slice_fusion), channel_id=1, source_target_pairs={{0,1},{1,0},{2,3},{3,2},{4,5},{5,4},{6,7},{7,6},{8,9},{9,8},{10,11... | collective-permute-start | bytes 589832 | tf_op jit(solution)/shard_map/ppermute | solution.py:77
  32.4 6.5 %collective-permute-start.11 = (f32[128,128]{1,0:T(8,128)S(1)}, f32[128,128]{1,0:T(8,128)S(1)}, u32[]{:S(2)}, u32[]{:S(2)}) collective-permute-start(f32[128,128]{1,0:T(8,128)S(1)} %pad_maximum_fusion.19), channel_id=1, source_target_pairs={{2,0},{3,1},{4,2},{5,3},{6,4},{7,5},{0,6},{1,7},{10,8},{11,9},{12,... | collective-permute-start | bytes 196616 | tf_op jit(solution)/shard_map/ppermute | solution.py:248
  44.5 1.3 %collective-permute-start.12 = (f32[8,128]{1,0:T(8,128)S(1)}, f32[8,128]{1,0:T(8,128)S(1)}, u32[]{:S(2)}, u32[]{:S(2)}) collective-permute-start(f32[8,128]{1,0:T(8,128)S(1)} %stack.327), channel_id=1, source_target_pairs={{0,1},{1,0},{2,3},{3,2},{4,5},{5,4},{6,7},{7,6},{8,9},{9,8},{10,11... | collective-permute-start | bytes 12296 | tf_op jit(solution)/shard_map/ppermute | solution.py:77
  45.8 4.5 %collective-permute-start.15 = (f32[8,128]{1,0:T(8,128)S(1)}, f32[8,128]{1,0:T(8,128)S(1)}, u32[]{:S(2)}, u32[]{:S(2)}) collective-permute-start(f32[8,128]{1,0:T(8,128)S(1)} %add.497), channel_id=1, source_target_pairs={{0,6},{1,7},{2,4},{3,5},{4,2},{5,3},{6,0},{7,1},{8,14},{9,15},{10,... | collective-permute-start | bytes 12296 | tf_op jit(solution)/shard_map/ppermute | solution.py:77
  48.2 3.6 %collective-permute-start.14 = (f32[8,128]{1,0:T(8,128)S(1)}, f32[8,128]{1,0:T(8,128)S(1)}, u32[]{:S(2)}, u32[]{:S(2)}) collective-permute-start(f32[8,128]{1,0:T(8,128)S(1)} %add.497), channel_id=1, source_target_pairs={{0,4},{1,5},{2,6},{3,7},{4,0},{5,1},{6,2},{7,3},{8,12},{9,13},{10,... | collective-permute-start | bytes 12296 | tf_op jit(solution)/shard_map/ppermute | solution.py:77
  48.9 3.6 %collective-permute-start.13 = (f32[8,128]{1,0:T(8,128)S(1)}, f32[8,128]{1,0:T(8,128)S(1)}, u32[]{:S(2)}, u32[]{:S(2)}) collective-permute-start(f32[8,128]{1,0:T(8,128)S(1)} %add.497), channel_id=1, source_target_pairs={{0,2},{1,3},{2,0},{3,1},{4,6},{5,7},{6,4},{7,5},{8,10},{9,11},{10,... | collective-permute-start | bytes 12296 | tf_op jit(solution)/shard_map/ppermute | solution.py:77

commit v3 on v1

v3 whole, which is shorter than its diff:
```python
import functools

import jax
import jax.numpy as jnp
from jax import lax
from jax.experimental import pallas as pl
from jax.experimental.pallas import tpu as pltpu
from jax.sharding import PartitionSpec as P

DOUBLINGS = 5
SMALL = 2.0**-13
VMEM_BYTES = 16 * 1024 * 1024

dot = functools.partial(
    jnp.dot, precision=lax.Precision.HIGHEST, preferred_element_type=jnp.float32
)


def run(kernel, outs, *args, scratch=(), flops=0):
    vmem = pl.BlockSpec(memory_space=pltpu.VMEM)
    shapes = tuple(jax.ShapeDtypeStruct(shape, jnp.float32) for shape in outs)
    moved = sum(4 * a.size for a in args) + sum(4 * s.size for s in shapes)
    return pl.pallas_call(
        kernel,
        out_shape=shapes,
        in_specs=[vmem] * len(args),
        out_specs=(vmem,) * len(shapes),
        scratch_shapes=list(scratch),
        compiler_params=pltpu.CompilerParams(vmem_limit_bytes=VMEM_BYTES),
        cost_estimate=pl.CostEstimate(flops=flops, bytes_accessed=moved, transcendentals=0),
    )(*args)


def iota(shape, axis):
    return lax.broadcasted_iota(jnp.int32, shape, axis)


def to_column(row):
    count = row.shape[1]
    square = jnp.broadcast_to(row, (count, count))
    keep = iota((count, count), 0) == iota((count, count), 1)
    return jnp.sum(jnp.where(keep, square, 0.0), axis=1, keepdims=True)


def slot_column(table):
    sources, slots = table.shape
    spread = jnp.concatenate(
        [jnp.broadcast_to(table[s : s + 1], (slots, slots)) for s in range(sources)], axis=0
    )
    keep = iota(spread.shape, 0) % slots == iota(spread.shape, 1)
    return jnp.sum(jnp.where(keep, spread, 0.0), axis=1, keepdims=True)


def source_column(row, slots):
    sources = row.shape[1]
    spread = jnp.broadcast_to(row, (sources * slots, sources))
    keep = iota(spread.shape, 0) // slots == iota(spread.shape, 1)
    return jnp.sum(jnp.where(keep, spread, 0.0), axis=1, keepdims=True)


def start_kernel(nets, edge, volt_ref, driver_ref, gain_ref, out_ref):
    tiles, nodes, patterns = volt_ref.shape
    odd = lax.axis_index("col") % 2 == 1
    picked = to_column(driver_ref[...].astype(jnp.float32))
    drivers = jnp.zeros((nets, patterns), jnp.float32)
    for t in range(tiles):
        block = volt_ref[t]
        block = jnp.concatenate([block] * (-(-nets // nodes)), axis=0)[:nets]
        drivers = jnp.where(picked == t, block, drivers)
    low, high = volt_ref[0, :edge], volt_ref[tiles - 1, :edge]
    out_ref[:nets] = drivers
    out_ref[nets : nets + edge] = jnp.where(odd, low, high)
    out_ref[nets + edge : nets + 2 * edge] = jnp.where(odd, high, low)
    out_ref[nets + 2 * edge :] = jnp.zeros((8, patterns), jnp.float32)
    out_ref[nets + 2 * edge : nets + 2 * edge + 1, :edge] = gain_ref[tiles - 1, 0:1]


def pair_kernel(nets, edge, mine_ref, mate_ref, out_ref):
    out_ref[:nets] = mine_ref[:nets]
    out_ref[nets : 2 * nets] = mate_ref[:nets]
    out_ref[2 * nets :] = mate_ref[nets + edge :]


def tile_kernel(
    nets,
    edge,
    conduct_ref,
    cap_ref,
    volt_ref,
    inject_ref,
    gain_ref,
    net_ref,
    count_ref,
    tile_ref,
    node_ref,
    weight_ref,
    inverse_ref,
    rest_ref,
    table_ref,
    take_ref,
    put_ref,
    sum_ref,
    power_ref,
):
    tiles, nodes = conduct_ref.shape[0], conduct_ref.shape[1]
    eye = jnp.where(iota((nodes, nodes), 0) == iota((nodes, nodes), 1), 1.0, 0.0)
    sums, powers, scales = [], [], []
    for t in range(tiles):
        conduct = conduct_ref[t]
        diagonal = (conduct + cap_ref[t : t + 1, :]) * eye
        down = jnp.sum(diagonal, axis=1, keepdims=True)
        across = jnp.sum(diagonal, axis=0, keepdims=True)
        power = (conduct * eye - conduct) / down
        sums.append(eye + power)
        powers.append(dot(power, power))
        scales.append(1.0 / across)
        rest_ref[t] = inject_ref[t] - dot(conduct, volt_ref[t])

    def step(sums, powers):
        out_sums, out_powers, largest = [], [], jnp.float32(0.0)
        for total, power in zip(sums, powers):
            both = dot(jnp.concatenate([total, power], axis=0), power)
            out_sums.append(total + both[:nodes])
            out_powers.append(both[nodes:])
            largest = jnp.maximum(largest, jnp.max(jnp.sum(power, axis=1)))
        return out_sums, out_powers, largest

    for _ in range(DOUBLINGS):
        sums, powers, largest = step(sums, powers)
    for t in range(tiles):
        sum_ref[t], power_ref[t] = sums[t], powers[t]

    def again(carry):
        sums, powers, largest = step(
            [sum_ref[t] for t in range(tiles)], [power_ref[t] for t in range(tiles)]
        )
        for t in range(tiles):
            sum_ref[t], power_ref[t] = sums[t], powers[t]
        return largest, carry[1] + 1

    lax.while_loop(
        lambda carry: (carry[0] > SMALL) & (carry[1] < 40), again, (largest, jnp.int32(0))
    )
    lane = iota((edge, nodes), 1)
    table = jnp.zeros((edge, nodes), jnp.float32)
    for t in range(tiles):
        inverse = sum_ref[t] * scales[t]
        inverse_ref[t] = inverse
        corner = inverse[:edge] if t == 0 else pltpu.roll(inverse[:edge], t * edge, 1)
        table = jnp.where((lane >= t * edge) & (lane < (t + 1) * edge), corner, table)
        for side in range(2):
            gain = to_column(gain_ref[t, side : side + 1])
            table = jnp.where(lane == tiles * edge + side * tiles + t, gain, table)
    table_ref[...] = table

    sources, slots = net_ref.shape
    mine = lax.axis_index("col")
    block = iota((sources, slots), 0) ^ mine
    place = slot_column((block * nets + net_ref[...]).astype(jnp.float32))
    target = slot_column((tile_ref[...] * nodes + node_ref[...]).astype(jnp.float32))
    live = source_column(count_ref[...].astype(jnp.float32), slots)
    slot = (iota(live.shape, 0) % slots).astype(jnp.float32)
    weight = jnp.where(slot < live, slot_column(weight_ref[...]), 0.0)
    take_ref[...] = jnp.where(place == iota(take_ref.shape, 1).astype(jnp.float32), 1.0, 0.0)
    put_ref[...] = jnp.where(target == iota(put_ref.shape, 1).astype(jnp.float32), weight, 0.0)


def residual_kernel(
    nets,
    edge,
    cols,
    volt_ref,
    mate_ref,
    inverse_ref,
    rest_ref,
    table_ref,
    take_ref,
    put_ref,
    *refs,
):
    *group_refs, message_ref, precond_ref = refs
    tiles, nodes, patterns = volt_ref.shape
    mine = lax.axis_index("col")
    odd = mine % 2 == 1
    stride = 2 * nets + edge + 8
    blocks = [(ref, base) for ref in group_refs for base in range(0, ref.shape[0], stride)]
    values = sum(
        dot(take_ref[:, j * 2 * nets : (j + 1) * 2 * nets], ref[base : base + 2 * nets])
        for j, (ref, base) in enumerate(blocks)
    )
    injected = lax.dot_general(
        put_ref[...],
        values,
        (((0,), (0,)), ((), ())),
        precision=lax.Precision.HIGHEST,
        preferred_element_type=jnp.float32,
    )
    beyond = lax.rem(jnp.where(odd, mine + 1, mine + cols - 1), cols) ^ 1
    which = (mine ^ beyond) // 2
    outer = jnp.zeros((edge + 8, patterns), jnp.float32)
    for j, (ref, base) in enumerate(blocks):
        outer = jnp.where(which == j, ref[base + 2 * nets : base + stride], outer)
    inner = mate_ref[nets : nets + edge]
    inner_gain = mate_ref[nets + 2 * edge : nets + 2 * edge + 1]
    has_west = jnp.where(mine > 0, 1.0, 0.0)
    has_east = jnp.where(mine < cols - 1, 1.0, 0.0)
    west = jnp.where(odd, inner, outer[:edge]) * has_west
    east = jnp.where(odd, outer[:edge], inner) * has_east
    west_gain = to_column(jnp.where(odd, inner_gain, outer[edge : edge + 1])[:, :edge]) * has_west
    first_gain = tiles * edge
    gains = [west_gain] + [
        table_ref[:, first_gain + t : first_gain + t + 1] for t in range(tiles)
    ]
    rims = [west] + [volt_ref[t, :edge] for t in range(tiles)] + [east]
    flows = [gains[t] * (rims[t] - rims[t + 1]) for t in range(tiles + 1)]
    first = jnp.zeros((1, patterns), jnp.float32)
    for t in range(tiles):
        residual = rest_ref[t] + injected[t * nodes : (t + 1) * nodes]
        residual = jnp.concatenate(
            [residual[:edge] - (flows[t + 1] - flows[t]), residual[edge:]], axis=0
        )
        precond = dot(inverse_ref[t], residual)
        precond_ref[t] = precond
        first = first + jnp.sum(residual * precond, axis=0, keepdims=True)
        message_ref[t * edge : (t + 1) * edge] = precond[:edge]
        message_ref[(tiles + t) * edge : (tiles + t + 1) * edge] = volt_ref[t, :edge]
    message_ref[2 * tiles * edge : (2 * tiles + 1) * edge] = table_ref[...]
    message_ref[(2 * tiles + 1) * edge :] = jnp.broadcast_to(first, (8, patterns))


def corners(tables, tiles, edge):
    lane = iota((edge, tables.shape[1]), 1)
    parts = [
        jnp.where((lane >= t * edge) & (lane < (t + 1) * edge), tables, 0.0) for t in range(tiles)
    ]
    return jnp.concatenate(parts, axis=0)[:, : tiles * edge]


def row_masks(rows):
    place = lax.axis_index("row")
    index = [lax.rem(place + k, rows) for k in range(rows)]
    not_first = [jnp.where(i > 0, 1.0, 0.0) for i in index]
    not_last = [jnp.where(i < rows - 1, 1.0, 0.0) for i in index]
    return not_first, not_last


def rim_kernel(rows, tiles, edge, *refs):
    column_refs, (message_ref, far_ref, flow_ref, first_ref) = refs[:rows], refs[rows:]
    patterns = message_ref.shape[1]
    span, gain_lane = tiles * edge, tiles * edge + tiles
    not_first, not_last = row_masks(rows)
    start = [ref[span : 2 * span] for ref in column_refs]
    tables = [ref[2 * span : 2 * span + edge] for ref in column_refs]
    south = []
    for k in range(rows):
        gain = jnp.concatenate(
            [
                jnp.broadcast_to(tables[k][:, gain_lane + t : gain_lane + t + 1], (edge, patterns))
                for t in range(tiles)
            ],
            axis=0,
        )
        south.append(gain * (start[k] - start[(k + 1) % rows] * not_last[k]))
    first = sum(ref[2 * span + edge : 2 * span + edge + 1] for ref in column_refs)
    dropped = jnp.zeros((span, patterns), jnp.float32)
    stride = span + edge
    for k in range(rows):
        flow = south[k] - south[k - 1] * not_first[k]
        raw = column_refs[k][:span]
        rim = raw - dot(corners(tables[k], tiles, edge), flow)
        dropped = dropped + flow * (raw + rim)
        message_ref[k * stride : k * stride + span] = rim
        message_ref[k * stride + span : (k + 1) * stride] = tables[k]
        far_ref[k * edge : (k + 1) * edge] = rim[:edge]
        if k == 0:
            flow_ref[...] = flow
    first = first - jnp.sum(dropped, axis=0, keepdims=True)
    first_ref[...] = jnp.broadcast_to(first, first_ref.shape)


def moment_kernel(
    rows, cols, tiles, edge, own_ref, inner_ref, outer_ref, far_ref, first_ref, moment_ref, t0_ref, t1_ref
):
    patterns = own_ref.shape[1]
    mine = lax.axis_index("col")
    odd = mine % 2 == 1
    has_west = jnp.where(mine > 0, 1.0, 0.0)
    has_east = jnp.where(mine < cols - 1, 1.0, 0.0)
    has_far = jnp.where(mine < cols - 2, 1.0, 0.0)
    not_first, not_last = row_masks(rows)
    span = tiles * edge
    stride = span + edge
    easts, souths, u0, mats = [], [], [], []
    for k in range(rows):
        piece = slice(k * stride, (k + 1) * stride)
        own = own_ref[piece]
        west = jnp.where(odd, inner_ref[piece], outer_ref[piece]) * has_west
        east = jnp.where(odd, outer_ref[piece], inner_ref[piece]) * has_east
        far = far_ref[k * edge : (k + 1) * edge] * has_far
        u0.append(
            [block[t * edge : (t + 1) * edge] for block in (west, own, east) for t in range(tiles)]
            + [far]
        )
        tables = [block[span:] for block in (west, own, east)]

        def gain(table, lane):
            return jnp.broadcast_to(table[:, lane : lane + 1], (edge, patterns))

        easts.append([gain(table, span + t) for table in tables for t in range(tiles)])
        souths.append([gain(table, span + tiles + t) for table in tables for t in range(tiles)])
        mats.append([corners(table, tiles, edge) for table in tables])

    def net_flow(rims, low, high):
        flows = []
        for k in range(rows):
            below, above = (k + 1) % rows, k - 1
            row = []
            for c in range(low, high):
                flow = easts[k][c] * (rims[k][c] - rims[k][c + 1])
                flow = flow - easts[k][c - 1] * (rims[k][c - 1] - rims[k][c])
                flow = flow + souths[k][c] * (rims[k][c] - rims[below][c] * not_last[k])
                back = souths[above][c] * (rims[k][c] - rims[above][c])
                row.append(flow + back * not_first[k])
            flows.append([None] * low + row)
        return flows

    def spread(flows, devices, low, high):
        out = []
        for k in range(rows):
            row = []
            for d in devices:
                block = [
                    flows[k][c] if low <= c < high else jnp.zeros((edge, patterns), jnp.float32)
                    for c in range(d * tiles, (d + 1) * tiles)
                ]
                block = dot(mats[k][d], jnp.concatenate(block, axis=0))
                row += [block[t * edge : (t + 1) * edge] for t in range(tiles)]
            out.append([None] * (devices[0] * tiles) + row)
        return out

    t0 = net_flow(u0, tiles - 1, 3 * tiles)
    u1 = spread(t0, [0, 1, 2], tiles - 1, 3 * tiles)
    t1 = net_flow(u1, tiles, 2 * tiles + 1)
    u2 = spread(t1, [1, 2], tiles, 2 * tiles + 1)
    zero = jnp.zeros((edge, patterns), jnp.float32)
    sums = [zero] * 5
    for k in range(rows):
        for c in range(tiles, 2 * tiles):
            ahead = u2[k][c] - u2[k][c + 1]
            drop = u2[k][c] - u2[(k + 1) % rows][c] * not_last[k]
            parts = (
                u0[k][c] * t0[k][c],
                u1[k][c] * t0[k][c],
                u1[k][c] * t1[k][c],
                u2[k][c] * t1[k][c],
                easts[k][c] * ahead * ahead + souths[k][c] * drop * drop,
            )
            sums = [total + part for total, part in zip(sums, parts)]
    moment_ref[0:1] = first_ref[0:1]
    for i, total in enumerate(sums):
        moment_ref[i + 1 : i + 2] = jnp.sum(total, axis=0, keepdims=True)
    moment_ref[6:8] = jnp.zeros((2, patterns), jnp.float32)
    t0_ref[...] = jnp.concatenate(t0[0][tiles : 2 * tiles], axis=0)
    t1_ref[...] = jnp.concatenate(t1[0][tiles : 2 * tiles], axis=0)


def final_kernel(edge, volt_ref, precond_ref, inverse_ref, flow_ref, t0_ref, t1_ref, *refs):
    *sum_refs, out_ref = refs
    tiles = volt_ref.shape[0]
    sums = sum(ref[...] for ref in sum_refs)
    m = [sums[i : i + 1] for i in range(6)]
    a00, a01, a02 = m[0] + m[1], m[1] + m[2], m[2] + m[3]
    a12, a22 = m[3] + m[4], m[4] + m[5]
    l1, l2 = a01 / a00, a02 / a00
    d1 = a02 - l1 * a01
    e12 = a12 - l2 * a01
    l12 = e12 / d1
    d2 = a22 - l2 * a02 - l12 * e12
    y1 = m[1] - l1 * m[0]
    y2 = m[2] - l2 * m[0] - l12 * y1
    c2 = y2 / d2
    c1 = y1 / d1 - l12 * c2
    c0 = m[0] / a00 - l1 * c1 - l2 * c2
    mixed = c1 * t0_ref[...] + c2 * t1_ref[...] - c0 * flow_ref[...]
    for t in range(tiles):
        update = dot(inverse_ref[t, :, :edge], mixed[t * edge : (t + 1) * edge])
        out_ref[t] = volt_ref[t] + c0 * precond_ref[t] + update


def other(block, axis, count, distance):
    return lax.ppermute(block, axis, [(i, i ^ distance) for i in range(count)])


def stages(count, held):
    while held < count:
        reach = 2 if (count // held).bit_length() % 2 == 0 else 4
        yield [held * k for k in range(1, reach)]
        held *= reach


def outer_swap(block, axis, count):
    pairs = [(i, (i + 1) % count if i % 2 else (i - 1) % count) for i in range(count)]
    return lax.ppermute(block, axis, pairs)


def local(
    initial_voltage,
    inject,
    conduct,
    capacitance,
    track_gain,
    driver_tile,
    sink_net,
    sink_count,
    sink_tile,
    sink_node,
    sink_gain,
):
    rows, cols = lax.axis_size("row"), lax.axis_size("col")
    tiles, nodes, patterns = initial_voltage.shape[1:]
    edge, nets = track_gain.shape[-1], driver_tile.shape[-1]
    slots = cols * sink_net.shape[-1]
    voltage = initial_voltage[0]
    field = (tiles, nodes, patterns)
    span = tiles * edge

    mine = run(
        functools.partial(start_kernel, nets, edge),
        [(nets + 2 * edge + 8, patterns)],
        voltage,
        driver_tile[0],
        track_gain[0],
    )[0]
    mate = other(mine, "col", cols, 1)
    pair = run(
        functools.partial(pair_kernel, nets, edge), [(2 * nets + edge + 8, patterns)], mine, mate
    )[0]
    pair, conduct = lax.optimization_barrier((pair, conduct))
    groups = [pair]
    for distances in stages(cols, 2):
        whole = groups[0] if len(groups) == 1 else jnp.concatenate(groups)
        groups = [whole] + [other(whole, "col", cols, d) for d in distances]

    inverse, rest, table, take, put = run(
        functools.partial(tile_kernel, nets, edge),
        [field, field, (edge, patterns), (slots, cols * nets), (slots, tiles * nodes)],
        conduct[0],
        capacitance[0],
        voltage,
        inject[0],
        track_gain[0],
        sink_net[0, 0],
        sink_count[0],
        sink_tile[0, 0],
        sink_node[0, 0],
        sink_gain[0, 0],
        scratch=[pltpu.VMEM(field, jnp.float32)] * 2,
        flops=16 * 2 * tiles * nodes**3 * 6,
    )

    message, precond = run(
        functools.partial(residual_kernel, nets, edge, cols),
        [(2 * span + edge + 8, patterns), field],
        voltage,
        mate,
        inverse,
        rest,
        table,
        take,
        put,
        *groups,
    )

    column = [message] + [
        lax.ppermute(message, "row", [((i + k) % rows, i) for i in range(rows)])
        for k in range(1, rows)
    ]
    message, far, flow, first = run(
        functools.partial(rim_kernel, rows, tiles, edge),
        [(rows * (span + edge), patterns), (rows * edge, patterns), (span, patterns), (8, patterns)],
        *column,
    )

    inner = other(message, "col", cols, 1)
    beyond = outer_swap(message, "col", cols)
    far = lax.ppermute(far, "col", [((i + 2) % cols, i) for i in range(cols)])
    moments, t0, t1 = run(
        functools.partial(moment_kernel, rows, cols, tiles, edge),
        [(8, patterns), (span, patterns), (span, patterns)],
        message,
        inner,
        beyond,
        far,
        first,
    )

    sums = [moments]
    for distances in stages(cols, 1):
        moments = sum(sums[1:], sums[0])
        sums = [moments] + [other(moments, "col", cols, d) for d in distances]
    return run(
        functools.partial(final_kernel, edge),
        [field],
        voltage,
        precond,
        inverse,
        flow,
        t0,
        t1,
        *sums,
    )[0][None]


def solution(mesh):
    whole = P("row", "col", None, None)
    third = P("row", "col", None)
    placed = (whole, whole, whole, third, whole, third, whole, third, whole, whole, whole)
    return jax.shard_map(local, mesh=mesh, in_specs=placed, out_specs=whole, check_vma=False)
```

time: 59.8 us -> 42.2 us (0.71); the launches traced: 59.1 us -> 42.2 us
  local copies, waits for them, and re-layouts: 11.1 us -> 2.29 us
  matrix products: 3.7 us -> 0 us
  other arithmetic: 3.66 us -> 0.01 us
  Pallas kernels: 3.79 us -> 5.83 us
  waiting for transfers between devices: 17.6 us -> 16.1 us
  starting transfers between devices: 18.6 us -> 18 us
    dot_general x8 -> x0, matrix products: 3.7 us -> none  [the longest x3 1.02 us: spread(): return jnp.einsum('rcij,rcjp->rcip', cores, flow, precision=PRECISE)]
    unnamed x46 -> x24, local copies, waits for them, and re-layouts: 5.8 us -> 2.29 us
    ppermute x3 -> x2, starting transfers between devices: 5.51 us -> 2.05 us  [the longest x1 1.18 us: local(): far = lax.ppermute(far, 'col', [((i + 2) % cols, i) for i in range(cols)])]
    slice x27 -> x0, local copies, waits for them, and re-layouts: 2.6 us -> none  [the longest x6 0.86 us: net_flow(): jnp.roll(south, 1, axis=0) * not_first]
    pallas_call x1 -> x7, Pallas kernels: 3.79 us -> 5.83 us  [run(): pl.pallas_call(kernel, out_shape=shapes, in_specs=[vmem] * len(args), out...]
    squeeze x8 -> x0, local copies, waits for them, and re-layouts: 2.01 us -> none  [the longest x2 0.85 us: local(): south_gain[1]]
    ppermute x10 -> x9, starting transfers between devices: 8.81 us -> 10.3 us  [other(): return lax.ppermute(block, axis, [(i, i ^ distance) for i in range(count)])]
    sub x7 -> x0, other arithmetic: 1.29 us -> none  [the longest x2 1.16 us: net_flow(): east[:, 1:] - east[:, :-1] + south - jnp.roll(south, 1, axis=0) * not_first]
  transfers between devices with their start and end apart: 16 -> 14, of which waited for: 10 -> 10; matrix products, arithmetic and copies ran while one was open for 5% -> 0% of each run, Pallas kernels for 6% -> 5%
where the time goes in v3:
time: 42.2 us
  starting transfers between devices  18 us (43%)
  waiting for transfers between devices  16.1 us (38%)
  Pallas kernels  5.83 us (14%)
  local copies, waits for them, and re-layouts  2.29 us (5%)
    ppermute x9, starting transfers between devices, other(): return lax.ppermute(block, axis, [(i, i ^ distance) for i in range(count)])  10.3 us
    ppermute x9, waiting for transfers between devices, other(): return lax.ppermute(block, axis, [(i, i ^ distance) for i in range(count)])  6.63 us
    pallas_call x7, Pallas kernels, run(): pl.pallas_call(kernel, out_shape=shapes, in_specs=[vmem] * len(args), out...  5.83 us
    ppermute x3, starting transfers between devices, local(): lax.ppermute(message, 'row', [((i + k) % rows, i) for i in range(rows)])  5.57 us
    ppermute x1, waiting for transfers between devices, local(): far = lax.ppermute(far, 'col', [((i + 2) % cols, i) for i in range(cols)])  4.98 us
    ppermute x3, waiting for transfers between devices, local(): lax.ppermute(message, 'row', [((i + k) % rows, i) for i in range(rows)])  4.44 us
    unnamed x24, local copies, waits for them, and re-layouts  2.29 us
    ppermute x1, starting transfers between devices, local(): far = lax.ppermute(far, 'col', [((i + 2) % cols, i) for i in range(cols)])  1.18 us
  transfers between devices with their start and end apart: 14, of which 10 were waited for; matrix products, arithmetic and copies ran while one was open for 0% of the time, Pallas kernels for 5%

profile of v3, /device:TPU:0, one launch (start us, length us, event | category | flops | bytes accessed | tf_op | source)
XLA Modules:
  0.0 42.2 jit_solution(2627449754708350649)
XLA Ops:
  0.0 0.0 copy-start.2
  0.0 0.7 %copy-done.2 = f32[1,2,2,32]{3,2,1,0:T(2,128)S(1)} copy-done((f32[1,2,2,32]{3,2,1,0:T(2,128)S(1)}, f32[1,2,2,32]{3,2,1,0:T(2,128)}, u32[]{:S(2)}) %copy-start.2) | copy-done | bytes 536
  0.7 0.0 copy-done.3
  0.7 0.9 %copy-done = f32[1,2,128,128]{3,2,1,0:T(8,128)S(1)} copy-done((f32[1,2,128,128]{3,2,1,0:T(8,128)S(1)}, f32[1,2,128,128]{3,2,1,0:T(8,128)}, u32[]{:S(2)}) %copy-start) | copy-done | bytes 131096
  1.6 0.1 shard_map.109.mine_ref
  1.7 0.5 %collective-permute-start = (f32[136,128]{1,0:T(8,128)S(1)}, f32[136,128]{1,0:T(8,128)S(1)}, u32[]{:S(2)}, u32[]{:S(2)}) collective-permute-start(f32[136,128]{1,0:T(8,128)S(1)} %shard_map.109.mine_ref), channel_id=1, source_target_pairs={{0,1},{1,0},{2,3},{3,2},{4,5},{5,4},{6,7},{7,6},{8,9},{9,8},{10,11... | collective-permute-start | bytes 208904 | tf_op jit(solution)/shard_map/ppermute | solution.py:391
  2.2 0.9 %collective-permute-done.mate_ref = f32[136,128]{1,0:T(8,128)S(1)} collective-permute-done((f32[136,128]{1,0:T(8,128)S(1)}, f32[136,128]{1,0:T(8,128)S(1)}, u32[]{:S(2)}, u32[]{:S(2)}) %collective-permute-start) | collective-permute-done | bytes 69664 | tf_op jit(solution)/shard_map/ppermute | solution.py:391
  3.1 3.9 %collective-permute-start.3 = (f32[168,128]{1,0:T(8,128)S(1)}, f32[168,128]{1,0:T(8,128)S(1)}, u32[]{:S(2)}, u32[]{:S(2)}) collective-permute-start(f32[168,128]{1,0:T(8,128)S(1)} %shard_map.110.refs_0_), channel_id=1, source_target_pairs={{0,6},{1,7},{2,4},{3,5},{4,2},{5,3},{6,0},{7,1},{8,14},{9,15},{10,... | collective-permute-start | bytes 258056 | tf_op jit(solution)/shard_map/ppermute | solution.py:391
  7.0 0.5 %collective-permute-start.2 = (f32[168,128]{1,0:T(8,128)S(1)}, f32[168,128]{1,0:T(8,128)S(1)}, u32[]{:S(2)}, u32[]{:S(2)}) collective-permute-start(f32[168,128]{1,0:T(8,128)S(1)} %shard_map.110.refs_0_), channel_id=1, source_target_pairs={{0,4},{1,5},{2,6},{3,7},{4,0},{5,1},{6,2},{7,3},{8,12},{9,13},{10,... | collective-permute-start | bytes 258056 | tf_op jit(solution)/shard_map/ppermute | solution.py:391
  7.5 0.1 collective-permute-start.1
  7.6 0.0 copy-start.10
  7.7 0.0 copy-done.4
  7.7 0.0 copy-done.5
  7.7 0.0 copy-done.1
  7.7 0.0 copy-done.9
  7.7 0.6 %copy-done.8 = s32[1,1,8,8]{3,2,1,0:T(8,128)S(1)} copy-done((s32[1,1,8,8]{3,2,1,0:T(8,128)S(1)}, s32[1,1,8,8]{3,2,1,0:T(8,128)}, u32[]{:S(2)}) %copy-start.8) | copy-done | bytes 280
  8.3 0.0 copy-done.11
  8.3 0.0 copy-done.7
  8.4 0.0 copy-done.6
  8.4 0.0 copy-done.10
  8.4 2.2 %shard_map.111 = (f32[2,128,128]{2,1,0:T(8,128)S(1)}, f32[2,128,128]{2,1,0:T(8,128)S(1)}, f32[32,128]{1,0:T(8,128)S(1)}, f32[64,512]{1,0:T(8,128)S(1)}, f32[64,256]{1,0:T(8,128)S(1)}) custom-call(f32[2,128,128]{2,1,0:T(8,128)S(1)} %bitcast.19, f32[2,128]{1,0:T(2,128)S(1)} %bitcast.25, f32[2,128,128]{2,1,0:T(8,128)S(1)} %bitcast.13, ...), custom_call_target="tpu_custom_call" | custom-call | flops 805306368 | bytes 870944 | tf_op jit(solution)/shard_map/pallas_call | solution.py:23
  10.6 0.0 collective-permute-done.3.refs_3_
  10.6 1.1 %collective-permute-done.2.refs_2_ = f32[168,128]{1,0:T(8,128)S(1)} collective-permute-done((f32[168,128]{1,0:T(8,128)S(1)}, f32[168,128]{1,0:T(8,128)S(1)}, u32[]{:S(2)}, u32[]{:S(2)}) %collective-permute-start.2) | collective-permute-done | bytes 86048 | tf_op jit(solution)/shard_map/ppermute | solution.py:391
  11.7 0.3 collective-permute-done.1.refs_1_
  12.0 1.2 %shard_map.112 = (f32[168,128]{1,0:T(8,128)S(1)}, f32[2,128,128]{2,1,0:T(8,128)S(1)}) custom-call(f32[2,128,128]{2,1,0:T(8,128)S(1)} %bitcast.14, f32[136,128]{1,0:T(8,128)S(1)} %collective-permute-done.mate_ref, f32[2,128,128]{2,1,0:T(8,128)S(1)} %get-tuple-element.22.inverse_ref, f32[2,128,128]{2,1,0:T(8,128)S(1)} %get-tuple-element.23.rest_ref, ...), custom_call_target="tpu_custom_call" | custom-call | bytes 1236992 | tf_op jit(solution)/shard_map/pallas_call | solution.py:23
  13.2 1.6 %collective-permute-start.6 = (f32[168,128]{1,0:T(8,128)S(1)}, f32[168,128]{1,0:T(8,128)S(1)}, u32[]{:S(2)}, u32[]{:S(2)}) collective-permute-start(f32[168,128]{1,0:T(8,128)S(1)} %get-tuple-element.29.refs_0_), channel_id=1, source_target_pairs={{24,0},{0,8},{8,16},{16,24},{25,1},{1,9},{9,17},{17,25},{26,2},{2,... | collective-permute-start | bytes 258056 | tf_op jit(solution)/shard_map/ppermute | solution.py:475
  14.8 2.6 %collective-permute-start.5 = (f32[168,128]{1,0:T(8,128)S(1)}, f32[168,128]{1,0:T(8,128)S(1)}, u32[]{:S(2)}, u32[]{:S(2)}) collective-permute-start(f32[168,128]{1,0:T(8,128)S(1)} %get-tuple-element.29.refs_0_), channel_id=1, source_target_pairs={{16,0},{24,8},{0,16},{8,24},{17,1},{25,9},{1,17},{9,25},{18,2},{26... | collective-permute-start | bytes 258056 | tf_op jit(solution)/shard_map/ppermute | solution.py:475
  17.4 1.3 %collective-permute-start.4 = (f32[168,128]{1,0:T(8,128)S(1)}, f32[168,128]{1,0:T(8,128)S(1)}, u32[]{:S(2)}, u32[]{:S(2)}) collective-permute-start(f32[168,128]{1,0:T(8,128)S(1)} %get-tuple-element.29.refs_0_), channel_id=1, source_target_pairs={{8,0},{16,8},{24,16},{0,24},{9,1},{17,9},{25,17},{1,25},{10,2},{18... | collective-permute-start | bytes 258056 | tf_op jit(solution)/shard_map/ppermute | solution.py:475
  18.7 1.8 %collective-permute-done.6.refs_3_ = f32[168,128]{1,0:T(8,128)S(1)} collective-permute-done((f32[168,128]{1,0:T(8,128)S(1)}, f32[168,128]{1,0:T(8,128)S(1)}, u32[]{:S(2)}, u32[]{:S(2)}) %collective-permute-start.6) | collective-permute-done | bytes 86048 | tf_op jit(solution)/shard_map/ppermute | solution.py:475
  20.5 2.7 %collective-permute-done.5.refs_2_ = f32[168,128]{1,0:T(8,128)S(1)} collective-permute-done((f32[168,128]{1,0:T(8,128)S(1)}, f32[168,128]{1,0:T(8,128)S(1)}, u32[]{:S(2)}, u32[]{:S(2)}) %collective-permute-start.5) | collective-permute-done | bytes 86048 | tf_op jit(solution)/shard_map/ppermute | solution.py:475
  23.2 0.0 collective-permute-done.4.refs_1_
  23.2 0.4 shard_map.113
  23.5 0.9 %collective-permute-start.8 = (f32[384,128]{1,0:T(8,128)S(1)}, f32[384,128]{1,0:T(8,128)S(1)}, u32[]{:S(2)}, u32[]{:S(2)}) collective-permute-start(f32[384,128]{1,0:T(8,128)S(1)} %get-tuple-element.31.own_ref), channel_id=1, source_target_pairs={{0,7},{1,2},{2,1},{3,4},{4,3},{5,6},{6,5},{7,0},{8,15},{9,10},{10,... | collective-permute-start | bytes 589832 | tf_op jit(solution)/shard_map/ppermute | solution.py:403
  24.4 1.1 %collective-permute-start.7 = (f32[384,128]{1,0:T(8,128)S(1)}, f32[384,128]{1,0:T(8,128)S(1)}, u32[]{:S(2)}, u32[]{:S(2)}) collective-permute-start(f32[384,128]{1,0:T(8,128)S(1)} %get-tuple-element.31.own_ref), channel_id=1, source_target_pairs={{0,1},{1,0},{2,3},{3,2},{4,5},{5,4},{6,7},{7,6},{8,9},{9,8},{10,11... | collective-permute-start | bytes 589832 | tf_op jit(solution)/shard_map/ppermute | solution.py:391
  25.5 1.2 %collective-permute-start.9 = (f32[128,128]{1,0:T(8,128)S(1)}, f32[128,128]{1,0:T(8,128)S(1)}, u32[]{:S(2)}, u32[]{:S(2)}) collective-permute-start(f32[128,128]{1,0:T(8,128)S(1)} %get-tuple-element.32), channel_id=1, source_target_pairs={{2,0},{3,1},{4,2},{5,3},{6,4},{7,5},{0,6},{1,7},{10,8},{11,9},{12,... | collective-permute-start | bytes 196616 | tf_op jit(solution)/shard_map/ppermute | solution.py:486
  26.7 5.0 %collective-permute-done.9.far_ref = f32[128,128]{1,0:T(8,128)S(1)} collective-permute-done((f32[128,128]{1,0:T(8,128)S(1)}, f32[128,128]{1,0:T(8,128)S(1)}, u32[]{:S(2)}, u32[]{:S(2)}) %collective-permute-start.9) | collective-permute-done | bytes 65568 | tf_op jit(solution)/shard_map/ppermute | solution.py:486
  31.6 0.0 collective-permute-done.8.outer_ref
  31.6 0.0 collective-permute-done.7.inner_ref
  31.6 1.1 %shard_map.114 = (f32[8,128]{1,0:T(8,128)S(1)}, f32[64,128]{1,0:T(8,128)S(1)}, f32[64,128]{1,0:T(8,128)S(1)}) custom-call(f32[384,128]{1,0:T(8,128)S(1)} %get-tuple-element.31.own_ref, f32[384,128]{1,0:T(8,128)S(1)} %collective-permute-done.7.inner_ref, f32[384,128]{1,0:T(8,128)S(1)} %collective-permute-done.8.outer_ref, ...), custom_call_target="tpu_custom_call" | custom-call | bytes 729088 | tf_op jit(solution)/shard_map/pallas_call | solution.py:23
  32.7 0.8 %collective-permute-start.10 = (f32[8,128]{1,0:T(8,128)S(1)}, f32[8,128]{1,0:T(8,128)S(1)}, u32[]{:S(2)}, u32[]{:S(2)}) collective-permute-start(f32[8,128]{1,0:T(8,128)S(1)} %get-tuple-element.36), channel_id=1, source_target_pairs={{0,1},{1,0},{2,3},{3,2},{4,5},{5,4},{6,7},{7,6},{8,9},{9,8},{10,11... | collective-permute-start | bytes 12296 | tf_op jit(solution)/shard_map/ppermute | solution.py:391
  33.5 0.8 %collective-permute-done.10 = f32[8,128]{1,0:T(8,128)S(1)} collective-permute-done((f32[8,128]{1,0:T(8,128)S(1)}, f32[8,128]{1,0:T(8,128)S(1)}, u32[]{:S(2)}, u32[]{:S(2)}) %collective-permute-start.10) | collective-permute-done | bytes 4128 | tf_op jit(solution)/shard_map/ppermute | solution.py:391
  34.3 2.2 %collective-permute-start.13 = (f32[8,128]{1,0:T(8,128)S(1)}, f32[8,128]{1,0:T(8,128)S(1)}, u32[]{:S(2)}, u32[]{:S(2)}) collective-permute-start(f32[8,128]{1,0:T(8,128)S(1)} %add.3.refs_0_), channel_id=1, source_target_pairs={{0,6},{1,7},{2,4},{3,5},{4,2},{5,3},{6,0},{7,1},{8,14},{9,15},{10,... | collective-permute-start | bytes 12296 | tf_op jit(solution)/shard_map/ppermute | solution.py:391
  36.5 1.2 %collective-permute-start.12 = (f32[8,128]{1,0:T(8,128)S(1)}, f32[8,128]{1,0:T(8,128)S(1)}, u32[]{:S(2)}, u32[]{:S(2)}) collective-permute-start(f32[8,128]{1,0:T(8,128)S(1)} %add.3.refs_0_), channel_id=1, source_target_pairs={{0,4},{1,5},{2,6},{3,7},{4,0},{5,1},{6,2},{7,3},{8,12},{9,13},{10,... | collective-permute-start | bytes 12296 | tf_op jit(solution)/shard_map/ppermute | solution.py:391
  37.7 0.1 collective-permute-start.11
  37.8 1.0 %collective-permute-done.13.refs_3_ = f32[8,128]{1,0:T(8,128)S(1)} collective-permute-done((f32[8,128]{1,0:T(8,128)S(1)}, f32[8,128]{1,0:T(8,128)S(1)}, u32[]{:S(2)}, u32[]{:S(2)}) %collective-permute-start.13) | collective-permute-done | bytes 4128 | tf_op jit(solution)/shard_map/ppermute | solution.py:391
  38.8 1.3 %collective-permute-done.12.refs_2_ = f32[8,128]{1,0:T(8,128)S(1)} collective-permute-done((f32[8,128]{1,0:T(8,128)S(1)}, f32[8,128]{1,0:T(8,128)S(1)}, u32[]{:S(2)}, u32[]{:S(2)}) %collective-permute-start.12) | collective-permute-done | bytes 4128 | tf_op jit(solution)/shard_map/ppermute | solution.py:391
  40.1 1.2 %collective-permute-done.11.refs_1_ = f32[8,128]{1,0:T(8,128)S(1)} collective-permute-done((f32[8,128]{1,0:T(8,128)S(1)}, f32[8,128]{1,0:T(8,128)S(1)}, u32[]{:S(2)}, u32[]{:S(2)}) %collective-permute-start.11) | collective-permute-done | bytes 4128 | tf_op jit(solution)/shard_map/ppermute | solution.py:391
  41.3 0.9 %shard_map.115 = f32[2,128,128]{2,1,0:T(8,128)} custom-call(f32[2,128,128]{2,1,0:T(8,128)S(1)} %bitcast.15, f32[2,128,128]{2,1,0:T(8,128)S(1)} %get-tuple-element.28.precond_ref, f32[2,128,128]{2,1,0:T(8,128)S(1)} %get-tuple-element.22.inverse_ref, f32[64,128]{1,0:T(8,128)S(1)} %get-tuple-element.30.flow_ref, f32[64,128]{1,0:T(8,128)S(1)} %get-tuple-element.34.t0_ref, ...), custom_call_target="tpu_custom_call" | custom-call | bytes 638976 | tf_op jit(solution)/shard_map/pallas_call | solution.py:23
  (12 shorter events, 0.0 us)
Async XLA Ops:
  0.0 0.7 %copy-start.2 = (f32[1,2,2,32]{3,2,1,0:T(2,128)S(1)}, f32[1,2,2,32]{3,2,1,0:T(2,128)}, u32[]{:S(2)}) copy-start(f32[1,2,2,32]{3,2,1,0:T(2,128)} %param.15) | copy-start | bytes 1540
  0.0 0.7 %copy-start.3 = (s32[1,1,64]{2,1,0:T(1,128)S(1)}, s32[1,1,64]{2,1,0:T(1,128)}, u32[]{:S(2)}) copy-start(s32[1,1,64]{2,1,0:T(1,128)} %param.16) | copy-start | bytes 772
  0.7 0.9 %copy-start = (f32[1,2,128,128]{3,2,1,0:T(8,128)S(1)}, f32[1,2,128,128]{3,2,1,0:T(8,128)}, u32[]{:S(2)}) copy-start(f32[1,2,128,128]{3,2,1,0:T(8,128)} %param.11) | copy-start | bytes 393220
  1.6 6.1 %copy-start.4 = (f32[1,2,128,128]{3,2,1,0:T(8,128)S(1)}, f32[1,2,128,128]{3,2,1,0:T(8,128)}, u32[]{:S(2)}) copy-start(f32[1,2,128,128]{3,2,1,0:T(8,128)} %param.13) | copy-start | bytes 393220
  1.6 6.1 %copy-start.5 = (f32[1,2,128,128]{3,2,1,0:T(8,128)S(1)}, f32[1,2,128,128]{3,2,1,0:T(8,128)}, u32[]{:S(2)}) copy-start(f32[1,2,128,128]{3,2,1,0:T(8,128)} %param.12) | copy-start | bytes 393220
  1.7 6.0 %copy-start.1 = (f32[1,2,128,128]{3,2,1,0:T(8,128)S(1)}, f32[1,2,128,128]{3,2,1,0:T(8,128)}, u32[]{:S(2)}) copy-start(f32[1,2,128,128]{3,2,1,0:T(8,128)} %param.11) | copy-start | bytes 393220
  1.7 1.4 %collective-permute-start = (f32[136,128]{1,0:T(8,128)S(1)}, f32[136,128]{1,0:T(8,128)S(1)}, u32[]{:S(2)}, u32[]{:S(2)}) collective-permute-start(f32[136,128]{1,0:T(8,128)S(1)} %shard_map.109.mine_ref), channel_id=1, source_target_pairs={{0,1},{1,0},{2,3},{3,2},{4,5},{5,4},{6,7},{7,6},{8,9},{9,8},{10,11... | collective-permute-start | bytes 208904 | tf_op jit(solution)/shard_map/ppermute | solution.py:391
  3.1 4.6 %copy-start.9 = (f32[1,1,8,8]{3,2,1,0:T(8,128)S(1)}, f32[1,1,8,8]{3,2,1,0:T(8,128)}, u32[]{:S(2)}) copy-start(f32[1,1,8,8]{3,2,1,0:T(8,128)} %param.21) | copy-start | bytes 772
  3.1 7.4 %collective-permute-start.3 = (f32[168,128]{1,0:T(8,128)S(1)}, f32[168,128]{1,0:T(8,128)S(1)}, u32[]{:S(2)}, u32[]{:S(2)}) collective-permute-start(f32[168,128]{1,0:T(8,128)S(1)} %shard_map.110.refs_0_), channel_id=1, source_target_pairs={{0,6},{1,7},{2,4},{3,5},{4,2},{5,3},{6,0},{7,1},{8,14},{9,15},{10,... | collective-permute-start | bytes 258056 | tf_op jit(solution)/shard_map/ppermute | solution.py:391
  7.0 4.7 %collective-permute-start.2 = (f32[168,128]{1,0:T(8,128)S(1)}, f32[168,128]{1,0:T(8,128)S(1)}, u32[]{:S(2)}, u32[]{:S(2)}) collective-permute-start(f32[168,128]{1,0:T(8,128)S(1)} %shard_map.110.refs_0_), channel_id=1, source_target_pairs={{0,4},{1,5},{2,6},{3,7},{4,0},{5,1},{6,2},{7,3},{8,12},{9,13},{10,... | collective-permute-start | bytes 258056 | tf_op jit(solution)/shard_map/ppermute | solution.py:391
  7.5 4.5 %collective-permute-start.1 = (f32[168,128]{1,0:T(8,128)S(1)}, f32[168,128]{1,0:T(8,128)S(1)}, u32[]{:S(2)}, u32[]{:S(2)}) collective-permute-start(f32[168,128]{1,0:T(8,128)S(1)} %shard_map.110.refs_0_), channel_id=1, source_target_pairs={{0,2},{1,3},{2,0},{3,1},{4,6},{5,7},{6,4},{7,5},{8,10},{9,11},{10,... | collective-permute-start | bytes 258056 | tf_op jit(solution)/shard_map/ppermute | solution.py:391
  7.6 0.7 %copy-start.8 = (s32[1,1,8,8]{3,2,1,0:T(8,128)S(1)}, s32[1,1,8,8]{3,2,1,0:T(8,128)}, u32[]{:S(2)}) copy-start(s32[1,1,8,8]{3,2,1,0:T(8,128)} %param.20) | copy-start | bytes 772
  7.6 0.7 %copy-start.11 = (s32[1,1,8]{2,1,0:T(1,128)S(1)}, s32[1,1,8]{2,1,0:T(1,128)}, u32[]{:S(2)}) copy-start(s32[1,1,8]{2,1,0:T(1,128)} %param.18) | copy-start | bytes 100
  7.6 0.7 %copy-start.7 = (s32[1,1,8,8]{3,2,1,0:T(8,128)S(1)}, s32[1,1,8,8]{3,2,1,0:T(8,128)}, u32[]{:S(2)}) copy-start(s32[1,1,8,8]{3,2,1,0:T(8,128)} %param.19) | copy-start | bytes 772
  7.6 0.7 %copy-start.6 = (s32[1,1,8,8]{3,2,1,0:T(8,128)S(1)}, s32[1,1,8,8]{3,2,1,0:T(8,128)}, u32[]{:S(2)}) copy-start(s32[1,1,8,8]{3,2,1,0:T(8,128)} %param.17) | copy-start | bytes 772
  7.6 0.7 %copy-start.10 = (f32[1,2,128]{2,1,0:T(2,128)S(1)}, f32[1,2,128]{2,1,0:T(2,128)}, u32[]{:S(2)}) copy-start(f32[1,2,128]{2,1,0:T(2,128)} %param.14) | copy-start | bytes 3076
  13.2 7.4 %collective-permute-start.6 = (f32[168,128]{1,0:T(8,128)S(1)}, f32[168,128]{1,0:T(8,128)S(1)}, u32[]{:S(2)}, u32[]{:S(2)}) collective-permute-start(f32[168,128]{1,0:T(8,128)S(1)} %get-tuple-element.29.refs_0_), channel_id=1, source_target_pairs={{24,0},{0,8},{8,16},{16,24},{25,1},{1,9},{9,17},{17,25},{26,2},{2,... | collective-permute-start | bytes 258056 | tf_op jit(solution)/shard_map/ppermute | solution.py:475
  14.8 8.4 %collective-permute-start.5 = (f32[168,128]{1,0:T(8,128)S(1)}, f32[168,128]{1,0:T(8,128)S(1)}, u32[]{:S(2)}, u32[]{:S(2)}) collective-permute-start(f32[168,128]{1,0:T(8,128)S(1)} %get-tuple-element.29.refs_0_), channel_id=1, source_target_pairs={{16,0},{24,8},{0,16},{8,24},{17,1},{25,9},{1,17},{9,25},{18,2},{26... | collective-permute-start | bytes 258056 | tf_op jit(solution)/shard_map/ppermute | solution.py:475
  17.4 5.8 %collective-permute-start.4 = (f32[168,128]{1,0:T(8,128)S(1)}, f32[168,128]{1,0:T(8,128)S(1)}, u32[]{:S(2)}, u32[]{:S(2)}) collective-permute-start(f32[168,128]{1,0:T(8,128)S(1)} %get-tuple-element.29.refs_0_), channel_id=1, source_target_pairs={{8,0},{16,8},{24,16},{0,24},{9,1},{17,9},{25,17},{1,25},{10,2},{18... | collective-permute-start | bytes 258056 | tf_op jit(solution)/shard_map/ppermute | solution.py:475
  23.5 8.1 %collective-permute-start.8 = (f32[384,128]{1,0:T(8,128)S(1)}, f32[384,128]{1,0:T(8,128)S(1)}, u32[]{:S(2)}, u32[]{:S(2)}) collective-permute-start(f32[384,128]{1,0:T(8,128)S(1)} %get-tuple-element.31.own_ref), channel_id=1, source_target_pairs={{0,7},{1,2},{2,1},{3,4},{4,3},{5,6},{6,5},{7,0},{8,15},{9,10},{10,... | collective-permute-start | bytes 589832 | tf_op jit(solution)/shard_map/ppermute | solution.py:403
  24.4 7.2 %collective-permute-start.7 = (f32[384,128]{1,0:T(8,128)S(1)}, f32[384,128]{1,0:T(8,128)S(1)}, u32[]{:S(2)}, u32[]{:S(2)}) collective-permute-start(f32[384,128]{1,0:T(8,128)S(1)} %get-tuple-element.31.own_ref), channel_id=1, source_target_pairs={{0,1},{1,0},{2,3},{3,2},{4,5},{5,4},{6,7},{7,6},{8,9},{9,8},{10,11... | collective-permute-start | bytes 589832 | tf_op jit(solution)/shard_map/ppermute | solution.py:391
  25.5 6.2 %collective-permute-start.9 = (f32[128,128]{1,0:T(8,128)S(1)}, f32[128,128]{1,0:T(8,128)S(1)}, u32[]{:S(2)}, u32[]{:S(2)}) collective-permute-start(f32[128,128]{1,0:T(8,128)S(1)} %get-tuple-element.32), channel_id=1, source_target_pairs={{2,0},{3,1},{4,2},{5,3},{6,4},{7,5},{0,6},{1,7},{10,8},{11,9},{12,... | collective-permute-start | bytes 196616 | tf_op jit(solution)/shard_map/ppermute | solution.py:486
  32.7 1.6 %collective-permute-start.10 = (f32[8,128]{1,0:T(8,128)S(1)}, f32[8,128]{1,0:T(8,128)S(1)}, u32[]{:S(2)}, u32[]{:S(2)}) collective-permute-start(f32[8,128]{1,0:T(8,128)S(1)} %get-tuple-element.36), channel_id=1, source_target_pairs={{0,1},{1,0},{2,3},{3,2},{4,5},{5,4},{6,7},{7,6},{8,9},{9,8},{10,11... | collective-permute-start | bytes 12296 | tf_op jit(solution)/shard_map/ppermute | solution.py:391
  34.3 4.5 %collective-permute-start.13 = (f32[8,128]{1,0:T(8,128)S(1)}, f32[8,128]{1,0:T(8,128)S(1)}, u32[]{:S(2)}, u32[]{:S(2)}) collective-permute-start(f32[8,128]{1,0:T(8,128)S(1)} %add.3.refs_0_), channel_id=1, source_target_pairs={{0,6},{1,7},{2,4},{3,5},{4,2},{5,3},{6,0},{7,1},{8,14},{9,15},{10,... | collective-permute-start | bytes 12296 | tf_op jit(solution)/shard_map/ppermute | solution.py:391
  36.5 3.6 %collective-permute-start.12 = (f32[8,128]{1,0:T(8,128)S(1)}, f32[8,128]{1,0:T(8,128)S(1)}, u32[]{:S(2)}, u32[]{:S(2)}) collective-permute-start(f32[8,128]{1,0:T(8,128)S(1)} %add.3.refs_0_), channel_id=1, source_target_pairs={{0,4},{1,5},{2,6},{3,7},{4,0},{5,1},{6,2},{7,3},{8,12},{9,13},{10,... | collective-permute-start | bytes 12296 | tf_op jit(solution)/shard_map/ppermute | solution.py:391
  37.7 3.6 %collective-permute-start.11 = (f32[8,128]{1,0:T(8,128)S(1)}, f32[8,128]{1,0:T(8,128)S(1)}, u32[]{:S(2)}, u32[]{:S(2)}) collective-permute-start(f32[8,128]{1,0:T(8,128)S(1)} %add.3.refs_0_), channel_id=1, source_target_pairs={{0,2},{1,3},{2,0},{3,1},{4,6},{5,7},{6,4},{7,5},{8,10},{9,11},{10,... | collective-permute-start | bytes 12296 | tf_op jit(solution)/shard_map/ppermute | solution.py:391

commit v4 on v3

v4 whole, which is shorter than its diff:
```python
import functools

import jax
import jax.numpy as jnp
from jax import lax
from jax.experimental import pallas as pl
from jax.experimental.pallas import tpu as pltpu
from jax.sharding import PartitionSpec as P

DOUBLINGS = 5
SMALL = 2.0**-13
VMEM_BYTES = 16 * 1024 * 1024

dot = functools.partial(
    jnp.dot, precision=lax.Precision.HIGHEST, preferred_element_type=jnp.float32
)


def split(block):
    high = block.astype(jnp.bfloat16)
    return high, (block - high.astype(jnp.float32)).astype(jnp.bfloat16)


def narrow(left, right):
    return jnp.dot(left, right, preferred_element_type=jnp.float32)


def dot3(left, right):
    (left_high, left_low), (right_high, right_low) = split(left), split(right)
    return narrow(left_high, right_high) + (
        narrow(left_high, right_low) + narrow(left_low, right_high)
    )


def select(onehot, block):
    high = block.astype(jnp.bfloat16)
    rest = block - high.astype(jnp.float32)
    middle, low = split(rest)
    return narrow(onehot, high) + (narrow(onehot, middle) + narrow(onehot, low))


def run(kernel, outs, *args, scratch=(), flops=4_000_000_000):
    vmem = pl.BlockSpec(memory_space=pltpu.VMEM)
    shapes = tuple(
        o if isinstance(o, jax.ShapeDtypeStruct) else jax.ShapeDtypeStruct(o, jnp.float32)
        for o in outs
    )
    moved = sum(4 * a.size for a in args) + sum(4 * s.size for s in shapes)
    return pl.pallas_call(
        kernel,
        out_shape=shapes,
        in_specs=[vmem] * len(args),
        out_specs=(vmem,) * len(shapes),
        scratch_shapes=list(scratch),
        compiler_params=pltpu.CompilerParams(vmem_limit_bytes=VMEM_BYTES),
        cost_estimate=pl.CostEstimate(flops=flops, bytes_accessed=moved, transcendentals=0),
    )(*args)


def iota(shape, axis):
    return lax.broadcasted_iota(jnp.int32, shape, axis)


def to_column(row):
    count = row.shape[1]
    square = jnp.broadcast_to(row, (count, count))
    keep = iota((count, count), 0) == iota((count, count), 1)
    return jnp.sum(jnp.where(keep, square, 0.0), axis=1, keepdims=True)


def slot_column(table):
    sources, slots = table.shape
    spread = jnp.concatenate(
        [jnp.broadcast_to(table[s : s + 1], (slots, slots)) for s in range(sources)], axis=0
    )
    keep = iota(spread.shape, 0) % slots == iota(spread.shape, 1)
    return jnp.sum(jnp.where(keep, spread, 0.0), axis=1, keepdims=True)


def source_column(row, slots):
    sources = row.shape[1]
    spread = jnp.broadcast_to(row, (sources * slots, sources))
    keep = iota(spread.shape, 0) // slots == iota(spread.shape, 1)
    return jnp.sum(jnp.where(keep, spread, 0.0), axis=1, keepdims=True)


def pair_kernel(nets, edge, volt_ref, picked_ref, mate_ref, mate_driver_ref, mate_gain_ref, out_ref):
    tiles, nodes, patterns = volt_ref.shape
    odd = lax.axis_index("col") % 2 == 1
    mate_picked = to_column(mate_driver_ref[...].astype(jnp.float32))
    for i, (field, picked) in enumerate(((volt_ref, picked_ref[...]), (mate_ref, mate_picked))):
        rows = jnp.zeros((nets, patterns), jnp.float32)
        for t in range(tiles):
            block = jnp.concatenate([field[t]] * (-(-nets // nodes)), axis=0)[:nets]
            rows = jnp.where(picked == t, block, rows)
        out_ref[i * nets : (i + 1) * nets] = rows
    base = 2 * nets
    out_ref[base : base + edge] = jnp.where(odd, mate_ref[0, :edge], mate_ref[tiles - 1, :edge])
    out_ref[base + edge :] = jnp.zeros((8, patterns), jnp.float32)
    out_ref[base + edge : base + edge + 1, :edge] = mate_gain_ref[tiles - 1, 0:1]


def eye_kernel(out_ref):
    out_ref[...] = jnp.where(iota(out_ref.shape, 0) == iota(out_ref.shape, 1), 1.0, 0.0)


def sink_kernel(
    nets,
    edge,
    conduct_ref,
    volt_ref,
    inject_ref,
    gain_ref,
    net_ref,
    count_ref,
    tile_ref,
    node_ref,
    weight_ref,
    driver_ref,
    rest_ref,
    gains_ref,
    take_ref,
    put_ref,
    scale_ref,
    picked_ref,
):
    picked_ref[...] = jnp.broadcast_to(
        to_column(driver_ref[...].astype(jnp.float32)), picked_ref.shape
    )
    tiles, nodes = conduct_ref.shape[0], conduct_ref.shape[1]
    for t in range(tiles):
        rest_ref[t] = inject_ref[t] - dot(conduct_ref[t], volt_ref[t])
    lane = iota((edge, nodes), 1)
    table = jnp.zeros((edge, nodes), jnp.float32)
    gains_ref[edge:] = jnp.zeros((8, nodes), jnp.float32)
    for side in range(2):
        for t in range(tiles):
            i = side * tiles + t
            gain = gain_ref[t, side : side + 1]
            table = jnp.where(lane == i, to_column(gain), table)
            gains_ref[edge : edge + 1, i * edge : (i + 1) * edge] = gain
    gains_ref[:edge] = table

    sources, slots = net_ref.shape
    mine = lax.axis_index("col")
    block = iota((sources, slots), 0) ^ mine
    place = slot_column((block * nets + net_ref[...]).astype(jnp.float32))
    target = slot_column((tile_ref[...] * nodes + node_ref[...]).astype(jnp.float32))
    live = source_column(count_ref[...].astype(jnp.float32), slots)
    slot = (iota(live.shape, 0) % slots).astype(jnp.float32)
    weight = jnp.where(slot < live, slot_column(weight_ref[...]), 0.0)
    take = jnp.where(place == iota(take_ref.shape, 1).astype(jnp.float32), 1.0, 0.0)
    put = jnp.where(target == iota(put_ref.shape, 1).astype(jnp.float32), 1.0, 0.0)
    take_ref[...] = take.astype(jnp.bfloat16)
    put_ref[...] = put.astype(jnp.bfloat16)
    scale_ref[...] = jnp.broadcast_to(weight, scale_ref.shape)


def tile_kernel(edge, eye_ref, conduct_ref, cap_ref, after_ref, inverse_ref, fold_ref, sum_ref, power_ref):
    tiles, nodes = conduct_ref.shape[0], conduct_ref.shape[1]
    eye = eye_ref[...]
    sums, powers, scales = [], [], []
    for t in range(tiles):
        conduct = conduct_ref[t]
        diagonal = (conduct + cap_ref[t : t + 1, :]) * eye
        down = jnp.sum(diagonal, axis=1, keepdims=True)
        across = jnp.sum(diagonal, axis=0, keepdims=True)
        power = (conduct * eye - conduct) / down
        sums.append(eye + power)
        powers.append(dot(power, power))
        scales.append(1.0 / across)

    def step(sums, powers):
        out_sums, out_powers, largest = [], [], jnp.float32(0.0)
        for total, power in zip(sums, powers):
            both = dot(jnp.concatenate([total, power], axis=0), power)
            out_sums.append(total + both[:nodes])
            out_powers.append(both[nodes:])
            largest = jnp.maximum(largest, jnp.max(jnp.sum(power, axis=1)))
        return out_sums, out_powers, largest

    for _ in range(DOUBLINGS):
        sums, powers, largest = step(sums, powers)
    for t in range(tiles):
        sum_ref[t], power_ref[t] = sums[t], powers[t]

    def again(carry):
        sums, powers, largest = step(
            [sum_ref[t] for t in range(tiles)], [power_ref[t] for t in range(tiles)]
        )
        for t in range(tiles):
            sum_ref[t], power_ref[t] = sums[t], powers[t]
        return largest, carry[1] + 1

    lax.while_loop(
        lambda carry: (carry[0] > SMALL) & (carry[1] < 40), again, (largest, jnp.int32(0))
    )
    parts = nodes // edge
    depth = edge // parts
    lane = iota((depth, nodes), 1)
    for t in range(tiles):
        inverse = sum_ref[t] * scales[t]
        inverse_ref[t] = inverse
        fold = jnp.zeros((depth, nodes), jnp.float32)
        for j in range(parts):
            piece = jnp.where(lane < edge, inverse[j * depth : (j + 1) * depth], 0.0)
            fold = fold + (pltpu.roll(piece, j * edge, 1) if j else piece)
        fold_ref[t * depth : (t + 1) * depth] = fold


def residual_kernel(
    nets,
    edge,
    cols,
    volt_ref,
    mate_ref,
    mate_gain_ref,
    inverse_ref,
    fold_ref,
    rest_ref,
    gains_ref,
    take_ref,
    put_ref,
    scale_ref,
    *refs,
):
    *group_refs, message_ref, precond_ref = refs
    tiles, nodes, patterns = volt_ref.shape
    mine = lax.axis_index("col")
    odd = mine % 2 == 1
    stride = 2 * nets + edge + 8
    blocks = [(ref, base) for ref in group_refs for base in range(0, ref.shape[0], stride)]
    values = sum(
        select(take_ref[:, j * 2 * nets : (j + 1) * 2 * nets], ref[base : base + 2 * nets])
        for j, (ref, base) in enumerate(blocks)
    )
    values = values * scale_ref[...]
    beyond = lax.rem(jnp.where(odd, mine + 1, mine + cols - 1), cols) ^ 1
    which = (mine ^ beyond) // 2
    outer = jnp.zeros((edge + 8, patterns), jnp.float32)
    for j, (ref, base) in enumerate(blocks):
        outer = jnp.where(which == j, ref[base + 2 * nets : base + stride], outer)
    inner = jnp.where(odd, mate_ref[tiles - 1, :edge], mate_ref[0, :edge])
    inner_gain = to_column(mate_gain_ref[tiles - 1, 0:1])
    has_west = jnp.where(mine > 0, 1.0, 0.0)
    has_east = jnp.where(mine < cols - 1, 1.0, 0.0)
    west = jnp.where(odd, inner, outer[:edge]) * has_west
    east = jnp.where(odd, outer[:edge], inner) * has_east
    west_gain = jnp.where(odd, inner_gain, to_column(outer[edge : edge + 1, :edge])) * has_west
    gains = [west_gain] + [gains_ref[:edge, t : t + 1] for t in range(tiles)]
    rims = [west] + [volt_ref[t, :edge] for t in range(tiles)] + [east]
    flows = [gains[t] * (rims[t] - rims[t + 1]) for t in range(tiles + 1)]
    first = jnp.zeros((1, patterns), jnp.float32)
    high, low = split(values)
    for t in range(tiles):
        put = put_ref[:, t * nodes : (t + 1) * nodes]
        injected = sum(
            lax.dot_general(
                put, part, (((0,), (0,)), ((), ())), preferred_element_type=jnp.float32
            )
            for part in (high, low)
        )
        residual = rest_ref[t] + injected
        residual = jnp.concatenate(
            [residual[:edge] - (flows[t + 1] - flows[t]), residual[edge:]], axis=0
        )
        precond = dot3(inverse_ref[t], residual)
        precond_ref[t] = precond
        first = first + jnp.sum(residual * precond, axis=0, keepdims=True)
        message_ref[t * edge : (t + 1) * edge] = precond[:edge]
        message_ref[(tiles + t) * edge : (tiles + t + 1) * edge] = volt_ref[t, :edge]
    base = 2 * tiles * edge
    depth = fold_ref.shape[0]
    message_ref[base : base + depth] = fold_ref[...]
    message_ref[base + depth : base + depth + 8] = gains_ref[edge:]
    message_ref[base + depth + 1 : base + depth + 2] = first


def corners(fold, tiles, edge):
    depth, lanes = fold.shape[0] // tiles, fold.shape[1]
    lane = iota((depth, lanes), 1)
    rows = []
    for t in range(tiles):
        piece = fold[t * depth : (t + 1) * depth]
        for j in range(lanes // edge):
            turn = (t - j) * edge % lanes
            turned = pltpu.roll(piece, turn, 1) if turn else piece
            rows.append(jnp.where((lane >= t * edge) & (lane < (t + 1) * edge), turned, 0.0))
    return jnp.concatenate(rows, axis=0)[:, : tiles * edge]


def turned(rows):
    count, lanes = rows.shape
    full = jnp.concatenate([rows, jnp.zeros((lanes - count, lanes), jnp.float32)], axis=0)
    return jnp.transpose(full)


def row_masks(rows):
    place = lax.axis_index("row")
    index = [lax.rem(place + k, rows) for k in range(rows)]
    not_first = [jnp.where(i > 0, 1.0, 0.0) for i in index]
    not_last = [jnp.where(i < rows - 1, 1.0, 0.0) for i in index]
    return not_first, not_last


def rim_kernel(rows, tiles, edge, depth, *refs):
    column_refs, (message_ref, far_ref, flow_ref, first_ref) = refs[:rows], refs[rows:]
    patterns = message_ref.shape[1]
    span = tiles * edge
    not_first, not_last = row_masks(rows)
    start = [ref[span : 2 * span] for ref in column_refs]
    folds = [ref[2 * span : 2 * span + depth] for ref in column_refs]
    base = 2 * span + depth
    gains = jnp.concatenate([ref[base : base + 1] for ref in column_refs], axis=0)
    columns = turned(gains)
    first = sum(ref[base + 1 : base + 2] for ref in column_refs)
    south = [
        columns[span : 2 * span, k : k + 1] * (start[k] - start[(k + 1) % rows] * not_last[k])
        for k in range(rows)
    ]
    dropped = jnp.zeros((span, patterns), jnp.float32)
    stride = span + depth
    for k in range(rows):
        flow = south[k] - south[k - 1] * not_first[k]
        raw = column_refs[k][:span]
        rim = raw - dot3(corners(folds[k], tiles, edge), flow)
        dropped = dropped + flow * (raw + rim)
        message_ref[k * stride : k * stride + span] = rim
        message_ref[k * stride + span : (k + 1) * stride] = folds[k]
        far_ref[k * edge : (k + 1) * edge] = rim[:edge]
        if k == 0:
            flow_ref[...] = flow
    message_ref[rows * stride : rows * stride + rows] = gains
    if message_ref.shape[0] > rows * stride + rows:
        rest_rows = message_ref.shape[0] - rows * stride - rows
        message_ref[rows * stride + rows :] = jnp.zeros((rest_rows, patterns), jnp.float32)
    first = first - jnp.sum(dropped, axis=0, keepdims=True)
    first_ref[...] = jnp.broadcast_to(first, first_ref.shape)


def moment_kernel(
    rows,
    cols,
    tiles,
    edge,
    depth,
    own_ref,
    inner_ref,
    outer_ref,
    far_ref,
    first_ref,
    moment_ref,
    t0_ref,
    t1_ref,
):
    patterns = own_ref.shape[1]
    mine = lax.axis_index("col")
    odd = mine % 2 == 1
    has_west = jnp.where(mine > 0, 1.0, 0.0)
    has_east = jnp.where(mine < cols - 1, 1.0, 0.0)
    has_far = jnp.where(mine < cols - 2, 1.0, 0.0)
    not_first, not_last = row_masks(rows)
    span = tiles * edge
    stride = span + depth

    def sides(piece):
        west = jnp.where(odd, inner_ref[piece], outer_ref[piece]) * has_west
        east = jnp.where(odd, outer_ref[piece], inner_ref[piece]) * has_east
        return west, own_ref[piece], east

    gains = [turned(block) for block in sides(slice(rows * stride, None))]
    easts, souths, u0, mats = [], [], [], []
    for k in range(rows):
        blocks = sides(slice(k * stride, (k + 1) * stride))
        far = far_ref[k * edge : (k + 1) * edge] * has_far
        u0.append(
            [block[t * edge : (t + 1) * edge] for block in blocks for t in range(tiles)] + [far]
        )

        def gain(columns, base):
            return jnp.broadcast_to(columns[base : base + edge, k : k + 1], (edge, patterns))

        easts.append([gain(g, t * edge) for g in gains for t in range(tiles)])
        souths.append([gain(g, span + t * edge) for g in gains for t in range(tiles)])
        mats.append([corners(block[span:], tiles, edge) for block in blocks])

    def net_flow(rims, low, high):
        flows = []
        for k in range(rows):
            below, above = (k + 1) % rows, k - 1
            row = []
            for c in range(low, high):
                flow = easts[k][c] * (rims[k][c] - rims[k][c + 1])
                flow = flow - easts[k][c - 1] * (rims[k][c - 1] - rims[k][c])
                flow = flow + souths[k][c] * (rims[k][c] - rims[below][c] * not_last[k])
                back = souths[above][c] * (rims[k][c] - rims[above][c])
                row.append(flow + back * not_first[k])
            flows.append([None] * low + row)
        return flows

    def spread(flows, devices, low, high):
        out = []
        for k in range(rows):
            row = []
            for d in devices:
                block = [
                    flows[k][c] if low <= c < high else jnp.zeros((edge, patterns), jnp.float32)
                    for c in range(d * tiles, (d + 1) * tiles)
                ]
                block = dot3(mats[k][d], jnp.concatenate(block, axis=0))
                row += [block[t * edge : (t + 1) * edge] for t in range(tiles)]
            out.append([None] * (devices[0] * tiles) + row)
        return out

    t0 = net_flow(u0, tiles - 1, 3 * tiles)
    u1 = spread(t0, [0, 1, 2], tiles - 1, 3 * tiles)
    t1 = net_flow(u1, tiles, 2 * tiles + 1)
    u2 = spread(t1, [1, 2], tiles, 2 * tiles + 1)
    zero = jnp.zeros((edge, patterns), jnp.float32)
    sums = [zero] * 5
    for k in range(rows):
        for c in range(tiles, 2 * tiles):
            ahead = u2[k][c] - u2[k][c + 1]
            drop = u2[k][c] - u2[(k + 1) % rows][c] * not_last[k]
            parts = (
                u0[k][c] * t0[k][c],
                u1[k][c] * t0[k][c],
                u1[k][c] * t1[k][c],
                u2[k][c] * t1[k][c],
                easts[k][c] * ahead * ahead + souths[k][c] * drop * drop,
            )
            sums = [total + part for total, part in zip(sums, parts)]
    moment_ref[0:1] = first_ref[0:1]
    for i, total in enumerate(sums):
        moment_ref[i + 1 : i + 2] = jnp.sum(total, axis=0, keepdims=True)
    moment_ref[6:8] = jnp.zeros((2, patterns), jnp.float32)
    t0_ref[...] = jnp.concatenate(t0[0][tiles : 2 * tiles], axis=0)
    t1_ref[...] = jnp.concatenate(t1[0][tiles : 2 * tiles], axis=0)


def direction_kernel(edge, precond_ref, inverse_ref, flow_ref, t0_ref, t1_ref, *out_refs):
    for t in range(precond_ref.shape[0]):
        rim = slice(t * edge, (t + 1) * edge)
        flows = jnp.concatenate([flow_ref[rim], t0_ref[rim], t1_ref[rim]], axis=1)
        spread = dot3(inverse_ref[t, :, :edge], flows)
        width = spread.shape[1] // 3
        out_refs[0][t] = precond_ref[t] - spread[:, :width]
        out_refs[1][t] = spread[:, width : 2 * width]
        out_refs[2][t] = spread[:, 2 * width :]


def final_kernel(volt_ref, z0_ref, z1_ref, z2_ref, *refs):
    *sum_refs, out_ref = refs
    tiles = volt_ref.shape[0]
    sums = sum(ref[...] for ref in sum_refs)
    m = [sums[i : i + 1] for i in range(6)]
    a00, a01, a02 = m[0] + m[1], m[1] + m[2], m[2] + m[3]
    a12, a22 = m[3] + m[4], m[4] + m[5]
    l1, l2 = a01 / a00, a02 / a00
    d1 = a02 - l1 * a01
    e12 = a12 - l2 * a01
    l12 = e12 / d1
    d2 = a22 - l2 * a02 - l12 * e12
    y1 = m[1] - l1 * m[0]
    y2 = m[2] - l2 * m[0] - l12 * y1
    c2 = y2 / d2
    c1 = y1 / d1 - l12 * c2
    c0 = m[0] / a00 - l1 * c1 - l2 * c2
    for t in range(tiles):
        out_ref[t] = volt_ref[t] + c0 * z0_ref[t] + c1 * z1_ref[t] + c2 * z2_ref[t]


def other(block, axis, count, distance):
    return lax.ppermute(block, axis, [(i, i ^ distance) for i in range(count)])


def stages(count, held):
    while held < count:
        reach = 2 if (count // held).bit_length() % 2 == 0 else 4
        yield [held * k for k in range(1, reach)]
        held *= reach


def outer_swap(block, axis, count):
    pairs = [(i, (i + 1) % count if i % 2 else (i - 1) % count) for i in range(count)]
    return lax.ppermute(block, axis, pairs)


def local(
    initial_voltage,
    inject,
    conduct,
    capacitance,
    track_gain,
    driver_tile,
    sink_net,
    sink_count,
    sink_tile,
    sink_node,
    sink_gain,
):
    rows, cols = lax.axis_size("row"), lax.axis_size("col")
    tiles, nodes, patterns = initial_voltage.shape[1:]
    edge, nets = track_gain.shape[-1], driver_tile.shape[-1]
    slots = cols * sink_net.shape[-1]
    voltage = initial_voltage[0]
    field = (tiles, nodes, patterns)
    span = tiles * edge

    mate = other(initial_voltage, "col", cols, 1)[0]
    mate_driver = other(driver_tile, "col", cols, 1)[0]
    mate_gain = other(track_gain, "col", cols, 1)[0]
    eye = run(eye_kernel, [(nodes, nodes)])[0]
    narrow_type = functools.partial(jax.ShapeDtypeStruct, dtype=jnp.bfloat16)
    rest, gains, take, put, scale, picked = run(
        functools.partial(sink_kernel, nets, edge),
        [
            field,
            (edge + 8, patterns),
            narrow_type((slots, cols * nets)),
            narrow_type((slots, tiles * nodes)),
            (slots, patterns),
            (nets, patterns),
        ],
        conduct[0],
        voltage,
        inject[0],
        track_gain[0],
        sink_net[0, 0],
        sink_count[0],
        sink_tile[0, 0],
        sink_node[0, 0],
        sink_gain[0, 0],
        driver_tile[0],
    )
    pair = run(
        functools.partial(pair_kernel, nets, edge),
        [(2 * nets + edge + 8, patterns)],
        voltage,
        picked,
        mate,
        mate_driver,
        mate_gain,
    )[0]
    groups = [pair]
    for distances in stages(cols, 2):
        whole = groups[0] if len(groups) == 1 else jnp.concatenate(groups)
        groups = [whole] + [other(whole, "col", cols, d) for d in distances]
    depth = tiles * edge * edge // nodes
    inverse, fold = run(
        functools.partial(tile_kernel, edge),
        [field, (depth, nodes)],
        eye,
        conduct[0],
        capacitance[0],
        pair,
        scratch=[pltpu.VMEM(field, jnp.float32)] * 2,
    )

    message, precond = run(
        functools.partial(residual_kernel, nets, edge, cols),
        [(2 * span + depth + 8, patterns), field],
        voltage,
        mate,
        mate_gain,
        inverse,
        fold,
        rest,
        gains,
        take,
        put,
        scale,
        *groups,
    )

    column = [message] + [
        lax.ppermute(message, "row", [((i + k) % rows, i) for i in range(rows)])
        for k in range(1, rows)
    ]
    height = rows * (span + depth) + -(-rows // 8) * 8
    message, far, flow, first = run(
        functools.partial(rim_kernel, rows, tiles, edge, depth),
        [(height, patterns), (rows * edge, patterns), (span, patterns), (8, patterns)],
        *column,
    )

    inner = other(message, "col", cols, 1)
    beyond = outer_swap(message, "col", cols)
    far = lax.ppermute(far, "col", [((i + 2) % cols, i) for i in range(cols)])
    moments, t0, t1 = run(
        functools.partial(moment_kernel, rows, cols, tiles, edge, depth),
        [(8, patterns), (span, patterns), (span, patterns)],
        message,
        inner,
        beyond,
        far,
        first,
    )

    sums = [moments]
    for distances in stages(cols, 1):
        moments = sum(sums[1:], sums[0])
        sums = [moments] + [other(moments, "col", cols, d) for d in distances]
    directions = run(
        functools.partial(direction_kernel, edge), [field] * 3, precond, inverse, flow, t0, t1
    )
    return run(final_kernel, [field], voltage, *directions, *sums)[0][None]


def solution(mesh):
    whole = P("row", "col", None, None)
    third = P("row", "col", None)
    placed = (whole, whole, whole, third, whole, third, whole, third, whole, whole, whole)
    return jax.shard_map(local, mesh=mesh, in_specs=placed, out_specs=whole, check_vma=False)
```

time: 42.2 us -> 39.5 us (0.936)
  waiting for transfers between devices: 16.1 us -> 14.4 us
  local copies, waits for them, and re-layouts: 2.29 us -> 0.69 us
    unnamed x24 -> x22, local copies, waits for them, and re-layouts: 2.29 us -> 0.69 us
    ppermute x9 -> x11, starting transfers between devices: 10.3 us -> 11.2 us  [other(): return lax.ppermute(block, axis, [(i, i ^ distance) for i in range(count)])]
    ppermute x1, waiting for transfers between devices: 4.98 us -> 4.18 us  [local(): far = lax.ppermute(far, 'col', [((i + 2) % cols, i) for i in range(cols)])]
    ppermute x1, starting transfers between devices: 0.87 us -> 0.07 us  [outer_swap(): return lax.ppermute(block, axis, pairs)]
    ppermute x9 -> x11, waiting for transfers between devices: 6.63 us -> 5.86 us  [other(): return lax.ppermute(block, axis, [(i, i ^ distance) for i in range(count)])]
    pallas_call x7 -> x9, Pallas kernels: 5.83 us -> 5.9 us  [run(): pl.pallas_call(kernel, out_shape=shapes, in_specs=[vmem] * len(args), out...]
  transfers between devices with their start and end apart: 14 -> 16, of which waited for: 10 -> 12; matrix products, arithmetic and copies ran while one was open for 0% -> 0% of each run, Pallas kernels for 5% -> 7%
where the time goes in v4:
time: 39.5 us; the launch traced here: 39.3 us
  starting transfers between devices  18.2 us (46%)
  waiting for transfers between devices  14.4 us (36%)
  Pallas kernels  5.9 us (15%)
  local copies, waits for them, and re-layouts  0.69 us (2%)
    ppermute x11, starting transfers between devices, other(): return lax.ppermute(block, axis, [(i, i ^ distance) for i in range(count)])  11.2 us
    pallas_call x9, Pallas kernels, run(): pl.pallas_call(kernel, out_shape=shapes, in_specs=[vmem] * len(args), out...  5.9 us
    ppermute x11, waiting for transfers between devices, other(): return lax.ppermute(block, axis, [(i, i ^ distance) for i in range(count)])  5.86 us
    ppermute x3, starting transfers between devices, local(): lax.ppermute(message, 'row', [((i + k) % rows, i) for i in range(rows)])  5.57 us
    ppermute x1, waiting for transfers between devices, local(): far = lax.ppermute(far, 'col', [((i + 2) % cols, i) for i in range(cols)])  4.18 us
    ppermute x3, waiting for transfers between devices, local(): lax.ppermute(message, 'row', [((i + k) % rows, i) for i in range(rows)])  4.08 us
    ppermute x1, starting transfers between devices, local(): far = lax.ppermute(far, 'col', [((i + 2) % cols, i) for i in range(cols)])  1.35 us
  transfers between devices with their start and end apart: 16, of which 12 were waited for; matrix products, arithmetic and copies ran while one was open for 0% of the time, Pallas kernels for 7%

profile of v4, /device:TPU:0, one launch (start us, length us, event | category | flops | bytes accessed | tf_op | source)
XLA Modules:
  0.0 39.3 jit_solution(15948105820624872146)
XLA Ops:
  0.0 0.5 %collective-permute-start.2 = (s32[1,1,64]{2,1,0:T(1,128)}, s32[1,1,64]{2,1,0:T(1,128)S(1)}, u32[]{:S(2)}, u32[]{:S(2)}) collective-permute-start(s32[1,1,64]{2,1,0:T(1,128)} %param.16), channel_id=1, source_target_pairs={{0,1},{1,0},{2,3},{3,2},{4,5},{5,4},{6,7},{7,6},{8,9},{9,8},{10,11... | collective-permute-start | bytes 776 | tf_op jit(solution)/shard_map/ppermute | solution.py:474
  0.5 0.1 collective-permute-start.1
  0.6 0.4 %collective-permute-start = (f32[1,2,128,128]{3,2,1,0:T(8,128)}, f32[1,2,128,128]{3,2,1,0:T(8,128)S(1)}, u32[]{:S(2)}, u32[]{:S(2)}) collective-permute-start(f32[1,2,128,128]{3,2,1,0:T(8,128)} %param.11), channel_id=1, source_target_pairs={{0,1},{1,0},{2,3},{3,2},{4,5},{5,4},{6,7},{7,6},{8,9},{9,8},{10,11... | collective-permute-start | bytes 393224 | tf_op jit(solution)/shard_map/ppermute | solution.py:474
  1.1 0.0 copy-start.4
  1.1 0.0 copy-start.3
  1.1 0.0 copy-start.9
  1.1 0.0 copy-start.10
  1.1 0.6 %copy-done.5 = s32[1,1,8,8]{3,2,1,0:T(8,128)S(1)} copy-done((s32[1,1,8,8]{3,2,1,0:T(8,128)S(1)}, s32[1,1,8,8]{3,2,1,0:T(8,128)}, u32[]{:S(2)}) %copy-start.5) | copy-done | bytes 280
  1.7 0.0 copy-done.6
  1.7 0.0 copy-done.7
  1.8 0.0 copy-done.4
  1.8 0.0 copy-done.3
  1.8 0.3 shard_map.110
  2.1 0.0 collective-permute-done.2
  2.1 0.1 collective-permute-done
  2.2 0.1 shard_map.111.after_ref.refs_0_
  2.3 3.9 %collective-permute-start.5 = (f32[168,128]{1,0:T(8,128)S(1)}, f32[168,128]{1,0:T(8,128)S(1)}, u32[]{:S(2)}, u32[]{:S(2)}) collective-permute-start(f32[168,128]{1,0:T(8,128)S(1)} %shard_map.111.after_ref.refs_0_), channel_id=1, source_target_pairs={{0,6},{1,7},{2,4},{3,5},{4,2},{5,3},{6,0},{7,1},{8,14},{9,15},{10,... | collective-permute-start | bytes 258056 | tf_op jit(solution)/shard_map/ppermute | solution.py:474
  6.2 0.5 %collective-permute-start.4 = (f32[168,128]{1,0:T(8,128)S(1)}, f32[168,128]{1,0:T(8,128)S(1)}, u32[]{:S(2)}, u32[]{:S(2)}) collective-permute-start(f32[168,128]{1,0:T(8,128)S(1)} %shard_map.111.after_ref.refs_0_), channel_id=1, source_target_pairs={{0,4},{1,5},{2,6},{3,7},{4,0},{5,1},{6,2},{7,3},{8,12},{9,13},{10,... | collective-permute-start | bytes 258056 | tf_op jit(solution)/shard_map/ppermute | solution.py:474
  6.7 0.1 collective-permute-start.3
  6.8 2.2 %shard_map.112 = (f32[2,128,128]{2,1,0:T(8,128)S(1)}, f32[16,128]{1,0:T(8,128)S(1)}) custom-call(f32[128,128]{1,0:T(8,128)S(1)} %shard_map.109.eye_ref, f32[2,128,128]{2,1,0:T(8,128)S(1)} %bitcast.17, f32[2,128]{1,0:T(2,128)S(1)} %bitcast.31, f32[168,128]{1,0:T(8,128)S(1)} %shard_map.111.after_ref.refs_0_), custom_call_target="tpu_custom_call" | custom-call | flops 4000000000 | bytes 422912 | tf_op jit(solution)/shard_map/pallas_call | solution.py:49
  9.1 0.1 collective-permute-done.5.refs_3_
  9.1 1.7 %collective-permute-done.4.refs_2_ = f32[168,128]{1,0:T(8,128)S(1)} collective-permute-done((f32[168,128]{1,0:T(8,128)S(1)}, f32[168,128]{1,0:T(8,128)S(1)}, u32[]{:S(2)}, u32[]{:S(2)}) %collective-permute-start.4) | collective-permute-done | bytes 86048 | tf_op jit(solution)/shard_map/ppermute | solution.py:474
  10.9 0.3 collective-permute-done.3.refs_1_
  11.2 0.9 %shard_map.113 = (f32[152,128]{1,0:T(8,128)S(1)}, f32[2,128,128]{2,1,0:T(8,128)S(1)}) custom-call(f32[2,128,128]{2,1,0:T(8,128)S(1)} %bitcast.20, f32[2,128,128]{2,1,0:T(8,128)S(1)} %bitcast.23, f32[2,2,32]{2,1,0:T(2,128)S(1)} %bitcast.30, f32[2,128,128]{2,1,0:T(8,128)S(1)} %get-tuple-element.26.inverse_ref, f32[16,128]{1,0:T(8,128)S(1)} %get-tuple-element.27.fold_ref, ...), custom_call_target="tpu_custom_call" | custom-call | flops 4000000000 | bytes 1335808 | tf_op jit(solution)/shard_map/pallas_call | solution.py:49
  12.1 1.6 %collective-permute-start.8 = (f32[152,128]{1,0:T(8,128)S(1)}, f32[152,128]{1,0:T(8,128)S(1)}, u32[]{:S(2)}, u32[]{:S(2)}) collective-permute-start(f32[152,128]{1,0:T(8,128)S(1)} %get-tuple-element.34.refs_0_), channel_id=1, source_target_pairs={{24,0},{0,8},{8,16},{16,24},{25,1},{1,9},{9,17},{17,25},{26,2},{2,... | collective-permute-start | bytes 233480 | tf_op jit(solution)/shard_map/ppermute | solution.py:577
  13.7 2.6 %collective-permute-start.7 = (f32[152,128]{1,0:T(8,128)S(1)}, f32[152,128]{1,0:T(8,128)S(1)}, u32[]{:S(2)}, u32[]{:S(2)}) collective-permute-start(f32[152,128]{1,0:T(8,128)S(1)} %get-tuple-element.34.refs_0_), channel_id=1, source_target_pairs={{16,0},{24,8},{0,16},{8,24},{17,1},{25,9},{1,17},{9,25},{18,2},{26... | collective-permute-start | bytes 233480 | tf_op jit(solution)/shard_map/ppermute | solution.py:577
  16.3 1.3 %collective-permute-start.6 = (f32[152,128]{1,0:T(8,128)S(1)}, f32[152,128]{1,0:T(8,128)S(1)}, u32[]{:S(2)}, u32[]{:S(2)}) collective-permute-start(f32[152,128]{1,0:T(8,128)S(1)} %get-tuple-element.34.refs_0_), channel_id=1, source_target_pairs={{8,0},{16,8},{24,16},{0,24},{9,1},{17,9},{25,17},{1,25},{10,2},{18... | collective-permute-start | bytes 233480 | tf_op jit(solution)/shard_map/ppermute | solution.py:577
  17.6 1.7 %collective-permute-done.8.refs_3_ = f32[152,128]{1,0:T(8,128)S(1)} collective-permute-done((f32[152,128]{1,0:T(8,128)S(1)}, f32[152,128]{1,0:T(8,128)S(1)}, u32[]{:S(2)}, u32[]{:S(2)}) %collective-permute-start.8) | collective-permute-done | bytes 77856 | tf_op jit(solution)/shard_map/ppermute | solution.py:577
  19.3 2.4 %collective-permute-done.7.refs_2_ = f32[152,128]{1,0:T(8,128)S(1)} collective-permute-done((f32[152,128]{1,0:T(8,128)S(1)}, f32[152,128]{1,0:T(8,128)S(1)}, u32[]{:S(2)}, u32[]{:S(2)}) %collective-permute-start.7) | collective-permute-done | bytes 77856 | tf_op jit(solution)/shard_map/ppermute | solution.py:577
  21.7 0.0 collective-permute-done.6.refs_1_
  21.7 0.4 %shard_map.114 = (f32[328,128]{1,0:T(8,128)S(1)}, f32[128,128]{1,0:T(8,128)S(1)}, f32[64,128]{1,0:T(8,128)S(1)}, f32[8,128]{1,0:T(8,128)S(1)}) custom-call(f32[152,128]{1,0:T(8,128)S(1)} %get-tuple-element.34.refs_0_, f32[152,128]{1,0:T(8,128)S(1)} %collective-permute-done.6.refs_1_, f32[152,128]{1,0:T(8,128)S(1)} %collective-permute-done.7.refs_2_, ...), custom_call_target="tpu_custom_call" | custom-call | flops 4000000000 | bytes 581632 | tf_op jit(solution)/shard_map/pallas_call | solution.py:49
  22.1 0.1 collective-permute-start.10
  22.2 1.7 %collective-permute-start.9 = (f32[328,128]{1,0:T(8,128)S(1)}, f32[328,128]{1,0:T(8,128)S(1)}, u32[]{:S(2)}, u32[]{:S(2)}) collective-permute-start(f32[328,128]{1,0:T(8,128)S(1)} %get-tuple-element.36.own_ref), channel_id=1, source_target_pairs={{0,1},{1,0},{2,3},{3,2},{4,5},{5,4},{6,7},{7,6},{8,9},{9,8},{10,11... | collective-permute-start | bytes 503816 | tf_op jit(solution)/shard_map/ppermute | solution.py:474
  23.9 1.4 %collective-permute-start.11 = (f32[128,128]{1,0:T(8,128)S(1)}, f32[128,128]{1,0:T(8,128)S(1)}, u32[]{:S(2)}, u32[]{:S(2)}) collective-permute-start(f32[128,128]{1,0:T(8,128)S(1)} %get-tuple-element.37), channel_id=1, source_target_pairs={{2,0},{3,1},{4,2},{5,3},{6,4},{7,5},{0,6},{1,7},{10,8},{11,9},{12,... | collective-permute-start | bytes 196616 | tf_op jit(solution)/shard_map/ppermute | solution.py:589
  25.2 4.2 %collective-permute-done.11.far_ref = f32[128,128]{1,0:T(8,128)S(1)} collective-permute-done((f32[128,128]{1,0:T(8,128)S(1)}, f32[128,128]{1,0:T(8,128)S(1)}, u32[]{:S(2)}, u32[]{:S(2)}) %collective-permute-start.11) | collective-permute-done | bytes 65568 | tf_op jit(solution)/shard_map/ppermute | solution.py:589
  29.4 0.3 collective-permute-done.10.outer_ref
  29.7 0.0 collective-permute-done.9.inner_ref
  29.7 1.0 %shard_map.115 = (f32[8,128]{1,0:T(8,128)S(1)}, f32[64,128]{1,0:T(8,128)S(1)}, f32[64,128]{1,0:T(8,128)S(1)}) custom-call(f32[328,128]{1,0:T(8,128)S(1)} %get-tuple-element.36.own_ref, f32[328,128]{1,0:T(8,128)S(1)} %collective-permute-done.9.inner_ref, f32[328,128]{1,0:T(8,128)S(1)} %collective-permute-done.10.outer_ref, ...), custom_call_target="tpu_custom_call" | custom-call | flops 4000000000 | bytes 643072 | tf_op jit(solution)/shard_map/pallas_call | solution.py:49
  30.7 0.5 %collective-permute-start.12 = (f32[8,128]{1,0:T(8,128)S(1)}, f32[8,128]{1,0:T(8,128)S(1)}, u32[]{:S(2)}, u32[]{:S(2)}) collective-permute-start(f32[8,128]{1,0:T(8,128)S(1)} %get-tuple-element.44), channel_id=1, source_target_pairs={{0,1},{1,0},{2,3},{3,2},{4,5},{5,4},{6,7},{7,6},{8,9},{9,8},{10,11... | collective-permute-start | bytes 12296 | tf_op jit(solution)/shard_map/ppermute | solution.py:474
  31.2 0.8 %collective-permute-done.12 = f32[8,128]{1,0:T(8,128)S(1)} collective-permute-done((f32[8,128]{1,0:T(8,128)S(1)}, f32[8,128]{1,0:T(8,128)S(1)}, u32[]{:S(2)}, u32[]{:S(2)}) %collective-permute-start.12) | collective-permute-done | bytes 4128 | tf_op jit(solution)/shard_map/ppermute | solution.py:474
  32.0 1.4 %collective-permute-start.15 = (f32[8,128]{1,0:T(8,128)S(1)}, f32[8,128]{1,0:T(8,128)S(1)}, u32[]{:S(2)}, u32[]{:S(2)}) collective-permute-start(f32[8,128]{1,0:T(8,128)S(1)} %add.3.refs_0_), channel_id=1, source_target_pairs={{0,6},{1,7},{2,4},{3,5},{4,2},{5,3},{6,0},{7,1},{8,14},{9,15},{10,... | collective-permute-start | bytes 12296 | tf_op jit(solution)/shard_map/ppermute | solution.py:474
  33.4 1.6 %collective-permute-start.14 = (f32[8,128]{1,0:T(8,128)S(1)}, f32[8,128]{1,0:T(8,128)S(1)}, u32[]{:S(2)}, u32[]{:S(2)}) collective-permute-start(f32[8,128]{1,0:T(8,128)S(1)} %add.3.refs_0_), channel_id=1, source_target_pairs={{0,4},{1,5},{2,6},{3,7},{4,0},{5,1},{6,2},{7,3},{8,12},{9,13},{10,... | collective-permute-start | bytes 12296 | tf_op jit(solution)/shard_map/ppermute | solution.py:474
  35.0 0.5 %collective-permute-start.13 = (f32[8,128]{1,0:T(8,128)S(1)}, f32[8,128]{1,0:T(8,128)S(1)}, u32[]{:S(2)}, u32[]{:S(2)}) collective-permute-start(f32[8,128]{1,0:T(8,128)S(1)} %add.3.refs_0_), channel_id=1, source_target_pairs={{0,2},{1,3},{2,0},{3,1},{4,6},{5,7},{6,4},{7,5},{8,10},{9,11},{10,... | collective-permute-start | bytes 12296 | tf_op jit(solution)/shard_map/ppermute | solution.py:474
  35.5 0.3 shard_map.116
  35.8 0.7 %collective-permute-done.15.refs_3_ = f32[8,128]{1,0:T(8,128)S(1)} collective-permute-done((f32[8,128]{1,0:T(8,128)S(1)}, f32[8,128]{1,0:T(8,128)S(1)}, u32[]{:S(2)}, u32[]{:S(2)}) %collective-permute-start.15) | collective-permute-done | bytes 4128 | tf_op jit(solution)/shard_map/ppermute | solution.py:474
  36.5 0.5 %collective-permute-done.14.refs_2_ = f32[8,128]{1,0:T(8,128)S(1)} collective-permute-done((f32[8,128]{1,0:T(8,128)S(1)}, f32[8,128]{1,0:T(8,128)S(1)}, u32[]{:S(2)}, u32[]{:S(2)}) %collective-permute-start.14) | collective-permute-done | bytes 4128 | tf_op jit(solution)/shard_map/ppermute | solution.py:474
  37.0 1.6 %collective-permute-done.13.refs_1_ = f32[8,128]{1,0:T(8,128)S(1)} collective-permute-done((f32[8,128]{1,0:T(8,128)S(1)}, f32[8,128]{1,0:T(8,128)S(1)}, u32[]{:S(2)}, u32[]{:S(2)}) %collective-permute-start.13) | collective-permute-done | bytes 4128 | tf_op jit(solution)/shard_map/ppermute | solution.py:474
  38.6 0.7 %shard_map.117 = f32[2,128,128]{2,1,0:T(8,128)} custom-call(f32[2,128,128]{2,1,0:T(8,128)S(1)} %bitcast.21, f32[2,128,128]{2,1,0:T(8,128)S(1)} %get-tuple-element.41.z0_ref, f32[2,128,128]{2,1,0:T(8,128)S(1)} %get-tuple-element.42.z1_ref, f32[2,128,128]{2,1,0:T(8,128)S(1)} %get-tuple-element.43.z2_ref, f32[8,128]{1,0:T(8,128)S(1)} %add.3.refs_0_, ...), custom_call_target="tpu_custom_call" | custom-call | flops 4000000000 | bytes 671744 | tf_op jit(solution)/shard_map/pallas_call | solution.py:49
  (16 shorter events, 0.0 us)
Async XLA Ops:
  0.0 1.1 %copy-start.2 = (f32[1,2,128,128]{3,2,1,0:T(8,128)S(1)}, f32[1,2,128,128]{3,2,1,0:T(8,128)}, u32[]{:S(2)}) copy-start(f32[1,2,128,128]{3,2,1,0:T(8,128)} %param.11) | copy-start | bytes 393220
  0.0 1.1 %copy-start.1 = (f32[1,2,128,128]{3,2,1,0:T(8,128)S(1)}, f32[1,2,128,128]{3,2,1,0:T(8,128)}, u32[]{:S(2)}) copy-start(f32[1,2,128,128]{3,2,1,0:T(8,128)} %param.13) | copy-start | bytes 393220
  0.0 1.1 %copy-start = (f32[1,2,128,128]{3,2,1,0:T(8,128)S(1)}, f32[1,2,128,128]{3,2,1,0:T(8,128)}, u32[]{:S(2)}) copy-start(f32[1,2,128,128]{3,2,1,0:T(8,128)} %param.12) | copy-start | bytes 393220
  0.0 2.1 %collective-permute-start.2 = (s32[1,1,64]{2,1,0:T(1,128)}, s32[1,1,64]{2,1,0:T(1,128)S(1)}, u32[]{:S(2)}, u32[]{:S(2)}) collective-permute-start(s32[1,1,64]{2,1,0:T(1,128)} %param.16), channel_id=1, source_target_pairs={{0,1},{1,0},{2,3},{3,2},{4,5},{5,4},{6,7},{7,6},{8,9},{9,8},{10,11... | collective-permute-start | bytes 776 | tf_op jit(solution)/shard_map/ppermute | solution.py:474
  0.5 1.6 %collective-permute-start.1 = (f32[1,2,2,32]{3,2,1,0:T(2,128)}, f32[1,2,2,32]{3,2,1,0:T(2,128)S(1)}, u32[]{:S(2)}, u32[]{:S(2)}) collective-permute-start(f32[1,2,2,32]{3,2,1,0:T(2,128)} %param.15), channel_id=1, source_target_pairs={{0,1},{1,0},{2,3},{3,2},{4,5},{5,4},{6,7},{7,6},{8,9},{9,8},{10,11... | collective-permute-start | bytes 1544 | tf_op jit(solution)/shard_map/ppermute | solution.py:474
  0.6 1.6 %collective-permute-start = (f32[1,2,128,128]{3,2,1,0:T(8,128)}, f32[1,2,128,128]{3,2,1,0:T(8,128)S(1)}, u32[]{:S(2)}, u32[]{:S(2)}) collective-permute-start(f32[1,2,128,128]{3,2,1,0:T(8,128)} %param.11), channel_id=1, source_target_pairs={{0,1},{1,0},{2,3},{3,2},{4,5},{5,4},{6,7},{7,6},{8,9},{9,8},{10,11... | collective-permute-start | bytes 393224 | tf_op jit(solution)/shard_map/ppermute | solution.py:474
  1.0 0.7 %copy-start.5 = (s32[1,1,8,8]{3,2,1,0:T(8,128)S(1)}, s32[1,1,8,8]{3,2,1,0:T(8,128)}, u32[]{:S(2)}) copy-start(s32[1,1,8,8]{3,2,1,0:T(8,128)} %param.20) | copy-start | bytes 772
  1.0 0.7 %copy-start.6 = (f32[1,1,8,8]{3,2,1,0:T(8,128)S(1)}, f32[1,1,8,8]{3,2,1,0:T(8,128)}, u32[]{:S(2)}) copy-start(f32[1,1,8,8]{3,2,1,0:T(8,128)} %param.21) | copy-start | bytes 772
  1.0 0.7 %copy-start.7 = (f32[1,2,2,32]{3,2,1,0:T(2,128)S(1)}, f32[1,2,2,32]{3,2,1,0:T(2,128)}, u32[]{:S(2)}) copy-start(f32[1,2,2,32]{3,2,1,0:T(2,128)} %param.15) | copy-start | bytes 1540
  1.1 0.7 %copy-start.4 = (s32[1,1,8,8]{3,2,1,0:T(8,128)S(1)}, s32[1,1,8,8]{3,2,1,0:T(8,128)}, u32[]{:S(2)}) copy-start(s32[1,1,8,8]{3,2,1,0:T(8,128)} %param.19) | copy-start | bytes 772
  1.1 0.7 %copy-start.3 = (s32[1,1,8,8]{3,2,1,0:T(8,128)S(1)}, s32[1,1,8,8]{3,2,1,0:T(8,128)}, u32[]{:S(2)}) copy-start(s32[1,1,8,8]{3,2,1,0:T(8,128)} %param.17) | copy-start | bytes 772
  1.1 0.7 %copy-start.9 = (s32[1,1,8]{2,1,0:T(1,128)S(1)}, s32[1,1,8]{2,1,0:T(1,128)}, u32[]{:S(2)}) copy-start(s32[1,1,8]{2,1,0:T(1,128)} %param.18) | copy-start | bytes 100
  1.1 0.7 %copy-start.10 = (s32[1,1,64]{2,1,0:T(1,128)S(1)}, s32[1,1,64]{2,1,0:T(1,128)}, u32[]{:S(2)}) copy-start(s32[1,1,64]{2,1,0:T(1,128)} %param.16) | copy-start | bytes 772
  2.3 4.5 %copy-start.8 = (f32[1,2,128]{2,1,0:T(2,128)S(1)}, f32[1,2,128]{2,1,0:T(2,128)}, u32[]{:S(2)}) copy-start(f32[1,2,128]{2,1,0:T(2,128)} %param.14) | copy-start | bytes 3076
  2.3 6.8 %collective-permute-start.5 = (f32[168,128]{1,0:T(8,128)S(1)}, f32[168,128]{1,0:T(8,128)S(1)}, u32[]{:S(2)}, u32[]{:S(2)}) collective-permute-start(f32[168,128]{1,0:T(8,128)S(1)} %shard_map.111.after_ref.refs_0_), channel_id=1, source_target_pairs={{0,6},{1,7},{2,4},{3,5},{4,2},{5,3},{6,0},{7,1},{8,14},{9,15},{10,... | collective-permute-start | bytes 258056 | tf_op jit(solution)/shard_map/ppermute | solution.py:474
  6.2 4.7 %collective-permute-start.4 = (f32[168,128]{1,0:T(8,128)S(1)}, f32[168,128]{1,0:T(8,128)S(1)}, u32[]{:S(2)}, u32[]{:S(2)}) collective-permute-start(f32[168,128]{1,0:T(8,128)S(1)} %shard_map.111.after_ref.refs_0_), channel_id=1, source_target_pairs={{0,4},{1,5},{2,6},{3,7},{4,0},{5,1},{6,2},{7,3},{8,12},{9,13},{10,... | collective-permute-start | bytes 258056 | tf_op jit(solution)/shard_map/ppermute | solution.py:474
  6.7 4.5 %collective-permute-start.3 = (f32[168,128]{1,0:T(8,128)S(1)}, f32[168,128]{1,0:T(8,128)S(1)}, u32[]{:S(2)}, u32[]{:S(2)}) collective-permute-start(f32[168,128]{1,0:T(8,128)S(1)} %shard_map.111.after_ref.refs_0_), channel_id=1, source_target_pairs={{0,2},{1,3},{2,0},{3,1},{4,6},{5,7},{6,4},{7,5},{8,10},{9,11},{10,... | collective-permute-start | bytes 258056 | tf_op jit(solution)/shard_map/ppermute | solution.py:474
  12.1 7.2 %collective-permute-start.8 = (f32[152,128]{1,0:T(8,128)S(1)}, f32[152,128]{1,0:T(8,128)S(1)}, u32[]{:S(2)}, u32[]{:S(2)}) collective-permute-start(f32[152,128]{1,0:T(8,128)S(1)} %get-tuple-element.34.refs_0_), channel_id=1, source_target_pairs={{24,0},{0,8},{8,16},{16,24},{25,1},{1,9},{9,17},{17,25},{26,2},{2,... | collective-permute-start | bytes 233480 | tf_op jit(solution)/shard_map/ppermute | solution.py:577
  13.7 8.0 %collective-permute-start.7 = (f32[152,128]{1,0:T(8,128)S(1)}, f32[152,128]{1,0:T(8,128)S(1)}, u32[]{:S(2)}, u32[]{:S(2)}) collective-permute-start(f32[152,128]{1,0:T(8,128)S(1)} %get-tuple-element.34.refs_0_), channel_id=1, source_target_pairs={{16,0},{24,8},{0,16},{8,24},{17,1},{25,9},{1,17},{9,25},{18,2},{26... | collective-permute-start | bytes 233480 | tf_op jit(solution)/shard_map/ppermute | solution.py:577
  16.3 5.4 %collective-permute-start.6 = (f32[152,128]{1,0:T(8,128)S(1)}, f32[152,128]{1,0:T(8,128)S(1)}, u32[]{:S(2)}, u32[]{:S(2)}) collective-permute-start(f32[152,128]{1,0:T(8,128)S(1)} %get-tuple-element.34.refs_0_), channel_id=1, source_target_pairs={{8,0},{16,8},{24,16},{0,24},{9,1},{17,9},{25,17},{1,25},{10,2},{18... | collective-permute-start | bytes 233480 | tf_op jit(solution)/shard_map/ppermute | solution.py:577
  22.1 7.6 %collective-permute-start.10 = (f32[328,128]{1,0:T(8,128)S(1)}, f32[328,128]{1,0:T(8,128)S(1)}, u32[]{:S(2)}, u32[]{:S(2)}) collective-permute-start(f32[328,128]{1,0:T(8,128)S(1)} %get-tuple-element.36.own_ref), channel_id=1, source_target_pairs={{0,7},{1,2},{2,1},{3,4},{4,3},{5,6},{6,5},{7,0},{8,15},{9,10},{10,... | collective-permute-start | bytes 503816 | tf_op jit(solution)/shard_map/ppermute | solution.py:486
  22.2 7.5 %collective-permute-start.9 = (f32[328,128]{1,0:T(8,128)S(1)}, f32[328,128]{1,0:T(8,128)S(1)}, u32[]{:S(2)}, u32[]{:S(2)}) collective-permute-start(f32[328,128]{1,0:T(8,128)S(1)} %get-tuple-element.36.own_ref), channel_id=1, source_target_pairs={{0,1},{1,0},{2,3},{3,2},{4,5},{5,4},{6,7},{7,6},{8,9},{9,8},{10,11... | collective-permute-start | bytes 503816 | tf_op jit(solution)/shard_map/ppermute | solution.py:474
  23.9 5.5 %collective-permute-start.11 = (f32[128,128]{1,0:T(8,128)S(1)}, f32[128,128]{1,0:T(8,128)S(1)}, u32[]{:S(2)}, u32[]{:S(2)}) collective-permute-start(f32[128,128]{1,0:T(8,128)S(1)} %get-tuple-element.37), channel_id=1, source_target_pairs={{2,0},{3,1},{4,2},{5,3},{6,4},{7,5},{0,6},{1,7},{10,8},{11,9},{12,... | collective-permute-start | bytes 196616 | tf_op jit(solution)/shard_map/ppermute | solution.py:589
  30.7 1.3 %collective-permute-start.12 = (f32[8,128]{1,0:T(8,128)S(1)}, f32[8,128]{1,0:T(8,128)S(1)}, u32[]{:S(2)}, u32[]{:S(2)}) collective-permute-start(f32[8,128]{1,0:T(8,128)S(1)} %get-tuple-element.44), channel_id=1, source_target_pairs={{0,1},{1,0},{2,3},{3,2},{4,5},{5,4},{6,7},{7,6},{8,9},{9,8},{10,11... | collective-permute-start | bytes 12296 | tf_op jit(solution)/shard_map/ppermute | solution.py:474
  32.0 4.5 %collective-permute-start.15 = (f32[8,128]{1,0:T(8,128)S(1)}, f32[8,128]{1,0:T(8,128)S(1)}, u32[]{:S(2)}, u32[]{:S(2)}) collective-permute-start(f32[8,128]{1,0:T(8,128)S(1)} %add.3.refs_0_), channel_id=1, source_target_pairs={{0,6},{1,7},{2,4},{3,5},{4,2},{5,3},{6,0},{7,1},{8,14},{9,15},{10,... | collective-permute-start | bytes 12296 | tf_op jit(solution)/shard_map/ppermute | solution.py:474
  33.4 3.6 %collective-permute-start.14 = (f32[8,128]{1,0:T(8,128)S(1)}, f32[8,128]{1,0:T(8,128)S(1)}, u32[]{:S(2)}, u32[]{:S(2)}) collective-permute-start(f32[8,128]{1,0:T(8,128)S(1)} %add.3.refs_0_), channel_id=1, source_target_pairs={{0,4},{1,5},{2,6},{3,7},{4,0},{5,1},{6,2},{7,3},{8,12},{9,13},{10,... | collective-permute-start | bytes 12296 | tf_op jit(solution)/shard_map/ppermute | solution.py:474
  35.0 3.6 %collective-permute-start.13 = (f32[8,128]{1,0:T(8,128)S(1)}, f32[8,128]{1,0:T(8,128)S(1)}, u32[]{:S(2)}, u32[]{:S(2)}) collective-permute-start(f32[8,128]{1,0:T(8,128)S(1)} %add.3.refs_0_), channel_id=1, source_target_pairs={{0,2},{1,3},{2,0},{3,1},{4,6},{5,7},{6,4},{7,5},{8,10},{9,11},{10,... | collective-permute-start | bytes 12296 | tf_op jit(solution)/shard_map/ppermute | solution.py:474

commit v5 on v4

--- a/solution.py
+++ b/solution.py
@@ -107,6 +107,7 @@
 def sink_kernel(
     nets,
     edge,
+    eye_ref,
     conduct_ref,
     volt_ref,
     inject_ref,
@@ -481,6 +482,23 @@
         held *= reach
 
 
+def sum_stages(block, axis, count):
+    held, terms = 2, [block]
+    while held < count:
+        block = sum(terms[1:], terms[0])
+        if (count // held).bit_length() % 2 == 0:
+            terms = [block, other(block, axis, count, held)]
+            held *= 2
+            continue
+        route = [(i, i ^ (2 * held if i % 2 else held)) for i in range(count)]
+        brought = lax.ppermute(block, axis, route)
+        third = other(block, axis, count, 3 * held)
+        brought, third = lax.optimization_barrier((brought, third))
+        terms = [block, brought, third, other(brought, axis, count, 1)]
+        held *= 4
+    return terms
+
+
 def outer_swap(block, axis, count):
     pairs = [(i, (i + 1) % count if i % 2 else (i - 1) % count) for i in range(count)]
     return lax.ppermute(block, axis, pairs)
@@ -522,6 +540,7 @@
             (slots, patterns),
             (nets, patterns),
         ],
+        eye,
         conduct[0],
         voltage,
         inject[0],
@@ -597,10 +616,7 @@
         first,
     )
 
-    sums = [moments]
-    for distances in stages(cols, 1):
-        moments = sum(sums[1:], sums[0])
-        sums = [moments] + [other(moments, "col", cols, d) for d in distances]
+    sums = sum_stages(moments + other(moments, "col", cols, 1), "col", cols)
     directions = run(
         functools.partial(direction_kernel, edge), [field] * 3, precond, inverse, flow, t0, t1
     )

time: 39.5 us -> 39.1 us (0.990)
    ppermute x11 -> x10, starting transfers between devices: 11.2 us -> 9.13 us  [other(): return lax.ppermute(block, axis, [(i, i ^ distance) for i in range(count)])]
    ppermute x0 -> x1, starting transfers between devices: none -> 1.86 us  [sum_stages(): brought = lax.ppermute(block, axis, route)]
    ppermute x11 -> x10, waiting for transfers between devices: 5.86 us -> 5.22 us  [other(): return lax.ppermute(block, axis, [(i, i ^ distance) for i in range(count)])]
    ppermute x0 -> x1, waiting for transfers between devices: none -> 0.48 us  [sum_stages(): brought = lax.ppermute(block, axis, route)]
where the time goes in v5:
time: 39.1 us; the launch traced here: 38.9 us
  starting transfers between devices  18 us (46%)
  waiting for transfers between devices  14.2 us (36%)
  Pallas kernels  5.89 us (15%)
  local copies, waits for them, and re-layouts  0.69 us (2%)
    ppermute x10, starting transfers between devices, other(): return lax.ppermute(block, axis, [(i, i ^ distance) for i in range(count)])  9.13 us
    pallas_call x9, Pallas kernels, run(): pl.pallas_call(kernel, out_shape=shapes, in_specs=[vmem] * len(args), out...  5.89 us
    ppermute x3, starting transfers between devices, local(): lax.ppermute(message, 'row', [((i + k) % rows, i) for i in range(rows)])  5.57 us
    ppermute x10, waiting for transfers between devices, other(): return lax.ppermute(block, axis, [(i, i ^ distance) for i in range(count)])  5.22 us
    ppermute x1, waiting for transfers between devices, local(): far = lax.ppermute(far, 'col', [((i + 2) % cols, i) for i in range(cols)])  4.18 us
    ppermute x3, waiting for transfers between devices, local(): lax.ppermute(message, 'row', [((i + k) % rows, i) for i in range(rows)])  4.08 us
    ppermute x1, starting transfers between devices, sum_stages(): brought = lax.ppermute(block, axis, route)  1.86 us
    ppermute x1, starting transfers between devices, local(): far = lax.ppermute(far, 'col', [((i + 2) % cols, i) for i in range(cols)])  1.35 us
  transfers between devices with their start and end apart: 16, of which 12 were waited for; matrix products, arithmetic and copies ran while one was open for 0% of the time, Pallas kernels for 7%

profile of v5, /device:TPU:0, one launch (start us, length us, event | category | flops | bytes accessed | tf_op | source)
XLA Modules:
  0.0 38.9 jit_solution(7048041130401461943)
XLA Ops:
  0.0 0.5 %collective-permute-start.2 = (s32[1,1,64]{2,1,0:T(1,128)}, s32[1,1,64]{2,1,0:T(1,128)S(1)}, u32[]{:S(2)}, u32[]{:S(2)}) collective-permute-start(s32[1,1,64]{2,1,0:T(1,128)} %param.16), channel_id=1, source_target_pairs={{0,1},{1,0},{2,3},{3,2},{4,5},{5,4},{6,7},{7,6},{8,9},{9,8},{10,11... | collective-permute-start | bytes 776 | tf_op jit(solution)/shard_map/ppermute | solution.py:475
  0.5 0.1 collective-permute-start.1
  0.6 0.4 %collective-permute-start = (f32[1,2,128,128]{3,2,1,0:T(8,128)}, f32[1,2,128,128]{3,2,1,0:T(8,128)S(1)}, u32[]{:S(2)}, u32[]{:S(2)}) collective-permute-start(f32[1,2,128,128]{3,2,1,0:T(8,128)} %param.11), channel_id=1, source_target_pairs={{0,1},{1,0},{2,3},{3,2},{4,5},{5,4},{6,7},{7,6},{8,9},{9,8},{10,11... | collective-permute-start | bytes 393224 | tf_op jit(solution)/shard_map/ppermute | solution.py:475
  1.1 0.0 copy-start.4
  1.1 0.0 copy-start.3
  1.1 0.0 copy-start.9
  1.1 0.0 copy-start.10
  1.1 0.6 %copy-done.5 = s32[1,1,8,8]{3,2,1,0:T(8,128)S(1)} copy-done((s32[1,1,8,8]{3,2,1,0:T(8,128)S(1)}, s32[1,1,8,8]{3,2,1,0:T(8,128)}, u32[]{:S(2)}) %copy-start.5) | copy-done | bytes 280
  1.7 0.0 copy-done.6
  1.7 0.0 copy-done.7
  1.8 0.0 copy-done.4
  1.8 0.0 copy-done.3
  1.8 0.3 shard_map.110
  2.1 0.0 collective-permute-done.2
  2.1 0.0 collective-permute-done.1
  2.1 0.1 collective-permute-done
  2.2 0.1 shard_map.111.after_ref.refs_0_
  2.3 3.9 %collective-permute-start.5 = (f32[168,128]{1,0:T(8,128)S(1)}, f32[168,128]{1,0:T(8,128)S(1)}, u32[]{:S(2)}, u32[]{:S(2)}) collective-permute-start(f32[168,128]{1,0:T(8,128)S(1)} %shard_map.111.after_ref.refs_0_), channel_id=1, source_target_pairs={{0,6},{1,7},{2,4},{3,5},{4,2},{5,3},{6,0},{7,1},{8,14},{9,15},{10,... | collective-permute-start | bytes 258056 | tf_op jit(solution)/shard_map/ppermute | solution.py:475
  6.2 0.5 %collective-permute-start.4 = (f32[168,128]{1,0:T(8,128)S(1)}, f32[168,128]{1,0:T(8,128)S(1)}, u32[]{:S(2)}, u32[]{:S(2)}) collective-permute-start(f32[168,128]{1,0:T(8,128)S(1)} %shard_map.111.after_ref.refs_0_), channel_id=1, source_target_pairs={{0,4},{1,5},{2,6},{3,7},{4,0},{5,1},{6,2},{7,3},{8,12},{9,13},{10,... | collective-permute-start | bytes 258056 | tf_op jit(solution)/shard_map/ppermute | solution.py:475
  6.7 0.1 collective-permute-start.3
  6.8 2.2 %shard_map.112 = (f32[2,128,128]{2,1,0:T(8,128)S(1)}, f32[16,128]{1,0:T(8,128)S(1)}) custom-call(f32[128,128]{1,0:T(8,128)S(1)} %shard_map.109.eye_ref, f32[2,128,128]{2,1,0:T(8,128)S(1)} %bitcast.17, f32[2,128]{1,0:T(2,128)S(1)} %bitcast.31, f32[168,128]{1,0:T(8,128)S(1)} %shard_map.111.after_ref.refs_0_), custom_call_target="tpu_custom_call" | custom-call | flops 4000000000 | bytes 422912 | tf_op jit(solution)/shard_map/pallas_call | solution.py:49
  9.1 0.1 collective-permute-done.5.refs_3_
  9.1 1.7 %collective-permute-done.4.refs_2_ = f32[168,128]{1,0:T(8,128)S(1)} collective-permute-done((f32[168,128]{1,0:T(8,128)S(1)}, f32[168,128]{1,0:T(8,128)S(1)}, u32[]{:S(2)}, u32[]{:S(2)}) %collective-permute-start.4) | collective-permute-done | bytes 86048 | tf_op jit(solution)/shard_map/ppermute | solution.py:475
  10.9 0.3 collective-permute-done.3.refs_1_
  11.2 0.9 %shard_map.113 = (f32[152,128]{1,0:T(8,128)S(1)}, f32[2,128,128]{2,1,0:T(8,128)S(1)}) custom-call(f32[2,128,128]{2,1,0:T(8,128)S(1)} %bitcast.20, f32[2,128,128]{2,1,0:T(8,128)S(1)} %bitcast.23, f32[2,2,32]{2,1,0:T(2,128)S(1)} %bitcast.30, f32[2,128,128]{2,1,0:T(8,128)S(1)} %get-tuple-element.28.inverse_ref, f32[16,128]{1,0:T(8,128)S(1)} %get-tuple-element.29.fold_ref, ...), custom_call_target="tpu_custom_call" | custom-call | flops 4000000000 | bytes 1335808 | tf_op jit(solution)/shard_map/pallas_call | solution.py:49
  12.1 1.6 %collective-permute-start.8 = (f32[152,128]{1,0:T(8,128)S(1)}, f32[152,128]{1,0:T(8,128)S(1)}, u32[]{:S(2)}, u32[]{:S(2)}) collective-permute-start(f32[152,128]{1,0:T(8,128)S(1)} %get-tuple-element.36.refs_0_), channel_id=1, source_target_pairs={{24,0},{0,8},{8,16},{16,24},{25,1},{1,9},{9,17},{17,25},{26,2},{2,... | collective-permute-start | bytes 233480 | tf_op jit(solution)/shard_map/ppermute | solution.py:596
  13.7 2.6 %collective-permute-start.7 = (f32[152,128]{1,0:T(8,128)S(1)}, f32[152,128]{1,0:T(8,128)S(1)}, u32[]{:S(2)}, u32[]{:S(2)}) collective-permute-start(f32[152,128]{1,0:T(8,128)S(1)} %get-tuple-element.36.refs_0_), channel_id=1, source_target_pairs={{16,0},{24,8},{0,16},{8,24},{17,1},{25,9},{1,17},{9,25},{18,2},{26... | collective-permute-start | bytes 233480 | tf_op jit(solution)/shard_map/ppermute | solution.py:596
  16.3 1.3 %collective-permute-start.6 = (f32[152,128]{1,0:T(8,128)S(1)}, f32[152,128]{1,0:T(8,128)S(1)}, u32[]{:S(2)}, u32[]{:S(2)}) collective-permute-start(f32[152,128]{1,0:T(8,128)S(1)} %get-tuple-element.36.refs_0_), channel_id=1, source_target_pairs={{8,0},{16,8},{24,16},{0,24},{9,1},{17,9},{25,17},{1,25},{10,2},{18... | collective-permute-start | bytes 233480 | tf_op jit(solution)/shard_map/ppermute | solution.py:596
  17.6 1.7 %collective-permute-done.8.refs_3_ = f32[152,128]{1,0:T(8,128)S(1)} collective-permute-done((f32[152,128]{1,0:T(8,128)S(1)}, f32[152,128]{1,0:T(8,128)S(1)}, u32[]{:S(2)}, u32[]{:S(2)}) %collective-permute-start.8) | collective-permute-done | bytes 77856 | tf_op jit(solution)/shard_map/ppermute | solution.py:596
  19.3 2.4 %collective-permute-done.7.refs_2_ = f32[152,128]{1,0:T(8,128)S(1)} collective-permute-done((f32[152,128]{1,0:T(8,128)S(1)}, f32[152,128]{1,0:T(8,128)S(1)}, u32[]{:S(2)}, u32[]{:S(2)}) %collective-permute-start.7) | collective-permute-done | bytes 77856 | tf_op jit(solution)/shard_map/ppermute | solution.py:596
  21.7 0.0 collective-permute-done.6.refs_1_
  21.7 0.4 %shard_map.114 = (f32[328,128]{1,0:T(8,128)S(1)}, f32[128,128]{1,0:T(8,128)S(1)}, f32[64,128]{1,0:T(8,128)S(1)}, f32[8,128]{1,0:T(8,128)S(1)}) custom-call(f32[152,128]{1,0:T(8,128)S(1)} %get-tuple-element.36.refs_0_, f32[152,128]{1,0:T(8,128)S(1)} %collective-permute-done.6.refs_1_, f32[152,128]{1,0:T(8,128)S(1)} %collective-permute-done.7.refs_2_, ...), custom_call_target="tpu_custom_call" | custom-call | flops 4000000000 | bytes 581632 | tf_op jit(solution)/shard_map/pallas_call | solution.py:49
  22.1 0.1 collective-permute-start.10
  22.2 1.7 %collective-permute-start.9 = (f32[328,128]{1,0:T(8,128)S(1)}, f32[328,128]{1,0:T(8,128)S(1)}, u32[]{:S(2)}, u32[]{:S(2)}) collective-permute-start(f32[328,128]{1,0:T(8,128)S(1)} %get-tuple-element.38.own_ref), channel_id=1, source_target_pairs={{0,1},{1,0},{2,3},{3,2},{4,5},{5,4},{6,7},{7,6},{8,9},{9,8},{10,11... | collective-permute-start | bytes 503816 | tf_op jit(solution)/shard_map/ppermute | solution.py:475
  23.9 1.4 %collective-permute-start.11 = (f32[128,128]{1,0:T(8,128)S(1)}, f32[128,128]{1,0:T(8,128)S(1)}, u32[]{:S(2)}, u32[]{:S(2)}) collective-permute-start(f32[128,128]{1,0:T(8,128)S(1)} %get-tuple-element.39), channel_id=1, source_target_pairs={{2,0},{3,1},{4,2},{5,3},{6,4},{7,5},{0,6},{1,7},{10,8},{11,9},{12,... | collective-permute-start | bytes 196616 | tf_op jit(solution)/shard_map/ppermute | solution.py:608
  25.2 4.2 %collective-permute-done.11.far_ref = f32[128,128]{1,0:T(8,128)S(1)} collective-permute-done((f32[128,128]{1,0:T(8,128)S(1)}, f32[128,128]{1,0:T(8,128)S(1)}, u32[]{:S(2)}, u32[]{:S(2)}) %collective-permute-start.11) | collective-permute-done | bytes 65568 | tf_op jit(solution)/shard_map/ppermute | solution.py:608
  29.4 0.3 collective-permute-done.10.outer_ref
  29.7 1.0 %shard_map.115 = (f32[8,128]{1,0:T(8,128)S(1)}, f32[64,128]{1,0:T(8,128)S(1)}, f32[64,128]{1,0:T(8,128)S(1)}) custom-call(f32[328,128]{1,0:T(8,128)S(1)} %get-tuple-element.38.own_ref, f32[328,128]{1,0:T(8,128)S(1)} %collective-permute-done.9.inner_ref, f32[328,128]{1,0:T(8,128)S(1)} %collective-permute-done.10.outer_ref, ...), custom_call_target="tpu_custom_call" | custom-call | flops 4000000000 | bytes 643072 | tf_op jit(solution)/shard_map/pallas_call | solution.py:49
  30.7 0.5 %collective-permute-start.12 = (f32[8,128]{1,0:T(8,128)S(1)}, f32[8,128]{1,0:T(8,128)S(1)}, u32[]{:S(2)}, u32[]{:S(2)}) collective-permute-start(f32[8,128]{1,0:T(8,128)S(1)} %get-tuple-element.46), channel_id=1, source_target_pairs={{0,1},{1,0},{2,3},{3,2},{4,5},{5,4},{6,7},{7,6},{8,9},{9,8},{10,11... | collective-permute-start | bytes 12296 | tf_op jit(solution)/shard_map/ppermute | solution.py:475
  31.2 0.8 %collective-permute-done.12 = f32[8,128]{1,0:T(8,128)S(1)} collective-permute-done((f32[8,128]{1,0:T(8,128)S(1)}, f32[8,128]{1,0:T(8,128)S(1)}, u32[]{:S(2)}, u32[]{:S(2)}) %collective-permute-start.12) | collective-permute-done | bytes 4128 | tf_op jit(solution)/shard_map/ppermute | solution.py:475
  32.0 1.4 %collective-permute-start.14 = (f32[8,128]{1,0:T(8,128)S(1)}, f32[8,128]{1,0:T(8,128)S(1)}, u32[]{:S(2)}, u32[]{:S(2)}) collective-permute-start(f32[8,128]{1,0:T(8,128)S(1)} %add.3.refs_0_), channel_id=1, source_target_pairs={{0,6},{1,7},{2,4},{3,5},{4,2},{5,3},{6,0},{7,1},{8,14},{9,15},{10,... | collective-permute-start | bytes 12296 | tf_op jit(solution)/shard_map/ppermute | solution.py:475
  33.4 1.9 %collective-permute-start.13 = (f32[8,128]{1,0:T(8,128)S(1)}, f32[8,128]{1,0:T(8,128)S(1)}, u32[]{:S(2)}, u32[]{:S(2)}) collective-permute-start(f32[8,128]{1,0:T(8,128)S(1)} %add.3.refs_0_), channel_id=1, source_target_pairs={{0,2},{1,5},{2,0},{3,7},{4,6},{5,1},{6,4},{7,3},{8,10},{9,13},{10,... | collective-permute-start | bytes 12296 | tf_op jit(solution)/shard_map/ppermute | solution.py:494
  35.3 1.3 %collective-permute-done.14.refs_2_ = f32[8,128]{1,0:T(8,128)S(1)} collective-permute-done((f32[8,128]{1,0:T(8,128)S(1)}, f32[8,128]{1,0:T(8,128)S(1)}, u32[]{:S(2)}, u32[]{:S(2)}) %collective-permute-start.14) | collective-permute-done | bytes 4128 | tf_op jit(solution)/shard_map/ppermute | solution.py:475
  36.5 0.5 %collective-permute-done.13.refs_1_ = f32[8,128]{1,0:T(8,128)S(1)} collective-permute-done((f32[8,128]{1,0:T(8,128)S(1)}, f32[8,128]{1,0:T(8,128)S(1)}, u32[]{:S(2)}, u32[]{:S(2)}) %collective-permute-start.13) | collective-permute-done | bytes 4128 | tf_op jit(solution)/shard_map/ppermute | solution.py:494
  37.0 0.0 collective-permute-start.15
  37.0 0.3 shard_map.116
  37.3 0.9 %collective-permute-done.15.refs_3_ = f32[8,128]{1,0:T(8,128)S(1)} collective-permute-done((f32[8,128]{1,0:T(8,128)S(1)}, f32[8,128]{1,0:T(8,128)S(1)}, u32[]{:S(2)}, u32[]{:S(2)}) %collective-permute-start.15) | collective-permute-done | bytes 4128 | tf_op jit(solution)/shard_map/ppermute | solution.py:475
  38.2 0.7 %shard_map.117 = f32[2,128,128]{2,1,0:T(8,128)} custom-call(f32[2,128,128]{2,1,0:T(8,128)S(1)} %bitcast.21, f32[2,128,128]{2,1,0:T(8,128)S(1)} %get-tuple-element.43.z0_ref, f32[2,128,128]{2,1,0:T(8,128)S(1)} %get-tuple-element.44.z1_ref, f32[2,128,128]{2,1,0:T(8,128)S(1)} %get-tuple-element.45.z2_ref, f32[8,128]{1,0:T(8,128)S(1)} %add.3.refs_0_, ...), custom_call_target="tpu_custom_call" | custom-call | flops 4000000000 | bytes 671744 | tf_op jit(solution)/shard_map/pallas_call | solution.py:49
  (16 shorter events, 0.0 us)
Async XLA Ops:
  0.0 1.1 %copy-start.2 = (f32[1,2,128,128]{3,2,1,0:T(8,128)S(1)}, f32[1,2,128,128]{3,2,1,0:T(8,128)}, u32[]{:S(2)}) copy-start(f32[1,2,128,128]{3,2,1,0:T(8,128)} %param.11) | copy-start | bytes 393220
  0.0 1.1 %copy-start.1 = (f32[1,2,128,128]{3,2,1,0:T(8,128)S(1)}, f32[1,2,128,128]{3,2,1,0:T(8,128)}, u32[]{:S(2)}) copy-start(f32[1,2,128,128]{3,2,1,0:T(8,128)} %param.13) | copy-start | bytes 393220
  0.0 1.1 %copy-start = (f32[1,2,128,128]{3,2,1,0:T(8,128)S(1)}, f32[1,2,128,128]{3,2,1,0:T(8,128)}, u32[]{:S(2)}) copy-start(f32[1,2,128,128]{3,2,1,0:T(8,128)} %param.12) | copy-start | bytes 393220
  0.0 2.1 %collective-permute-start.2 = (s32[1,1,64]{2,1,0:T(1,128)}, s32[1,1,64]{2,1,0:T(1,128)S(1)}, u32[]{:S(2)}, u32[]{:S(2)}) collective-permute-start(s32[1,1,64]{2,1,0:T(1,128)} %param.16), channel_id=1, source_target_pairs={{0,1},{1,0},{2,3},{3,2},{4,5},{5,4},{6,7},{7,6},{8,9},{9,8},{10,11... | collective-permute-start | bytes 776 | tf_op jit(solution)/shard_map/ppermute | solution.py:475
  0.5 1.6 %collective-permute-start.1 = (f32[1,2,2,32]{3,2,1,0:T(2,128)}, f32[1,2,2,32]{3,2,1,0:T(2,128)S(1)}, u32[]{:S(2)}, u32[]{:S(2)}) collective-permute-start(f32[1,2,2,32]{3,2,1,0:T(2,128)} %param.15), channel_id=1, source_target_pairs={{0,1},{1,0},{2,3},{3,2},{4,5},{5,4},{6,7},{7,6},{8,9},{9,8},{10,11... | collective-permute-start | bytes 1544 | tf_op jit(solution)/shard_map/ppermute | solution.py:475
  0.6 1.6 %collective-permute-start = (f32[1,2,128,128]{3,2,1,0:T(8,128)}, f32[1,2,128,128]{3,2,1,0:T(8,128)S(1)}, u32[]{:S(2)}, u32[]{:S(2)}) collective-permute-start(f32[1,2,128,128]{3,2,1,0:T(8,128)} %param.11), channel_id=1, source_target_pairs={{0,1},{1,0},{2,3},{3,2},{4,5},{5,4},{6,7},{7,6},{8,9},{9,8},{10,11... | collective-permute-start | bytes 393224 | tf_op jit(solution)/shard_map/ppermute | solution.py:475
  1.0 0.7 %copy-start.5 = (s32[1,1,8,8]{3,2,1,0:T(8,128)S(1)}, s32[1,1,8,8]{3,2,1,0:T(8,128)}, u32[]{:S(2)}) copy-start(s32[1,1,8,8]{3,2,1,0:T(8,128)} %param.20) | copy-start | bytes 772
  1.0 0.7 %copy-start.6 = (f32[1,1,8,8]{3,2,1,0:T(8,128)S(1)}, f32[1,1,8,8]{3,2,1,0:T(8,128)}, u32[]{:S(2)}) copy-start(f32[1,1,8,8]{3,2,1,0:T(8,128)} %param.21) | copy-start | bytes 772
  1.0 0.7 %copy-start.7 = (f32[1,2,2,32]{3,2,1,0:T(2,128)S(1)}, f32[1,2,2,32]{3,2,1,0:T(2,128)}, u32[]{:S(2)}) copy-start(f32[1,2,2,32]{3,2,1,0:T(2,128)} %param.15) | copy-start | bytes 1540
  1.1 0.7 %copy-start.4 = (s32[1,1,8,8]{3,2,1,0:T(8,128)S(1)}, s32[1,1,8,8]{3,2,1,0:T(8,128)}, u32[]{:S(2)}) copy-start(s32[1,1,8,8]{3,2,1,0:T(8,128)} %param.19) | copy-start | bytes 772
  1.1 0.7 %copy-start.3 = (s32[1,1,8,8]{3,2,1,0:T(8,128)S(1)}, s32[1,1,8,8]{3,2,1,0:T(8,128)}, u32[]{:S(2)}) copy-start(s32[1,1,8,8]{3,2,1,0:T(8,128)} %param.17) | copy-start | bytes 772
  1.1 0.7 %copy-start.9 = (s32[1,1,8]{2,1,0:T(1,128)S(1)}, s32[1,1,8]{2,1,0:T(1,128)}, u32[]{:S(2)}) copy-start(s32[1,1,8]{2,1,0:T(1,128)} %param.18) | copy-start | bytes 100
  1.1 0.7 %copy-start.10 = (s32[1,1,64]{2,1,0:T(1,128)S(1)}, s32[1,1,64]{2,1,0:T(1,128)}, u32[]{:S(2)}) copy-start(s32[1,1,64]{2,1,0:T(1,128)} %param.16) | copy-start | bytes 772
  2.3 4.5 %copy-start.8 = (f32[1,2,128]{2,1,0:T(2,128)S(1)}, f32[1,2,128]{2,1,0:T(2,128)}, u32[]{:S(2)}) copy-start(f32[1,2,128]{2,1,0:T(2,128)} %param.14) | copy-start | bytes 3076
  2.3 6.8 %collective-permute-start.5 = (f32[168,128]{1,0:T(8,128)S(1)}, f32[168,128]{1,0:T(8,128)S(1)}, u32[]{:S(2)}, u32[]{:S(2)}) collective-permute-start(f32[168,128]{1,0:T(8,128)S(1)} %shard_map.111.after_ref.refs_0_), channel_id=1, source_target_pairs={{0,6},{1,7},{2,4},{3,5},{4,2},{5,3},{6,0},{7,1},{8,14},{9,15},{10,... | collective-permute-start | bytes 258056 | tf_op jit(solution)/shard_map/ppermute | solution.py:475
  6.2 4.7 %collective-permute-start.4 = (f32[168,128]{1,0:T(8,128)S(1)}, f32[168,128]{1,0:T(8,128)S(1)}, u32[]{:S(2)}, u32[]{:S(2)}) collective-permute-start(f32[168,128]{1,0:T(8,128)S(1)} %shard_map.111.after_ref.refs_0_), channel_id=1, source_target_pairs={{0,4},{1,5},{2,6},{3,7},{4,0},{5,1},{6,2},{7,3},{8,12},{9,13},{10,... | collective-permute-start | bytes 258056 | tf_op jit(solution)/shard_map/ppermute | solution.py:475
  6.7 4.5 %collective-permute-start.3 = (f32[168,128]{1,0:T(8,128)S(1)}, f32[168,128]{1,0:T(8,128)S(1)}, u32[]{:S(2)}, u32[]{:S(2)}) collective-permute-start(f32[168,128]{1,0:T(8,128)S(1)} %shard_map.111.after_ref.refs_0_), channel_id=1, source_target_pairs={{0,2},{1,3},{2,0},{3,1},{4,6},{5,7},{6,4},{7,5},{8,10},{9,11},{10,... | collective-permute-start | bytes 258056 | tf_op jit(solution)/shard_map/ppermute | solution.py:475
  12.1 7.2 %collective-permute-start.8 = (f32[152,128]{1,0:T(8,128)S(1)}, f32[152,128]{1,0:T(8,128)S(1)}, u32[]{:S(2)}, u32[]{:S(2)}) collective-permute-start(f32[152,128]{1,0:T(8,128)S(1)} %get-tuple-element.36.refs_0_), channel_id=1, source_target_pairs={{24,0},{0,8},{8,16},{16,24},{25,1},{1,9},{9,17},{17,25},{26,2},{2,... | collective-permute-start | bytes 233480 | tf_op jit(solution)/shard_map/ppermute | solution.py:596
  13.7 8.0 %collective-permute-start.7 = (f32[152,128]{1,0:T(8,128)S(1)}, f32[152,128]{1,0:T(8,128)S(1)}, u32[]{:S(2)}, u32[]{:S(2)}) collective-permute-start(f32[152,128]{1,0:T(8,128)S(1)} %get-tuple-element.36.refs_0_), channel_id=1, source_target_pairs={{16,0},{24,8},{0,16},{8,24},{17,1},{25,9},{1,17},{9,25},{18,2},{26... | collective-permute-start | bytes 233480 | tf_op jit(solution)/shard_map/ppermute | solution.py:596
  16.3 5.4 %collective-permute-start.6 = (f32[152,128]{1,0:T(8,128)S(1)}, f32[152,128]{1,0:T(8,128)S(1)}, u32[]{:S(2)}, u32[]{:S(2)}) collective-permute-start(f32[152,128]{1,0:T(8,128)S(1)} %get-tuple-element.36.refs_0_), channel_id=1, source_target_pairs={{8,0},{16,8},{24,16},{0,24},{9,1},{17,9},{25,17},{1,25},{10,2},{18... | collective-permute-start | bytes 233480 | tf_op jit(solution)/shard_map/ppermute | solution.py:596
  22.1 7.5 %collective-permute-start.10 = (f32[328,128]{1,0:T(8,128)S(1)}, f32[328,128]{1,0:T(8,128)S(1)}, u32[]{:S(2)}, u32[]{:S(2)}) collective-permute-start(f32[328,128]{1,0:T(8,128)S(1)} %get-tuple-element.38.own_ref), channel_id=1, source_target_pairs={{0,7},{1,2},{2,1},{3,4},{4,3},{5,6},{6,5},{7,0},{8,15},{9,10},{10,... | collective-permute-start | bytes 503816 | tf_op jit(solution)/shard_map/ppermute | solution.py:504
  22.2 7.5 %collective-permute-start.9 = (f32[328,128]{1,0:T(8,128)S(1)}, f32[328,128]{1,0:T(8,128)S(1)}, u32[]{:S(2)}, u32[]{:S(2)}) collective-permute-start(f32[328,128]{1,0:T(8,128)S(1)} %get-tuple-element.38.own_ref), channel_id=1, source_target_pairs={{0,1},{1,0},{2,3},{3,2},{4,5},{5,4},{6,7},{7,6},{8,9},{9,8},{10,11... | collective-permute-start | bytes 503816 | tf_op jit(solution)/shard_map/ppermute | solution.py:475
  23.9 5.5 %collective-permute-start.11 = (f32[128,128]{1,0:T(8,128)S(1)}, f32[128,128]{1,0:T(8,128)S(1)}, u32[]{:S(2)}, u32[]{:S(2)}) collective-permute-start(f32[128,128]{1,0:T(8,128)S(1)} %get-tuple-element.39), channel_id=1, source_target_pairs={{2,0},{3,1},{4,2},{5,3},{6,4},{7,5},{0,6},{1,7},{10,8},{11,9},{12,... | collective-permute-start | bytes 196616 | tf_op jit(solution)/shard_map/ppermute | solution.py:608
  30.7 1.4 %collective-permute-start.12 = (f32[8,128]{1,0:T(8,128)S(1)}, f32[8,128]{1,0:T(8,128)S(1)}, u32[]{:S(2)}, u32[]{:S(2)}) collective-permute-start(f32[8,128]{1,0:T(8,128)S(1)} %get-tuple-element.46), channel_id=1, source_target_pairs={{0,1},{1,0},{2,3},{3,2},{4,5},{5,4},{6,7},{7,6},{8,9},{9,8},{10,11... | collective-permute-start | bytes 12296 | tf_op jit(solution)/shard_map/ppermute | solution.py:475
  32.0 4.5 %collective-permute-start.14 = (f32[8,128]{1,0:T(8,128)S(1)}, f32[8,128]{1,0:T(8,128)S(1)}, u32[]{:S(2)}, u32[]{:S(2)}) collective-permute-start(f32[8,128]{1,0:T(8,128)S(1)} %add.3.refs_0_), channel_id=1, source_target_pairs={{0,6},{1,7},{2,4},{3,5},{4,2},{5,3},{6,0},{7,1},{8,14},{9,15},{10,... | collective-permute-start | bytes 12296 | tf_op jit(solution)/shard_map/ppermute | solution.py:475
  33.4 3.6 %collective-permute-start.13 = (f32[8,128]{1,0:T(8,128)S(1)}, f32[8,128]{1,0:T(8,128)S(1)}, u32[]{:S(2)}, u32[]{:S(2)}) collective-permute-start(f32[8,128]{1,0:T(8,128)S(1)} %add.3.refs_0_), channel_id=1, source_target_pairs={{0,2},{1,5},{2,0},{3,7},{4,6},{5,1},{6,4},{7,3},{8,10},{9,13},{10,... | collective-permute-start | bytes 12296 | tf_op jit(solution)/shard_map/ppermute | solution.py:494
  37.0 1.2 %collective-permute-start.15 = (f32[8,128]{1,0:T(8,128)S(1)}, f32[8,128]{1,0:T(8,128)S(1)}, u32[]{:S(2)}, u32[]{:S(2)}) collective-permute-start(f32[8,128]{1,0:T(8,128)S(1)} %collective-permute-done.13.refs_1_), channel_id=1, source_target_pairs={{0,1},{1,0},{2,3},{3,2},{4,5},{5,4},{6,7},{7,6},{8,9},{9,8},{10,11... | collective-permute-start | bytes 12296 | tf_op jit(solution)/shard_map/ppermute | solution.py:475

commit v6 on v5

--- a/solution.py
+++ b/solution.py
@@ -157,7 +157,21 @@
     scale_ref[...] = jnp.broadcast_to(weight, scale_ref.shape)
 
 
-def tile_kernel(edge, eye_ref, conduct_ref, cap_ref, after_ref, inverse_ref, fold_ref, sum_ref, power_ref):
+def tile_kernel(
+    edge,
+    eye_ref,
+    conduct_ref,
+    cap_ref,
+    rest_ref,
+    put_ref,
+    after_ref,
+    inverse_ref,
+    fold_ref,
+    part_ref,
+    reach_ref,
+    sum_ref,
+    power_ref,
+):
     tiles, nodes = conduct_ref.shape[0], conduct_ref.shape[1]
     eye = eye_ref[...]
     sums, powers, scales = [], [], []
@@ -207,6 +221,14 @@
             piece = jnp.where(lane < edge, inverse[j * depth : (j + 1) * depth], 0.0)
             fold = fold + (pltpu.roll(piece, j * edge, 1) if j else piece)
         fold_ref[t * depth : (t + 1) * depth] = fold
+        part_ref[t] = dot3(inverse, rest_ref[t])
+        put = put_ref[:, t * nodes : (t + 1) * nodes]
+        reach_ref[t] = sum(
+            lax.dot_general(
+                piece, put, (((1,), (1,)), ((), ())), preferred_element_type=jnp.float32
+            )
+            for piece in split(inverse)
+        )
 
 
 def residual_kernel(
@@ -218,6 +240,8 @@
     mate_gain_ref,
     inverse_ref,
     fold_ref,
+    part_ref,
+    reach_ref,
     rest_ref,
     gains_ref,
     take_ref,
@@ -254,6 +278,10 @@
     first = jnp.zeros((1, patterns), jnp.float32)
     high, low = split(values)
     for t in range(tiles):
+        out = flows[t + 1] - flows[t]
+        precond = part_ref[t] + (
+            dot3(reach_ref[t], values) - dot3(inverse_ref[t, :, :edge], out)
+        )
         put = put_ref[:, t * nodes : (t + 1) * nodes]
         injected = sum(
             lax.dot_general(
@@ -262,10 +290,7 @@
             for part in (high, low)
         )
         residual = rest_ref[t] + injected
-        residual = jnp.concatenate(
-            [residual[:edge] - (flows[t + 1] - flows[t]), residual[edge:]], axis=0
-        )
-        precond = dot3(inverse_ref[t], residual)
+        residual = jnp.concatenate([residual[:edge] - out, residual[edge:]], axis=0)
         precond_ref[t] = precond
         first = first + jnp.sum(residual * precond, axis=0, keepdims=True)
         message_ref[t * edge : (t + 1) * edge] = precond[:edge]
@@ -566,12 +591,14 @@
         whole = groups[0] if len(groups) == 1 else jnp.concatenate(groups)
         groups = [whole] + [other(whole, "col", cols, d) for d in distances]
     depth = tiles * edge * edge // nodes
-    inverse, fold = run(
+    inverse, fold, part, reach = run(
         functools.partial(tile_kernel, edge),
-        [field, (depth, nodes)],
+        [field, (depth, nodes), field, (tiles, nodes, slots)],
         eye,
         conduct[0],
         capacitance[0],
+        rest,
+        put,
         pair,
         scratch=[pltpu.VMEM(field, jnp.float32)] * 2,
     )
@@ -584,6 +611,8 @@
         mate_gain,
         inverse,
         fold,
+        part,
+        reach,
         rest,
         gains,
         take,

time: 39.1 us -> 39.3 us (level)
  waiting for transfers between devices: 14.2 us -> 13.4 us
  local copies, waits for them, and re-layouts: 0.69 us -> 1.37 us
    ppermute x10, waiting for transfers between devices: 5.22 us -> 4.37 us  [other(): return lax.ppermute(block, axis, [(i, i ^ distance) for i in range(count)])]
    unnamed x22, local copies, waits for them, and re-layouts: 0.69 us -> 1.37 us
  transfers between devices with their start and end apart: 16 -> 16, of which waited for: 12 -> 11; matrix products, arithmetic and copies ran while one was open for 0% -> 0% of each run, Pallas kernels for 7% -> 8%
where the time goes in v6:
time: 39.3 us; the launch traced here: 38.8 us
  starting transfers between devices  18 us (46%)
  waiting for transfers between devices  13.4 us (34%)
  Pallas kernels  5.92 us (15%)
  local copies, waits for them, and re-layouts  1.37 us (3%)
    ppermute x10, starting transfers between devices, other(): return lax.ppermute(block, axis, [(i, i ^ distance) for i in range(count)])  9.11 us
    pallas_call x9, Pallas kernels, run(): pl.pallas_call(kernel, out_shape=shapes, in_specs=[vmem] * len(args), out...  5.92 us
    ppermute x3, starting transfers between devices, local(): lax.ppermute(message, 'row', [((i + k) % rows, i) for i in range(rows)])  5.57 us
    ppermute x10, waiting for transfers between devices, other(): return lax.ppermute(block, axis, [(i, i ^ distance) for i in range(count)])  4.37 us
    ppermute x1, waiting for transfers between devices, local(): far = lax.ppermute(far, 'col', [((i + 2) % cols, i) for i in range(cols)])  4.18 us
    ppermute x3, waiting for transfers between devices, local(): lax.ppermute(message, 'row', [((i + k) % rows, i) for i in range(rows)])  4.08 us
    ppermute x1, starting transfers between devices, sum_stages(): brought = lax.ppermute(block, axis, route)  1.86 us
    unnamed x22, local copies, waits for them, and re-layouts  1.37 us
  transfers between devices with their start and end apart: 16, of which 11 were waited for; matrix products, arithmetic and copies ran while one was open for 0% of the time, Pallas kernels for 8%

profile of v6, /device:TPU:0, one launch (start us, length us, event | category | flops | bytes accessed | tf_op | source)
XLA Modules:
  0.0 38.8 jit_solution(13346198201325366585)
XLA Ops:
  0.0 0.5 %collective-permute-start.2 = (s32[1,1,64]{2,1,0:T(1,128)}, s32[1,1,64]{2,1,0:T(1,128)S(1)}, u32[]{:S(2)}, u32[]{:S(2)}) collective-permute-start(s32[1,1,64]{2,1,0:T(1,128)} %param.16), channel_id=1, source_target_pairs={{0,1},{1,0},{2,3},{3,2},{4,5},{5,4},{6,7},{7,6},{8,9},{9,8},{10,11... | collective-permute-start | bytes 776 | tf_op jit(solution)/shard_map/ppermute | solution.py:500
  0.5 0.1 collective-permute-start.1
  0.6 0.4 %collective-permute-start = (f32[1,2,128,128]{3,2,1,0:T(8,128)}, f32[1,2,128,128]{3,2,1,0:T(8,128)S(1)}, u32[]{:S(2)}, u32[]{:S(2)}) collective-permute-start(f32[1,2,128,128]{3,2,1,0:T(8,128)} %param.11), channel_id=1, source_target_pairs={{0,1},{1,0},{2,3},{3,2},{4,5},{5,4},{6,7},{7,6},{8,9},{9,8},{10,11... | collective-permute-start | bytes 393224 | tf_op jit(solution)/shard_map/ppermute | solution.py:500
  1.1 0.0 copy-start.4
  1.1 0.0 copy-start.3
  1.1 0.0 copy-start.9
  1.1 0.0 copy-start.10
  1.1 0.6 %copy-done.5 = s32[1,1,8,8]{3,2,1,0:T(8,128)S(1)} copy-done((s32[1,1,8,8]{3,2,1,0:T(8,128)S(1)}, s32[1,1,8,8]{3,2,1,0:T(8,128)}, u32[]{:S(2)}) %copy-start.5) | copy-done | bytes 280
  1.7 0.0 copy-done.6
  1.7 0.0 copy-done.7
  1.8 0.0 copy-done.4
  1.8 0.0 copy-done.3
  1.8 0.3 shard_map.110
  2.1 0.0 collective-permute-done.2
  2.1 0.1 collective-permute-done
  2.2 0.1 shard_map.111.after_ref.refs_0_
  2.3 3.9 %collective-permute-start.5 = (f32[168,128]{1,0:T(8,128)S(1)}, f32[168,128]{1,0:T(8,128)S(1)}, u32[]{:S(2)}, u32[]{:S(2)}) collective-permute-start(f32[168,128]{1,0:T(8,128)S(1)} %shard_map.111.after_ref.refs_0_), channel_id=1, source_target_pairs={{0,6},{1,7},{2,4},{3,5},{4,2},{5,3},{6,0},{7,1},{8,14},{9,15},{10,... | collective-permute-start | bytes 258056 | tf_op jit(solution)/shard_map/ppermute | solution.py:500
  6.2 0.5 %collective-permute-start.4 = (f32[168,128]{1,0:T(8,128)S(1)}, f32[168,128]{1,0:T(8,128)S(1)}, u32[]{:S(2)}, u32[]{:S(2)}) collective-permute-start(f32[168,128]{1,0:T(8,128)S(1)} %shard_map.111.after_ref.refs_0_), channel_id=1, source_target_pairs={{0,4},{1,5},{2,6},{3,7},{4,0},{5,1},{6,2},{7,3},{8,12},{9,13},{10,... | collective-permute-start | bytes 258056 | tf_op jit(solution)/shard_map/ppermute | solution.py:500
  6.7 0.1 collective-permute-start.3
  6.8 0.7 %copy-done.8 = f32[1,2,128]{2,1,0:T(2,128)S(1)} copy-done((f32[1,2,128]{2,1,0:T(2,128)S(1)}, f32[1,2,128]{2,1,0:T(2,128)}, u32[]{:S(2)}) %copy-start.8) | copy-done | bytes 1048
  7.5 2.4 %shard_map.112 = (f32[2,128,128]{2,1,0:T(8,128)S(1)}, f32[16,128]{1,0:T(8,128)S(1)}, f32[2,128,128]{2,1,0:T(8,128)S(1)}, f32[2,128,64]{2,1,0:T(8,128)S(1)}) custom-call(f32[128,128]{1,0:T(8,128)S(1)} %shard_map.109.eye_ref, f32[2,128,128]{2,1,0:T(8,128)S(1)} %bitcast.17, f32[2,128]{1,0:T(2,128)S(1)} %bitcast.31, ...), custom_call_target="tpu_custom_call" | custom-call | flops 4000000000 | bytes 816128 | tf_op jit(solution)/shard_map/pallas_call | solution.py:49
  9.9 0.0 collective-permute-done.5.refs_3_
  9.9 0.9 %collective-permute-done.4.refs_2_ = f32[168,128]{1,0:T(8,128)S(1)} collective-permute-done((f32[168,128]{1,0:T(8,128)S(1)}, f32[168,128]{1,0:T(8,128)S(1)}, u32[]{:S(2)}, u32[]{:S(2)}) %collective-permute-start.4) | collective-permute-done | bytes 86048 | tf_op jit(solution)/shard_map/ppermute | solution.py:500
  10.9 0.3 collective-permute-done.3.refs_1_
  11.2 0.7 %shard_map.113 = (f32[152,128]{1,0:T(8,128)S(1)}, f32[2,128,128]{2,1,0:T(8,128)S(1)}) custom-call(f32[2,128,128]{2,1,0:T(8,128)S(1)} %bitcast.20, f32[2,128,128]{2,1,0:T(8,128)S(1)} %bitcast.23, f32[2,2,32]{2,1,0:T(2,128)S(1)} %bitcast.30, f32[2,128,128]{2,1,0:T(8,128)S(1)} %get-tuple-element.32.inverse_ref, f32[16,128]{1,0:T(8,128)S(1)} %get-tuple-element.33.fold_ref, ...), custom_call_target="tpu_custom_call" | custom-call | flops 4000000000 | bytes 1532416 | tf_op jit(solution)/shard_map/pallas_call | solution.py:49
  11.9 1.6 %collective-permute-start.8 = (f32[152,128]{1,0:T(8,128)S(1)}, f32[152,128]{1,0:T(8,128)S(1)}, u32[]{:S(2)}, u32[]{:S(2)}) collective-permute-start(f32[152,128]{1,0:T(8,128)S(1)} %get-tuple-element.40.refs_0_), channel_id=1, source_target_pairs={{24,0},{0,8},{8,16},{16,24},{25,1},{1,9},{9,17},{17,25},{26,2},{2,... | collective-permute-start | bytes 233480 | tf_op jit(solution)/shard_map/ppermute | solution.py:625
  13.5 2.6 %collective-permute-start.7 = (f32[152,128]{1,0:T(8,128)S(1)}, f32[152,128]{1,0:T(8,128)S(1)}, u32[]{:S(2)}, u32[]{:S(2)}) collective-permute-start(f32[152,128]{1,0:T(8,128)S(1)} %get-tuple-element.40.refs_0_), channel_id=1, source_target_pairs={{16,0},{24,8},{0,16},{8,24},{17,1},{25,9},{1,17},{9,25},{18,2},{26... | collective-permute-start | bytes 233480 | tf_op jit(solution)/shard_map/ppermute | solution.py:625
  16.1 1.3 %collective-permute-start.6 = (f32[152,128]{1,0:T(8,128)S(1)}, f32[152,128]{1,0:T(8,128)S(1)}, u32[]{:S(2)}, u32[]{:S(2)}) collective-permute-start(f32[152,128]{1,0:T(8,128)S(1)} %get-tuple-element.40.refs_0_), channel_id=1, source_target_pairs={{8,0},{16,8},{24,16},{0,24},{9,1},{17,9},{25,17},{1,25},{10,2},{18... | collective-permute-start | bytes 233480 | tf_op jit(solution)/shard_map/ppermute | solution.py:625
  17.5 1.7 %collective-permute-done.8.refs_3_ = f32[152,128]{1,0:T(8,128)S(1)} collective-permute-done((f32[152,128]{1,0:T(8,128)S(1)}, f32[152,128]{1,0:T(8,128)S(1)}, u32[]{:S(2)}, u32[]{:S(2)}) %collective-permute-start.8) | collective-permute-done | bytes 77856 | tf_op jit(solution)/shard_map/ppermute | solution.py:625
  19.1 2.4 %collective-permute-done.7.refs_2_ = f32[152,128]{1,0:T(8,128)S(1)} collective-permute-done((f32[152,128]{1,0:T(8,128)S(1)}, f32[152,128]{1,0:T(8,128)S(1)}, u32[]{:S(2)}, u32[]{:S(2)}) %collective-permute-start.7) | collective-permute-done | bytes 77856 | tf_op jit(solution)/shard_map/ppermute | solution.py:625
  21.6 0.0 collective-permute-done.6.refs_1_
  21.6 0.4 %shard_map.114 = (f32[328,128]{1,0:T(8,128)S(1)}, f32[128,128]{1,0:T(8,128)S(1)}, f32[64,128]{1,0:T(8,128)S(1)}, f32[8,128]{1,0:T(8,128)S(1)}) custom-call(f32[152,128]{1,0:T(8,128)S(1)} %get-tuple-element.40.refs_0_, f32[152,128]{1,0:T(8,128)S(1)} %collective-permute-done.6.refs_1_, f32[152,128]{1,0:T(8,128)S(1)} %collective-permute-done.7.refs_2_, ...), custom_call_target="tpu_custom_call" | custom-call | flops 4000000000 | bytes 581632 | tf_op jit(solution)/shard_map/pallas_call | solution.py:49
  22.0 0.1 collective-permute-start.10
  22.1 1.7 %collective-permute-start.9 = (f32[328,128]{1,0:T(8,128)S(1)}, f32[328,128]{1,0:T(8,128)S(1)}, u32[]{:S(2)}, u32[]{:S(2)}) collective-permute-start(f32[328,128]{1,0:T(8,128)S(1)} %get-tuple-element.42.own_ref), channel_id=1, source_target_pairs={{0,1},{1,0},{2,3},{3,2},{4,5},{5,4},{6,7},{7,6},{8,9},{9,8},{10,11... | collective-permute-start | bytes 503816 | tf_op jit(solution)/shard_map/ppermute | solution.py:500
  23.7 1.4 %collective-permute-start.11 = (f32[128,128]{1,0:T(8,128)S(1)}, f32[128,128]{1,0:T(8,128)S(1)}, u32[]{:S(2)}, u32[]{:S(2)}) collective-permute-start(f32[128,128]{1,0:T(8,128)S(1)} %get-tuple-element.43), channel_id=1, source_target_pairs={{2,0},{3,1},{4,2},{5,3},{6,4},{7,5},{0,6},{1,7},{10,8},{11,9},{12,... | collective-permute-start | bytes 196616 | tf_op jit(solution)/shard_map/ppermute | solution.py:637
  25.1 4.2 %collective-permute-done.11.far_ref = f32[128,128]{1,0:T(8,128)S(1)} collective-permute-done((f32[128,128]{1,0:T(8,128)S(1)}, f32[128,128]{1,0:T(8,128)S(1)}, u32[]{:S(2)}, u32[]{:S(2)}) %collective-permute-start.11) | collective-permute-done | bytes 65568 | tf_op jit(solution)/shard_map/ppermute | solution.py:637
  29.3 0.3 collective-permute-done.10.outer_ref
  29.5 0.0 collective-permute-done.9.inner_ref
  29.5 1.0 %shard_map.115 = (f32[8,128]{1,0:T(8,128)S(1)}, f32[64,128]{1,0:T(8,128)S(1)}, f32[64,128]{1,0:T(8,128)S(1)}) custom-call(f32[328,128]{1,0:T(8,128)S(1)} %get-tuple-element.42.own_ref, f32[328,128]{1,0:T(8,128)S(1)} %collective-permute-done.9.inner_ref, f32[328,128]{1,0:T(8,128)S(1)} %collective-permute-done.10.outer_ref, ...), custom_call_target="tpu_custom_call" | custom-call | flops 4000000000 | bytes 643072 | tf_op jit(solution)/shard_map/pallas_call | solution.py:49
  30.5 0.5 %collective-permute-start.12 = (f32[8,128]{1,0:T(8,128)S(1)}, f32[8,128]{1,0:T(8,128)S(1)}, u32[]{:S(2)}, u32[]{:S(2)}) collective-permute-start(f32[8,128]{1,0:T(8,128)S(1)} %get-tuple-element.50), channel_id=1, source_target_pairs={{0,1},{1,0},{2,3},{3,2},{4,5},{5,4},{6,7},{7,6},{8,9},{9,8},{10,11... | collective-permute-start | bytes 12296 | tf_op jit(solution)/shard_map/ppermute | solution.py:500
  31.1 0.8 %collective-permute-done.12 = f32[8,128]{1,0:T(8,128)S(1)} collective-permute-done((f32[8,128]{1,0:T(8,128)S(1)}, f32[8,128]{1,0:T(8,128)S(1)}, u32[]{:S(2)}, u32[]{:S(2)}) %collective-permute-start.12) | collective-permute-done | bytes 4128 | tf_op jit(solution)/shard_map/ppermute | solution.py:500
  31.9 1.4 %collective-permute-start.14 = (f32[8,128]{1,0:T(8,128)S(1)}, f32[8,128]{1,0:T(8,128)S(1)}, u32[]{:S(2)}, u32[]{:S(2)}) collective-permute-start(f32[8,128]{1,0:T(8,128)S(1)} %add.3.refs_0_), channel_id=1, source_target_pairs={{0,6},{1,7},{2,4},{3,5},{4,2},{5,3},{6,0},{7,1},{8,14},{9,15},{10,... | collective-permute-start | bytes 12296 | tf_op jit(solution)/shard_map/ppermute | solution.py:500
  33.3 1.9 %collective-permute-start.13 = (f32[8,128]{1,0:T(8,128)S(1)}, f32[8,128]{1,0:T(8,128)S(1)}, u32[]{:S(2)}, u32[]{:S(2)}) collective-permute-start(f32[8,128]{1,0:T(8,128)S(1)} %add.3.refs_0_), channel_id=1, source_target_pairs={{0,2},{1,5},{2,0},{3,7},{4,6},{5,1},{6,4},{7,3},{8,10},{9,13},{10,... | collective-permute-start | bytes 12296 | tf_op jit(solution)/shard_map/ppermute | solution.py:519
  35.1 1.3 %collective-permute-done.14.refs_2_ = f32[8,128]{1,0:T(8,128)S(1)} collective-permute-done((f32[8,128]{1,0:T(8,128)S(1)}, f32[8,128]{1,0:T(8,128)S(1)}, u32[]{:S(2)}, u32[]{:S(2)}) %collective-permute-start.14) | collective-permute-done | bytes 4128 | tf_op jit(solution)/shard_map/ppermute | solution.py:500
  36.4 0.5 %collective-permute-done.13.refs_1_ = f32[8,128]{1,0:T(8,128)S(1)} collective-permute-done((f32[8,128]{1,0:T(8,128)S(1)}, f32[8,128]{1,0:T(8,128)S(1)}, u32[]{:S(2)}, u32[]{:S(2)}) %collective-permute-start.13) | collective-permute-done | bytes 4128 | tf_op jit(solution)/shard_map/ppermute | solution.py:519
  36.9 0.3 shard_map.116
  37.2 0.9 %collective-permute-done.15.refs_3_ = f32[8,128]{1,0:T(8,128)S(1)} collective-permute-done((f32[8,128]{1,0:T(8,128)S(1)}, f32[8,128]{1,0:T(8,128)S(1)}, u32[]{:S(2)}, u32[]{:S(2)}) %collective-permute-start.15) | collective-permute-done | bytes 4128 | tf_op jit(solution)/shard_map/ppermute | solution.py:500
  38.0 0.7 %shard_map.117 = f32[2,128,128]{2,1,0:T(8,128)} custom-call(f32[2,128,128]{2,1,0:T(8,128)S(1)} %bitcast.21, f32[2,128,128]{2,1,0:T(8,128)S(1)} %get-tuple-element.47.z0_ref, f32[2,128,128]{2,1,0:T(8,128)S(1)} %get-tuple-element.48.z1_ref, f32[2,128,128]{2,1,0:T(8,128)S(1)} %get-tuple-element.49.z2_ref, f32[8,128]{1,0:T(8,128)S(1)} %add.3.refs_0_, ...), custom_call_target="tpu_custom_call" | custom-call | flops 4000000000 | bytes 671744 | tf_op jit(solution)/shard_map/pallas_call | solution.py:49
  (16 shorter events, 0.0 us)
Async XLA Ops:
  0.0 1.1 %copy-start.2 = (f32[1,2,128,128]{3,2,1,0:T(8,128)S(1)}, f32[1,2,128,128]{3,2,1,0:T(8,128)}, u32[]{:S(2)}) copy-start(f32[1,2,128,128]{3,2,1,0:T(8,128)} %param.11) | copy-start | bytes 393220
  0.0 1.1 %copy-start.1 = (f32[1,2,128,128]{3,2,1,0:T(8,128)S(1)}, f32[1,2,128,128]{3,2,1,0:T(8,128)}, u32[]{:S(2)}) copy-start(f32[1,2,128,128]{3,2,1,0:T(8,128)} %param.13) | copy-start | bytes 393220
  0.0 1.1 %copy-start = (f32[1,2,128,128]{3,2,1,0:T(8,128)S(1)}, f32[1,2,128,128]{3,2,1,0:T(8,128)}, u32[]{:S(2)}) copy-start(f32[1,2,128,128]{3,2,1,0:T(8,128)} %param.12) | copy-start | bytes 393220
  0.0 2.1 %collective-permute-start.2 = (s32[1,1,64]{2,1,0:T(1,128)}, s32[1,1,64]{2,1,0:T(1,128)S(1)}, u32[]{:S(2)}, u32[]{:S(2)}) collective-permute-start(s32[1,1,64]{2,1,0:T(1,128)} %param.16), channel_id=1, source_target_pairs={{0,1},{1,0},{2,3},{3,2},{4,5},{5,4},{6,7},{7,6},{8,9},{9,8},{10,11... | collective-permute-start | bytes 776 | tf_op jit(solution)/shard_map/ppermute | solution.py:500
  0.5 1.6 %collective-permute-start.1 = (f32[1,2,2,32]{3,2,1,0:T(2,128)}, f32[1,2,2,32]{3,2,1,0:T(2,128)S(1)}, u32[]{:S(2)}, u32[]{:S(2)}) collective-permute-start(f32[1,2,2,32]{3,2,1,0:T(2,128)} %param.15), channel_id=1, source_target_pairs={{0,1},{1,0},{2,3},{3,2},{4,5},{5,4},{6,7},{7,6},{8,9},{9,8},{10,11... | collective-permute-start | bytes 1544 | tf_op jit(solution)/shard_map/ppermute | solution.py:500
  0.6 1.6 %collective-permute-start = (f32[1,2,128,128]{3,2,1,0:T(8,128)}, f32[1,2,128,128]{3,2,1,0:T(8,128)S(1)}, u32[]{:S(2)}, u32[]{:S(2)}) collective-permute-start(f32[1,2,128,128]{3,2,1,0:T(8,128)} %param.11), channel_id=1, source_target_pairs={{0,1},{1,0},{2,3},{3,2},{4,5},{5,4},{6,7},{7,6},{8,9},{9,8},{10,11... | collective-permute-start | bytes 393224 | tf_op jit(solution)/shard_map/ppermute | solution.py:500
  1.0 0.7 %copy-start.5 = (s32[1,1,8,8]{3,2,1,0:T(8,128)S(1)}, s32[1,1,8,8]{3,2,1,0:T(8,128)}, u32[]{:S(2)}) copy-start(s32[1,1,8,8]{3,2,1,0:T(8,128)} %param.20) | copy-start | bytes 772
  1.0 0.7 %copy-start.6 = (f32[1,1,8,8]{3,2,1,0:T(8,128)S(1)}, f32[1,1,8,8]{3,2,1,0:T(8,128)}, u32[]{:S(2)}) copy-start(f32[1,1,8,8]{3,2,1,0:T(8,128)} %param.21) | copy-start | bytes 772
  1.0 0.7 %copy-start.7 = (f32[1,2,2,32]{3,2,1,0:T(2,128)S(1)}, f32[1,2,2,32]{3,2,1,0:T(2,128)}, u32[]{:S(2)}) copy-start(f32[1,2,2,32]{3,2,1,0:T(2,128)} %param.15) | copy-start | bytes 1540
  1.1 0.7 %copy-start.4 = (s32[1,1,8,8]{3,2,1,0:T(8,128)S(1)}, s32[1,1,8,8]{3,2,1,0:T(8,128)}, u32[]{:S(2)}) copy-start(s32[1,1,8,8]{3,2,1,0:T(8,128)} %param.19) | copy-start | bytes 772
  1.1 0.7 %copy-start.3 = (s32[1,1,8,8]{3,2,1,0:T(8,128)S(1)}, s32[1,1,8,8]{3,2,1,0:T(8,128)}, u32[]{:S(2)}) copy-start(s32[1,1,8,8]{3,2,1,0:T(8,128)} %param.17) | copy-start | bytes 772
  1.1 0.7 %copy-start.9 = (s32[1,1,8]{2,1,0:T(1,128)S(1)}, s32[1,1,8]{2,1,0:T(1,128)}, u32[]{:S(2)}) copy-start(s32[1,1,8]{2,1,0:T(1,128)} %param.18) | copy-start | bytes 100
  1.1 0.7 %copy-start.10 = (s32[1,1,64]{2,1,0:T(1,128)S(1)}, s32[1,1,64]{2,1,0:T(1,128)}, u32[]{:S(2)}) copy-start(s32[1,1,64]{2,1,0:T(1,128)} %param.16) | copy-start | bytes 772
  2.3 7.6 %collective-permute-start.5 = (f32[168,128]{1,0:T(8,128)S(1)}, f32[168,128]{1,0:T(8,128)S(1)}, u32[]{:S(2)}, u32[]{:S(2)}) collective-permute-start(f32[168,128]{1,0:T(8,128)S(1)} %shard_map.111.after_ref.refs_0_), channel_id=1, source_target_pairs={{0,6},{1,7},{2,4},{3,5},{4,2},{5,3},{6,0},{7,1},{8,14},{9,15},{10,... | collective-permute-start | bytes 258056 | tf_op jit(solution)/shard_map/ppermute | solution.py:500
  6.2 4.7 %collective-permute-start.4 = (f32[168,128]{1,0:T(8,128)S(1)}, f32[168,128]{1,0:T(8,128)S(1)}, u32[]{:S(2)}, u32[]{:S(2)}) collective-permute-start(f32[168,128]{1,0:T(8,128)S(1)} %shard_map.111.after_ref.refs_0_), channel_id=1, source_target_pairs={{0,4},{1,5},{2,6},{3,7},{4,0},{5,1},{6,2},{7,3},{8,12},{9,13},{10,... | collective-permute-start | bytes 258056 | tf_op jit(solution)/shard_map/ppermute | solution.py:500
  6.7 4.5 %collective-permute-start.3 = (f32[168,128]{1,0:T(8,128)S(1)}, f32[168,128]{1,0:T(8,128)S(1)}, u32[]{:S(2)}, u32[]{:S(2)}) collective-permute-start(f32[168,128]{1,0:T(8,128)S(1)} %shard_map.111.after_ref.refs_0_), channel_id=1, source_target_pairs={{0,2},{1,3},{2,0},{3,1},{4,6},{5,7},{6,4},{7,5},{8,10},{9,11},{10,... | collective-permute-start | bytes 258056 | tf_op jit(solution)/shard_map/ppermute | solution.py:500
  6.8 0.7 %copy-start.8 = (f32[1,2,128]{2,1,0:T(2,128)S(1)}, f32[1,2,128]{2,1,0:T(2,128)}, u32[]{:S(2)}) copy-start(f32[1,2,128]{2,1,0:T(2,128)} %param.14) | copy-start | bytes 3076
  11.9 7.2 %collective-permute-start.8 = (f32[152,128]{1,0:T(8,128)S(1)}, f32[152,128]{1,0:T(8,128)S(1)}, u32[]{:S(2)}, u32[]{:S(2)}) collective-permute-start(f32[152,128]{1,0:T(8,128)S(1)} %get-tuple-element.40.refs_0_), channel_id=1, source_target_pairs={{24,0},{0,8},{8,16},{16,24},{25,1},{1,9},{9,17},{17,25},{26,2},{2,... | collective-permute-start | bytes 233480 | tf_op jit(solution)/shard_map/ppermute | solution.py:625
  13.5 8.0 %collective-permute-start.7 = (f32[152,128]{1,0:T(8,128)S(1)}, f32[152,128]{1,0:T(8,128)S(1)}, u32[]{:S(2)}, u32[]{:S(2)}) collective-permute-start(f32[152,128]{1,0:T(8,128)S(1)} %get-tuple-element.40.refs_0_), channel_id=1, source_target_pairs={{16,0},{24,8},{0,16},{8,24},{17,1},{25,9},{1,17},{9,25},{18,2},{26... | collective-permute-start | bytes 233480 | tf_op jit(solution)/shard_map/ppermute | solution.py:625
  16.1 5.4 %collective-permute-start.6 = (f32[152,128]{1,0:T(8,128)S(1)}, f32[152,128]{1,0:T(8,128)S(1)}, u32[]{:S(2)}, u32[]{:S(2)}) collective-permute-start(f32[152,128]{1,0:T(8,128)S(1)} %get-tuple-element.40.refs_0_), channel_id=1, source_target_pairs={{8,0},{16,8},{24,16},{0,24},{9,1},{17,9},{25,17},{1,25},{10,2},{18... | collective-permute-start | bytes 233480 | tf_op jit(solution)/shard_map/ppermute | solution.py:625
  22.0 7.5 %collective-permute-start.10 = (f32[328,128]{1,0:T(8,128)S(1)}, f32[328,128]{1,0:T(8,128)S(1)}, u32[]{:S(2)}, u32[]{:S(2)}) collective-permute-start(f32[328,128]{1,0:T(8,128)S(1)} %get-tuple-element.42.own_ref), channel_id=1, source_target_pairs={{0,7},{1,2},{2,1},{3,4},{4,3},{5,6},{6,5},{7,0},{8,15},{9,10},{10,... | collective-permute-start | bytes 503816 | tf_op jit(solution)/shard_map/ppermute | solution.py:529
  22.1 7.5 %collective-permute-start.9 = (f32[328,128]{1,0:T(8,128)S(1)}, f32[328,128]{1,0:T(8,128)S(1)}, u32[]{:S(2)}, u32[]{:S(2)}) collective-permute-start(f32[328,128]{1,0:T(8,128)S(1)} %get-tuple-element.42.own_ref), channel_id=1, source_target_pairs={{0,1},{1,0},{2,3},{3,2},{4,5},{5,4},{6,7},{7,6},{8,9},{9,8},{10,11... | collective-permute-start | bytes 503816 | tf_op jit(solution)/shard_map/ppermute | solution.py:500
  23.7 5.5 %collective-permute-start.11 = (f32[128,128]{1,0:T(8,128)S(1)}, f32[128,128]{1,0:T(8,128)S(1)}, u32[]{:S(2)}, u32[]{:S(2)}) collective-permute-start(f32[128,128]{1,0:T(8,128)S(1)} %get-tuple-element.43), channel_id=1, source_target_pairs={{2,0},{3,1},{4,2},{5,3},{6,4},{7,5},{0,6},{1,7},{10,8},{11,9},{12,... | collective-permute-start | bytes 196616 | tf_op jit(solution)/shard_map/ppermute | solution.py:637
  30.5 1.4 %collective-permute-start.12 = (f32[8,128]{1,0:T(8,128)S(1)}, f32[8,128]{1,0:T(8,128)S(1)}, u32[]{:S(2)}, u32[]{:S(2)}) collective-permute-start(f32[8,128]{1,0:T(8,128)S(1)} %get-tuple-element.50), channel_id=1, source_target_pairs={{0,1},{1,0},{2,3},{3,2},{4,5},{5,4},{6,7},{7,6},{8,9},{9,8},{10,11... | collective-permute-start | bytes 12296 | tf_op jit(solution)/shard_map/ppermute | solution.py:500
  31.9 4.5 %collective-permute-start.14 = (f32[8,128]{1,0:T(8,128)S(1)}, f32[8,128]{1,0:T(8,128)S(1)}, u32[]{:S(2)}, u32[]{:S(2)}) collective-permute-start(f32[8,128]{1,0:T(8,128)S(1)} %add.3.refs_0_), channel_id=1, source_target_pairs={{0,6},{1,7},{2,4},{3,5},{4,2},{5,3},{6,0},{7,1},{8,14},{9,15},{10,... | collective-permute-start | bytes 12296 | tf_op jit(solution)/shard_map/ppermute | solution.py:500
  33.3 3.6 %collective-permute-start.13 = (f32[8,128]{1,0:T(8,128)S(1)}, f32[8,128]{1,0:T(8,128)S(1)}, u32[]{:S(2)}, u32[]{:S(2)}) collective-permute-start(f32[8,128]{1,0:T(8,128)S(1)} %add.3.refs_0_), channel_id=1, source_target_pairs={{0,2},{1,5},{2,0},{3,7},{4,6},{5,1},{6,4},{7,3},{8,10},{9,13},{10,... | collective-permute-start | bytes 12296 | tf_op jit(solution)/shard_map/ppermute | solution.py:519
  36.9 1.2 %collective-permute-start.15 = (f32[8,128]{1,0:T(8,128)S(1)}, f32[8,128]{1,0:T(8,128)S(1)}, u32[]{:S(2)}, u32[]{:S(2)}) collective-permute-start(f32[8,128]{1,0:T(8,128)S(1)} %collective-permute-done.13.refs_1_), channel_id=1, source_target_pairs={{0,1},{1,0},{2,3},{3,2},{4,5},{5,4},{6,7},{7,6},{8,9},{9,8},{10,11... | collective-permute-start | bytes 12296 | tf_op jit(solution)/shard_map/ppermute | solution.py:500

commit v7 on v6

--- a/solution.py
+++ b/solution.py
@@ -19,6 +19,12 @@
 def split(block):
     high = block.astype(jnp.bfloat16)
     return high, (block - high.astype(jnp.float32)).astype(jnp.bfloat16)
+
+
+def thirds(block):
+    high = block.astype(jnp.bfloat16)
+    middle, low = split(block - high.astype(jnp.float32))
+    return low, middle, high
 
 
 def narrow(left, right):
@@ -221,13 +227,13 @@
             piece = jnp.where(lane < edge, inverse[j * depth : (j + 1) * depth], 0.0)
             fold = fold + (pltpu.roll(piece, j * edge, 1) if j else piece)
         fold_ref[t * depth : (t + 1) * depth] = fold
-        part_ref[t] = dot3(inverse, rest_ref[t])
+        part_ref[t] = dot(inverse, rest_ref[t])
         put = put_ref[:, t * nodes : (t + 1) * nodes]
         reach_ref[t] = sum(
             lax.dot_general(
                 piece, put, (((1,), (1,)), ((), ())), preferred_element_type=jnp.float32
             )
-            for piece in split(inverse)
+            for piece in thirds(inverse)
         )
 
 
@@ -468,7 +474,7 @@
     for t in range(precond_ref.shape[0]):
         rim = slice(t * edge, (t + 1) * edge)
         flows = jnp.concatenate([flow_ref[rim], t0_ref[rim], t1_ref[rim]], axis=1)
-        spread = dot3(inverse_ref[t, :, :edge], flows)
+        spread = dot(inverse_ref[t, :, :edge], flows)
         width = spread.shape[1] // 3
         out_refs[0][t] = precond_ref[t] - spread[:, :width]
         out_refs[1][t] = spread[:, width : 2 * width]
@@ -485,12 +491,12 @@
     l1, l2 = a01 / a00, a02 / a00
     d1 = a02 - l1 * a01
     e12 = a12 - l2 * a01
-    l12 = e12 / d1
+    l12 = jnp.where(d1 > 0.0, e12 / d1, 0.0)
     d2 = a22 - l2 * a02 - l12 * e12
     y1 = m[1] - l1 * m[0]
     y2 = m[2] - l2 * m[0] - l12 * y1
-    c2 = y2 / d2
-    c1 = y1 / d1 - l12 * c2
+    c2 = jnp.where(d2 > 0.0, y2 / d2, 0.0)
+    c1 = jnp.where(d1 > 0.0, y1 / d1 - l12 * c2, 0.0)
     c0 = m[0] / a00 - l1 * c1 - l2 * c2
     for t in range(tiles):
         out_ref[t] = volt_ref[t] + c0 * z0_ref[t] + c1 * z1_ref[t] + c2 * z2_ref[t]

time: 39.3 us -> 38.9 us (0.990); the launches traced: 38.8 us -> 38.8 us
  no operation moved by 1% of the time
where the time goes in v7:
time: 38.9 us; the launch traced here: 38.8 us
  starting transfers between devices  18 us (46%)
  waiting for transfers between devices  13.1 us (34%)
  Pallas kernels  6.16 us (16%)
  local copies, waits for them, and re-layouts  1.37 us (4%)
    ppermute x10, starting transfers between devices, other(): return lax.ppermute(block, axis, [(i, i ^ distance) for i in range(count)])  9.11 us
    pallas_call x9, Pallas kernels, run(): pl.pallas_call(kernel, out_shape=shapes, in_specs=[vmem] * len(args), out...  6.16 us
    ppermute x3, starting transfers between devices, local(): lax.ppermute(message, 'row', [((i + k) % rows, i) for i in range(rows)])  5.57 us
    ppermute x1, waiting for transfers between devices, local(): far = lax.ppermute(far, 'col', [((i + 2) % cols, i) for i in range(cols)])  4.18 us
    ppermute x10, waiting for transfers between devices, other(): return lax.ppermute(block, axis, [(i, i ^ distance) for i in range(count)])  4.14 us
    ppermute x3, waiting for transfers between devices, local(): lax.ppermute(message, 'row', [((i + k) % rows, i) for i in range(rows)])  4.08 us
    ppermute x1, starting transfers between devices, sum_stages(): brought = lax.ppermute(block, axis, route)  1.86 us
    unnamed x22, local copies, waits for them, and re-layouts  1.37 us
  transfers between devices with their start and end apart: 16, of which 11 were waited for; matrix products, arithmetic and copies ran while one was open for 0% of the time, Pallas kernels for 8%

profile of v7, /device:TPU:0, one launch (start us, length us, event | category | flops | bytes accessed | tf_op | source)
XLA Modules:
  0.0 38.8 jit_solution(3865731087449130254)
XLA Ops:
  0.0 0.5 %collective-permute-start.2 = (s32[1,1,64]{2,1,0:T(1,128)}, s32[1,1,64]{2,1,0:T(1,128)S(1)}, u32[]{:S(2)}, u32[]{:S(2)}) collective-permute-start(s32[1,1,64]{2,1,0:T(1,128)} %param.16), channel_id=1, source_target_pairs={{0,1},{1,0},{2,3},{3,2},{4,5},{5,4},{6,7},{7,6},{8,9},{9,8},{10,11... | collective-permute-start | bytes 776 | tf_op jit(solution)/shard_map/ppermute | solution.py:506
  0.5 0.1 collective-permute-start.1
  0.6 0.4 %collective-permute-start = (f32[1,2,128,128]{3,2,1,0:T(8,128)}, f32[1,2,128,128]{3,2,1,0:T(8,128)S(1)}, u32[]{:S(2)}, u32[]{:S(2)}) collective-permute-start(f32[1,2,128,128]{3,2,1,0:T(8,128)} %param.11), channel_id=1, source_target_pairs={{0,1},{1,0},{2,3},{3,2},{4,5},{5,4},{6,7},{7,6},{8,9},{9,8},{10,11... | collective-permute-start | bytes 393224 | tf_op jit(solution)/shard_map/ppermute | solution.py:506
  1.1 0.0 copy-start.4
  1.1 0.0 copy-start.3
  1.1 0.0 copy-start.9
  1.1 0.0 copy-start.10
  1.1 0.6 %copy-done.5 = s32[1,1,8,8]{3,2,1,0:T(8,128)S(1)} copy-done((s32[1,1,8,8]{3,2,1,0:T(8,128)S(1)}, s32[1,1,8,8]{3,2,1,0:T(8,128)}, u32[]{:S(2)}) %copy-start.5) | copy-done | bytes 280
  1.7 0.0 copy-done.6
  1.7 0.0 copy-done.7
  1.8 0.0 copy-done.4
  1.8 0.0 copy-done.3
  1.8 0.3 shard_map.110
  2.1 0.0 collective-permute-done.2
  2.1 0.0 collective-permute-done.1
  2.1 0.1 collective-permute-done
  2.2 0.1 shard_map.111.after_ref.refs_0_
  2.3 3.9 %collective-permute-start.5 = (f32[168,128]{1,0:T(8,128)S(1)}, f32[168,128]{1,0:T(8,128)S(1)}, u32[]{:S(2)}, u32[]{:S(2)}) collective-permute-start(f32[168,128]{1,0:T(8,128)S(1)} %shard_map.111.after_ref.refs_0_), channel_id=1, source_target_pairs={{0,6},{1,7},{2,4},{3,5},{4,2},{5,3},{6,0},{7,1},{8,14},{9,15},{10,... | collective-permute-start | bytes 258056 | tf_op jit(solution)/shard_map/ppermute | solution.py:506
  6.2 0.5 %collective-permute-start.4 = (f32[168,128]{1,0:T(8,128)S(1)}, f32[168,128]{1,0:T(8,128)S(1)}, u32[]{:S(2)}, u32[]{:S(2)}) collective-permute-start(f32[168,128]{1,0:T(8,128)S(1)} %shard_map.111.after_ref.refs_0_), channel_id=1, source_target_pairs={{0,4},{1,5},{2,6},{3,7},{4,0},{5,1},{6,2},{7,3},{8,12},{9,13},{10,... | collective-permute-start | bytes 258056 | tf_op jit(solution)/shard_map/ppermute | solution.py:506
  6.7 0.1 collective-permute-start.3
  6.8 0.7 %copy-done.8 = f32[1,2,128]{2,1,0:T(2,128)S(1)} copy-done((f32[1,2,128]{2,1,0:T(2,128)S(1)}, f32[1,2,128]{2,1,0:T(2,128)}, u32[]{:S(2)}) %copy-start.8) | copy-done | bytes 1048
  7.5 2.5 %shard_map.112 = (f32[2,128,128]{2,1,0:T(8,128)S(1)}, f32[16,128]{1,0:T(8,128)S(1)}, f32[2,128,128]{2,1,0:T(8,128)S(1)}, f32[2,128,64]{2,1,0:T(8,128)S(1)}) custom-call(f32[128,128]{1,0:T(8,128)S(1)} %shard_map.109.eye_ref, f32[2,128,128]{2,1,0:T(8,128)S(1)} %bitcast.17, f32[2,128]{1,0:T(2,128)S(1)} %bitcast.31, ...), custom_call_target="tpu_custom_call" | custom-call | flops 4000000000 | bytes 816128 | tf_op jit(solution)/shard_map/pallas_call | solution.py:55
  10.0 0.0 collective-permute-done.5.refs_3_
  10.0 0.9 %collective-permute-done.4.refs_2_ = f32[168,128]{1,0:T(8,128)S(1)} collective-permute-done((f32[168,128]{1,0:T(8,128)S(1)}, f32[168,128]{1,0:T(8,128)S(1)}, u32[]{:S(2)}, u32[]{:S(2)}) %collective-permute-start.4) | collective-permute-done | bytes 86048 | tf_op jit(solution)/shard_map/ppermute | solution.py:506
  10.9 0.3 collective-permute-done.3.refs_1_
  11.2 0.7 %shard_map.113 = (f32[152,128]{1,0:T(8,128)S(1)}, f32[2,128,128]{2,1,0:T(8,128)S(1)}) custom-call(f32[2,128,128]{2,1,0:T(8,128)S(1)} %bitcast.20, f32[2,128,128]{2,1,0:T(8,128)S(1)} %bitcast.23, f32[2,2,32]{2,1,0:T(2,128)S(1)} %bitcast.30, f32[2,128,128]{2,1,0:T(8,128)S(1)} %get-tuple-element.32.inverse_ref, f32[16,128]{1,0:T(8,128)S(1)} %get-tuple-element.33.fold_ref, ...), custom_call_target="tpu_custom_call" | custom-call | flops 4000000000 | bytes 1532416 | tf_op jit(solution)/shard_map/pallas_call | solution.py:55
  11.9 1.6 %collective-permute-start.8 = (f32[152,128]{1,0:T(8,128)S(1)}, f32[152,128]{1,0:T(8,128)S(1)}, u32[]{:S(2)}, u32[]{:S(2)}) collective-permute-start(f32[152,128]{1,0:T(8,128)S(1)} %get-tuple-element.40.refs_0_), channel_id=1, source_target_pairs={{24,0},{0,8},{8,16},{16,24},{25,1},{1,9},{9,17},{17,25},{26,2},{2,... | collective-permute-start | bytes 233480 | tf_op jit(solution)/shard_map/ppermute | solution.py:631
  13.5 2.6 %collective-permute-start.7 = (f32[152,128]{1,0:T(8,128)S(1)}, f32[152,128]{1,0:T(8,128)S(1)}, u32[]{:S(2)}, u32[]{:S(2)}) collective-permute-start(f32[152,128]{1,0:T(8,128)S(1)} %get-tuple-element.40.refs_0_), channel_id=1, source_target_pairs={{16,0},{24,8},{0,16},{8,24},{17,1},{25,9},{1,17},{9,25},{18,2},{26... | collective-permute-start | bytes 233480 | tf_op jit(solution)/shard_map/ppermute | solution.py:631
  16.1 1.3 %collective-permute-start.6 = (f32[152,128]{1,0:T(8,128)S(1)}, f32[152,128]{1,0:T(8,128)S(1)}, u32[]{:S(2)}, u32[]{:S(2)}) collective-permute-start(f32[152,128]{1,0:T(8,128)S(1)} %get-tuple-element.40.refs_0_), channel_id=1, source_target_pairs={{8,0},{16,8},{24,16},{0,24},{9,1},{17,9},{25,17},{1,25},{10,2},{18... | collective-permute-start | bytes 233480 | tf_op jit(solution)/shard_map/ppermute | solution.py:631
  17.5 1.7 %collective-permute-done.8.refs_3_ = f32[152,128]{1,0:T(8,128)S(1)} collective-permute-done((f32[152,128]{1,0:T(8,128)S(1)}, f32[152,128]{1,0:T(8,128)S(1)}, u32[]{:S(2)}, u32[]{:S(2)}) %collective-permute-start.8) | collective-permute-done | bytes 77856 | tf_op jit(solution)/shard_map/ppermute | solution.py:631
  19.1 2.4 %collective-permute-done.7.refs_2_ = f32[152,128]{1,0:T(8,128)S(1)} collective-permute-done((f32[152,128]{1,0:T(8,128)S(1)}, f32[152,128]{1,0:T(8,128)S(1)}, u32[]{:S(2)}, u32[]{:S(2)}) %collective-permute-start.7) | collective-permute-done | bytes 77856 | tf_op jit(solution)/shard_map/ppermute | solution.py:631
  21.6 0.0 collective-permute-done.6.refs_1_
  21.6 0.4 %shard_map.114 = (f32[328,128]{1,0:T(8,128)S(1)}, f32[128,128]{1,0:T(8,128)S(1)}, f32[64,128]{1,0:T(8,128)S(1)}, f32[8,128]{1,0:T(8,128)S(1)}) custom-call(f32[152,128]{1,0:T(8,128)S(1)} %get-tuple-element.40.refs_0_, f32[152,128]{1,0:T(8,128)S(1)} %collective-permute-done.6.refs_1_, f32[152,128]{1,0:T(8,128)S(1)} %collective-permute-done.7.refs_2_, ...), custom_call_target="tpu_custom_call" | custom-call | flops 4000000000 | bytes 581632 | tf_op jit(solution)/shard_map/pallas_call | solution.py:55
  22.0 0.1 collective-permute-start.10
  22.1 1.7 %collective-permute-start.9 = (f32[328,128]{1,0:T(8,128)S(1)}, f32[328,128]{1,0:T(8,128)S(1)}, u32[]{:S(2)}, u32[]{:S(2)}) collective-permute-start(f32[328,128]{1,0:T(8,128)S(1)} %get-tuple-element.42.own_ref), channel_id=1, source_target_pairs={{0,1},{1,0},{2,3},{3,2},{4,5},{5,4},{6,7},{7,6},{8,9},{9,8},{10,11... | collective-permute-start | bytes 503816 | tf_op jit(solution)/shard_map/ppermute | solution.py:506
  23.7 1.4 %collective-permute-start.11 = (f32[128,128]{1,0:T(8,128)S(1)}, f32[128,128]{1,0:T(8,128)S(1)}, u32[]{:S(2)}, u32[]{:S(2)}) collective-permute-start(f32[128,128]{1,0:T(8,128)S(1)} %get-tuple-element.43), channel_id=1, source_target_pairs={{2,0},{3,1},{4,2},{5,3},{6,4},{7,5},{0,6},{1,7},{10,8},{11,9},{12,... | collective-permute-start | bytes 196616 | tf_op jit(solution)/shard_map/ppermute | solution.py:643
  25.1 4.2 %collective-permute-done.11.far_ref = f32[128,128]{1,0:T(8,128)S(1)} collective-permute-done((f32[128,128]{1,0:T(8,128)S(1)}, f32[128,128]{1,0:T(8,128)S(1)}, u32[]{:S(2)}, u32[]{:S(2)}) %collective-permute-start.11) | collective-permute-done | bytes 65568 | tf_op jit(solution)/shard_map/ppermute | solution.py:643
  29.3 0.3 collective-permute-done.10.outer_ref
  29.5 1.0 %shard_map.115 = (f32[8,128]{1,0:T(8,128)S(1)}, f32[64,128]{1,0:T(8,128)S(1)}, f32[64,128]{1,0:T(8,128)S(1)}) custom-call(f32[328,128]{1,0:T(8,128)S(1)} %get-tuple-element.42.own_ref, f32[328,128]{1,0:T(8,128)S(1)} %collective-permute-done.9.inner_ref, f32[328,128]{1,0:T(8,128)S(1)} %collective-permute-done.10.outer_ref, ...), custom_call_target="tpu_custom_call" | custom-call | flops 4000000000 | bytes 643072 | tf_op jit(solution)/shard_map/pallas_call | solution.py:55
  30.5 0.5 %collective-permute-start.12 = (f32[8,128]{1,0:T(8,128)S(1)}, f32[8,128]{1,0:T(8,128)S(1)}, u32[]{:S(2)}, u32[]{:S(2)}) collective-permute-start(f32[8,128]{1,0:T(8,128)S(1)} %get-tuple-element.50), channel_id=1, source_target_pairs={{0,1},{1,0},{2,3},{3,2},{4,5},{5,4},{6,7},{7,6},{8,9},{9,8},{10,11... | collective-permute-start | bytes 12296 | tf_op jit(solution)/shard_map/ppermute | solution.py:506
  31.1 0.8 %collective-permute-done.12 = f32[8,128]{1,0:T(8,128)S(1)} collective-permute-done((f32[8,128]{1,0:T(8,128)S(1)}, f32[8,128]{1,0:T(8,128)S(1)}, u32[]{:S(2)}, u32[]{:S(2)}) %collective-permute-start.12) | collective-permute-done | bytes 4128 | tf_op jit(solution)/shard_map/ppermute | solution.py:506
  31.9 1.4 %collective-permute-start.14 = (f32[8,128]{1,0:T(8,128)S(1)}, f32[8,128]{1,0:T(8,128)S(1)}, u32[]{:S(2)}, u32[]{:S(2)}) collective-permute-start(f32[8,128]{1,0:T(8,128)S(1)} %add.3.refs_0_), channel_id=1, source_target_pairs={{0,6},{1,7},{2,4},{3,5},{4,2},{5,3},{6,0},{7,1},{8,14},{9,15},{10,... | collective-permute-start | bytes 12296 | tf_op jit(solution)/shard_map/ppermute | solution.py:506
  33.3 1.9 %collective-permute-start.13 = (f32[8,128]{1,0:T(8,128)S(1)}, f32[8,128]{1,0:T(8,128)S(1)}, u32[]{:S(2)}, u32[]{:S(2)}) collective-permute-start(f32[8,128]{1,0:T(8,128)S(1)} %add.3.refs_0_), channel_id=1, source_target_pairs={{0,2},{1,5},{2,0},{3,7},{4,6},{5,1},{6,4},{7,3},{8,10},{9,13},{10,... | collective-permute-start | bytes 12296 | tf_op jit(solution)/shard_map/ppermute | solution.py:525
  35.1 1.3 %collective-permute-done.14.refs_2_ = f32[8,128]{1,0:T(8,128)S(1)} collective-permute-done((f32[8,128]{1,0:T(8,128)S(1)}, f32[8,128]{1,0:T(8,128)S(1)}, u32[]{:S(2)}, u32[]{:S(2)}) %collective-permute-start.14) | collective-permute-done | bytes 4128 | tf_op jit(solution)/shard_map/ppermute | solution.py:506
  36.4 0.5 %collective-permute-done.13.refs_1_ = f32[8,128]{1,0:T(8,128)S(1)} collective-permute-done((f32[8,128]{1,0:T(8,128)S(1)}, f32[8,128]{1,0:T(8,128)S(1)}, u32[]{:S(2)}, u32[]{:S(2)}) %collective-permute-start.13) | collective-permute-done | bytes 4128 | tf_op jit(solution)/shard_map/ppermute | solution.py:525
  36.9 0.4 %shard_map.116 = (f32[2,128,128]{2,1,0:T(8,128)S(1)}, f32[2,128,128]{2,1,0:T(8,128)S(1)}, f32[2,128,128]{2,1,0:T(8,128)S(1)}) custom-call(f32[2,128,128]{2,1,0:T(8,128)S(1)} %get-tuple-element.39.precond_ref, f32[2,128,128]{2,1,0:T(8,128)S(1)} %get-tuple-element.32.inverse_ref, f32[64,128]{1,0:T(8,128)S(1)} %get-tuple-element.41.flow_ref, ...), custom_call_target="tpu_custom_call" | custom-call | flops 4000000000 | bytes 753664 | tf_op jit(solution)/shard_map/pallas_call | solution.py:55
  37.3 0.7 %collective-permute-done.15.refs_3_ = f32[8,128]{1,0:T(8,128)S(1)} collective-permute-done((f32[8,128]{1,0:T(8,128)S(1)}, f32[8,128]{1,0:T(8,128)S(1)}, u32[]{:S(2)}, u32[]{:S(2)}) %collective-permute-start.15) | collective-permute-done | bytes 4128 | tf_op jit(solution)/shard_map/ppermute | solution.py:506
  38.0 0.7 %shard_map.117 = f32[2,128,128]{2,1,0:T(8,128)} custom-call(f32[2,128,128]{2,1,0:T(8,128)S(1)} %bitcast.21, f32[2,128,128]{2,1,0:T(8,128)S(1)} %get-tuple-element.47.z0_ref, f32[2,128,128]{2,1,0:T(8,128)S(1)} %get-tuple-element.48.z1_ref, f32[2,128,128]{2,1,0:T(8,128)S(1)} %get-tuple-element.49.z2_ref, f32[8,128]{1,0:T(8,128)S(1)} %add.3.refs_0_, ...), custom_call_target="tpu_custom_call" | custom-call | flops 4000000000 | bytes 671744 | tf_op jit(solution)/shard_map/pallas_call | solution.py:55
  (16 shorter events, 0.0 us)
Async XLA Ops:
  0.0 1.1 %copy-start.2 = (f32[1,2,128,128]{3,2,1,0:T(8,128)S(1)}, f32[1,2,128,128]{3,2,1,0:T(8,128)}, u32[]{:S(2)}) copy-start(f32[1,2,128,128]{3,2,1,0:T(8,128)} %param.11) | copy-start | bytes 393220
  0.0 1.1 %copy-start.1 = (f32[1,2,128,128]{3,2,1,0:T(8,128)S(1)}, f32[1,2,128,128]{3,2,1,0:T(8,128)}, u32[]{:S(2)}) copy-start(f32[1,2,128,128]{3,2,1,0:T(8,128)} %param.13) | copy-start | bytes 393220
  0.0 1.1 %copy-start = (f32[1,2,128,128]{3,2,1,0:T(8,128)S(1)}, f32[1,2,128,128]{3,2,1,0:T(8,128)}, u32[]{:S(2)}) copy-start(f32[1,2,128,128]{3,2,1,0:T(8,128)} %param.12) | copy-start | bytes 393220
  0.0 2.1 %collective-permute-start.2 = (s32[1,1,64]{2,1,0:T(1,128)}, s32[1,1,64]{2,1,0:T(1,128)S(1)}, u32[]{:S(2)}, u32[]{:S(2)}) collective-permute-start(s32[1,1,64]{2,1,0:T(1,128)} %param.16), channel_id=1, source_target_pairs={{0,1},{1,0},{2,3},{3,2},{4,5},{5,4},{6,7},{7,6},{8,9},{9,8},{10,11... | collective-permute-start | bytes 776 | tf_op jit(solution)/shard_map/ppermute | solution.py:506
  0.5 1.6 %collective-permute-start.1 = (f32[1,2,2,32]{3,2,1,0:T(2,128)}, f32[1,2,2,32]{3,2,1,0:T(2,128)S(1)}, u32[]{:S(2)}, u32[]{:S(2)}) collective-permute-start(f32[1,2,2,32]{3,2,1,0:T(2,128)} %param.15), channel_id=1, source_target_pairs={{0,1},{1,0},{2,3},{3,2},{4,5},{5,4},{6,7},{7,6},{8,9},{9,8},{10,11... | collective-permute-start | bytes 1544 | tf_op jit(solution)/shard_map/ppermute | solution.py:506
  0.6 1.6 %collective-permute-start = (f32[1,2,128,128]{3,2,1,0:T(8,128)}, f32[1,2,128,128]{3,2,1,0:T(8,128)S(1)}, u32[]{:S(2)}, u32[]{:S(2)}) collective-permute-start(f32[1,2,128,128]{3,2,1,0:T(8,128)} %param.11), channel_id=1, source_target_pairs={{0,1},{1,0},{2,3},{3,2},{4,5},{5,4},{6,7},{7,6},{8,9},{9,8},{10,11... | collective-permute-start | bytes 393224 | tf_op jit(solution)/shard_map/ppermute | solution.py:506
  1.0 0.7 %copy-start.5 = (s32[1,1,8,8]{3,2,1,0:T(8,128)S(1)}, s32[1,1,8,8]{3,2,1,0:T(8,128)}, u32[]{:S(2)}) copy-start(s32[1,1,8,8]{3,2,1,0:T(8,128)} %param.20) | copy-start | bytes 772
  1.0 0.7 %copy-start.6 = (f32[1,1,8,8]{3,2,1,0:T(8,128)S(1)}, f32[1,1,8,8]{3,2,1,0:T(8,128)}, u32[]{:S(2)}) copy-start(f32[1,1,8,8]{3,2,1,0:T(8,128)} %param.21) | copy-start | bytes 772
  1.0 0.7 %copy-start.7 = (f32[1,2,2,32]{3,2,1,0:T(2,128)S(1)}, f32[1,2,2,32]{3,2,1,0:T(2,128)}, u32[]{:S(2)}) copy-start(f32[1,2,2,32]{3,2,1,0:T(2,128)} %param.15) | copy-start | bytes 1540
  1.1 0.7 %copy-start.4 = (s32[1,1,8,8]{3,2,1,0:T(8,128)S(1)}, s32[1,1,8,8]{3,2,1,0:T(8,128)}, u32[]{:S(2)}) copy-start(s32[1,1,8,8]{3,2,1,0:T(8,128)} %param.19) | copy-start | bytes 772
  1.1 0.7 %copy-start.3 = (s32[1,1,8,8]{3,2,1,0:T(8,128)S(1)}, s32[1,1,8,8]{3,2,1,0:T(8,128)}, u32[]{:S(2)}) copy-start(s32[1,1,8,8]{3,2,1,0:T(8,128)} %param.17) | copy-start | bytes 772
  1.1 0.7 %copy-start.9 = (s32[1,1,8]{2,1,0:T(1,128)S(1)}, s32[1,1,8]{2,1,0:T(1,128)}, u32[]{:S(2)}) copy-start(s32[1,1,8]{2,1,0:T(1,128)} %param.18) | copy-start | bytes 100
  1.1 0.7 %copy-start.10 = (s32[1,1,64]{2,1,0:T(1,128)S(1)}, s32[1,1,64]{2,1,0:T(1,128)}, u32[]{:S(2)}) copy-start(s32[1,1,64]{2,1,0:T(1,128)} %param.16) | copy-start | bytes 772
  2.3 7.7 %collective-permute-start.5 = (f32[168,128]{1,0:T(8,128)S(1)}, f32[168,128]{1,0:T(8,128)S(1)}, u32[]{:S(2)}, u32[]{:S(2)}) collective-permute-start(f32[168,128]{1,0:T(8,128)S(1)} %shard_map.111.after_ref.refs_0_), channel_id=1, source_target_pairs={{0,6},{1,7},{2,4},{3,5},{4,2},{5,3},{6,0},{7,1},{8,14},{9,15},{10,... | collective-permute-start | bytes 258056 | tf_op jit(solution)/shard_map/ppermute | solution.py:506
  6.2 4.7 %collective-permute-start.4 = (f32[168,128]{1,0:T(8,128)S(1)}, f32[168,128]{1,0:T(8,128)S(1)}, u32[]{:S(2)}, u32[]{:S(2)}) collective-permute-start(f32[168,128]{1,0:T(8,128)S(1)} %shard_map.111.after_ref.refs_0_), channel_id=1, source_target_pairs={{0,4},{1,5},{2,6},{3,7},{4,0},{5,1},{6,2},{7,3},{8,12},{9,13},{10,... | collective-permute-start | bytes 258056 | tf_op jit(solution)/shard_map/ppermute | solution.py:506
  6.7 4.5 %collective-permute-start.3 = (f32[168,128]{1,0:T(8,128)S(1)}, f32[168,128]{1,0:T(8,128)S(1)}, u32[]{:S(2)}, u32[]{:S(2)}) collective-permute-start(f32[168,128]{1,0:T(8,128)S(1)} %shard_map.111.after_ref.refs_0_), channel_id=1, source_target_pairs={{0,2},{1,3},{2,0},{3,1},{4,6},{5,7},{6,4},{7,5},{8,10},{9,11},{10,... | collective-permute-start | bytes 258056 | tf_op jit(solution)/shard_map/ppermute | solution.py:506
  6.8 0.7 %copy-start.8 = (f32[1,2,128]{2,1,0:T(2,128)S(1)}, f32[1,2,128]{2,1,0:T(2,128)}, u32[]{:S(2)}) copy-start(f32[1,2,128]{2,1,0:T(2,128)} %param.14) | copy-start | bytes 3076
  11.9 7.2 %collective-permute-start.8 = (f32[152,128]{1,0:T(8,128)S(1)}, f32[152,128]{1,0:T(8,128)S(1)}, u32[]{:S(2)}, u32[]{:S(2)}) collective-permute-start(f32[152,128]{1,0:T(8,128)S(1)} %get-tuple-element.40.refs_0_), channel_id=1, source_target_pairs={{24,0},{0,8},{8,16},{16,24},{25,1},{1,9},{9,17},{17,25},{26,2},{2,... | collective-permute-start | bytes 233480 | tf_op jit(solution)/shard_map/ppermute | solution.py:631
  13.5 8.0 %collective-permute-start.7 = (f32[152,128]{1,0:T(8,128)S(1)}, f32[152,128]{1,0:T(8,128)S(1)}, u32[]{:S(2)}, u32[]{:S(2)}) collective-permute-start(f32[152,128]{1,0:T(8,128)S(1)} %get-tuple-element.40.refs_0_), channel_id=1, source_target_pairs={{16,0},{24,8},{0,16},{8,24},{17,1},{25,9},{1,17},{9,25},{18,2},{26... | collective-permute-start | bytes 233480 | tf_op jit(solution)/shard_map/ppermute | solution.py:631
  16.1 5.4 %collective-permute-start.6 = (f32[152,128]{1,0:T(8,128)S(1)}, f32[152,128]{1,0:T(8,128)S(1)}, u32[]{:S(2)}, u32[]{:S(2)}) collective-permute-start(f32[152,128]{1,0:T(8,128)S(1)} %get-tuple-element.40.refs_0_), channel_id=1, source_target_pairs={{8,0},{16,8},{24,16},{0,24},{9,1},{17,9},{25,17},{1,25},{10,2},{18... | collective-permute-start | bytes 233480 | tf_op jit(solution)/shard_map/ppermute | solution.py:631
  22.0 7.5 %collective-permute-start.10 = (f32[328,128]{1,0:T(8,128)S(1)}, f32[328,128]{1,0:T(8,128)S(1)}, u32[]{:S(2)}, u32[]{:S(2)}) collective-permute-start(f32[328,128]{1,0:T(8,128)S(1)} %get-tuple-element.42.own_ref), channel_id=1, source_target_pairs={{0,7},{1,2},{2,1},{3,4},{4,3},{5,6},{6,5},{7,0},{8,15},{9,10},{10,... | collective-permute-start | bytes 503816 | tf_op jit(solution)/shard_map/ppermute | solution.py:535
  22.1 7.5 %collective-permute-start.9 = (f32[328,128]{1,0:T(8,128)S(1)}, f32[328,128]{1,0:T(8,128)S(1)}, u32[]{:S(2)}, u32[]{:S(2)}) collective-permute-start(f32[328,128]{1,0:T(8,128)S(1)} %get-tuple-element.42.own_ref), channel_id=1, source_target_pairs={{0,1},{1,0},{2,3},{3,2},{4,5},{5,4},{6,7},{7,6},{8,9},{9,8},{10,11... | collective-permute-start | bytes 503816 | tf_op jit(solution)/shard_map/ppermute | solution.py:506
  23.7 5.5 %collective-permute-start.11 = (f32[128,128]{1,0:T(8,128)S(1)}, f32[128,128]{1,0:T(8,128)S(1)}, u32[]{:S(2)}, u32[]{:S(2)}) collective-permute-start(f32[128,128]{1,0:T(8,128)S(1)} %get-tuple-element.43), channel_id=1, source_target_pairs={{2,0},{3,1},{4,2},{5,3},{6,4},{7,5},{0,6},{1,7},{10,8},{11,9},{12,... | collective-permute-start | bytes 196616 | tf_op jit(solution)/shard_map/ppermute | solution.py:643
  30.5 1.4 %collective-permute-start.12 = (f32[8,128]{1,0:T(8,128)S(1)}, f32[8,128]{1,0:T(8,128)S(1)}, u32[]{:S(2)}, u32[]{:S(2)}) collective-permute-start(f32[8,128]{1,0:T(8,128)S(1)} %get-tuple-element.50), channel_id=1, source_target_pairs={{0,1},{1,0},{2,3},{3,2},{4,5},{5,4},{6,7},{7,6},{8,9},{9,8},{10,11... | collective-permute-start | bytes 12296 | tf_op jit(solution)/shard_map/ppermute | solution.py:506
  31.9 4.5 %collective-permute-start.14 = (f32[8,128]{1,0:T(8,128)S(1)}, f32[8,128]{1,0:T(8,128)S(1)}, u32[]{:S(2)}, u32[]{:S(2)}) collective-permute-start(f32[8,128]{1,0:T(8,128)S(1)} %add.3.refs_0_), channel_id=1, source_target_pairs={{0,6},{1,7},{2,4},{3,5},{4,2},{5,3},{6,0},{7,1},{8,14},{9,15},{10,... | collective-permute-start | bytes 12296 | tf_op jit(solution)/shard_map/ppermute | solution.py:506
  33.3 3.6 %collective-permute-start.13 = (f32[8,128]{1,0:T(8,128)S(1)}, f32[8,128]{1,0:T(8,128)S(1)}, u32[]{:S(2)}, u32[]{:S(2)}) collective-permute-start(f32[8,128]{1,0:T(8,128)S(1)} %add.3.refs_0_), channel_id=1, source_target_pairs={{0,2},{1,5},{2,0},{3,7},{4,6},{5,1},{6,4},{7,3},{8,10},{9,13},{10,... | collective-permute-start | bytes 12296 | tf_op jit(solution)/shard_map/ppermute | solution.py:525
  36.9 1.2 %collective-permute-start.15 = (f32[8,128]{1,0:T(8,128)S(1)}, f32[8,128]{1,0:T(8,128)S(1)}, u32[]{:S(2)}, u32[]{:S(2)}) collective-permute-start(f32[8,128]{1,0:T(8,128)S(1)} %collective-permute-done.13.refs_1_), channel_id=1, source_target_pairs={{0,1},{1,0},{2,3},{3,2},{4,5},{5,4},{6,7},{7,6},{8,9},{9,8},{10,11... | collective-permute-start | bytes 12296 | tf_op jit(solution)/shard_map/ppermute | solution.py:506

commit v8 on v7

--- a/solution.py
+++ b/solution.py
@@ -124,13 +124,16 @@
     node_ref,
     weight_ref,
     driver_ref,
+    cap_ref,
     rest_ref,
     gains_ref,
     take_ref,
     put_ref,
     scale_ref,
     picked_ref,
+    held_ref,
 ):
+    held_ref[...] = cap_ref[...]
     picked_ref[...] = jnp.broadcast_to(
         to_column(driver_ref[...].astype(jnp.float32)), picked_ref.shape
     )
@@ -561,7 +564,7 @@
     mate_gain = other(track_gain, "col", cols, 1)[0]
     eye = run(eye_kernel, [(nodes, nodes)])[0]
     narrow_type = functools.partial(jax.ShapeDtypeStruct, dtype=jnp.bfloat16)
-    rest, gains, take, put, scale, picked = run(
+    rest, gains, take, put, scale, picked, held = run(
         functools.partial(sink_kernel, nets, edge),
         [
             field,
@@ -570,6 +573,7 @@
             narrow_type((slots, tiles * nodes)),
             (slots, patterns),
             (nets, patterns),
+            (tiles, nodes),
         ],
         eye,
         conduct[0],
@@ -582,6 +586,7 @@
         sink_node[0, 0],
         sink_gain[0, 0],
         driver_tile[0],
+        capacitance[0],
     )
     pair = run(
         functools.partial(pair_kernel, nets, edge),
@@ -602,7 +607,7 @@
         [field, (depth, nodes), field, (tiles, nodes, slots)],
         eye,
         conduct[0],
-        capacitance[0],
+        held,
         rest,
         put,
         pair,

time: 38.9 us -> 38.9 us (level)
  waiting for transfers between devices: 13.1 us -> 13.8 us
  local copies, waits for them, and re-layouts: 1.37 us -> 0.71 us
    unnamed x22, local copies, waits for them, and re-layouts: 1.37 us -> 0.71 us
    ppermute x10, waiting for transfers between devices: 4.14 us -> 4.78 us  [other(): return lax.ppermute(block, axis, [(i, i ^ distance) for i in range(count)])]
where the time goes in v8:
time: 38.9 us; the launch traced here: 38.8 us
  starting transfers between devices  18 us (46%)
  waiting for transfers between devices  13.8 us (35%)
  Pallas kernels  6.16 us (16%)
  local copies, waits for them, and re-layouts  0.71 us (2%)
    ppermute x10, starting transfers between devices, other(): return lax.ppermute(block, axis, [(i, i ^ distance) for i in range(count)])  9.11 us
    pallas_call x9, Pallas kernels, run(): pl.pallas_call(kernel, out_shape=shapes, in_specs=[vmem] * len(args), out...  6.16 us
    ppermute x3, starting transfers between devices, local(): lax.ppermute(message, 'row', [((i + k) % rows, i) for i in range(rows)])  5.57 us
    ppermute x10, waiting for transfers between devices, other(): return lax.ppermute(block, axis, [(i, i ^ distance) for i in range(count)])  4.78 us
    ppermute x1, waiting for transfers between devices, local(): far = lax.ppermute(far, 'col', [((i + 2) % cols, i) for i in range(cols)])  4.18 us
    ppermute x3, waiting for transfers between devices, local(): lax.ppermute(message, 'row', [((i + k) % rows, i) for i in range(rows)])  4.08 us
    ppermute x1, starting transfers between devices, sum_stages(): brought = lax.ppermute(block, axis, route)  1.86 us
    ppermute x1, starting transfers between devices, local(): far = lax.ppermute(far, 'col', [((i + 2) % cols, i) for i in range(cols)])  1.35 us
  transfers between devices with their start and end apart: 16, of which 11 were waited for; matrix products, arithmetic and copies ran while one was open for 0% of the time, Pallas kernels for 8%

profile of v8, /device:TPU:0, one launch (start us, length us, event | category | flops | bytes accessed | tf_op | source)
XLA Modules:
  0.0 38.8 jit_solution(4221529148881574711)
XLA Ops:
  0.0 0.5 %collective-permute-start.2 = (s32[1,1,64]{2,1,0:T(1,128)}, s32[1,1,64]{2,1,0:T(1,128)S(1)}, u32[]{:S(2)}, u32[]{:S(2)}) collective-permute-start(s32[1,1,64]{2,1,0:T(1,128)} %param.16), channel_id=1, source_target_pairs={{0,1},{1,0},{2,3},{3,2},{4,5},{5,4},{6,7},{7,6},{8,9},{9,8},{10,11... | collective-permute-start | bytes 776 | tf_op jit(solution)/shard_map/ppermute | solution.py:509
  0.5 0.1 collective-permute-start.1
  0.6 0.4 %collective-permute-start = (f32[1,2,128,128]{3,2,1,0:T(8,128)}, f32[1,2,128,128]{3,2,1,0:T(8,128)S(1)}, u32[]{:S(2)}, u32[]{:S(2)}) collective-permute-start(f32[1,2,128,128]{3,2,1,0:T(8,128)} %param.11), channel_id=1, source_target_pairs={{0,1},{1,0},{2,3},{3,2},{4,5},{5,4},{6,7},{7,6},{8,9},{9,8},{10,11... | collective-permute-start | bytes 393224 | tf_op jit(solution)/shard_map/ppermute | solution.py:509
  1.1 0.0 copy-start.4
  1.1 0.0 copy-start.3
  1.1 0.0 copy-start.8
  1.1 0.6 %copy-done.5 = s32[1,1,8,8]{3,2,1,0:T(8,128)S(1)} copy-done((s32[1,1,8,8]{3,2,1,0:T(8,128)S(1)}, s32[1,1,8,8]{3,2,1,0:T(8,128)}, u32[]{:S(2)}) %copy-start.5) | copy-done | bytes 280
  1.7 0.0 copy-done.6
  1.7 0.0 copy-done.7
  1.8 0.0 copy-done.10
  1.8 0.0 copy-done.4
  1.8 0.0 copy-done.3
  1.8 0.0 copy-done.8
  1.8 0.3 shard_map.110
  2.1 0.0 collective-permute-done.2
  2.1 0.0 collective-permute-done.1
  2.1 0.1 collective-permute-done
  2.2 0.1 shard_map.111.after_ref.refs_0_
  2.3 3.9 %collective-permute-start.5 = (f32[168,128]{1,0:T(8,128)S(1)}, f32[168,128]{1,0:T(8,128)S(1)}, u32[]{:S(2)}, u32[]{:S(2)}) collective-permute-start(f32[168,128]{1,0:T(8,128)S(1)} %shard_map.111.after_ref.refs_0_), channel_id=1, source_target_pairs={{0,6},{1,7},{2,4},{3,5},{4,2},{5,3},{6,0},{7,1},{8,14},{9,15},{10,... | collective-permute-start | bytes 258056 | tf_op jit(solution)/shard_map/ppermute | solution.py:509
  6.2 0.5 %collective-permute-start.4 = (f32[168,128]{1,0:T(8,128)S(1)}, f32[168,128]{1,0:T(8,128)S(1)}, u32[]{:S(2)}, u32[]{:S(2)}) collective-permute-start(f32[168,128]{1,0:T(8,128)S(1)} %shard_map.111.after_ref.refs_0_), channel_id=1, source_target_pairs={{0,4},{1,5},{2,6},{3,7},{4,0},{5,1},{6,2},{7,3},{8,12},{9,13},{10,... | collective-permute-start | bytes 258056 | tf_op jit(solution)/shard_map/ppermute | solution.py:509
  6.7 0.1 collective-permute-start.3
  6.8 2.5 %shard_map.112 = (f32[2,128,128]{2,1,0:T(8,128)S(1)}, f32[16,128]{1,0:T(8,128)S(1)}, f32[2,128,128]{2,1,0:T(8,128)S(1)}, f32[2,128,64]{2,1,0:T(8,128)S(1)}) custom-call(f32[128,128]{1,0:T(8,128)S(1)} %shard_map.109.eye_ref, f32[2,128,128]{2,1,0:T(8,128)S(1)} %bitcast.17, f32[2,128]{1,0:T(2,128)S(1)} %get-tuple-element.30.cap_ref, ...), custom_call_target="tpu_custom_call" | custom-call | flops 4000000000 | bytes 816128 | tf_op jit(solution)/shard_map/pallas_call | solution.py:55
  9.3 0.0 collective-permute-done.5.refs_3_
  9.3 1.5 %collective-permute-done.4.refs_2_ = f32[168,128]{1,0:T(8,128)S(1)} collective-permute-done((f32[168,128]{1,0:T(8,128)S(1)}, f32[168,128]{1,0:T(8,128)S(1)}, u32[]{:S(2)}, u32[]{:S(2)}) %collective-permute-start.4) | collective-permute-done | bytes 86048 | tf_op jit(solution)/shard_map/ppermute | solution.py:509
  10.9 0.3 collective-permute-done.3.refs_1_
  11.2 0.7 %shard_map.113 = (f32[152,128]{1,0:T(8,128)S(1)}, f32[2,128,128]{2,1,0:T(8,128)S(1)}) custom-call(f32[2,128,128]{2,1,0:T(8,128)S(1)} %bitcast.20, f32[2,128,128]{2,1,0:T(8,128)S(1)} %bitcast.23, f32[2,2,32]{2,1,0:T(2,128)S(1)} %bitcast.30, f32[2,128,128]{2,1,0:T(8,128)S(1)} %get-tuple-element.34.inverse_ref, f32[16,128]{1,0:T(8,128)S(1)} %get-tuple-element.35.fold_ref, ...), custom_call_target="tpu_custom_call" | custom-call | flops 4000000000 | bytes 1532416 | tf_op jit(solution)/shard_map/pallas_call | solution.py:55
  11.9 1.6 %collective-permute-start.8 = (f32[152,128]{1,0:T(8,128)S(1)}, f32[152,128]{1,0:T(8,128)S(1)}, u32[]{:S(2)}, u32[]{:S(2)}) collective-permute-start(f32[152,128]{1,0:T(8,128)S(1)} %get-tuple-element.42.refs_0_), channel_id=1, source_target_pairs={{24,0},{0,8},{8,16},{16,24},{25,1},{1,9},{9,17},{17,25},{26,2},{2,... | collective-permute-start | bytes 233480 | tf_op jit(solution)/shard_map/ppermute | solution.py:636
  13.5 2.6 %collective-permute-start.7 = (f32[152,128]{1,0:T(8,128)S(1)}, f32[152,128]{1,0:T(8,128)S(1)}, u32[]{:S(2)}, u32[]{:S(2)}) collective-permute-start(f32[152,128]{1,0:T(8,128)S(1)} %get-tuple-element.42.refs_0_), channel_id=1, source_target_pairs={{16,0},{24,8},{0,16},{8,24},{17,1},{25,9},{1,17},{9,25},{18,2},{26... | collective-permute-start | bytes 233480 | tf_op jit(solution)/shard_map/ppermute | solution.py:636
  16.1 1.3 %collective-permute-start.6 = (f32[152,128]{1,0:T(8,128)S(1)}, f32[152,128]{1,0:T(8,128)S(1)}, u32[]{:S(2)}, u32[]{:S(2)}) collective-permute-start(f32[152,128]{1,0:T(8,128)S(1)} %get-tuple-element.42.refs_0_), channel_id=1, source_target_pairs={{8,0},{16,8},{24,16},{0,24},{9,1},{17,9},{25,17},{1,25},{10,2},{18... | collective-permute-start | bytes 233480 | tf_op jit(solution)/shard_map/ppermute | solution.py:636
  17.5 1.7 %collective-permute-done.8.refs_3_ = f32[152,128]{1,0:T(8,128)S(1)} collective-permute-done((f32[152,128]{1,0:T(8,128)S(1)}, f32[152,128]{1,0:T(8,128)S(1)}, u32[]{:S(2)}, u32[]{:S(2)}) %collective-permute-start.8) | collective-permute-done | bytes 77856 | tf_op jit(solution)/shard_map/ppermute | solution.py:636
  19.1 2.4 %collective-permute-done.7.refs_2_ = f32[152,128]{1,0:T(8,128)S(1)} collective-permute-done((f32[152,128]{1,0:T(8,128)S(1)}, f32[152,128]{1,0:T(8,128)S(1)}, u32[]{:S(2)}, u32[]{:S(2)}) %collective-permute-start.7) | collective-permute-done | bytes 77856 | tf_op jit(solution)/shard_map/ppermute | solution.py:636
  21.6 0.0 collective-permute-done.6.refs_1_
  21.6 0.4 %shard_map.114 = (f32[328,128]{1,0:T(8,128)S(1)}, f32[128,128]{1,0:T(8,128)S(1)}, f32[64,128]{1,0:T(8,128)S(1)}, f32[8,128]{1,0:T(8,128)S(1)}) custom-call(f32[152,128]{1,0:T(8,128)S(1)} %get-tuple-element.42.refs_0_, f32[152,128]{1,0:T(8,128)S(1)} %collective-permute-done.6.refs_1_, f32[152,128]{1,0:T(8,128)S(1)} %collective-permute-done.7.refs_2_, ...), custom_call_target="tpu_custom_call" | custom-call | flops 4000000000 | bytes 581632 | tf_op jit(solution)/shard_map/pallas_call | solution.py:55
  22.0 0.1 collective-permute-start.10
  22.1 1.7 %collective-permute-start.9 = (f32[328,128]{1,0:T(8,128)S(1)}, f32[328,128]{1,0:T(8,128)S(1)}, u32[]{:S(2)}, u32[]{:S(2)}) collective-permute-start(f32[328,128]{1,0:T(8,128)S(1)} %get-tuple-element.44.own_ref), channel_id=1, source_target_pairs={{0,1},{1,0},{2,3},{3,2},{4,5},{5,4},{6,7},{7,6},{8,9},{9,8},{10,11... | collective-permute-start | bytes 503816 | tf_op jit(solution)/shard_map/ppermute | solution.py:509
  23.7 1.4 %collective-permute-start.11 = (f32[128,128]{1,0:T(8,128)S(1)}, f32[128,128]{1,0:T(8,128)S(1)}, u32[]{:S(2)}, u32[]{:S(2)}) collective-permute-start(f32[128,128]{1,0:T(8,128)S(1)} %get-tuple-element.45), channel_id=1, source_target_pairs={{2,0},{3,1},{4,2},{5,3},{6,4},{7,5},{0,6},{1,7},{10,8},{11,9},{12,... | collective-permute-start | bytes 196616 | tf_op jit(solution)/shard_map/ppermute | solution.py:648
  25.1 4.2 %collective-permute-done.11.far_ref = f32[128,128]{1,0:T(8,128)S(1)} collective-permute-done((f32[128,128]{1,0:T(8,128)S(1)}, f32[128,128]{1,0:T(8,128)S(1)}, u32[]{:S(2)}, u32[]{:S(2)}) %collective-permute-start.11) | collective-permute-done | bytes 65568 | tf_op jit(solution)/shard_map/ppermute | solution.py:648
  29.3 0.3 collective-permute-done.10.outer_ref
  29.5 1.0 %shard_map.115 = (f32[8,128]{1,0:T(8,128)S(1)}, f32[64,128]{1,0:T(8,128)S(1)}, f32[64,128]{1,0:T(8,128)S(1)}) custom-call(f32[328,128]{1,0:T(8,128)S(1)} %get-tuple-element.44.own_ref, f32[328,128]{1,0:T(8,128)S(1)} %collective-permute-done.9.inner_ref, f32[328,128]{1,0:T(8,128)S(1)} %collective-permute-done.10.outer_ref, ...), custom_call_target="tpu_custom_call" | custom-call | flops 4000000000 | bytes 643072 | tf_op jit(solution)/shard_map/pallas_call | solution.py:55
  30.5 0.5 %collective-permute-start.12 = (f32[8,128]{1,0:T(8,128)S(1)}, f32[8,128]{1,0:T(8,128)S(1)}, u32[]{:S(2)}, u32[]{:S(2)}) collective-permute-start(f32[8,128]{1,0:T(8,128)S(1)} %get-tuple-element.52), channel_id=1, source_target_pairs={{0,1},{1,0},{2,3},{3,2},{4,5},{5,4},{6,7},{7,6},{8,9},{9,8},{10,11... | collective-permute-start | bytes 12296 | tf_op jit(solution)/shard_map/ppermute | solution.py:509
  31.1 0.8 %collective-permute-done.12 = f32[8,128]{1,0:T(8,128)S(1)} collective-permute-done((f32[8,128]{1,0:T(8,128)S(1)}, f32[8,128]{1,0:T(8,128)S(1)}, u32[]{:S(2)}, u32[]{:S(2)}) %collective-permute-start.12) | collective-permute-done | bytes 4128 | tf_op jit(solution)/shard_map/ppermute | solution.py:509
  31.9 1.4 %collective-permute-start.14 = (f32[8,128]{1,0:T(8,128)S(1)}, f32[8,128]{1,0:T(8,128)S(1)}, u32[]{:S(2)}, u32[]{:S(2)}) collective-permute-start(f32[8,128]{1,0:T(8,128)S(1)} %add.3.refs_0_), channel_id=1, source_target_pairs={{0,6},{1,7},{2,4},{3,5},{4,2},{5,3},{6,0},{7,1},{8,14},{9,15},{10,... | collective-permute-start | bytes 12296 | tf_op jit(solution)/shard_map/ppermute | solution.py:509
  33.3 1.9 %collective-permute-start.13 = (f32[8,128]{1,0:T(8,128)S(1)}, f32[8,128]{1,0:T(8,128)S(1)}, u32[]{:S(2)}, u32[]{:S(2)}) collective-permute-start(f32[8,128]{1,0:T(8,128)S(1)} %add.3.refs_0_), channel_id=1, source_target_pairs={{0,2},{1,5},{2,0},{3,7},{4,6},{5,1},{6,4},{7,3},{8,10},{9,13},{10,... | collective-permute-start | bytes 12296 | tf_op jit(solution)/shard_map/ppermute | solution.py:528
  35.1 1.3 %collective-permute-done.14.refs_2_ = f32[8,128]{1,0:T(8,128)S(1)} collective-permute-done((f32[8,128]{1,0:T(8,128)S(1)}, f32[8,128]{1,0:T(8,128)S(1)}, u32[]{:S(2)}, u32[]{:S(2)}) %collective-permute-start.14) | collective-permute-done | bytes 4128 | tf_op jit(solution)/shard_map/ppermute | solution.py:509
  36.4 0.5 %collective-permute-done.13.refs_1_ = f32[8,128]{1,0:T(8,128)S(1)} collective-permute-done((f32[8,128]{1,0:T(8,128)S(1)}, f32[8,128]{1,0:T(8,128)S(1)}, u32[]{:S(2)}, u32[]{:S(2)}) %collective-permute-start.13) | collective-permute-done | bytes 4128 | tf_op jit(solution)/shard_map/ppermute | solution.py:528
  36.9 0.4 %shard_map.116 = (f32[2,128,128]{2,1,0:T(8,128)S(1)}, f32[2,128,128]{2,1,0:T(8,128)S(1)}, f32[2,128,128]{2,1,0:T(8,128)S(1)}) custom-call(f32[2,128,128]{2,1,0:T(8,128)S(1)} %get-tuple-element.41.precond_ref, f32[2,128,128]{2,1,0:T(8,128)S(1)} %get-tuple-element.34.inverse_ref, f32[64,128]{1,0:T(8,128)S(1)} %get-tuple-element.43.flow_ref, ...), custom_call_target="tpu_custom_call" | custom-call | flops 4000000000 | bytes 753664 | tf_op jit(solution)/shard_map/pallas_call | solution.py:55
  37.3 0.7 %collective-permute-done.15.refs_3_ = f32[8,128]{1,0:T(8,128)S(1)} collective-permute-done((f32[8,128]{1,0:T(8,128)S(1)}, f32[8,128]{1,0:T(8,128)S(1)}, u32[]{:S(2)}, u32[]{:S(2)}) %collective-permute-start.15) | collective-permute-done | bytes 4128 | tf_op jit(solution)/shard_map/ppermute | solution.py:509
  38.0 0.7 %shard_map.117 = f32[2,128,128]{2,1,0:T(8,128)} custom-call(f32[2,128,128]{2,1,0:T(8,128)S(1)} %bitcast.21, f32[2,128,128]{2,1,0:T(8,128)S(1)} %get-tuple-element.49.z0_ref, f32[2,128,128]{2,1,0:T(8,128)S(1)} %get-tuple-element.50.z1_ref, f32[2,128,128]{2,1,0:T(8,128)S(1)} %get-tuple-element.51.z2_ref, f32[8,128]{1,0:T(8,128)S(1)} %add.3.refs_0_, ...), custom_call_target="tpu_custom_call" | custom-call | flops 4000000000 | bytes 671744 | tf_op jit(solution)/shard_map/pallas_call | solution.py:55
  (16 shorter events, 0.0 us)
Async XLA Ops:
  0.0 1.1 %copy-start.2 = (f32[1,2,128,128]{3,2,1,0:T(8,128)S(1)}, f32[1,2,128,128]{3,2,1,0:T(8,128)}, u32[]{:S(2)}) copy-start(f32[1,2,128,128]{3,2,1,0:T(8,128)} %param.11) | copy-start | bytes 393220
  0.0 1.1 %copy-start.1 = (f32[1,2,128,128]{3,2,1,0:T(8,128)S(1)}, f32[1,2,128,128]{3,2,1,0:T(8,128)}, u32[]{:S(2)}) copy-start(f32[1,2,128,128]{3,2,1,0:T(8,128)} %param.13) | copy-start | bytes 393220
  0.0 1.1 %copy-start = (f32[1,2,128,128]{3,2,1,0:T(8,128)S(1)}, f32[1,2,128,128]{3,2,1,0:T(8,128)}, u32[]{:S(2)}) copy-start(f32[1,2,128,128]{3,2,1,0:T(8,128)} %param.12) | copy-start | bytes 393220
  0.0 2.1 %collective-permute-start.2 = (s32[1,1,64]{2,1,0:T(1,128)}, s32[1,1,64]{2,1,0:T(1,128)S(1)}, u32[]{:S(2)}, u32[]{:S(2)}) collective-permute-start(s32[1,1,64]{2,1,0:T(1,128)} %param.16), channel_id=1, source_target_pairs={{0,1},{1,0},{2,3},{3,2},{4,5},{5,4},{6,7},{7,6},{8,9},{9,8},{10,11... | collective-permute-start | bytes 776 | tf_op jit(solution)/shard_map/ppermute | solution.py:509
  0.5 1.6 %collective-permute-start.1 = (f32[1,2,2,32]{3,2,1,0:T(2,128)}, f32[1,2,2,32]{3,2,1,0:T(2,128)S(1)}, u32[]{:S(2)}, u32[]{:S(2)}) collective-permute-start(f32[1,2,2,32]{3,2,1,0:T(2,128)} %param.15), channel_id=1, source_target_pairs={{0,1},{1,0},{2,3},{3,2},{4,5},{5,4},{6,7},{7,6},{8,9},{9,8},{10,11... | collective-permute-start | bytes 1544 | tf_op jit(solution)/shard_map/ppermute | solution.py:509
  0.6 1.6 %collective-permute-start = (f32[1,2,128,128]{3,2,1,0:T(8,128)}, f32[1,2,128,128]{3,2,1,0:T(8,128)S(1)}, u32[]{:S(2)}, u32[]{:S(2)}) collective-permute-start(f32[1,2,128,128]{3,2,1,0:T(8,128)} %param.11), channel_id=1, source_target_pairs={{0,1},{1,0},{2,3},{3,2},{4,5},{5,4},{6,7},{7,6},{8,9},{9,8},{10,11... | collective-permute-start | bytes 393224 | tf_op jit(solution)/shard_map/ppermute | solution.py:509
  1.0 0.7 %copy-start.5 = (s32[1,1,8,8]{3,2,1,0:T(8,128)S(1)}, s32[1,1,8,8]{3,2,1,0:T(8,128)}, u32[]{:S(2)}) copy-start(s32[1,1,8,8]{3,2,1,0:T(8,128)} %param.20) | copy-start | bytes 772
  1.0 0.7 %copy-start.6 = (f32[1,1,8,8]{3,2,1,0:T(8,128)S(1)}, f32[1,1,8,8]{3,2,1,0:T(8,128)}, u32[]{:S(2)}) copy-start(f32[1,1,8,8]{3,2,1,0:T(8,128)} %param.21) | copy-start | bytes 772
  1.0 0.7 %copy-start.7 = (f32[1,2,2,32]{3,2,1,0:T(2,128)S(1)}, f32[1,2,2,32]{3,2,1,0:T(2,128)}, u32[]{:S(2)}) copy-start(f32[1,2,2,32]{3,2,1,0:T(2,128)} %param.15) | copy-start | bytes 1540
  1.0 0.7 %copy-start.9 = (s32[1,1,8]{2,1,0:T(1,128)S(1)}, s32[1,1,8]{2,1,0:T(1,128)}, u32[]{:S(2)}) copy-start(s32[1,1,8]{2,1,0:T(1,128)} %param.18) | copy-start | bytes 100
  1.1 0.7 %copy-start.10 = (s32[1,1,64]{2,1,0:T(1,128)S(1)}, s32[1,1,64]{2,1,0:T(1,128)}, u32[]{:S(2)}) copy-start(s32[1,1,64]{2,1,0:T(1,128)} %param.16) | copy-start | bytes 772
  1.1 0.7 %copy-start.4 = (s32[1,1,8,8]{3,2,1,0:T(8,128)S(1)}, s32[1,1,8,8]{3,2,1,0:T(8,128)}, u32[]{:S(2)}) copy-start(s32[1,1,8,8]{3,2,1,0:T(8,128)} %param.19) | copy-start | bytes 772
  1.1 0.7 %copy-start.3 = (s32[1,1,8,8]{3,2,1,0:T(8,128)S(1)}, s32[1,1,8,8]{3,2,1,0:T(8,128)}, u32[]{:S(2)}) copy-start(s32[1,1,8,8]{3,2,1,0:T(8,128)} %param.17) | copy-start | bytes 772
  1.1 0.7 %copy-start.8 = (f32[1,2,128]{2,1,0:T(2,128)S(1)}, f32[1,2,128]{2,1,0:T(2,128)}, u32[]{:S(2)}) copy-start(f32[1,2,128]{2,1,0:T(2,128)} %param.14) | copy-start | bytes 3076
  2.3 7.0 %collective-permute-start.5 = (f32[168,128]{1,0:T(8,128)S(1)}, f32[168,128]{1,0:T(8,128)S(1)}, u32[]{:S(2)}, u32[]{:S(2)}) collective-permute-start(f32[168,128]{1,0:T(8,128)S(1)} %shard_map.111.after_ref.refs_0_), channel_id=1, source_target_pairs={{0,6},{1,7},{2,4},{3,5},{4,2},{5,3},{6,0},{7,1},{8,14},{9,15},{10,... | collective-permute-start | bytes 258056 | tf_op jit(solution)/shard_map/ppermute | solution.py:509
  6.2 4.7 %collective-permute-start.4 = (f32[168,128]{1,0:T(8,128)S(1)}, f32[168,128]{1,0:T(8,128)S(1)}, u32[]{:S(2)}, u32[]{:S(2)}) collective-permute-start(f32[168,128]{1,0:T(8,128)S(1)} %shard_map.111.after_ref.refs_0_), channel_id=1, source_target_pairs={{0,4},{1,5},{2,6},{3,7},{4,0},{5,1},{6,2},{7,3},{8,12},{9,13},{10,... | collective-permute-start | bytes 258056 | tf_op jit(solution)/shard_map/ppermute | solution.py:509
  6.7 4.5 %collective-permute-start.3 = (f32[168,128]{1,0:T(8,128)S(1)}, f32[168,128]{1,0:T(8,128)S(1)}, u32[]{:S(2)}, u32[]{:S(2)}) collective-permute-start(f32[168,128]{1,0:T(8,128)S(1)} %shard_map.111.after_ref.refs_0_), channel_id=1, source_target_pairs={{0,2},{1,3},{2,0},{3,1},{4,6},{5,7},{6,4},{7,5},{8,10},{9,11},{10,... | collective-permute-start | bytes 258056 | tf_op jit(solution)/shard_map/ppermute | solution.py:509
  11.9 7.2 %collective-permute-start.8 = (f32[152,128]{1,0:T(8,128)S(1)}, f32[152,128]{1,0:T(8,128)S(1)}, u32[]{:S(2)}, u32[]{:S(2)}) collective-permute-start(f32[152,128]{1,0:T(8,128)S(1)} %get-tuple-element.42.refs_0_), channel_id=1, source_target_pairs={{24,0},{0,8},{8,16},{16,24},{25,1},{1,9},{9,17},{17,25},{26,2},{2,... | collective-permute-start | bytes 233480 | tf_op jit(solution)/shard_map/ppermute | solution.py:636
  13.5 8.0 %collective-permute-start.7 = (f32[152,128]{1,0:T(8,128)S(1)}, f32[152,128]{1,0:T(8,128)S(1)}, u32[]{:S(2)}, u32[]{:S(2)}) collective-permute-start(f32[152,128]{1,0:T(8,128)S(1)} %get-tuple-element.42.refs_0_), channel_id=1, source_target_pairs={{16,0},{24,8},{0,16},{8,24},{17,1},{25,9},{1,17},{9,25},{18,2},{26... | collective-permute-start | bytes 233480 | tf_op jit(solution)/shard_map/ppermute | solution.py:636
  16.1 5.4 %collective-permute-start.6 = (f32[152,128]{1,0:T(8,128)S(1)}, f32[152,128]{1,0:T(8,128)S(1)}, u32[]{:S(2)}, u32[]{:S(2)}) collective-permute-start(f32[152,128]{1,0:T(8,128)S(1)} %get-tuple-element.42.refs_0_), channel_id=1, source_target_pairs={{8,0},{16,8},{24,16},{0,24},{9,1},{17,9},{25,17},{1,25},{10,2},{18... | collective-permute-start | bytes 233480 | tf_op jit(solution)/shard_map/ppermute | solution.py:636
  22.0 7.5 %collective-permute-start.10 = (f32[328,128]{1,0:T(8,128)S(1)}, f32[328,128]{1,0:T(8,128)S(1)}, u32[]{:S(2)}, u32[]{:S(2)}) collective-permute-start(f32[328,128]{1,0:T(8,128)S(1)} %get-tuple-element.44.own_ref), channel_id=1, source_target_pairs={{0,7},{1,2},{2,1},{3,4},{4,3},{5,6},{6,5},{7,0},{8,15},{9,10},{10,... | collective-permute-start | bytes 503816 | tf_op jit(solution)/shard_map/ppermute | solution.py:538
  22.1 7.5 %collective-permute-start.9 = (f32[328,128]{1,0:T(8,128)S(1)}, f32[328,128]{1,0:T(8,128)S(1)}, u32[]{:S(2)}, u32[]{:S(2)}) collective-permute-start(f32[328,128]{1,0:T(8,128)S(1)} %get-tuple-element.44.own_ref), channel_id=1, source_target_pairs={{0,1},{1,0},{2,3},{3,2},{4,5},{5,4},{6,7},{7,6},{8,9},{9,8},{10,11... | collective-permute-start | bytes 503816 | tf_op jit(solution)/shard_map/ppermute | solution.py:509
  23.7 5.5 %collective-permute-start.11 = (f32[128,128]{1,0:T(8,128)S(1)}, f32[128,128]{1,0:T(8,128)S(1)}, u32[]{:S(2)}, u32[]{:S(2)}) collective-permute-start(f32[128,128]{1,0:T(8,128)S(1)} %get-tuple-element.45), channel_id=1, source_target_pairs={{2,0},{3,1},{4,2},{5,3},{6,4},{7,5},{0,6},{1,7},{10,8},{11,9},{12,... | collective-permute-start | bytes 196616 | tf_op jit(solution)/shard_map/ppermute | solution.py:648
  30.5 1.4 %collective-permute-start.12 = (f32[8,128]{1,0:T(8,128)S(1)}, f32[8,128]{1,0:T(8,128)S(1)}, u32[]{:S(2)}, u32[]{:S(2)}) collective-permute-start(f32[8,128]{1,0:T(8,128)S(1)} %get-tuple-element.52), channel_id=1, source_target_pairs={{0,1},{1,0},{2,3},{3,2},{4,5},{5,4},{6,7},{7,6},{8,9},{9,8},{10,11... | collective-permute-start | bytes 12296 | tf_op jit(solution)/shard_map/ppermute | solution.py:509
  31.9 4.5 %collective-permute-start.14 = (f32[8,128]{1,0:T(8,128)S(1)}, f32[8,128]{1,0:T(8,128)S(1)}, u32[]{:S(2)}, u32[]{:S(2)}) collective-permute-start(f32[8,128]{1,0:T(8,128)S(1)} %add.3.refs_0_), channel_id=1, source_target_pairs={{0,6},{1,7},{2,4},{3,5},{4,2},{5,3},{6,0},{7,1},{8,14},{9,15},{10,... | collective-permute-start | bytes 12296 | tf_op jit(solution)/shard_map/ppermute | solution.py:509
  33.3 3.6 %collective-permute-start.13 = (f32[8,128]{1,0:T(8,128)S(1)}, f32[8,128]{1,0:T(8,128)S(1)}, u32[]{:S(2)}, u32[]{:S(2)}) collective-permute-start(f32[8,128]{1,0:T(8,128)S(1)} %add.3.refs_0_), channel_id=1, source_target_pairs={{0,2},{1,5},{2,0},{3,7},{4,6},{5,1},{6,4},{7,3},{8,10},{9,13},{10,... | collective-permute-start | bytes 12296 | tf_op jit(solution)/shard_map/ppermute | solution.py:528
  36.9 1.2 %collective-permute-start.15 = (f32[8,128]{1,0:T(8,128)S(1)}, f32[8,128]{1,0:T(8,128)S(1)}, u32[]{:S(2)}, u32[]{:S(2)}) collective-permute-start(f32[8,128]{1,0:T(8,128)S(1)} %collective-permute-done.13.refs_1_), channel_id=1, source_target_pairs={{0,1},{1,0},{2,3},{3,2},{4,5},{5,4},{6,7},{7,6},{8,9},{9,8},{10,11... | collective-permute-start | bytes 12296 | tf_op jit(solution)/shard_map/ppermute | solution.py:509

commit v9 on v7

--- a/solution.py
+++ b/solution.py
@@ -435,12 +435,16 @@
         for k in range(rows):
             row = []
             for d in devices:
+                inside = range(d * tiles, (d + 1) * tiles)
                 block = [
                     flows[k][c] if low <= c < high else jnp.zeros((edge, patterns), jnp.float32)
-                    for c in range(d * tiles, (d + 1) * tiles)
+                    for c in inside
                 ]
-                block = dot3(mats[k][d], jnp.concatenate(block, axis=0))
-                row += [block[t * edge : (t + 1) * edge] for t in range(tiles)]
+                used = [c - d * tiles for c in inside if low <= c < high]
+                place = slice(used[0] * edge, (used[-1] + 1) * edge)
+                block = dot3(mats[k][d][place], jnp.concatenate(block, axis=0))
+                found = [block[i * edge : (i + 1) * edge] for i in range(len(used))]
+                row += [None] * used[0] + found + [None] * (tiles - 1 - used[-1])
             out.append([None] * (devices[0] * tiles) + row)
         return out
 

time: 38.9 us -> 39 us (level)
  no operation moved by 1% of the time
where the time goes in v9:
time: 39 us; the launch traced here: 38.8 us
  starting transfers between devices  18 us (46%)
  waiting for transfers between devices  13.1 us (34%)
  Pallas kernels  6.19 us (16%)
  local copies, waits for them, and re-layouts  1.37 us (4%)
    ppermute x10, starting transfers between devices, other(): return lax.ppermute(block, axis, [(i, i ^ distance) for i in range(count)])  9.12 us
    pallas_call x9, Pallas kernels, run(): pl.pallas_call(kernel, out_shape=shapes, in_specs=[vmem] * len(args), out...  6.19 us
    ppermute x3, starting transfers between devices, local(): lax.ppermute(message, 'row', [((i + k) % rows, i) for i in range(rows)])  5.57 us
    ppermute x1, waiting for transfers between devices, local(): far = lax.ppermute(far, 'col', [((i + 2) % cols, i) for i in range(cols)])  4.18 us
    ppermute x10, waiting for transfers between devices, other(): return lax.ppermute(block, axis, [(i, i ^ distance) for i in range(count)])  4.13 us
    ppermute x3, waiting for transfers between devices, local(): lax.ppermute(message, 'row', [((i + k) % rows, i) for i in range(rows)])  4.08 us
    ppermute x1, starting transfers between devices, sum_stages(): brought = lax.ppermute(block, axis, route)  1.86 us
    unnamed x22, local copies, waits for them, and re-layouts  1.37 us
  transfers between devices with their start and end apart: 16, of which 11 were waited for; matrix products, arithmetic and copies ran while one was open for 0% of the time, Pallas kernels for 8%

profile of v9, /device:TPU:0, one launch (start us, length us, event | category | flops | bytes accessed | tf_op | source)
XLA Modules:
  0.0 38.8 jit_solution(3116652884803692460)
XLA Ops:
  0.0 0.5 %collective-permute-start.2 = (s32[1,1,64]{2,1,0:T(1,128)}, s32[1,1,64]{2,1,0:T(1,128)S(1)}, u32[]{:S(2)}, u32[]{:S(2)}) collective-permute-start(s32[1,1,64]{2,1,0:T(1,128)} %param.16), channel_id=1, source_target_pairs={{0,1},{1,0},{2,3},{3,2},{4,5},{5,4},{6,7},{7,6},{8,9},{9,8},{10,11... | collective-permute-start | bytes 776 | tf_op jit(solution)/shard_map/ppermute | solution.py:510
  0.5 0.1 collective-permute-start.1
  0.6 0.4 %collective-permute-start = (f32[1,2,128,128]{3,2,1,0:T(8,128)}, f32[1,2,128,128]{3,2,1,0:T(8,128)S(1)}, u32[]{:S(2)}, u32[]{:S(2)}) collective-permute-start(f32[1,2,128,128]{3,2,1,0:T(8,128)} %param.11), channel_id=1, source_target_pairs={{0,1},{1,0},{2,3},{3,2},{4,5},{5,4},{6,7},{7,6},{8,9},{9,8},{10,11... | collective-permute-start | bytes 393224 | tf_op jit(solution)/shard_map/ppermute | solution.py:510
  1.1 0.0 copy-start.4
  1.1 0.0 copy-start.3
  1.1 0.0 copy-start.9
  1.1 0.0 copy-start.10
  1.1 0.6 %copy-done.5 = s32[1,1,8,8]{3,2,1,0:T(8,128)S(1)} copy-done((s32[1,1,8,8]{3,2,1,0:T(8,128)S(1)}, s32[1,1,8,8]{3,2,1,0:T(8,128)}, u32[]{:S(2)}) %copy-start.5) | copy-done | bytes 280
  1.7 0.0 copy-done.6
  1.7 0.0 copy-done.7
  1.8 0.0 copy-done.4
  1.8 0.0 copy-done.3
  1.8 0.3 shard_map.110
  2.1 0.0 collective-permute-done.2
  2.1 0.1 collective-permute-done
  2.2 0.1 shard_map.111.after_ref.refs_0_
  2.3 3.9 %collective-permute-start.5 = (f32[168,128]{1,0:T(8,128)S(1)}, f32[168,128]{1,0:T(8,128)S(1)}, u32[]{:S(2)}, u32[]{:S(2)}) collective-permute-start(f32[168,128]{1,0:T(8,128)S(1)} %shard_map.111.after_ref.refs_0_), channel_id=1, source_target_pairs={{0,6},{1,7},{2,4},{3,5},{4,2},{5,3},{6,0},{7,1},{8,14},{9,15},{10,... | collective-permute-start | bytes 258056 | tf_op jit(solution)/shard_map/ppermute | solution.py:510
  6.2 0.5 %collective-permute-start.4 = (f32[168,128]{1,0:T(8,128)S(1)}, f32[168,128]{1,0:T(8,128)S(1)}, u32[]{:S(2)}, u32[]{:S(2)}) collective-permute-start(f32[168,128]{1,0:T(8,128)S(1)} %shard_map.111.after_ref.refs_0_), channel_id=1, source_target_pairs={{0,4},{1,5},{2,6},{3,7},{4,0},{5,1},{6,2},{7,3},{8,12},{9,13},{10,... | collective-permute-start | bytes 258056 | tf_op jit(solution)/shard_map/ppermute | solution.py:510
  6.7 0.1 collective-permute-start.3
  6.8 0.7 %copy-done.8 = f32[1,2,128]{2,1,0:T(2,128)S(1)} copy-done((f32[1,2,128]{2,1,0:T(2,128)S(1)}, f32[1,2,128]{2,1,0:T(2,128)}, u32[]{:S(2)}) %copy-start.8) | copy-done | bytes 1048
  7.5 2.5 %shard_map.112 = (f32[2,128,128]{2,1,0:T(8,128)S(1)}, f32[16,128]{1,0:T(8,128)S(1)}, f32[2,128,128]{2,1,0:T(8,128)S(1)}, f32[2,128,64]{2,1,0:T(8,128)S(1)}) custom-call(f32[128,128]{1,0:T(8,128)S(1)} %shard_map.109.eye_ref, f32[2,128,128]{2,1,0:T(8,128)S(1)} %bitcast.17, f32[2,128]{1,0:T(2,128)S(1)} %bitcast.31, ...), custom_call_target="tpu_custom_call" | custom-call | flops 4000000000 | bytes 816128 | tf_op jit(solution)/shard_map/pallas_call | solution.py:55
  10.0 0.0 collective-permute-done.5.refs_3_
  10.0 0.9 %collective-permute-done.4.refs_2_ = f32[168,128]{1,0:T(8,128)S(1)} collective-permute-done((f32[168,128]{1,0:T(8,128)S(1)}, f32[168,128]{1,0:T(8,128)S(1)}, u32[]{:S(2)}, u32[]{:S(2)}) %collective-permute-start.4) | collective-permute-done | bytes 86048 | tf_op jit(solution)/shard_map/ppermute | solution.py:510
  10.9 0.3 collective-permute-done.3.refs_1_
  11.2 0.7 %shard_map.113 = (f32[152,128]{1,0:T(8,128)S(1)}, f32[2,128,128]{2,1,0:T(8,128)S(1)}) custom-call(f32[2,128,128]{2,1,0:T(8,128)S(1)} %bitcast.20, f32[2,128,128]{2,1,0:T(8,128)S(1)} %bitcast.23, f32[2,2,32]{2,1,0:T(2,128)S(1)} %bitcast.30, f32[2,128,128]{2,1,0:T(8,128)S(1)} %get-tuple-element.32.inverse_ref, f32[16,128]{1,0:T(8,128)S(1)} %get-tuple-element.33.fold_ref, ...), custom_call_target="tpu_custom_call" | custom-call | flops 4000000000 | bytes 1532416 | tf_op jit(solution)/shard_map/pallas_call | solution.py:55
  11.9 1.6 %collective-permute-start.8 = (f32[152,128]{1,0:T(8,128)S(1)}, f32[152,128]{1,0:T(8,128)S(1)}, u32[]{:S(2)}, u32[]{:S(2)}) collective-permute-start(f32[152,128]{1,0:T(8,128)S(1)} %get-tuple-element.40.refs_0_), channel_id=1, source_target_pairs={{24,0},{0,8},{8,16},{16,24},{25,1},{1,9},{9,17},{17,25},{26,2},{2,... | collective-permute-start | bytes 233480 | tf_op jit(solution)/shard_map/ppermute | solution.py:635
  13.5 2.6 %collective-permute-start.7 = (f32[152,128]{1,0:T(8,128)S(1)}, f32[152,128]{1,0:T(8,128)S(1)}, u32[]{:S(2)}, u32[]{:S(2)}) collective-permute-start(f32[152,128]{1,0:T(8,128)S(1)} %get-tuple-element.40.refs_0_), channel_id=1, source_target_pairs={{16,0},{24,8},{0,16},{8,24},{17,1},{25,9},{1,17},{9,25},{18,2},{26... | collective-permute-start | bytes 233480 | tf_op jit(solution)/shard_map/ppermute | solution.py:635
  16.1 1.3 %collective-permute-start.6 = (f32[152,128]{1,0:T(8,128)S(1)}, f32[152,128]{1,0:T(8,128)S(1)}, u32[]{:S(2)}, u32[]{:S(2)}) collective-permute-start(f32[152,128]{1,0:T(8,128)S(1)} %get-tuple-element.40.refs_0_), channel_id=1, source_target_pairs={{8,0},{16,8},{24,16},{0,24},{9,1},{17,9},{25,17},{1,25},{10,2},{18... | collective-permute-start | bytes 233480 | tf_op jit(solution)/shard_map/ppermute | solution.py:635
  17.5 1.7 %collective-permute-done.8.refs_3_ = f32[152,128]{1,0:T(8,128)S(1)} collective-permute-done((f32[152,128]{1,0:T(8,128)S(1)}, f32[152,128]{1,0:T(8,128)S(1)}, u32[]{:S(2)}, u32[]{:S(2)}) %collective-permute-start.8) | collective-permute-done | bytes 77856 | tf_op jit(solution)/shard_map/ppermute | solution.py:635
  19.1 2.4 %collective-permute-done.7.refs_2_ = f32[152,128]{1,0:T(8,128)S(1)} collective-permute-done((f32[152,128]{1,0:T(8,128)S(1)}, f32[152,128]{1,0:T(8,128)S(1)}, u32[]{:S(2)}, u32[]{:S(2)}) %collective-permute-start.7) | collective-permute-done | bytes 77856 | tf_op jit(solution)/shard_map/ppermute | solution.py:635
  21.6 0.0 collective-permute-done.6.refs_1_
  21.6 0.4 %shard_map.114 = (f32[328,128]{1,0:T(8,128)S(1)}, f32[128,128]{1,0:T(8,128)S(1)}, f32[64,128]{1,0:T(8,128)S(1)}, f32[8,128]{1,0:T(8,128)S(1)}) custom-call(f32[152,128]{1,0:T(8,128)S(1)} %get-tuple-element.40.refs_0_, f32[152,128]{1,0:T(8,128)S(1)} %collective-permute-done.6.refs_1_, f32[152,128]{1,0:T(8,128)S(1)} %collective-permute-done.7.refs_2_, ...), custom_call_target="tpu_custom_call" | custom-call | flops 4000000000 | bytes 581632 | tf_op jit(solution)/shard_map/pallas_call | solution.py:55
  22.0 0.1 collective-permute-start.10
  22.1 1.7 %collective-permute-start.9 = (f32[328,128]{1,0:T(8,128)S(1)}, f32[328,128]{1,0:T(8,128)S(1)}, u32[]{:S(2)}, u32[]{:S(2)}) collective-permute-start(f32[328,128]{1,0:T(8,128)S(1)} %get-tuple-element.42.own_ref), channel_id=1, source_target_pairs={{0,1},{1,0},{2,3},{3,2},{4,5},{5,4},{6,7},{7,6},{8,9},{9,8},{10,11... | collective-permute-start | bytes 503816 | tf_op jit(solution)/shard_map/ppermute | solution.py:510
  23.7 1.4 %collective-permute-start.11 = (f32[128,128]{1,0:T(8,128)S(1)}, f32[128,128]{1,0:T(8,128)S(1)}, u32[]{:S(2)}, u32[]{:S(2)}) collective-permute-start(f32[128,128]{1,0:T(8,128)S(1)} %get-tuple-element.43), channel_id=1, source_target_pairs={{2,0},{3,1},{4,2},{5,3},{6,4},{7,5},{0,6},{1,7},{10,8},{11,9},{12,... | collective-permute-start | bytes 196616 | tf_op jit(solution)/shard_map/ppermute | solution.py:647
  25.1 4.2 %collective-permute-done.11.far_ref = f32[128,128]{1,0:T(8,128)S(1)} collective-permute-done((f32[128,128]{1,0:T(8,128)S(1)}, f32[128,128]{1,0:T(8,128)S(1)}, u32[]{:S(2)}, u32[]{:S(2)}) %collective-permute-start.11) | collective-permute-done | bytes 65568 | tf_op jit(solution)/shard_map/ppermute | solution.py:647
  29.3 0.3 collective-permute-done.10.outer_ref
  29.5 0.0 collective-permute-done.9.inner_ref
  29.5 1.0 %shard_map.115 = (f32[8,128]{1,0:T(8,128)S(1)}, f32[64,128]{1,0:T(8,128)S(1)}, f32[64,128]{1,0:T(8,128)S(1)}) custom-call(f32[328,128]{1,0:T(8,128)S(1)} %get-tuple-element.42.own_ref, f32[328,128]{1,0:T(8,128)S(1)} %collective-permute-done.9.inner_ref, f32[328,128]{1,0:T(8,128)S(1)} %collective-permute-done.10.outer_ref, ...), custom_call_target="tpu_custom_call" | custom-call | flops 4000000000 | bytes 643072 | tf_op jit(solution)/shard_map/pallas_call | solution.py:55
  30.6 0.5 %collective-permute-start.12 = (f32[8,128]{1,0:T(8,128)S(1)}, f32[8,128]{1,0:T(8,128)S(1)}, u32[]{:S(2)}, u32[]{:S(2)}) collective-permute-start(f32[8,128]{1,0:T(8,128)S(1)} %get-tuple-element.50), channel_id=1, source_target_pairs={{0,1},{1,0},{2,3},{3,2},{4,5},{5,4},{6,7},{7,6},{8,9},{9,8},{10,11... | collective-permute-start | bytes 12296 | tf_op jit(solution)/shard_map/ppermute | solution.py:510
  31.1 0.8 %collective-permute-done.12 = f32[8,128]{1,0:T(8,128)S(1)} collective-permute-done((f32[8,128]{1,0:T(8,128)S(1)}, f32[8,128]{1,0:T(8,128)S(1)}, u32[]{:S(2)}, u32[]{:S(2)}) %collective-permute-start.12) | collective-permute-done | bytes 4128 | tf_op jit(solution)/shard_map/ppermute | solution.py:510
  31.9 1.4 %collective-permute-start.14 = (f32[8,128]{1,0:T(8,128)S(1)}, f32[8,128]{1,0:T(8,128)S(1)}, u32[]{:S(2)}, u32[]{:S(2)}) collective-permute-start(f32[8,128]{1,0:T(8,128)S(1)} %add.3.refs_0_), channel_id=1, source_target_pairs={{0,6},{1,7},{2,4},{3,5},{4,2},{5,3},{6,0},{7,1},{8,14},{9,15},{10,... | collective-permute-start | bytes 12296 | tf_op jit(solution)/shard_map/ppermute | solution.py:510
  33.3 1.9 %collective-permute-start.13 = (f32[8,128]{1,0:T(8,128)S(1)}, f32[8,128]{1,0:T(8,128)S(1)}, u32[]{:S(2)}, u32[]{:S(2)}) collective-permute-start(f32[8,128]{1,0:T(8,128)S(1)} %add.3.refs_0_), channel_id=1, source_target_pairs={{0,2},{1,5},{2,0},{3,7},{4,6},{5,1},{6,4},{7,3},{8,10},{9,13},{10,... | collective-permute-start | bytes 12296 | tf_op jit(solution)/shard_map/ppermute | solution.py:529
  35.1 1.3 %collective-permute-done.14.refs_2_ = f32[8,128]{1,0:T(8,128)S(1)} collective-permute-done((f32[8,128]{1,0:T(8,128)S(1)}, f32[8,128]{1,0:T(8,128)S(1)}, u32[]{:S(2)}, u32[]{:S(2)}) %collective-permute-start.14) | collective-permute-done | bytes 4128 | tf_op jit(solution)/shard_map/ppermute | solution.py:510
  36.4 0.5 %collective-permute-done.13.refs_1_ = f32[8,128]{1,0:T(8,128)S(1)} collective-permute-done((f32[8,128]{1,0:T(8,128)S(1)}, f32[8,128]{1,0:T(8,128)S(1)}, u32[]{:S(2)}, u32[]{:S(2)}) %collective-permute-start.13) | collective-permute-done | bytes 4128 | tf_op jit(solution)/shard_map/ppermute | solution.py:529
  36.9 0.4 %shard_map.116 = (f32[2,128,128]{2,1,0:T(8,128)S(1)}, f32[2,128,128]{2,1,0:T(8,128)S(1)}, f32[2,128,128]{2,1,0:T(8,128)S(1)}) custom-call(f32[2,128,128]{2,1,0:T(8,128)S(1)} %get-tuple-element.39.precond_ref, f32[2,128,128]{2,1,0:T(8,128)S(1)} %get-tuple-element.32.inverse_ref, f32[64,128]{1,0:T(8,128)S(1)} %get-tuple-element.41.flow_ref, ...), custom_call_target="tpu_custom_call" | custom-call | flops 4000000000 | bytes 753664 | tf_op jit(solution)/shard_map/pallas_call | solution.py:55
  37.4 0.7 %collective-permute-done.15.refs_3_ = f32[8,128]{1,0:T(8,128)S(1)} collective-permute-done((f32[8,128]{1,0:T(8,128)S(1)}, f32[8,128]{1,0:T(8,128)S(1)}, u32[]{:S(2)}, u32[]{:S(2)}) %collective-permute-start.15) | collective-permute-done | bytes 4128 | tf_op jit(solution)/shard_map/ppermute | solution.py:510
  38.1 0.7 %shard_map.117 = f32[2,128,128]{2,1,0:T(8,128)} custom-call(f32[2,128,128]{2,1,0:T(8,128)S(1)} %bitcast.21, f32[2,128,128]{2,1,0:T(8,128)S(1)} %get-tuple-element.47.z0_ref, f32[2,128,128]{2,1,0:T(8,128)S(1)} %get-tuple-element.48.z1_ref, f32[2,128,128]{2,1,0:T(8,128)S(1)} %get-tuple-element.49.z2_ref, f32[8,128]{1,0:T(8,128)S(1)} %add.3.refs_0_, ...), custom_call_target="tpu_custom_call" | custom-call | flops 4000000000 | bytes 671744 | tf_op jit(solution)/shard_map/pallas_call | solution.py:55
  (16 shorter events, 0.0 us)
Async XLA Ops:
  0.0 1.1 %copy-start.2 = (f32[1,2,128,128]{3,2,1,0:T(8,128)S(1)}, f32[1,2,128,128]{3,2,1,0:T(8,128)}, u32[]{:S(2)}) copy-start(f32[1,2,128,128]{3,2,1,0:T(8,128)} %param.11) | copy-start | bytes 393220
  0.0 1.1 %copy-start.1 = (f32[1,2,128,128]{3,2,1,0:T(8,128)S(1)}, f32[1,2,128,128]{3,2,1,0:T(8,128)}, u32[]{:S(2)}) copy-start(f32[1,2,128,128]{3,2,1,0:T(8,128)} %param.13) | copy-start | bytes 393220
  0.0 1.1 %copy-start = (f32[1,2,128,128]{3,2,1,0:T(8,128)S(1)}, f32[1,2,128,128]{3,2,1,0:T(8,128)}, u32[]{:S(2)}) copy-start(f32[1,2,128,128]{3,2,1,0:T(8,128)} %param.12) | copy-start | bytes 393220
  0.0 2.1 %collective-permute-start.2 = (s32[1,1,64]{2,1,0:T(1,128)}, s32[1,1,64]{2,1,0:T(1,128)S(1)}, u32[]{:S(2)}, u32[]{:S(2)}) collective-permute-start(s32[1,1,64]{2,1,0:T(1,128)} %param.16), channel_id=1, source_target_pairs={{0,1},{1,0},{2,3},{3,2},{4,5},{5,4},{6,7},{7,6},{8,9},{9,8},{10,11... | collective-permute-start | bytes 776 | tf_op jit(solution)/shard_map/ppermute | solution.py:510
  0.5 1.6 %collective-permute-start.1 = (f32[1,2,2,32]{3,2,1,0:T(2,128)}, f32[1,2,2,32]{3,2,1,0:T(2,128)S(1)}, u32[]{:S(2)}, u32[]{:S(2)}) collective-permute-start(f32[1,2,2,32]{3,2,1,0:T(2,128)} %param.15), channel_id=1, source_target_pairs={{0,1},{1,0},{2,3},{3,2},{4,5},{5,4},{6,7},{7,6},{8,9},{9,8},{10,11... | collective-permute-start | bytes 1544 | tf_op jit(solution)/shard_map/ppermute | solution.py:510
  0.6 1.6 %collective-permute-start = (f32[1,2,128,128]{3,2,1,0:T(8,128)}, f32[1,2,128,128]{3,2,1,0:T(8,128)S(1)}, u32[]{:S(2)}, u32[]{:S(2)}) collective-permute-start(f32[1,2,128,128]{3,2,1,0:T(8,128)} %param.11), channel_id=1, source_target_pairs={{0,1},{1,0},{2,3},{3,2},{4,5},{5,4},{6,7},{7,6},{8,9},{9,8},{10,11... | collective-permute-start | bytes 393224 | tf_op jit(solution)/shard_map/ppermute | solution.py:510
  1.0 0.7 %copy-start.5 = (s32[1,1,8,8]{3,2,1,0:T(8,128)S(1)}, s32[1,1,8,8]{3,2,1,0:T(8,128)}, u32[]{:S(2)}) copy-start(s32[1,1,8,8]{3,2,1,0:T(8,128)} %param.20) | copy-start | bytes 772
  1.0 0.7 %copy-start.6 = (f32[1,1,8,8]{3,2,1,0:T(8,128)S(1)}, f32[1,1,8,8]{3,2,1,0:T(8,128)}, u32[]{:S(2)}) copy-start(f32[1,1,8,8]{3,2,1,0:T(8,128)} %param.21) | copy-start | bytes 772
  1.0 0.7 %copy-start.7 = (f32[1,2,2,32]{3,2,1,0:T(2,128)S(1)}, f32[1,2,2,32]{3,2,1,0:T(2,128)}, u32[]{:S(2)}) copy-start(f32[1,2,2,32]{3,2,1,0:T(2,128)} %param.15) | copy-start | bytes 1540
  1.1 0.7 %copy-start.4 = (s32[1,1,8,8]{3,2,1,0:T(8,128)S(1)}, s32[1,1,8,8]{3,2,1,0:T(8,128)}, u32[]{:S(2)}) copy-start(s32[1,1,8,8]{3,2,1,0:T(8,128)} %param.19) | copy-start | bytes 772
  1.1 0.7 %copy-start.3 = (s32[1,1,8,8]{3,2,1,0:T(8,128)S(1)}, s32[1,1,8,8]{3,2,1,0:T(8,128)}, u32[]{:S(2)}) copy-start(s32[1,1,8,8]{3,2,1,0:T(8,128)} %param.17) | copy-start | bytes 772
  1.1 0.7 %copy-start.9 = (s32[1,1,8]{2,1,0:T(1,128)S(1)}, s32[1,1,8]{2,1,0:T(1,128)}, u32[]{:S(2)}) copy-start(s32[1,1,8]{2,1,0:T(1,128)} %param.18) | copy-start | bytes 100
  1.1 0.7 %copy-start.10 = (s32[1,1,64]{2,1,0:T(1,128)S(1)}, s32[1,1,64]{2,1,0:T(1,128)}, u32[]{:S(2)}) copy-start(s32[1,1,64]{2,1,0:T(1,128)} %param.16) | copy-start | bytes 772
  2.3 7.7 %collective-permute-start.5 = (f32[168,128]{1,0:T(8,128)S(1)}, f32[168,128]{1,0:T(8,128)S(1)}, u32[]{:S(2)}, u32[]{:S(2)}) collective-permute-start(f32[168,128]{1,0:T(8,128)S(1)} %shard_map.111.after_ref.refs_0_), channel_id=1, source_target_pairs={{0,6},{1,7},{2,4},{3,5},{4,2},{5,3},{6,0},{7,1},{8,14},{9,15},{10,... | collective-permute-start | bytes 258056 | tf_op jit(solution)/shard_map/ppermute | solution.py:510
  6.2 4.7 %collective-permute-start.4 = (f32[168,128]{1,0:T(8,128)S(1)}, f32[168,128]{1,0:T(8,128)S(1)}, u32[]{:S(2)}, u32[]{:S(2)}) collective-permute-start(f32[168,128]{1,0:T(8,128)S(1)} %shard_map.111.after_ref.refs_0_), channel_id=1, source_target_pairs={{0,4},{1,5},{2,6},{3,7},{4,0},{5,1},{6,2},{7,3},{8,12},{9,13},{10,... | collective-permute-start | bytes 258056 | tf_op jit(solution)/shard_map/ppermute | solution.py:510
  6.7 4.5 %collective-permute-start.3 = (f32[168,128]{1,0:T(8,128)S(1)}, f32[168,128]{1,0:T(8,128)S(1)}, u32[]{:S(2)}, u32[]{:S(2)}) collective-permute-start(f32[168,128]{1,0:T(8,128)S(1)} %shard_map.111.after_ref.refs_0_), channel_id=1, source_target_pairs={{0,2},{1,3},{2,0},{3,1},{4,6},{5,7},{6,4},{7,5},{8,10},{9,11},{10,... | collective-permute-start | bytes 258056 | tf_op jit(solution)/shard_map/ppermute | solution.py:510
  6.8 0.7 %copy-start.8 = (f32[1,2,128]{2,1,0:T(2,128)S(1)}, f32[1,2,128]{2,1,0:T(2,128)}, u32[]{:S(2)}) copy-start(f32[1,2,128]{2,1,0:T(2,128)} %param.14) | copy-start | bytes 3076
  11.9 7.2 %collective-permute-start.8 = (f32[152,128]{1,0:T(8,128)S(1)}, f32[152,128]{1,0:T(8,128)S(1)}, u32[]{:S(2)}, u32[]{:S(2)}) collective-permute-start(f32[152,128]{1,0:T(8,128)S(1)} %get-tuple-element.40.refs_0_), channel_id=1, source_target_pairs={{24,0},{0,8},{8,16},{16,24},{25,1},{1,9},{9,17},{17,25},{26,2},{2,... | collective-permute-start | bytes 233480 | tf_op jit(solution)/shard_map/ppermute | solution.py:635
  13.5 8.0 %collective-permute-start.7 = (f32[152,128]{1,0:T(8,128)S(1)}, f32[152,128]{1,0:T(8,128)S(1)}, u32[]{:S(2)}, u32[]{:S(2)}) collective-permute-start(f32[152,128]{1,0:T(8,128)S(1)} %get-tuple-element.40.refs_0_), channel_id=1, source_target_pairs={{16,0},{24,8},{0,16},{8,24},{17,1},{25,9},{1,17},{9,25},{18,2},{26... | collective-permute-start | bytes 233480 | tf_op jit(solution)/shard_map/ppermute | solution.py:635
  16.1 5.4 %collective-permute-start.6 = (f32[152,128]{1,0:T(8,128)S(1)}, f32[152,128]{1,0:T(8,128)S(1)}, u32[]{:S(2)}, u32[]{:S(2)}) collective-permute-start(f32[152,128]{1,0:T(8,128)S(1)} %get-tuple-element.40.refs_0_), channel_id=1, source_target_pairs={{8,0},{16,8},{24,16},{0,24},{9,1},{17,9},{25,17},{1,25},{10,2},{18... | collective-permute-start | bytes 233480 | tf_op jit(solution)/shard_map/ppermute | solution.py:635
  22.0 7.5 %collective-permute-start.10 = (f32[328,128]{1,0:T(8,128)S(1)}, f32[328,128]{1,0:T(8,128)S(1)}, u32[]{:S(2)}, u32[]{:S(2)}) collective-permute-start(f32[328,128]{1,0:T(8,128)S(1)} %get-tuple-element.42.own_ref), channel_id=1, source_target_pairs={{0,7},{1,2},{2,1},{3,4},{4,3},{5,6},{6,5},{7,0},{8,15},{9,10},{10,... | collective-permute-start | bytes 503816 | tf_op jit(solution)/shard_map/ppermute | solution.py:539
  22.1 7.5 %collective-permute-start.9 = (f32[328,128]{1,0:T(8,128)S(1)}, f32[328,128]{1,0:T(8,128)S(1)}, u32[]{:S(2)}, u32[]{:S(2)}) collective-permute-start(f32[328,128]{1,0:T(8,128)S(1)} %get-tuple-element.42.own_ref), channel_id=1, source_target_pairs={{0,1},{1,0},{2,3},{3,2},{4,5},{5,4},{6,7},{7,6},{8,9},{9,8},{10,11... | collective-permute-start | bytes 503816 | tf_op jit(solution)/shard_map/ppermute | solution.py:510
  23.7 5.5 %collective-permute-start.11 = (f32[128,128]{1,0:T(8,128)S(1)}, f32[128,128]{1,0:T(8,128)S(1)}, u32[]{:S(2)}, u32[]{:S(2)}) collective-permute-start(f32[128,128]{1,0:T(8,128)S(1)} %get-tuple-element.43), channel_id=1, source_target_pairs={{2,0},{3,1},{4,2},{5,3},{6,4},{7,5},{0,6},{1,7},{10,8},{11,9},{12,... | collective-permute-start | bytes 196616 | tf_op jit(solution)/shard_map/ppermute | solution.py:647
  30.6 1.3 %collective-permute-start.12 = (f32[8,128]{1,0:T(8,128)S(1)}, f32[8,128]{1,0:T(8,128)S(1)}, u32[]{:S(2)}, u32[]{:S(2)}) collective-permute-start(f32[8,128]{1,0:T(8,128)S(1)} %get-tuple-element.50), channel_id=1, source_target_pairs={{0,1},{1,0},{2,3},{3,2},{4,5},{5,4},{6,7},{7,6},{8,9},{9,8},{10,11... | collective-permute-start | bytes 12296 | tf_op jit(solution)/shard_map/ppermute | solution.py:510
  31.9 4.5 %collective-permute-start.14 = (f32[8,128]{1,0:T(8,128)S(1)}, f32[8,128]{1,0:T(8,128)S(1)}, u32[]{:S(2)}, u32[]{:S(2)}) collective-permute-start(f32[8,128]{1,0:T(8,128)S(1)} %add.3.refs_0_), channel_id=1, source_target_pairs={{0,6},{1,7},{2,4},{3,5},{4,2},{5,3},{6,0},{7,1},{8,14},{9,15},{10,... | collective-permute-start | bytes 12296 | tf_op jit(solution)/shard_map/ppermute | solution.py:510
  33.3 3.6 %collective-permute-start.13 = (f32[8,128]{1,0:T(8,128)S(1)}, f32[8,128]{1,0:T(8,128)S(1)}, u32[]{:S(2)}, u32[]{:S(2)}) collective-permute-start(f32[8,128]{1,0:T(8,128)S(1)} %add.3.refs_0_), channel_id=1, source_target_pairs={{0,2},{1,5},{2,0},{3,7},{4,6},{5,1},{6,4},{7,3},{8,10},{9,13},{10,... | collective-permute-start | bytes 12296 | tf_op jit(solution)/shard_map/ppermute | solution.py:529
  36.9 1.2 %collective-permute-start.15 = (f32[8,128]{1,0:T(8,128)S(1)}, f32[8,128]{1,0:T(8,128)S(1)}, u32[]{:S(2)}, u32[]{:S(2)}) collective-permute-start(f32[8,128]{1,0:T(8,128)S(1)} %collective-permute-done.13.refs_1_), channel_id=1, source_target_pairs={{0,1},{1,0},{2,3},{3,2},{4,5},{5,4},{6,7},{7,6},{8,9},{9,8},{10,11... | collective-permute-start | bytes 12296 | tf_op jit(solution)/shard_map/ppermute | solution.py:510
